TPU v7x, 32 devices: a whole 2x2x4 slice. The times are simulated.
32 devices in a mesh: tok: 8 (over z, x), ch: 4 (over y, core).
Axes of the slice: x: 2, y: 2, z: 4, core: 2. Of those that a mesh axis runs over, the one named last changes fastest.
Arguments:
- h_in: bfloat16 [16384, 768], P('tok'), may hold values from -6 to 6
- cotangent: bfloat16 [16384, 768], P('tok'), may hold values from -16 to 16
- carried: bfloat16 [2, 8, 256, 2, 768], P(None, 'tok', None, None, 'ch'), may hold values from -6 to 6
- centres: int32 [256], replicated, may hold values from 0 to 1023
- sticky: int32 [8, 3, 256], P('tok'), may hold values from 0 to 1023
- flags: int32 [8], P('tok'), may hold values 0 or 1
- w_qkv: float32 [2, 3, 768, 768], P(None, None, 'tok', 'ch'), may hold values from -0.21875 to 0.21875
- w_qkv_first: float32 [2, 3, 768, 768], P(None, None, 'tok', 'ch'), may hold values from -1 to 1
- w_qkv_second: float32 [2, 3, 768, 768], P(None, None, 'tok', 'ch'), may hold values from 0 to 1
- w_out_t: float32 [2, 768, 768], P(None, 'tok', 'ch'), may hold values from -3.5 to 3.5
- w_out_first: float32 [2, 768, 768], P(None, 'tok', 'ch'), may hold values from -1 to 1
- w_out_second: float32 [2, 768, 768], P(None, 'tok', 'ch'), may hold values from 0 to 1
- w_up: float32 [2, 768, 3072], P(None, 'tok', 'ch'), may hold values from -0.21875 to 0.21875
- w_up_first: float32 [2, 768, 3072], P(None, 'tok', 'ch'), may hold values from -1 to 1
- w_up_second: float32 [2, 768, 3072], P(None, 'tok', 'ch'), may hold values from 0 to 1
- w_down_t: float32 [2, 768, 3072], P(None, 'tok', 'ch'), may hold values from -1 to 1
- w_down_first: float32 [2, 768, 3072], P(None, 'tok', 'ch'), may hold values from -1 to 1
- w_down_second: float32 [2, 768, 3072], P(None, 'tok', 'ch'), may hold values from 0 to 1
- vec_d: float32 [2, 6, 768], replicated, may hold values from -3 to 3
- vec_d_first: float32 [2, 6, 768], replicated, may hold values from -1 to 1
- vec_d_second: float32 [2, 6, 768], replicated, may hold values from 0 to 1
- vec_c: float32 [2, 6, 768], P(None, None, 'ch'), may hold values from -3 to 3
- vec_c_first: float32 [2, 6, 768], P(None, None, 'ch'), may hold values from -1 to 1
- vec_c_second: float32 [2, 6, 768], P(None, None, 'ch'), may hold values from 0 to 1
Outputs:
- activations: float32 [16384, 768], P('tok')
- input_grad: float32 [16384, 768], P('tok')
- grad_norm: float32 [], replicated
- new_w_qkv: float32 [2, 3, 768, 768], P(None, None, 'tok', 'ch')
- new_qkv_first: float32 [2, 3, 768, 768], P(None, None, 'tok', 'ch')
- new_qkv_second: float32 [2, 3, 768, 768], P(None, None, 'tok', 'ch')
- new_w_out: float32 [2, 768, 768], P(None, 'tok', 'ch')
- new_out_first: float32 [2, 768, 768], P(None, 'tok', 'ch')
- new_out_second: float32 [2, 768, 768], P(None, 'tok', 'ch')
- new_w_up: float32 [2, 768, 3072], P(None, 'tok', 'ch')
- new_up_first: float32 [2, 768, 3072], P(None, 'tok', 'ch')
- new_up_second: float32 [2, 768, 3072], P(None, 'tok', 'ch')
- new_w_down: float32 [2, 768, 3072], P(None, 'tok', 'ch')
- new_down_first: float32 [2, 768, 3072], P(None, 'tok', 'ch')
- new_down_second: float32 [2, 768, 3072], P(None, 'tok', 'ch')
- new_vec_d: float32 [2, 6, 768], replicated
- new_vec_d_first: float32 [2, 6, 768], replicated
- new_vec_d_second: float32 [2, 6, 768], replicated
- new_vec_c: float32 [2, 6, 768], P(None, None, 'ch')
- new_vec_c_first: float32 [2, 6, 768], P(None, None, 'ch')
- new_vec_c_second: float32 [2, 6, 768], P(None, None, 'ch')
All inputs are finite; a program needn't handle non-finite values. No bound on the sum of `flags` on one device may be relied on, other than what follows from the above.
Results may differ from a plain program's by a relative error of at most 0.02.
Values may be sent and summed in bfloat16 or wider, within the bound.
No kernel may reach another device: no remote copies, remote signals or barrier semaphores. Data moves between devices by JAX's collectives and lax.ppermute only.
A program may use at most 256 MiB of HBM per device.

v0:
```python
from functools import partial

import jax
import jax.numpy as jnp
from jax import lax
from jax.sharding import PartitionSpec as P

HEAD_DIM = 64
BASIS = 256
SAMPLES = 256
SEG = 512
SEGS = 4
CRES = 1024
LAYERS = 2
STEP = 10


PRECISE = lax.Precision.HIGHEST
STICKY_RATIO = 0.5
RIDGE_WEIGHT = 0.5
BASIS_WIDTH = 0.01
NORM_EPS = 1e-05
CLIP_LIMIT = 1.0
FIRST_DECAY = 0.9
SECOND_DECAY = 0.95
ADAM_EPS = 1e-08
WEIGHT_DECAY = 0.1
RATE_QKV = 0.05
RATE_OUT = 0.5
RATE_UP = 0.05
RATE_DOWN = 0.03
RATE_VECTOR = 0.5
MASKED = -1e30


def layer_norm(inputs, gain_vec, shift_vec):
    mean_row = jnp.mean(inputs, axis=-1, keepdims=True)
    centred = inputs - mean_row
    variance = jnp.mean(centred * centred, axis=-1, keepdims=True)
    return centred * lax.rsqrt(variance + NORM_EPS) * gain_vec + shift_vec


def basis_table(centres, times):
    middle = (centres.astype(jnp.float32) + 0.5) / CRES
    offset = (times[None, :] - middle[:, None]) / BASIS_WIDTH
    return jnp.exp(-0.5 * offset * offset)


def gram_tables(centres, sticky):
    token_times = (
        STICKY_RATIO + (1.0 - STICKY_RATIO) * (jnp.arange(SEG).astype(jnp.float32) + 0.5) / SEG
    )
    token_basis = basis_table(centres, token_times)
    places = (sticky.astype(jnp.float32) + 0.5) / CRES
    old_basis = jax.vmap(partial(basis_table, centres))(places)
    new_basis = jax.vmap(partial(basis_table, centres))(STICKY_RATIO * places)
    design = jnp.concatenate(
        [new_basis, jnp.broadcast_to(token_basis, (places.shape[0],) + token_basis.shape)], axis=2
    )
    gram = jnp.einsum("snl,sml->snm", design, design, precision=PRECISE) + RIDGE_WEIGHT * jnp.eye(
        BASIS, dtype=jnp.float32
    )
    factor_lower = jnp.linalg.cholesky(gram)
    identity = jnp.broadcast_to(jnp.eye(BASIS, dtype=jnp.float32), gram.shape)
    inverse_factor = jax.scipy.linalg.solve_triangular(factor_lower, identity, lower=True)
    inverse = jnp.einsum("sln,slm->snm", inverse_factor, inverse_factor, precision=PRECISE)
    return (old_basis, design, inverse)


def adamw(weight, first, second, grad, rate, decay):
    first_new = FIRST_DECAY * first + (1.0 - FIRST_DECAY) * grad
    second_new = SECOND_DECAY * second + (1.0 - SECOND_DECAY) * grad * grad
    first_hat = first_new / (1.0 - FIRST_DECAY**STEP)
    second_hat = second_new / (1.0 - SECOND_DECAY**STEP)
    weight_new = weight * (1.0 - rate * decay) - rate * first_hat / (
        jnp.sqrt(second_hat) + ADAM_EPS
    )
    return (weight_new, first_new, second_new)


def sum_branch(partial_sum):
    return lax.psum(partial_sum.astype(jnp.bfloat16), "ch").astype(jnp.float32)


def sum_back(partial_grad):
    return lax.psum(partial_grad.astype(jnp.bfloat16), "ch").astype(jnp.float32)


def allowed_mask(flags, segment):
    row_index = jnp.arange(SEG)[:, None]
    col_index = jnp.arange(SEG + BASIS)[None, :]
    local_visible = (col_index < SEG) & (col_index <= row_index)
    memory_on = (flags > 0) | (segment > 0)
    memory_visible = (col_index >= SEG)[None] & memory_on[:, None, None]
    return (local_visible[None] | memory_visible)[:, None]


def scores_of(query_block, key_cat, allowed):
    raw_scores = jnp.einsum(
        "qihe,qjhe->qhij", query_block, key_cat, preferred_element_type=jnp.float32
    ) * HEAD_DIM ** (-0.5)
    return jnp.where(allowed, raw_scores, MASKED)


def memory_forward(key_rows, values, carried_start, tables, seq_count):
    old_basis, design, inverse = tables
    local_width = key_rows.shape[1]
    signal = (
        jnp.stack([key_rows, values], axis=1)
        .astype(jnp.float32)
        .reshape(seq_count, SEGS, SEG, 2 * local_width)
    )
    current = carried_start
    collected = [current]
    for segment in range(1, SEGS):
        sampled = jnp.einsum("qnp,qnc->qpc", old_basis[:, segment - 1], current, precision=PRECISE)
        stacked = jnp.concatenate([sampled, signal[:, segment - 1]], axis=1)
        fitted = jnp.einsum("qnl,qlc->qnc", design[:, segment - 1], stacked, precision=PRECISE)
        current = jnp.einsum("qmn,qnc->qmc", inverse[:, segment - 1], fitted, precision=PRECISE)
        collected.append(current)
    return jnp.stack(collected, axis=1)


def attention_forward(queries, key_rows, values, memory, flags, seq_count, head_count):
    block_shape = (seq_count, SEGS, SEG, head_count, HEAD_DIM)
    query_five = queries.reshape(block_shape)
    key_five = key_rows.reshape(block_shape)
    value_five = values.reshape(block_shape)
    outputs = []
    log_totals = []
    for segment in range(SEGS):
        key_cat = jnp.concatenate([key_five[:, segment], memory[:, segment, :, 0]], axis=1)
        value_cat = jnp.concatenate([value_five[:, segment], memory[:, segment, :, 1]], axis=1)
        scores = scores_of(query_five[:, segment], key_cat, allowed_mask(flags, segment))
        row_max = jnp.max(scores, axis=-1, keepdims=True)
        log_total = row_max + jnp.log(jnp.sum(jnp.exp(scores - row_max), axis=-1, keepdims=True))
        probabilities = jnp.exp(scores - log_total).astype(jnp.bfloat16)
        outputs.append(
            jnp.einsum(
                "qhij,qjhe->qihe", probabilities, value_cat, preferred_element_type=jnp.float32
            )
        )
        log_totals.append(log_total)
    attended = (
        jnp.stack(outputs, axis=1)
        .reshape(seq_count * SEGS * SEG, head_count * HEAD_DIM)
        .astype(jnp.bfloat16)
    )
    return (attended, log_totals)


def attention_backward(
    queries,
    key_rows,
    values,
    memory,
    log_totals,
    attended_grad,
    flags,
    tables,
    seq_count,
    head_count,
):
    old_basis, design, inverse = tables
    local_width = head_count * HEAD_DIM
    block_shape = (seq_count, SEGS, SEG, head_count, HEAD_DIM)
    query_five = queries.reshape(block_shape)
    key_five = key_rows.reshape(block_shape)
    value_five = values.reshape(block_shape)
    grad_five = attended_grad.reshape(block_shape)
    score_scale = HEAD_DIM ** (-0.5)
    query_parts = []
    key_parts = []
    value_parts = []
    memory_grads = []
    for segment in range(SEGS):
        key_cat = jnp.concatenate([key_five[:, segment], memory[:, segment, :, 0]], axis=1)
        value_cat = jnp.concatenate([value_five[:, segment], memory[:, segment, :, 1]], axis=1)
        scores = scores_of(query_five[:, segment], key_cat, allowed_mask(flags, segment))
        probabilities = jnp.exp(scores - log_totals[segment])
        out_grad = grad_five[:, segment]
        prob_grad = jnp.einsum(
            "qihe,qjhe->qhij", out_grad, value_cat, preferred_element_type=jnp.float32
        )
        value_cat_grad = jnp.einsum(
            "qhij,qihe->qjhe",
            probabilities.astype(jnp.bfloat16),
            out_grad,
            preferred_element_type=jnp.float32,
        )
        row_dots = jnp.sum(probabilities * prob_grad, axis=-1, keepdims=True)
        score_grad = (probabilities * (prob_grad - row_dots)).astype(jnp.bfloat16)
        query_parts.append(
            jnp.einsum("qhij,qjhe->qihe", score_grad, key_cat, preferred_element_type=jnp.float32)
            * score_scale
        )
        key_cat_grad = (
            jnp.einsum(
                "qhij,qihe->qjhe",
                score_grad,
                query_five[:, segment],
                preferred_element_type=jnp.float32,
            )
            * score_scale
        )
        key_parts.append(key_cat_grad[:, :SEG])
        value_parts.append(value_cat_grad[:, :SEG])
        memory_grads.append(
            jnp.stack([key_cat_grad[:, SEG:], value_cat_grad[:, SEG:]], axis=2).reshape(
                seq_count, BASIS, 2 * local_width
            )
        )
    signal_grads = [
        jnp.zeros((seq_count, SEG, 2 * local_width), jnp.float32) for segment in range(SEGS)
    ]
    carry_grad = memory_grads[SEGS - 1]
    for segment in range(SEGS - 1, 0, -1):
        fitted_grad = jnp.einsum(
            "qmn,qmc->qnc", inverse[:, segment - 1], carry_grad, precision=PRECISE
        )
        stacked_grad = jnp.einsum(
            "qnl,qnc->qlc", design[:, segment - 1], fitted_grad, precision=PRECISE
        )
        signal_grads[segment - 1] = stacked_grad[:, SAMPLES:]
        carry_grad = memory_grads[segment - 1] + jnp.einsum(
            "qnp,qpc->qnc", old_basis[:, segment - 1], stacked_grad[:, :SAMPLES], precision=PRECISE
        )
    total_rows = seq_count * SEGS * SEG
    signal_all = jnp.stack(signal_grads, axis=1).reshape(total_rows, 2, local_width)
    query_grad = jnp.stack(query_parts, axis=1).reshape(total_rows, local_width)
    key_grad = jnp.stack(key_parts, axis=1).reshape(total_rows, local_width) + signal_all[:, 0]
    value_grad = jnp.stack(value_parts, axis=1).reshape(total_rows, local_width) + signal_all[:, 1]
    return (query_grad, key_grad, value_grad)


def shards(
    h_in,
    cotangent,
    carried,
    centres,
    sticky,
    flags,
    w_qkv,
    w_qkv_first,
    w_qkv_second,
    w_out_t,
    w_out_first,
    w_out_second,
    w_up,
    w_up_first,
    w_up_second,
    w_down_t,
    w_down_first,
    w_down_second,
    vec_d,
    vec_d_first,
    vec_d_second,
    vec_c,
    vec_c_first,
    vec_c_second,
):
    tok_count = lax.axis_size("tok")
    ch_count = lax.axis_size("ch")
    tables = jax.vmap(partial(gram_tables, centres))(sticky)
    seq_count = sticky.shape[0]
    local_width = w_qkv.shape[3]
    head_count = local_width // HEAD_DIM
    flag_float = flags.astype(jnp.float32)
    stream = h_in.astype(jnp.float32)
    saved = []
    for layer_index in range(LAYERS):
        matrices = (
            lax.all_gather(w_qkv[layer_index].astype(jnp.bfloat16), "tok", axis=1, tiled=True),
            lax.all_gather(w_out_t[layer_index].astype(jnp.bfloat16), "tok", axis=0, tiled=True),
            lax.all_gather(w_up[layer_index].astype(jnp.bfloat16), "tok", axis=0, tiled=True),
            lax.all_gather(w_down_t[layer_index].astype(jnp.bfloat16), "tok", axis=0, tiled=True),
        )
        gain_rows = vec_d[layer_index]
        biases = vec_c[layer_index]
        normed = layer_norm(stream, gain_rows[0], gain_rows[1]).astype(jnp.bfloat16)
        projected = jnp.einsum(
            "td,kdc->ktc", normed, matrices[0], preferred_element_type=jnp.float32
        )
        queries = (projected[0] + biases[0]).astype(jnp.bfloat16)
        key_rows = projected[1].astype(jnp.bfloat16)
        values = (projected[2] + biases[1]).astype(jnp.bfloat16)
        carried_start = (
            carried[layer_index].astype(jnp.float32).reshape(seq_count, BASIS, 2 * local_width)
            * flag_float[:, None, None]
        )
        coefficients = memory_forward(key_rows, values, carried_start, tables, seq_count)
        memory = coefficients.astype(jnp.bfloat16).reshape(
            seq_count, SEGS, BASIS, 2, head_count, HEAD_DIM
        )
        attended, log_totals = attention_forward(
            queries, key_rows, values, memory, flags, seq_count, head_count
        )
        branch_part = jnp.einsum(
            "tc,dc->td", attended, matrices[1], preferred_element_type=jnp.float32
        )
        branch = sum_branch(branch_part)
        middle = stream + (branch + gain_rows[4])
        normed_own = layer_norm(middle, gain_rows[2], gain_rows[3]).astype(jnp.bfloat16)
        normed_two = normed_own
        up_bias = biases[2:6].T.reshape(-1)
        hidden = (
            jnp.einsum("td,df->tf", normed_two, matrices[2], preferred_element_type=jnp.float32)
            + up_bias
        )
        active = jax.nn.gelu(hidden, approximate=True).astype(jnp.bfloat16)
        mixed_part = jnp.einsum(
            "tf,df->td", active, matrices[3], preferred_element_type=jnp.float32
        )
        mixed_out = sum_branch(mixed_part)
        saved.append(
            (
                stream,
                matrices,
                normed,
                queries,
                key_rows,
                values,
                memory,
                log_totals,
                attended,
                middle,
                normed_two,
                hidden,
                active,
            )
        )
        stream = middle + (mixed_out + gain_rows[5])
    activations = stream
    stream_grad = cotangent.astype(jnp.float32)
    layer_grads = [None] * LAYERS
    vector_d = [None] * LAYERS
    vector_c = [None] * LAYERS
    for layer_index in reversed(range(LAYERS)):
        (
            stream,
            matrices,
            normed,
            queries,
            key_rows,
            values,
            memory,
            log_totals,
            attended,
            middle,
            normed_two,
            hidden,
            active,
        ) = saved[layer_index]
        gain_rows = vec_d[layer_index]
        down_own = stream_grad.astype(jnp.bfloat16)
        grad_down = jnp.einsum("td,tf->df", down_own, active, preferred_element_type=jnp.float32)
        grad_down_bias = jnp.sum(down_own.astype(jnp.float32), axis=0)
        active_grad = jnp.einsum(
            "td,df->tf", down_own, matrices[3], preferred_element_type=jnp.float32
        )
        unused_value, gelu_back = jax.vjp(partial(jax.nn.gelu, approximate=True), hidden)
        hidden_grad = gelu_back(active_grad)[0].astype(jnp.bfloat16)
        grad_up = jnp.einsum(
            "td,tf->df", normed_two, hidden_grad, preferred_element_type=jnp.float32
        )
        grad_up_bias = jnp.sum(hidden_grad.astype(jnp.float32), axis=0).reshape(local_width, 4).T
        normed_two_part = jnp.einsum(
            "tf,df->td", hidden_grad, matrices[2], preferred_element_type=jnp.float32
        )
        normed_two_grad = sum_back(normed_two_part)
        unused_value, norm_two_back = jax.vjp(layer_norm, middle, gain_rows[2], gain_rows[3])
        middle_grad, grad_gain_two, grad_shift_two = norm_two_back(normed_two_grad)
        stream_grad = stream_grad + middle_grad
        branch_own = stream_grad.astype(jnp.bfloat16)
        grad_out = jnp.einsum("td,tc->dc", branch_own, attended, preferred_element_type=jnp.float32)
        grad_out_bias = jnp.sum(branch_own.astype(jnp.float32), axis=0)
        attended_grad = jnp.einsum(
            "td,dc->tc", branch_own, matrices[1], preferred_element_type=jnp.float32
        ).astype(jnp.bfloat16)
        query_grad, key_grad, value_grad = attention_backward(
            queries,
            key_rows,
            values,
            memory,
            log_totals,
            attended_grad,
            flags,
            tables,
            seq_count,
            head_count,
        )
        stacked = jnp.stack([query_grad, key_grad, value_grad]).astype(jnp.bfloat16)
        grad_qkv = jnp.einsum("td,ktc->kdc", normed, stacked, preferred_element_type=jnp.float32)
        grad_query_bias = jnp.sum(stacked[0].astype(jnp.float32), axis=0)
        grad_value_bias = jnp.sum(stacked[2].astype(jnp.float32), axis=0)
        normed_part = jnp.einsum(
            "ktc,kdc->td", stacked, matrices[0], preferred_element_type=jnp.float32
        )
        normed_grad = sum_back(normed_part)
        unused_value, norm_back = jax.vjp(layer_norm, stream, gain_rows[0], gain_rows[1])
        input_part, grad_gain_one, grad_shift_one = norm_back(normed_grad)
        stream_grad = stream_grad + input_part
        vector_d[layer_index] = jnp.stack(
            [
                grad_gain_one,
                grad_shift_one,
                grad_gain_two,
                grad_shift_two,
                grad_out_bias,
                grad_down_bias,
            ]
        )
        vector_c[layer_index] = jnp.concatenate(
            [grad_query_bias[None], grad_value_bias[None], grad_up_bias], axis=0
        )
        matrix_grads = (grad_qkv, grad_out, grad_up, grad_down)
        layer_grads[layer_index] = matrix_grads
    d_divisor = float(ch_count)
    stacked_grads = tuple(
        (
            jnp.stack([layer_grads[index_layer][member] for index_layer in range(LAYERS)])
            for member in range(4)
        )
    )
    reduced = (
        lax.psum_scatter(stacked_grads[0], "tok", scatter_dimension=2, tiled=True),
        lax.psum_scatter(stacked_grads[1], "tok", scatter_dimension=1, tiled=True),
        lax.psum_scatter(stacked_grads[2], "tok", scatter_dimension=1, tiled=True),
        lax.psum_scatter(stacked_grads[3], "tok", scatter_dimension=1, tiled=True),
    )
    vec_d_grad = jnp.stack(vector_d)
    vec_c_grad = jnp.stack(vector_c)
    matrix_square = reduced[0].sum() * 0.0
    for member in range(4):
        matrix_square = matrix_square + jnp.sum(reduced[member] * reduced[member])
    offset = lax.axis_index("ch") * local_width
    spread_c = lax.dynamic_update_slice_in_dim(
        jnp.zeros((LAYERS, 6, local_width * ch_count), jnp.float32), vec_c_grad, offset, axis=2
    )
    summed_d, summed_c = lax.psum((vec_d_grad, spread_c), ("tok", "ch"))
    vec_d_grad = summed_d / d_divisor
    vec_c_grad = lax.dynamic_slice_in_dim(summed_c, offset, local_width, axis=2)
    local_square = matrix_square + (
        jnp.sum(vec_d_grad * vec_d_grad) + jnp.sum(summed_c * summed_c)
    ) / (tok_count * ch_count)
    total_square = lax.psum(local_square, ("tok", "ch"))
    grad_norm = jnp.sqrt(total_square)
    factor = CLIP_LIMIT / jnp.maximum(grad_norm, CLIP_LIMIT)
    attention_update = adamw(
        w_qkv, w_qkv_first, w_qkv_second, reduced[0] * factor, RATE_QKV, WEIGHT_DECAY
    )
    output_update = adamw(
        w_out_t, w_out_first, w_out_second, reduced[1] * factor, RATE_OUT, WEIGHT_DECAY
    )
    expand_update = adamw(w_up, w_up_first, w_up_second, reduced[2] * factor, RATE_UP, WEIGHT_DECAY)
    reduce_update = adamw(
        w_down_t, w_down_first, w_down_second, reduced[3] * factor, RATE_DOWN, WEIGHT_DECAY
    )
    width_update = adamw(vec_d, vec_d_first, vec_d_second, vec_d_grad * factor, RATE_VECTOR, 0.0)
    channel_update = adamw(vec_c, vec_c_first, vec_c_second, vec_c_grad * factor, RATE_VECTOR, 0.0)
    return (
        activations,
        stream_grad,
        grad_norm,
        attention_update[0],
        attention_update[1],
        attention_update[2],
        output_update[0],
        output_update[1],
        output_update[2],
        expand_update[0],
        expand_update[1],
        expand_update[2],
        reduce_update[0],
        reduce_update[1],
        reduce_update[2],
        width_update[0],
        width_update[1],
        width_update[2],
        channel_update[0],
        channel_update[1],
        channel_update[2],
    )


def solution(mesh):
    placed = (
        P("tok", None),
        P("tok", None),
        P(None, "tok", None, None, "ch"),
        P(),
        P("tok", None, None),
        P("tok"),
        P(None, None, "tok", "ch"),
        P(None, None, "tok", "ch"),
        P(None, None, "tok", "ch"),
        P(None, "tok", "ch"),
        P(None, "tok", "ch"),
        P(None, "tok", "ch"),
        P(None, "tok", "ch"),
        P(None, "tok", "ch"),
        P(None, "tok", "ch"),
        P(None, "tok", "ch"),
        P(None, "tok", "ch"),
        P(None, "tok", "ch"),
        P(),
        P(),
        P(),
        P(None, None, "ch"),
        P(None, None, "ch"),
        P(None, None, "ch"),
    )
    return jax.shard_map(
        shards,
        mesh=mesh,
        in_specs=placed,
        out_specs=(
            P("tok", None),
            P("tok", None),
            P(),
            P(None, None, "tok", "ch"),
            P(None, None, "tok", "ch"),
            P(None, None, "tok", "ch"),
            P(None, "tok", "ch"),
            P(None, "tok", "ch"),
            P(None, "tok", "ch"),
            P(None, "tok", "ch"),
            P(None, "tok", "ch"),
            P(None, "tok", "ch"),
            P(None, "tok", "ch"),
            P(None, "tok", "ch"),
            P(None, "tok", "ch"),
            P(),
            P(),
            P(),
            P(None, None, "ch"),
            P(None, None, "ch"),
            P(None, None, "ch"),
        ),
        check_vma=False,
    )
```

profile of v0, /device:TPU:0, one launch (start us, length us, event | category | flops | bytes accessed | tf_op | source)
XLA Modules:
  0.0 1887.7 jit_solution(13986996880348880789)
XLA Ops:
  18.0 40.5 %all-gather = bf16[1,3,768,192]{3,1,0,2:T(4,128)(2,1)} all-gather(bf16[1,3,96,192]{3,1,0,2:T(4,128)(2,1)S(1)} %get-tuple-element.279), channel_id=2, replica_groups=mesh['tok'=8,'ch'=4] {'tok'}, dimensions={2}, use_global_device_ids=true | all-gather | bytes 995328 | tf_op jit(solution)/shard_map/all_gather | solution.py:273
  79.8 33.4 %all-gather.1 = bf16[1,768,192]{2,1,0:T(8,128)(2,1)} all-gather(bf16[1,96,192]{2,1,0:T(8,128)(2,1)} %get-tuple-element.304), channel_id=3, replica_groups=mesh['tok'=8,'ch'=4] {'tok'}, dimensions={1}, use_global_device_ids=true | all-gather | bytes 331776 | tf_op jit(solution)/shard_map/all_gather | solution.py:274
  135.0 36.0 %custom-call.17 = f32[1,3,128,128]{3,2,1,0:T(8,128)S(1)} custom-call(f32[1,3,128,128]{3,2,1,0:T(8,128)} %cholesky.125), custom_call_target="Cholesky" | custom-call | tf_op jit(solution)/shard_map/vmap(jit(cholesky))/cholesky | solution.py:63
  171.7 30.9 %custom-call.18 = f32[1,3,1,128,128]{3,4,2,1,0:T(8,128)} custom-call(f32[1,3,1,128,128]{4,3,2,1,0:T(8,128)} %select_bitcast_fusion), custom_call_target="InvertDiagBlocksLowerTriangular" | custom-call | tf_op jit(solution)/shard_map/vmap(jit(cholesky))/cholesky | solution.py:63
  207.8 37.0 %custom-call.19 = f32[1,3,128,128]{3,2,1,0:T(8,128)} custom-call(f32[1,3,128,128]{3,2,1,0:T(8,128)} %fusion.149), custom_call_target="Cholesky" | custom-call | tf_op jit(solution)/shard_map/vmap(jit(cholesky))/cholesky | solution.py:63
  248.9 7.3 while.1
  256.3 60.4 %custom-call.20 = f32[1,3,2,128,128]{3,4,2,1,0:T(8,128)} custom-call(f32[1,3,2,128,128]{4,3,2,1,0:T(8,128)} %bitcast.1042), custom_call_target="InvertDiagBlocksLowerTriangular" | custom-call | tf_op jit(solution)/shard_map/vmap(jit(_solve_triangular))/vmap()/triangular_solve | solution.py:65
  344.6 5.2 reshape.2027
  349.8 7.2 slice_bitcast_fusion.15
  419.9 60.2 %all-reduce.12.cloned.1.call-done = bf16[2048,768]{1,0:T(8,128)(2,1)} async-done(((bf16[2048,768]{1,0:T(8,128)(2,1)}), bf16[2048,768]{1,0:T(8,128)(2,1)}) %all-reduce.12.cloned.1.call-update) | async-done | bytes 3145744 | tf_op jit(solution)/shard_map/psum | solution.py:82
  486.4 8.6 fusion.121
  498.7 8.8 convolution_convert_fusion.3
  508.9 37.7 %all-gather.4 = bf16[1,3,768,192]{3,1,0,2:T(4,128)(2,1)} all-gather(bf16[1,3,96,192]{3,1,0,2:T(4,128)(2,1)} %get-tuple-element.278), channel_id=6, replica_groups=mesh['tok'=8,'ch'=4] {'tok'}, dimensions={2}, use_global_device_ids=true | all-gather | bytes 995328 | tf_op jit(solution)/shard_map/all_gather | solution.py:273
  555.0 33.6 %all-gather.5 = bf16[1,768,192]{2,1,0:T(8,128)(2,1)} all-gather(bf16[1,96,192]{2,1,0:T(8,128)(2,1)} %get-tuple-element.303), channel_id=7, replica_groups=mesh['tok'=8,'ch'=4] {'tok'}, dimensions={1}, use_global_device_ids=true | all-gather | bytes 331776 | tf_op jit(solution)/shard_map/all_gather | solution.py:274
  620.9 7.4 slice_bitcast_fusion.12
  683.2 64.4 %all-reduce.16.cloned.1.call-done = bf16[2048,768]{1,0:T(8,128)(2,1)} async-done(((bf16[2048,768]{1,0:T(8,128)(2,1)}), bf16[2048,768]{1,0:T(8,128)(2,1)}) %all-reduce.16.cloned.1.call-update) | async-done | bytes 3145744 | tf_op jit(solution)/shard_map/psum | solution.py:82
  757.5 7.6 fusion.113
  766.3 9.4 convert_reduce_fusion.6
  782.0 66.8 %all-reduce.18.cloned.1.call-done = bf16[2048,768]{1,0:T(8,128)(2,1)} async-done(((bf16[2048,768]{1,0:T(8,128)(2,1)}), bf16[2048,768]{1,0:T(8,128)(2,1)}) %all-reduce.18.cloned.1.call-update) | async-done | bytes 3145744 | tf_op jit(solution)/shard_map/psum | solution.py:86
  848.7 5.7 fusion.33
  893.5 8.2 multiply_reduce_fusion.9
  901.8 6.5 multiply_convert_fusion.8
  975.2 68.6 %all-reduce.20.cloned.1.call-done = bf16[2048,768]{1,0:T(8,128)(2,1)} async-done(((bf16[2048,768]{1,0:T(8,128)(2,1)}), bf16[2048,768]{1,0:T(8,128)(2,1)}) %all-reduce.20.cloned.1.call-update) | async-done | bytes 3145744 | tf_op jit(solution)/shard_map/psum | solution.py:86
  1043.9 6.0 convert_reduce_fusion.2
  1049.9 5.8 fusion.34
  1055.7 6.2 convert_reduce_fusion.9
  1061.9 6.9 convert_reduce_fusion.7
  1074.6 8.9 convolution_convert_fusion.2
  1083.5 59.7 %all-reduce.22.cloned.1.call-done = bf16[2048,768]{1,0:T(8,128)(2,1)} async-done(((bf16[2048,768]{1,0:T(8,128)(2,1)}), bf16[2048,768]{1,0:T(8,128)(2,1)}) %all-reduce.22.cloned.1.call-update) | async-done | bytes 3145744 | tf_op jit(solution)/shard_map/psum | solution.py:86
  1143.2 5.6 convert_reduce_fusion.1
  1148.9 6.4 fusion.35
  1191.6 8.0 multiply_reduce_fusion.5
  1199.7 6.5 multiply_convert_fusion.4
  1261.2 5.3 reshape.1992
  1298.8 5.2 fusion.81
  1304.0 91.1 %all-reduce.26.cloned.1.call-done = (bf16[2048,768]{1,0:T(8,128)(2,1)}, bf16[2048,768]{1,0:T(8,128)(2,1)}) async-done(((bf16[2048,768]{1,0:T(8,128)(2,1)}, bf16[2048,768]{1,0:T(8,128)(2,1)}), (bf16[2048,768]{1,0:T(8,128)(2,1)}, bf16[2048,768]{1,0:T(8,128)(2,1)})) %all-reduce.26.cloned.1.call-update) | async-done | bytes 6291472 | tf_op jit(solution)/shard_map/psum | solution.py:82
  1408.4 6.9 copy.431
  1415.3 8.0 reshape.2047
  1423.4 5.7 convolution_bitcast_fusion.2
  1435.7 7.2 convolution_bitcast_fusion
  1443.0 7.6 convolution_bitcast_fusion.1
  1466.3 11.4 add_add_fusion.4
  1477.7 46.2 %all-reduce.24.cloned.1.call-done = (f32[2,6,768]{2,1,0:T(8,128)}, f32[2,6,768]{2,0,1:T(2,128)}) async-done(((f32[2,6,768]{2,1,0:T(8,128)}, f32[2,6,768]{2,0,1:T(2,128)}), (f32[2,6,768]{2,1,0:T(8,128)}, f32[2,6,768]{2,0,1:T(2,128)})) %all-reduce.24.cloned.1.call-update) | async-done | bytes 73744 | tf_op jit(solution)/shard_map/psum | solution.py:440
  1528.0 80.3 %reduce-scatter.13.cloned.1.call-done = f32[96,1152]{1,0:T(8,128)} async-done(((f32[768,1152]{1,0:T(8,128)}), f32[96,1152]{1,0:T(8,128)}) %reduce-scatter.13.cloned.1.call-update) | async-done | bytes 442384
  1613.9 92.6 %reduce-scatter.9.cloned.1.call-done = f32[2,96,768]{2,1,0:T(8,128)} async-done(((f32[2,768,768]{2,1,0:T(8,128)}), f32[2,96,768]{2,1,0:T(8,128)}) %reduce-scatter.9.cloned.1.call-update) | async-done | bytes 589840 | tf_op jit(solution)/shard_map/reduce_scatter | solution.py:428
  1709.0 95.9 %reduce-scatter.11.cloned.1.call-done = f32[2,96,768]{2,1,0:T(8,128)} async-done(((f32[2,768,768]{2,1,0:T(8,128)}), f32[2,96,768]{2,1,0:T(8,128)}) %reduce-scatter.11.cloned.1.call-update) | async-done | bytes 589840 | tf_op jit(solution)/shard_map/reduce_scatter | solution.py:429
  1807.4 7.2 add_add_fusion.7
  1814.6 40.5 %psum.87 = f32[]{:T(128)} all-reduce(f32[]{:T(128)S(6)} %add.668), channel_id=1, replica_groups=mesh['tok'=8,'ch'=4] {'tok','ch'}, use_global_device_ids=true, to_apply=%region_83.84 | all-reduce | flops 1 | bytes 8 | tf_op jit(solution)/shard_map/psum | solution.py:446
  (1047 shorter events, 584.9 us)
Async XLA Ops:
  8.0 472.0 %all-reduce.12.cloned.1.call-start = ((), (), s32[]{:S(2)}) async-start(), calls=%async_computation.4 | async-start | bytes 6291456 | tf_op jit(solution)/shard_map/psum | solution.py:82
  15.0 50.4 %copy-start.177 = (f32[2048]{0:T(1024)}, f32[2048]{0:T(1024)S(1)}, u32[]{:S(2)}) copy-start(f32[2048]{0:T(1024)S(1)} %broadcast_multiply_fusion.3) | copy-start | bytes 24580
  16.1 49.3 %copy-start.193 = (f32[2048]{0:T(1024)}, f32[2048]{0:T(1024)S(1)}, u32[]{:S(2)}) copy-start(f32[2048]{0:T(1024)S(1)} %fusion.229) | copy-start | bytes 24580
  16.8 48.6 %copy-start.219 = (f32[768]{0:T(1024)}, f32[768]{0:T(1024)S(1)}, u32[]{:S(2)}) copy-start(f32[768]{0:T(1024)S(1)} %get-tuple-element.176) | copy-start | bytes 9220
  16.8 48.6 %copy-start.259 = (f32[768]{0:T(1024)}, f32[768]{0:T(1024)S(1)}, u32[]{:S(2)}) copy-start(f32[768]{0:T(1024)S(1)} %get-tuple-element.175) | copy-start | bytes 9220
  16.8 469.7 %copy-start.187 = (f32[768]{0:T(1024)}, f32[768]{0:T(1024)S(1)}, u32[]{:S(2)}) copy-start(f32[768]{0:T(1024)S(1)} %get-tuple-element.173) | copy-start | bytes 9220
  16.8 573.4 %copy-start.172 = (f32[768]{0:T(1024)}, f32[768]{0:T(1024)S(1)}, u32[]{:S(2)}) copy-start(f32[768]{0:T(1024)S(1)} %get-tuple-element.174) | copy-start | bytes 9220
  122.3 48.7 %copy-start.224 = (pred[128,128]{1,0:T(8,128)(4,1)S(1)}, pred[128,128]{1,0:T(8,128)(4,1)}, u32[]{:S(2)}) copy-start(pred[128,128]{1,0:T(8,128)(4,1)} %iota_compare_fusion.3) | copy-start | bytes 49156
  124.8 120.0 %copy-start.223 = (pred[128,128]{1,0:T(8,128)(4,1)S(1)}, pred[128,128]{1,0:T(8,128)(4,1)}, u32[]{:S(2)}) copy-start(pred[128,128]{1,0:T(8,128)(4,1)} %iota_compare_fusion.4) | copy-start | bytes 49156
  129.6 117.1 %copy-start.174 = (pred[256,256]{1,0:T(8,128)(4,1)S(1)}, pred[256,256]{1,0:T(8,128)(4,1)}, u32[]{:S(2)}) copy-start(pred[256,256]{1,0:T(8,128)(4,1)} %iota_compare_fusion.2) | copy-start | bytes 196612
  129.6 119.3 %copy-start.269 = (s32[2]{0:T(128)S(1)}, s32[2]{0:T(128)}, u32[]{:S(2)}) copy-start(s32[2]{0:T(128)} %iota_multiply_fusion) | copy-start | bytes 28
  202.6 119.3 %copy-start.248 = (f32[1,1,192]{2,0,1:T(1,128)S(1)}, f32[1,1,192]{2,0,1:T(1,128)}, u32[]{:S(2)}) copy-start(f32[1,1,192]{2,0,1:T(1,128)} %get-tuple-element.308) | copy-start | bytes 2308
  412.3 74.2 %all-gather.13.cloned.1.call-start = ((), (), s32[]{:S(2)}) async-start(), calls=%async_computation.12 | async-start | bytes 1327104 | tf_op jit(solution)/shard_map/all_gather | solution.py:275
  414.2 84.5 %all-gather.15.cloned.1.call-start = ((), (), s32[]{:S(2)}) async-start(), calls=%async_computation.13 | async-start | bytes 1327104 | tf_op jit(solution)/shard_map/all_gather | solution.py:276
  416.1 174.1 %all-reduce.14.cloned.1.call-start = ((), (), s32[]{:S(2)}) async-start(), calls=%async_computation.5 | async-start | bytes 6291456 | tf_op jit(solution)/shard_map/psum | solution.py:82
  507.5 82.7 %copy-start.239 = (f32[768]{0:T(1024)S(1)}, f32[768]{0:T(1024)}, u32[]{:S(2)}) copy-start(f32[768]{0:T(1024)} %get-tuple-element.171) | copy-start | bytes 9220
  507.5 240.1 %all-reduce.16.cloned.1.call-start = ((), (), s32[]{:S(2)}) async-start(), calls=%async_computation.6 | async-start | bytes 6291456 | tf_op jit(solution)/shard_map/psum | solution.py:82
  675.6 72.1 %copy-start.241 = (f32[768]{0:T(1024)S(1)}, f32[768]{0:T(1024)}, u32[]{:S(2)}) copy-start(f32[768]{0:T(1024)} %get-tuple-element.168) | copy-start | bytes 9220
  679.5 78.0 %all-gather.17.cloned.1.call-start = ((), (), s32[]{:S(2)}) async-start(), calls=%async_computation.14 | async-start | bytes 1327104 | tf_op jit(solution)/shard_map/all_gather | solution.py:275
  680.1 86.2 %all-gather.19.cloned.1.call-start = ((), (), s32[]{:S(2)}) async-start(), calls=%async_computation.15 | async-start | bytes 1327104 | tf_op jit(solution)/shard_map/all_gather | solution.py:276
  680.8 167.9 %all-reduce.18.cloned.1.call-start = ((), (), s32[]{:S(2)}) async-start(), calls=%async_computation.7 | async-start | bytes 6291456 | tf_op jit(solution)/shard_map/psum | solution.py:86
  781.3 262.5 %all-reduce.20.cloned.1.call-start = ((), (), s32[]{:S(2)}) async-start(), calls=%async_computation.8 | async-start | bytes 6291456 | tf_op jit(solution)/shard_map/psum | solution.py:86
  971.1 72.8 %copy-start.171 = (f32[2048]{0:T(1024)S(1)}, f32[2048]{0:T(1024)}, u32[]{:S(2)}) copy-start(f32[2048]{0:T(1024)} %copy-done.170) | copy-start | bytes 24580
  971.1 72.8 %copy-start.190 = (f32[768]{0:T(1024)S(1)}, f32[768]{0:T(1024)}, u32[]{:S(2)}) copy-start(f32[768]{0:T(1024)} %get-tuple-element.170) | copy-start | bytes 9220
  975.2 74.7 %copy-start.216 = (f32[2048]{0:T(1024)S(1)}, f32[2048]{0:T(1024)}, u32[]{:S(2)}) copy-start(f32[2048]{0:T(1024)} %copy-done.215) | copy-start | bytes 24580
  975.2 74.7 %copy-start.186 = (f32[2048]{0:T(1024)S(1)}, f32[2048]{0:T(1024)}, u32[]{:S(2)}) copy-start(f32[2048]{0:T(1024)} %copy-done.185) | copy-start | bytes 24580
  975.2 168.0 %all-reduce.22.cloned.1.call-start = ((), (), s32[]{:S(2)}) async-start(), calls=%async_computation.9 | async-start | bytes 6291456 | tf_op jit(solution)/shard_map/psum | solution.py:86
  1074.5 68.7 %copy-start.1 = (bf16[2048,768]{1,0:T(8,128)(2,1)S(1)}, bf16[2048,768]{1,0:T(8,128)(2,1)}, u32[]{:S(2)}) copy-start(bf16[2048,768]{1,0:T(8,128)(2,1)} %param.24) | copy-start | bytes 9437188
  1074.5 68.7 %copy-start.169 = (f32[2048]{0:T(1024)S(1)}, f32[2048]{0:T(1024)}, u32[]{:S(2)}) copy-start(f32[2048]{0:T(1024)} %copy-done.168) | copy-start | bytes 24580
  1074.5 68.7 %copy-start.173 = (f32[768]{0:T(1024)S(1)}, f32[768]{0:T(1024)}, u32[]{:S(2)}) copy-start(f32[768]{0:T(1024)} %copy-done.172) | copy-start | bytes 9220
  1074.5 68.7 %copy-start.188 = (f32[768]{0:T(1024)S(1)}, f32[768]{0:T(1024)}, u32[]{:S(2)}) copy-start(f32[768]{0:T(1024)} %copy-done.187) | copy-start | bytes 9220
  1074.5 320.6 %all-reduce.26.cloned.1.call-start = ((), (), s32[]{:S(2)}) async-start(), calls=%async_computation.19 | async-start | bytes 12582912 | tf_op jit(solution)/shard_map/psum | solution.py:82
  1275.0 188.7 %reduce-scatter.15.cloned.1.call-start = ((), (), s32[]{:S(2)}) async-start(), calls=%async_computation.17 | async-start | bytes 1327104
  1298.4 225.5 %all-reduce.24.cloned.1.call-start = ((), (), s32[]{:S(2)}) async-start(), calls=%async_computation.18 | async-start | bytes 172032 | tf_op jit(solution)/shard_map/psum | solution.py:440
  1304.0 95.0 %copy-start.212 = (f32[2048]{0:T(1024)S(1)}, f32[2048]{0:T(1024)}, u32[]{:S(2)}) copy-start(f32[2048]{0:T(1024)} %copy-done.211) | copy-start | bytes 24580
  1404.0 204.3 %reduce-scatter.13.cloned.1.call-start = ((), (), s32[]{:S(2)}) async-start(), calls=%async_computation.16 | async-start | bytes 3981312
  1423.3 283.2 %reduce-scatter.9.cloned.1.call-start = ((), (), s32[]{:S(2)}) async-start(), calls=%async_computation.10 | async-start | bytes 5308416 | tf_op jit(solution)/shard_map/reduce_scatter | solution.py:428
  1435.0 369.8 %reduce-scatter.11.cloned.1.call-start = ((), (), s32[]{:S(2)}) async-start(), calls=%async_computation.11 | async-start | bytes 5308416 | tf_op jit(solution)/shard_map/reduce_scatter | solution.py:429
  1477.7 329.7 %copy-start.236 = (f32[768]{0:T(1024)S(1)}, f32[768]{0:T(1024)}, u32[]{:S(2)}) copy-start(f32[768]{0:T(1024)} %get-tuple-element.165) | copy-start | bytes 9220
  1807.4 48.4 %copy-start.76 = (f32[2,96,192]{1,2,0:T(8,128)S(1)}, f32[2,96,192]{1,2,0:T(8,128)}, u32[]{:S(2)}) copy-start(f32[2,96,192]{1,2,0:T(8,128)} %copy-done.75) | copy-start | bytes 442372
  1807.4 48.4 %copy-start.124 = (f32[2,96,192]{1,2,0:T(8,128)S(1)}, f32[2,96,192]{1,2,0:T(8,128)}, u32[]{:S(2)}) copy-start(f32[2,96,192]{1,2,0:T(8,128)} %copy.408) | copy-start | bytes 442372
  1807.4 48.4 %copy-start.125 = (f32[2,96,192]{1,2,0:T(8,128)S(1)}, f32[2,96,192]{1,2,0:T(8,128)}, u32[]{:S(2)}) copy-start(f32[2,96,192]{1,2,0:T(8,128)} %copy.409) | copy-start | bytes 442372
  1807.4 48.4 %copy-start.126 = (f32[2,96,192]{1,2,0:T(8,128)S(1)}, f32[2,96,192]{1,2,0:T(8,128)}, u32[]{:S(2)}) copy-start(f32[2,96,192]{1,2,0:T(8,128)} %copy.410) | copy-start | bytes 442372
  1807.4 50.1 %copy-start.67 = (f32[2,3,96,192]{2,3,1,0:T(8,128)S(1)}, f32[2,3,96,192]{2,3,1,0:T(8,128)}, u32[]{:S(2)}) copy-start(f32[2,3,96,192]{2,3,1,0:T(8,128)} %copy.405) | copy-start | bytes 1327108
  1807.4 50.1 %copy-start.68 = (f32[2,3,96,192]{2,3,1,0:T(8,128)S(1)}, f32[2,3,96,192]{2,3,1,0:T(8,128)}, u32[]{:S(2)}) copy-start(f32[2,3,96,192]{2,3,1,0:T(8,128)} %copy.406) | copy-start | bytes 1327108
  1856.7 16.2 copy-start.225
  1856.7 17.6 copy-start.63
  1856.7 17.6 copy-start.66
  (263 other events, 1208.7 us)
Sparse Core Ops, SparseCore 0:
  412.4 67.6 all-reduce.11
  507.6 66.9 all-reduce.13
  679.6 67.9 all-reduce.15
  781.4 67.2 all-reduce.17
  975.3 68.5 all-reduce.19
  1074.6 68.5 all-reduce.21
  1275.2 119.8 all-reduce.25
Sparse Core Ops, SparseCore 1:
  415.5 40.6 all-gather.12
  458.8 39.9 all-gather.14
  682.7 40.9 all-gather.16
  726.4 39.8 all-gather.18
  1298.5 64.5 reduce-scatter.14
  1404.1 119.8 all-reduce.23
  1527.4 80.9 reduce-scatter.12
  1611.8 94.6 reduce-scatter.8
  1710.0 94.8 reduce-scatter.10
where the time goes:
time: 1900 us; the launch traced here: 1890 us
  waiting for transfers between devices  732 us (39%)
  other arithmetic  389 us (20%)
  local copies, waits for them, and re-layouts  280 us (15%)
  matrix products  272 us (14%)
  blocking collectives  186 us (10%)
  between operations  27.9 us (1%)
    psum x4, waiting for transfers between devices, sum_branch(): return lax.psum(partial_sum.astype(jnp.bfloat16), 'ch').astype(jnp.float32)  216 us
    psum x3, waiting for transfers between devices, sum_back(): return lax.psum(partial_grad.astype(jnp.bfloat16), 'ch').astype(jnp.float32)  195 us
    another operation x10, other arithmetic, gram_tables(): factor_lower = jnp.linalg.cholesky(gram)  108 us
    reduce_scatter x1, waiting for transfers between devices, shards(): lax.psum_scatter(stacked_grads[3], 'tok', scatter_dimension=1, tiled=True)  95.9 us
    reduce_scatter x1, waiting for transfers between devices, shards(): lax.psum_scatter(stacked_grads[2], 'tok', scatter_dimension=1, tiled=True)  92.6 us
    unnamed x18, waiting for transfers between devices  81.7 us
    all_gather x2, blocking collectives, shards(): lax.all_gather(w_qkv[layer_index].astype(jnp.bfloat16), 'tok', axis=1, ti...  78.1 us
    unnamed x623, local copies, waits for them, and re-layouts  71.9 us
  transfers between devices with their start and end apart: 16, of which 12 were waited for; matrix products, arithmetic and copies ran while one was open for 9% of the time, Pallas kernels for 0%

commit v1 on v0

v1 whole, which is shorter than its diff:
```python
from functools import partial

import jax
import jax.numpy as jnp
from jax import lax
from jax.experimental import pallas as pl
from jax.experimental.pallas import tpu as pltpu
from jax.sharding import Mesh
from jax.sharding import PartitionSpec as P

HEAD_DIM = 64
BASIS = 256
SAMPLES = 256
SEG = 512
SEGS = 4
CRES = 1024
LAYERS = 2
STEP = 10

PRECISE = lax.Precision.HIGHEST
STICKY_RATIO = 0.5
RIDGE_WEIGHT = 0.5
BASIS_WIDTH = 0.01
NORM_EPS = 1e-05
CLIP_LIMIT = 1.0
FIRST_DECAY = 0.9
SECOND_DECAY = 0.95
ADAM_EPS = 1e-08
WEIGHT_DECAY = 0.1
RATE_QKV = 0.05
RATE_OUT = 0.5
RATE_UP = 0.05
RATE_DOWN = 0.03
RATE_VECTOR = 0.5
MASKED = -1e30
F32 = jnp.float32
BF16 = jnp.bfloat16
SWAP = ((0, 1), (1, 0))
NN = (((1,), (0,)), ((), ()))
NT = (((1,), (1,)), ((), ()))
TN = (((0,), (0,)), ((), ()))


def dot(left, right, dims, precision=None):
    return lax.dot_general(left, right, dims, precision=precision, preferred_element_type=F32)


def table_kernel(old_ref, design_ref, out_ref, inv_ref, gram_ref):
    design = design_ref[...]
    eye = (
        lax.broadcasted_iota(jnp.int32, (BASIS, BASIS), 0)
        == lax.broadcasted_iota(jnp.int32, (BASIS, BASIS), 1)
    ).astype(F32)
    gram = dot(design, design, NT, PRECISE) + RIDGE_WEIGHT * eye
    gram_ref[...] = gram
    bound = jnp.max(jnp.sum(jnp.abs(gram), axis=0))
    inv_ref[...] = eye * (1.0 / bound)

    def step(low):
        scale = 2.0 / (1.0 + low)
        now = inv_ref[...]
        inner = dot(gram_ref[...], now, NN, PRECISE)
        inv_ref[...] = scale * (2.0 * now - scale * dot(now, inner, NN, PRECISE))
        return 4.0 * low / ((1.0 + low) * (1.0 + low))

    lax.while_loop(lambda low: low < 0.999, step, 0.99 * RIDGE_WEIGHT / bound)
    for _ in range(2):
        now = inv_ref[...]
        inner = dot(gram_ref[...], now, NN, PRECISE)
        inv_ref[...] = 2.0 * now - dot(now, inner, NN, PRECISE)
    fitted = dot(inv_ref[...], design, NN, PRECISE)
    out_ref[:, BASIS:] = fitted[:, SAMPLES:].astype(BF16)
    out_ref[:, :BASIS] = dot(fitted[:, :SAMPLES], old_ref[...], NT, PRECISE).astype(BF16)


def basis_table(centres, times):
    middle = (centres.astype(F32) + 0.5) / CRES
    offset = (times[None, :] - middle[:, None]) / BASIS_WIDTH
    return jnp.exp(-0.5 * offset * offset)


def make_tables(centres, sticky_row):
    token_times = STICKY_RATIO + (1.0 - STICKY_RATIO) * (jnp.arange(SEG).astype(F32) + 0.5) / SEG
    places = (sticky_row.astype(F32) + 0.5) / CRES
    old_basis = basis_table(centres, places)
    design = basis_table(centres, jnp.concatenate([STICKY_RATIO * places, token_times]))
    return pl.pallas_call(
        table_kernel,
        out_shape=jax.ShapeDtypeStruct((BASIS, BASIS + SEG), BF16),
        scratch_shapes=[pltpu.VMEM((BASIS, BASIS), F32), pltpu.VMEM((BASIS, BASIS), F32)],
        compiler_params=pltpu.CompilerParams(vmem_limit_bytes=32 * 2**20),
        cost_estimate=pl.CostEstimate(flops=6 * 10**9, bytes_accessed=2 * 10**6, transcendentals=0),
    )(old_basis, design)


QT = 256


def causal(shape):
    return lax.broadcasted_iota(jnp.int32, shape, 0) <= lax.broadcasted_iota(jnp.int32, shape, 1)


def attention_forward_kernel(
    bias_ref, q_ref, k_ref, v_ref, mk_ref, mv_ref, out_ref, lse_ref
):
    memory_bias = bias_ref[pl.program_id(0)]
    pair = q_ref.shape[1] // HEAD_DIM
    queries = q_ref[...] * HEAD_DIM ** (-0.5)
    for tile in range(SEG // QT):
        rows = slice(tile * QT, (tile + 1) * QT)
        stacked = []
        for head in range(pair):
            lanes = slice(head * HEAD_DIM, (head + 1) * HEAD_DIM)
            query = queries[rows, lanes]
            scores = []
            values = []
            for part in range(tile + 1):
                keys = slice(part * QT, (part + 1) * QT)
                score = dot(k_ref[keys, lanes], query, NT)
                if part == tile:
                    score = jnp.where(causal(score.shape), score, MASKED)
                scores.append(score)
                values.append(v_ref[keys, lanes])
            scores.append(dot(mk_ref[0, :, lanes], query, NT) + memory_bias)
            values.append(mv_ref[0, :, lanes])
            top = scores[0].max(axis=0, keepdims=True)
            for score in scores[1:]:
                top = jnp.maximum(top, score.max(axis=0, keepdims=True))
            total = jnp.zeros_like(top)
            result = jnp.zeros((HEAD_DIM, QT), F32)
            for score, value in zip(scores, values):
                weight = jnp.exp(score - top)
                total = total + weight.sum(axis=0, keepdims=True)
                result = result + dot(value, weight.astype(BF16), TN)
            stacked.append(result / total)
            lse_ref[0, head : head + 1, rows] = top + jnp.log(total)
        out_ref[rows, :] = jnp.concatenate(stacked, axis=0).T.astype(BF16)


def attention_forward(qkv, memory, memory_bias):
    rows, width = qkv.shape[0], qkv.shape[1] // 3
    pairs = width // 128
    segs = rows // SEG
    return pl.pallas_call(
        attention_forward_kernel,
        grid=(segs, pairs),
        in_specs=[
            pl.BlockSpec(memory_space=pltpu.SMEM),
            pl.BlockSpec((SEG, 128), lambda s, h: (s, h)),
            pl.BlockSpec((SEG, 128), lambda s, h: (s, pairs + h)),
            pl.BlockSpec((SEG, 128), lambda s, h: (s, 2 * pairs + h)),
            pl.BlockSpec((1, BASIS, 128), lambda s, h: (s, 0, h)),
            pl.BlockSpec((1, BASIS, 128), lambda s, h: (s, 0, pairs + h)),
        ],
        out_specs=[
            pl.BlockSpec((SEG, 128), lambda s, h: (s, h)),
            pl.BlockSpec((1, 2, SEG), lambda s, h: (s * pairs + h, 0, 0)),
        ],
        out_shape=[
            jax.ShapeDtypeStruct((rows, width), BF16),
            jax.ShapeDtypeStruct((segs * pairs, 2, SEG), F32),
        ],
        compiler_params=pltpu.CompilerParams(vmem_limit_bytes=48 * 2**20),
        cost_estimate=pl.CostEstimate(
            flops=12 * 10**9, bytes_accessed=5 * 10**6, transcendentals=4 * 10**6
        ),
    )(memory_bias, qkv, qkv, qkv, memory, memory)


def attention_backward_kernel(
    bias_ref,
    q_ref,
    k_ref,
    v_ref,
    mk_ref,
    mv_ref,
    lse_ref,
    out_ref,
    grad_ref,
    dq_ref,
    dk_ref,
    dv_ref,
    dmk_ref,
    dmv_ref,
):
    memory_bias = bias_ref[pl.program_id(0)]
    pair = q_ref.shape[1] // HEAD_DIM
    scale = HEAD_DIM ** (-0.5)
    tiles = SEG // QT
    product = (out_ref[...].astype(F32) * grad_ref[...].astype(F32)).T
    query_grads = []
    for head in range(pair):
        lanes = slice(head * HEAD_DIM, (head + 1) * HEAD_DIM)
        query = q_ref[:, lanes] * scale
        grad = grad_ref[:, lanes]
        dots = product[lanes, :].sum(axis=0, keepdims=True)
        log_total = lse_ref[0, head : head + 1, :]
        head_grads = [jnp.zeros((HEAD_DIM, QT), F32) for _ in range(tiles)]
        for part in range(tiles + 1):
            if part < tiles:
                keys = slice(part * QT, (part + 1) * QT)
                key, value = k_ref[keys, lanes], v_ref[keys, lanes]
            else:
                key, value = mk_ref[0, :, lanes], mv_ref[0, :, lanes]
            key_grad = jnp.zeros((QT, HEAD_DIM), F32)
            value_grad = jnp.zeros((QT, HEAD_DIM), F32)
            for tile in range(part if part < tiles else 0, tiles):
                rows = slice(tile * QT, (tile + 1) * QT)
                score = dot(key, query[rows], NT)
                if part == tile:
                    score = jnp.where(causal(score.shape), score, MASKED)
                if part == tiles:
                    score = score + memory_bias
                weight = jnp.exp(score - log_total[:, rows])
                weight_grad = dot(value, grad[rows], NT)
                score_grad = (weight * (weight_grad - dots[:, rows])).astype(BF16)
                value_grad = value_grad + dot(weight.astype(BF16), grad[rows], NN)
                key_grad = key_grad + dot(score_grad, query[rows], NN)
                head_grads[tile] = head_grads[tile] + dot(key, score_grad, TN)
            if part < tiles:
                dk_ref[keys, lanes] = key_grad
                dv_ref[keys, lanes] = value_grad
            else:
                dmk_ref[0, :, lanes] = key_grad
                dmv_ref[0, :, lanes] = value_grad
        query_grads.append(jnp.concatenate(head_grads, axis=1) * scale)
    dq_ref[...] = jnp.concatenate(query_grads, axis=0).T.astype(BF16)


def attention_backward(qkv, memory, memory_bias, log_totals, attended, grad):
    rows, width = attended.shape
    pairs = width // 128
    segs = rows // SEG
    block = pl.BlockSpec((SEG, 128), lambda s, h: (s, h))
    memory_block = pl.BlockSpec((1, BASIS, 128), lambda s, h: (s, 0, h))
    return pl.pallas_call(
        attention_backward_kernel,
        grid=(segs, pairs),
        in_specs=[
            pl.BlockSpec(memory_space=pltpu.SMEM),
            block,
            pl.BlockSpec((SEG, 128), lambda s, h: (s, pairs + h)),
            pl.BlockSpec((SEG, 128), lambda s, h: (s, 2 * pairs + h)),
            memory_block,
            pl.BlockSpec((1, BASIS, 128), lambda s, h: (s, 0, pairs + h)),
            pl.BlockSpec((1, 2, SEG), lambda s, h: (s * pairs + h, 0, 0)),
            block,
            block,
        ],
        out_specs=[block, block, block, memory_block, memory_block],
        out_shape=[
            jax.ShapeDtypeStruct((rows, width), BF16),
            jax.ShapeDtypeStruct((rows, width), F32),
            jax.ShapeDtypeStruct((rows, width), F32),
            jax.ShapeDtypeStruct((segs, BASIS, width), F32),
            jax.ShapeDtypeStruct((segs, BASIS, width), F32),
        ],
        compiler_params=pltpu.CompilerParams(vmem_limit_bytes=48 * 2**20),
        cost_estimate=pl.CostEstimate(
            flops=24 * 10**9, bytes_accessed=9 * 10**6, transcendentals=4 * 10**6
        ),
    )(memory_bias, qkv, qkv, qkv, memory, memory, log_totals, attended, grad)


def adamw(weight, first, second, grad, rate, decay):
    first_new = FIRST_DECAY * first + (1.0 - FIRST_DECAY) * grad
    second_new = SECOND_DECAY * second + (1.0 - SECOND_DECAY) * grad * grad
    first_hat = first_new / (1.0 - FIRST_DECAY**STEP)
    second_hat = second_new / (1.0 - SECOND_DECAY**STEP)
    weight_new = weight * (1.0 - rate * decay) - rate * first_hat / (
        jnp.sqrt(second_hat) + ADAM_EPS
    )
    return (weight_new, first_new, second_new)


def norm_stats(inputs):
    mean_row = jnp.mean(inputs, axis=-1, keepdims=True)
    centred = inputs - mean_row
    variance = jnp.mean(centred * centred, axis=-1, keepdims=True)
    rstd = lax.rsqrt(variance + NORM_EPS)
    return centred * rstd, rstd


def layer_norm(inputs, gain_vec, shift_vec):
    unit, _ = norm_stats(inputs)
    return unit * gain_vec + shift_vec


def norm_backward(inputs, grad, gain_vec):
    unit, rstd = norm_stats(inputs)
    scaled = grad * gain_vec
    back = rstd * (
        scaled
        - jnp.mean(scaled, axis=-1, keepdims=True)
        - unit * jnp.mean(scaled * unit, axis=-1, keepdims=True)
    )
    return back, jnp.sum(grad * unit, axis=0), jnp.sum(grad, axis=0)


def flip(array, axis):
    return lax.ppermute(array, axis, SWAP)


def pair_sum(part):
    own = lax.optimization_barrier(part.astype(BF16))
    return own.astype(F32) + flip(own, "cc").astype(F32)


def swap_halves(array):
    shape = array.shape
    parts = array.reshape(shape[:-1] + (2, 2, shape[-1] // 4))
    return parts[..., ::-1, :].reshape(shape)


def all_gather_slabs(shard, depth, first_axis, second_axis):
    spread = jnp.broadcast_to(shard[None], (depth,) + shard.shape)
    own = lax.all_to_all(spread, "tz", 0, 0, tiled=True).reshape(-1, shard.shape[-1])
    near = flip(own, first_axis)
    far = flip(own, second_axis)
    both = flip(near, second_axis)
    return (own, near, far, both) if first_axis == "tx" else (own, far, near, both)


def reduce_slabs(slabs, depth, first_axis):
    own, by_x, by_y, by_both = slabs
    if first_axis == "cy":
        got_own, got_other = flip(by_y, "cy"), flip(by_both, "cy")
        keep, give, second_axis = own, by_x, "tx"
    else:
        got_own, got_other = flip(by_x, "tx"), flip(by_both, "tx")
        keep, give, second_axis = own, by_y, "cy"
    give = (give.astype(F32) + got_other.astype(F32)).astype(BF16)
    keep = keep.astype(F32) + got_own.astype(F32)
    total = (keep + flip(give, second_axis).astype(F32)).astype(BF16)
    pieces = total.reshape(depth, -1, total.shape[-1])
    return lax.all_to_all(pieces, "tz", 0, 0, tiled=True).astype(F32).sum(axis=0)


def butterfly(array, axes):
    for axis in axes:
        size = lax.axis_size(axis)
        bit = 1
        while bit < size:
            array = array + lax.ppermute(array, axis, [(i, i ^ bit) for i in range(size)])
            bit *= 2
    return array


def shards(
    h_in,
    cotangent,
    carried,
    centres,
    sticky,
    flags,
    w_qkv,
    w_qkv_first,
    w_qkv_second,
    w_out_t,
    w_out_first,
    w_out_second,
    w_up,
    w_up_first,
    w_up_second,
    w_down_t,
    w_down_first,
    w_down_second,
    vec_d,
    vec_d_first,
    vec_d_second,
    vec_c,
    vec_c_first,
    vec_c_second,
):
    depth = lax.axis_size("tz")
    tok_count = depth * 2
    ch_count = 2 * lax.axis_size("cc")
    context = lax.axis_index("cy")
    core = lax.axis_index("cc")
    x_place = lax.axis_index("tx")
    block_rows = w_qkv.shape[2]
    width = w_qkv.shape[1 + 2] * 1
    features = h_in.shape[1]
    half = features // 2
    rows = h_in.shape[0] // 2
    hidden_own = w_up.shape[2]

    place = jnp.arange(features)
    turned = place // half
    block_z = (place % half) // block_rows
    source = block_z * (2 * block_rows) + jnp.where(
        turned == 0, x_place, 1 - x_place
    ) * block_rows + place % block_rows
    order = (jnp.arange(features)[:, None] == source[None, :]).astype(BF16)
    order_wide = order.astype(F32)

    table_index = jnp.where(context == 0, core, 2)
    sticky_row = lax.dynamic_index_in_dim(sticky[0], table_index, 0, keepdims=False)
    table_own = make_tables(centres, sticky_row)
    table_other = flip(table_own, "cc")
    table_near = jnp.where(core == 0, table_own, table_other)
    table_far = jnp.where(core == 0, table_other, table_own)
    a_near, b_near = table_near[:, :BASIS], table_near[:, BASIS:]
    a_far, b_far = table_far[:, :BASIS], table_far[:, BASIS:]

    slabs = []
    for layer in range(LAYERS):
        attn_shard = jnp.concatenate(
            [w_qkv[layer, 0], w_qkv[layer, 1], w_qkv[layer, 2], w_out_t[layer]], axis=1
        ).astype(BF16)
        ffn_shard = jnp.concatenate([w_up[layer], w_down_t[layer]], axis=1).astype(BF16)
        slabs.append(
            (
                all_gather_slabs(attn_shard, depth, "tx", "cy"),
                all_gather_slabs(ffn_shard, depth, "cy", "tx"),
            )
        )

    def whole(parts, low, high):
        own, by_x, by_y, by_both = parts
        return (
            jnp.concatenate([own[:, low:high], by_x[:, low:high]], axis=0),
            jnp.concatenate([by_y[:, low:high], by_both[:, low:high]], axis=0),
        )

    vec_c_other = flip(vec_c, "cy")
    gains = jnp.dot(
        vec_d.reshape(-1, features), order_wide, precision=PRECISE
    ).reshape(vec_d.shape)
    flag_on = flags[0] > 0
    carried_own = carried[:, 0].reshape(LAYERS, BASIS, 2, width)
    carried_other = flip(carried_own, "cy")
    starts = jnp.stack([carried_own, carried_other], axis=3).reshape(LAYERS, BASIS, 4 * width)
    starts = jnp.where(flag_on, starts, jnp.zeros_like(starts))
    memory_bias = jnp.stack(
        [jnp.where((context == 0) & ~flag_on, MASKED, 0.0), jnp.float32(0.0)]
    ).astype(F32)

    own_h = lax.dynamic_slice_in_dim(h_in, context * rows, rows, axis=0)
    own_cot = lax.dynamic_slice_in_dim(cotangent, context * rows, rows, axis=0)
    stream = jnp.dot(own_h, order, preferred_element_type=F32)
    stream_grad = jnp.dot(own_cot, order, preferred_element_type=F32)

    saved = []
    for layer in range(LAYERS):
        attn_slabs, ffn_slabs = slabs[layer]
        wq, wk, wv = (whole(attn_slabs, i * width, (i + 1) * width) for i in range(3))
        w_in = jnp.concatenate([*wq, *wk, *wv], axis=1)
        w_out = jnp.concatenate(whole(attn_slabs, 3 * width, 4 * width), axis=1)
        w_big = jnp.concatenate(whole(ffn_slabs, 0, hidden_own), axis=1)
        w_small = jnp.concatenate(whole(ffn_slabs, hidden_own, 2 * hidden_own), axis=1)
        gain = gains[layer]
        bias_own, bias_other = vec_c[layer], vec_c_other[layer]
        zeros = jnp.zeros((2 * width,), F32)
        in_bias = jnp.concatenate(
            [bias_own[0], bias_other[0], zeros, bias_own[1], bias_other[1]]
        )
        up_bias = jnp.concatenate([bias_own[2:6].T.reshape(-1), bias_other[2:6].T.reshape(-1)])

        normed = layer_norm(stream, gain[0], gain[1]).astype(BF16)
        qkv = (dot(normed, w_in, NN) + in_bias).astype(BF16)
        signal = qkv[:, 2 * width :].reshape(2, SEG, 4 * width)
        fit_near = dot(b_near, signal[0], NN)
        fit_far = dot(b_far, signal[1], NN)
        ahead = dot(a_near, starts[layer], NN) + fit_near
        ahead = (dot(a_far, ahead.astype(BF16), NN) + fit_far).astype(BF16)
        received = lax.ppermute(swap_halves(ahead), "cy", ((0, 1),))
        memory_first = jnp.where(context == 0, starts[layer], received)
        memory_second = (dot(a_near, memory_first, NN) + fit_near).astype(BF16)
        memory = jnp.stack([memory_first, memory_second])
        attended, log_totals = attention_forward(qkv, memory, memory_bias)
        branch = pair_sum(dot(attended, w_out, NT))
        middle = stream + (branch + gain[4])
        normed_two = layer_norm(middle, gain[2], gain[3]).astype(BF16)
        hidden = dot(normed_two, w_big, NN) + up_bias
        active = jax.nn.gelu(hidden, approximate=True).astype(BF16)
        mixed = pair_sum(dot(active, w_small, NT))
        saved.append(
            (
                (w_in, w_out, w_big, w_small),
                stream,
                normed,
                qkv,
                memory,
                log_totals,
                attended,
                middle,
                normed_two,
                hidden,
                active,
            )
        )
        stream = middle + (mixed + gain[5])

    def gathered_rows(array):
        own = lax.optimization_barrier(array.astype(BF16))
        other = flip(own, "cy")
        both = jnp.where(
            context == 0,
            jnp.concatenate([own, other], axis=0),
            jnp.concatenate([other, own], axis=0),
        )
        return dot(both, order, NT)

    activations = gathered_rows(stream)

    vector_d = [None] * LAYERS
    vector_own = [None] * LAYERS
    vector_other = [None] * LAYERS
    reduced = [None] * LAYERS

    def grad_slabs(left, right):
        columns = right.shape[1] // 2
        return [
            dot(left[:, low : low + half], right[:, col : col + columns], TN).astype(BF16)
            for low, col in ((0, 0), (half, 0), (0, columns), (half, columns))
        ]

    for layer in reversed(range(LAYERS)):
        (
            (w_in, w_out, w_big, w_small),
            stream,
            normed,
            qkv,
            memory,
            log_totals,
            attended,
            middle,
            normed_two,
            hidden,
            active,
        ) = saved[layer]
        gain = gains[layer]
        down = stream_grad.astype(BF16)
        grad_down_bias = jnp.sum(down.astype(F32), axis=0)
        active_grad = dot(down, w_small, NN)
        _, gelu_back = jax.vjp(partial(jax.nn.gelu, approximate=True), hidden)
        hidden_grad = gelu_back(active_grad)[0].astype(BF16)
        grad_up_bias = jnp.sum(hidden_grad.astype(F32), axis=0)
        normed_two_grad = pair_sum(dot(hidden_grad, w_big, NT))
        down_slabs = grad_slabs(down, active)
        up_slabs = grad_slabs(normed_two, hidden_grad)
        reduced_down = reduce_slabs(down_slabs, depth, "cy")
        reduced_up = reduce_slabs(up_slabs, depth, "tx")
        middle_grad, grad_gain_two, grad_shift_two = norm_backward(
            middle, normed_two_grad, gain[2]
        )
        stream_grad = stream_grad + middle_grad
        branch_grad = stream_grad.astype(BF16)
        grad_out_bias = jnp.sum(branch_grad.astype(F32), axis=0)
        attended_grad = dot(branch_grad, w_out, NN).astype(BF16)
        out_slabs = grad_slabs(branch_grad, attended)
        reduced_out = reduce_slabs(out_slabs, depth, "cy")
        dq, dk, dv, dmk, dmv = attention_backward(
            qkv, memory, memory_bias, log_totals, attended, attended_grad
        )
        memory_grad = jnp.concatenate([dmk, dmv], axis=2)
        back = memory_grad[0] + dot(a_near, memory_grad[1].astype(BF16), TN)
        received = lax.ppermute(swap_halves(back.astype(BF16)), "cy", ((1, 0),))
        carry = (memory_grad[1] + dot(a_far, received, TN)).astype(BF16)
        signal_grad = jnp.concatenate([dot(b_near, carry, TN), dot(b_far, received, TN)], axis=0)
        dk = (dk + signal_grad[:, : 2 * width]).astype(BF16)
        dv = (dv + signal_grad[:, 2 * width :]).astype(BF16)
        grads_in = jnp.concatenate([dq, dk, dv], axis=1)
        normed_grad = pair_sum(dot(grads_in, w_in, NT))
        grad_query_bias = jnp.sum(dq.astype(F32), axis=0)
        grad_value_bias = jnp.sum(dv.astype(F32), axis=0)
        in_slabs = [grad_slabs(normed, member) for member in (dq, dk, dv)]
        in_slabs = [
            jnp.concatenate([in_slabs[i][j] for i in range(3)], axis=1) for j in range(4)
        ]
        reduced_in = reduce_slabs(in_slabs, depth, "tx")
        input_part, grad_gain_one, grad_shift_one = norm_backward(stream, normed_grad, gain[0])
        stream_grad = stream_grad + input_part
        vector_d[layer] = jnp.stack(
            [
                grad_gain_one,
                grad_shift_one,
                grad_gain_two,
                grad_shift_two,
                grad_out_bias,
                grad_down_bias,
            ]
        )
        ups = grad_up_bias.reshape(2, width, 4).transpose(0, 2, 1)
        pieces = [
            jnp.concatenate(
                [
                    grad_query_bias[None, side * width : (side + 1) * width],
                    grad_value_bias[None, side * width : (side + 1) * width],
                    ups[side],
                ],
                axis=0,
            )
            for side in range(2)
        ]
        vector_own[layer], vector_other[layer] = pieces
        reduced[layer] = (
            reduced_in.reshape(block_rows, 3, width).transpose(1, 0, 2),
            reduced_out,
            reduced_up,
            reduced_down,
        )
    input_grad = gathered_rows(stream_grad)

    matrix_grads = tuple(
        jnp.stack([reduced[layer][member] for layer in range(LAYERS)]) for member in range(4)
    )
    vec_d_grad = jnp.dot(
        jnp.stack(vector_d).reshape(-1, features), order_wide.T, precision=PRECISE
    ).reshape(-1)
    own_c = jnp.stack(vector_own).reshape(-1)
    other_c = jnp.stack(vector_other).reshape(-1)
    arrived = flip(jnp.concatenate([vec_d_grad, other_c]), "cy")
    vector = jnp.concatenate([vec_d_grad, own_c]) + arrived
    vector = butterfly(vector, ("tx", "tz"))
    vec_d_grad = vector[: vec_d.size].reshape(vec_d.shape)
    vec_c_grad = vector[vec_d.size :].reshape(vec_c.shape)

    square = sum(jnp.sum(grad * grad) for grad in matrix_grads)
    square = (
        square
        + jnp.sum(vec_d_grad * vec_d_grad) / (tok_count * ch_count)
        + jnp.sum(vec_c_grad * vec_c_grad) / tok_count
    )
    total_square = butterfly(jnp.full((8, 128), square), ("cc", "cy", "tx", "tz"))[0, 0]
    grad_norm = jnp.sqrt(total_square)
    factor = CLIP_LIMIT / jnp.maximum(grad_norm, CLIP_LIMIT)
    attention_update = adamw(
        w_qkv, w_qkv_first, w_qkv_second, matrix_grads[0] * factor, RATE_QKV, WEIGHT_DECAY
    )
    output_update = adamw(
        w_out_t, w_out_first, w_out_second, matrix_grads[1] * factor, RATE_OUT, WEIGHT_DECAY
    )
    expand_update = adamw(
        w_up, w_up_first, w_up_second, matrix_grads[2] * factor, RATE_UP, WEIGHT_DECAY
    )
    reduce_update = adamw(
        w_down_t, w_down_first, w_down_second, matrix_grads[3] * factor, RATE_DOWN, WEIGHT_DECAY
    )
    width_update = adamw(vec_d, vec_d_first, vec_d_second, vec_d_grad * factor, RATE_VECTOR, 0.0)
    channel_update = adamw(vec_c, vec_c_first, vec_c_second, vec_c_grad * factor, RATE_VECTOR, 0.0)
    return (
        activations,
        input_grad,
        grad_norm,
        *attention_update,
        *output_update,
        *expand_update,
        *reduce_update,
        *width_update,
        *channel_update,
    )


def solution(mesh):
    tok, ch = mesh.shape["tok"], mesh.shape["ch"]
    fine = Mesh(mesh.devices.reshape(tok // 2, 2, 2, ch // 2), ("tz", "tx", "cy", "cc"))
    t, c = ("tz", "tx"), ("cy", "cc")
    cube = P(None, None, t, c)
    matrix = P(None, t, c)
    channel = P(None, None, c)
    return jax.shard_map(
        shards,
        mesh=fine,
        in_specs=(
            P(t, None),
            P(t, None),
            P(None, t, None, None, c),
            P(),
            P(t, None, None),
            P(t),
            *(cube,) * 3,
            *(matrix,) * 9,
            *(P(),) * 3,
            *(channel,) * 3,
        ),
        out_specs=(
            P(t, None),
            P(t, None),
            P(),
            *(cube,) * 3,
            *(matrix,) * 9,
            *(P(),) * 3,
            *(channel,) * 3,
        ),
        check_vma=False,
    )
```

time: 1900 us -> 896 us (0.47)
  waiting for transfers between devices: 732 us -> 219 us
  other arithmetic: 389 us -> 117 us
  blocking collectives: 186 us -> 0 us
  local copies, waits for them, and re-layouts: 280 us -> 119 us
  starting transfers between devices: 1.32 us -> 121 us
  Pallas kernels: 0 us -> 72.2 us
  matrix products: 272 us -> 228 us
    psum x8 -> x0, waiting for transfers between devices: 457 us -> none  [the longest x4 216 us: sum_branch(): return lax.psum(partial_sum.astype(jnp.bfloat16), 'ch').astype(jnp.float32)]
    another operation x42 -> x16, other arithmetic: 206 us -> 2.51 us  [the longest x10 108 us: gram_tables(): factor_lower = jnp.linalg.cholesky(gram)]
    ppermute x0 -> x62, waiting for transfers between devices: none -> 201 us  [the longest x50 189 us: flip(): return lax.ppermute(array, axis, SWAP)]
    reduce_scatter x2 -> x0, waiting for transfers between devices: 189 us -> none  [the longest x1 95.9 us: shards(): lax.psum_scatter(stacked_grads[3], 'tok', scatter_dimension=1, tiled=True)]
    all_gather x4 -> x0, blocking collectives: 145 us -> none  [the longest x2 78.1 us: shards(): lax.all_gather(w_qkv[layer_index].astype(jnp.bfloat16), 'tok', axis=1, ti...]
    unnamed x18 -> x0, waiting for transfers between devices: 81.7 us -> none
    pallas_call x0 -> x5, Pallas kernels: none -> 72.2 us  [the longest x2 36.1 us: attention_backward(): pl.pallas_call(attention_backward_kernel, grid=(segs, pairs), in_specs=[p...]
    another operation x64 -> x1, local copies, waits for them, and re-layouts: 67.7 us -> 0.01 us
  transfers between devices with their start and end apart: 16 -> 74, of which waited for: 12 -> 29; matrix products, arithmetic and copies ran while one was open for 9% -> 44% of each run, Pallas kernels for 0% -> 8%
where the time goes in v1:
time: 896 us; the launch traced here: 885 us
  matrix products  228 us (25%)
  waiting for transfers between devices  219 us (24%)
  starting transfers between devices  121 us (14%)
  local copies, waits for them, and re-layouts  119 us (13%)
  other arithmetic  117 us (13%)
  Pallas kernels  72.2 us (8%)
  between operations  9.94 us (1%)
    dot_general x80, matrix products, dot(): lax.dot_general(left, right, dims, precision=precision, preferred_element...  217 us
    ppermute x50, waiting for transfers between devices, flip(): return lax.ppermute(array, axis, SWAP)  189 us
    ppermute x50, starting transfers between devices, flip(): return lax.ppermute(array, axis, SWAP)  43 us
    all_to_all x8, starting transfers between devices, reduce_slabs(): lax.all_to_all(pieces, 'tz', 0, 0, tiled=True).astype(F32).sum(axis=0)  36.9 us
    unnamed x355, local copies, waits for them, and re-layouts  36.4 us
    pallas_call x2, Pallas kernels, attention_backward(): pl.pallas_call(attention_backward_kernel, grid=(segs, pairs), in_specs=[p...  36.1 us
    pallas_call x2, Pallas kernels, attention_forward(): pl.pallas_call(attention_forward_kernel, grid=(segs, pairs), in_specs=[pl...  24.3 us
    all_to_all x4, starting transfers between devices, all_gather_slabs(): lax.all_to_all(spread, 'tz', 0, 0, tiled=True).reshape(-1, shard.shape[-1])  20.5 us
  transfers between devices with their start and end apart: 74, of which 29 were waited for; matrix products, arithmetic and copies ran while one was open for 44% of the time, Pallas kernels for 8%

profile of v1, /device:TPU:0, one launch (start us, length us, event | category | flops | bytes accessed | tf_op | source)
XLA Modules:
  0.0 885.2 jit_solution(6492281543001993851)
XLA Ops:
  8.0 4.9 all-to-all-start
  14.0 11.8 %shard_map.391 = bf16[256,768]{1,0:T(8,128)(2,1)S(1)} custom-call(f32[256,256]{1,0:T(8,128)S(1)} %fusion.364.old_ref, f32[256,768]{1,0:T(8,128)S(1)} %fusion.259.design_ref), custom_call_target="tpu_custom_call" | custom-call | flops 6000000000 | bytes 2000000 | tf_op jit(solution)/shard_map/pallas_call | solution.py:87
  48.8 5.6 all-to-all-start.1
  63.4 6.3 collective-permute-done
  77.2 10.4 %collective-permute-done.2 = bf16[384,768]{1,0:T(8,128)(2,1)S(1)} collective-permute-done((bf16[384,768]{1,0:T(8,128)(2,1)S(1)}, bf16[384,768]{1,0:T(8,128)(2,1)S(1)}, u32[]{:S(2)}, u32[]{:S(2)}) %collective-permute-start.2) | collective-permute-done | bytes 589856 | tf_op jit(solution)/shard_map/ppermute | solution.py:301
  122.2 5.0 all-to-all-start.2
  129.8 11.9 %shard_map.392 = (bf16[1024,384]{1,0:T(8,128)(2,1)S(1)}, f32[6,2,512]{2,1,0:T(2,128)S(1)}) custom-call(f32[2]{0:T(128)S(1)} %pad_maximum_fusion.36.bias_ref, bf16[1024,1152]{1,0:T(8,128)(2,1)S(1)} %copy-done.3, bf16[1024,1152]{1,0:T(8,128)(2,1)S(1)} %copy-done.3, bf16[1024,1152]{1,0:T(8,128)(2,1)S(1)} %copy-done.3, ...), custom_call_target="tpu_custom_call" | custom-call | flops 12000000000 | bytes 5000000 | tf_op jit(solution)/shard_map/pallas_call | solution.py:144
  148.2 5.2 collective-permute-done.9
  162.6 28.7 %collective-permute-done.10 = bf16[384,1536]{1,0:T(8,128)(2,1)S(1)} collective-permute-done((bf16[384,1536]{1,0:T(8,128)(2,1)}, bf16[384,1536]{1,0:T(8,128)(2,1)S(1)}, u32[]{:S(2)}, u32[]{:S(2)}) %collective-permute-start.10) | collective-permute-done | bytes 1179680 | tf_op jit(solution)/shard_map/ppermute | solution.py:301
  191.4 13.5 %multiply_convert_fusion.1 = (bf16[1024,1536]{1,0:T(8,128)(2,1)S(1)}, f32[1024,1536]{1,0:T(8,128)}) fusion(f32[1536]{0:T(1024)S(1)} %pad_maximum_fusion.33, bf16[1024,768]{0,1:T(8,128)(2,1)S(1)} %add_convert_fusion.6, bf16[384,768]{1,0:T(8,128)(2,1)S(1)} %get-tuple-element.218, bf16[384,768]{1,0:T(8,128)(2,1)S(1)} %get-tuple-element.216, ...), kind=kOutput, calls=%fused_computation.21 | convolution fusion | flops 2441084928 | bytes 13375488 | tf_op jit(solution)/shard_map/dot_general | solution.py:45
  204.9 11.5 %convolution_convert_fusion.5 = bf16[1024,768]{0,1:T(8,128)(2,1)} fusion(bf16[1024,1536]{1,0:T(8,128)(2,1)S(1)} %get-tuple-element.295, bf16[384,768]{1,0:T(8,128)(2,1)S(1)} %get-tuple-element.217, bf16[384,768]{1,0:T(8,128)(2,1)S(1)} %get-tuple-element.215, bf16[384,768]{1,0:T(8,128)(2,1)S(1)} %get-tuple-element.213, ...), kind=kOutput, calls=%fused_computation.120 | convolution fusion | flops 2426142720 | bytes 7077888 | tf_op jit(solution)/shard_map/dot_general | solution.py:45
  217.6 5.1 all-to-all-start.3
  229.4 9.8 %collective-permute-done.13 = bf16[384,768]{1,0:T(8,128)(2,1)S(1)} collective-permute-done((bf16[384,768]{1,0:T(8,128)(2,1)}, bf16[384,768]{1,0:T(8,128)(2,1)S(1)}, u32[]{:S(2)}, u32[]{:S(2)}) %collective-permute-start.13) | collective-permute-done | bytes 589856 | tf_op jit(solution)/shard_map/ppermute | solution.py:301
  240.1 11.0 %collective-permute-done.14 = bf16[384,768]{1,0:T(8,128)(2,1)S(1)} collective-permute-done((bf16[384,768]{1,0:T(8,128)(2,1)}, bf16[384,768]{1,0:T(8,128)(2,1)S(1)}, u32[]{:S(2)}, u32[]{:S(2)}) %collective-permute-start.14) | collective-permute-done | bytes 589856 | tf_op jit(solution)/shard_map/ppermute | solution.py:301
  279.1 4.3 collective-permute-start.15
  286.0 6.5 collective-permute-done.15
  294.4 12.4 %shard_map.393 = (bf16[1024,384]{1,0:T(8,128)(2,1)S(1)}, f32[6,2,512]{2,1,0:T(2,128)S(1)}) custom-call(f32[2]{0:T(128)S(1)} %pad_maximum_fusion.36.bias_ref, bf16[1024,1152]{1,0:T(8,128)(2,1)S(1)} %copy-done.5, bf16[1024,1152]{1,0:T(8,128)(2,1)S(1)} %copy-done.5, bf16[1024,1152]{1,0:T(8,128)(2,1)S(1)} %copy-done.5, ...), custom_call_target="tpu_custom_call" | custom-call | flops 12000000000 | bytes 5000000 | tf_op jit(solution)/shard_map/pallas_call | solution.py:144
  309.0 7.3 collective-permute-done.18
  328.6 14.4 %collective-permute-done.19 = bf16[384,1536]{1,0:T(8,128)(2,1)} collective-permute-done((bf16[384,1536]{1,0:T(8,128)(2,1)}, bf16[384,1536]{1,0:T(8,128)(2,1)}, u32[]{:S(2)}, u32[]{:S(2)}) %collective-permute-start.19) | collective-permute-done | bytes 1179680 | tf_op jit(solution)/shard_map/ppermute | solution.py:301
  352.8 15.2 %convert_reduce_fusion = (f32[1536]{0:T(1024)S(1)}, bf16[1024,1536]{1,0:T(8,128)(2,1)S(1)}) fusion(f32[1024,1536]{1,0:T(8,128)S(1)} %get-tuple-element.299, f32[1536]{0:T(1024)S(1)} %pad_maximum_fusion.34, bf16[1024,768]{1,0:T(8,128)(2,1)S(1)} %copy-done.161, bf16[384,768]{1,0:T(8,128)(2,1)S(1)} %get-tuple-element.209, ...), kind=kOutput, calls=%fused_computation.18 | convolution fusion | flops 2461530624 | bytes 13381632 | tf_op jit(solution)/shard_map/dot_general | solution.py:45
  368.1 11.3 %convolution_convert_fusion.3 = bf16[1024,768]{0,1:T(8,128)(2,1)} fusion(bf16[1024,1536]{1,0:T(8,128)(2,1)S(1)} %get-tuple-element.301, bf16[384,768]{1,0:T(8,128)(2,1)S(1)} %get-tuple-element.210, bf16[384,768]{1,0:T(8,128)(2,1)S(1)} %get-tuple-element.208, bf16[384,768]{1,0:T(8,128)(2,1)S(1)} %get-tuple-element.206, ...), kind=kOutput, calls=%fused_computation.118 | convolution fusion | flops 2426142720 | bytes 7077888 | tf_op jit(solution)/shard_map/dot_general | solution.py:45
  381.7 11.5 %convolution_convert_fusion.4 = bf16[1024,768]{0,1:T(8,128)(2,1)} fusion(bf16[1024,1536]{1,0:T(8,128)(2,1)S(1)} %get-tuple-element.298, bf16[384,768]{1,0:T(8,128)(2,1)S(1)} %get-tuple-element.209, bf16[384,768]{1,0:T(8,128)(2,1)S(1)} %get-tuple-element.207, bf16[384,768]{1,0:T(8,128)(2,1)S(1)} %get-tuple-element.205, ...), kind=kOutput, calls=%fused_computation.119 | convolution fusion | flops 2426142720 | bytes 7077888 | tf_op jit(solution)/shard_map/dot_general | solution.py:45
  401.4 8.4 collective-permute-done.45
  422.3 11.9 %collective-permute-done.46 = bf16[384,768]{1,0:T(8,128)(2,1)S(1)} collective-permute-done((bf16[384,768]{1,0:T(8,128)(2,1)S(1)}, bf16[384,768]{1,0:T(8,128)(2,1)S(1)}, u32[]{:S(2)}, u32[]{:S(2)}) %collective-permute-start.46) | collective-permute-done | bytes 589856 | tf_op jit(solution)/shard_map/ppermute | solution.py:301
  435.8 4.8 all-to-all-start.9
  446.9 5.8 convert_reduce_fusion.3
  454.6 18.1 %shard_map.394 = (bf16[1024,384]{1,0:T(8,128)(2,1)S(1)}, f32[1024,384]{1,0:T(8,128)}, f32[1024,384]{1,0:T(8,128)}, f32[2,256,384]{2,1,0:T(8,128)S(1)}, f32[2,256,384]{2,1,0:T(8,128)S(1)}) custom-call(f32[2]{0:T(128)S(1)} %pad_maximum_fusion.36.bias_ref, bf16[1024,1152]{1,0:T(8,128)(2,1)} %copy-done.4, bf16[1024,1152]{1,0:T(8,128)(2,1)} %copy-done.4, ...), custom_call_target="tpu_custom_call" | custom-call | flops 24000000000 | bytes 9000000 | tf_op jit(solution)/shard_map/pallas_call | solution.py:236
  487.9 9.6 %collective-permute-done.39 = bf16[384,192]{0,1:T(8,128)(2,1)S(1)} collective-permute-done((bf16[384,192]{0,1:T(8,128)(2,1)S(1)}, bf16[384,192]{0,1:T(8,128)(2,1)S(1)}, u32[]{:S(2)}, u32[]{:S(2)}) %collective-permute-start.39) | collective-permute-done | bytes 147488 | tf_op jit(solution)/shard_map/ppermute | solution.py:301
  525.7 4.8 all-to-all-start.11
  535.4 11.0 %all-to-all-done.11 = bf16[4,96,768]{2,1,0:T(8,128)(2,1)S(1)} async-done(((bf16[4,96,768]{2,1,0:T(8,128)(2,1)}), bf16[4,96,768]{2,1,0:T(8,128)(2,1)S(1)}, u32[]{:S(2)}, u32[]{:S(2)}) %all-to-all-start.11) | async-done | bytes 589856 | tf_op jit(solution)/shard_map/all_to_all | solution.py:336
  563.7 4.3 all-to-all-start.5
  571.7 5.3 convert_reduce_fusion.4
  577.1 15.0 %convert_reduce_fusion.1 = (f32[1536]{0:T(1024)S(1)}, bf16[1024,1536]{1,0:T(8,128)(2,1)S(1)}) fusion(f32[1024,1536]{1,0:T(8,128)S(1)} %bitcast.237, f32[1536]{0:T(1024)S(1)} %copy-done.145, bf16[1024,768]{0,1:T(8,128)(2,1)S(1)} %get-tuple-element.184, bf16[384,768]{1,0:T(8,128)(2,1)S(1)} %copy-done.93, bf16[384,768]{1,0:T(8,128)(2,1)S(1)} %copy-done.85, ...), kind=kOutput, calls=%fused_computation.19 | convolution fusion | flops 2461530624 | bytes 13381632 | tf_op jit(solution)/shard_map/dot_general | solution.py:45
  592.1 11.7 %convolution_convert_fusion.2 = bf16[1024,768]{0,1:T(8,128)(2,1)} fusion(bf16[1024,1536]{1,0:T(8,128)(2,1)S(1)} %get-tuple-element.303, bf16[384,768]{1,0:T(8,128)(2,1)S(1)} %copy-done.91, bf16[384,768]{1,0:T(8,128)(2,1)S(1)} %copy-done.83, bf16[384,768]{1,0:T(8,128)(2,1)S(1)} %copy-done.87, bf16[384,768]{1,0:T(8,128)(2,1)S(1)} %copy-done.79), kind=kOutput, calls=%fused_computation.117 | convolution fusion | flops 2426142720 | bytes 7077888 | tf_op jit(solution)/shard_map/dot_general | solution.py:45
  612.9 9.8 %collective-permute-done.42 = bf16[384,768]{1,0:T(8,128)(2,1)S(1)} collective-permute-done((bf16[384,768]{1,0:T(8,128)(2,1)S(1)}, bf16[384,768]{1,0:T(8,128)(2,1)S(1)}, u32[]{:S(2)}, u32[]{:S(2)}) %collective-permute-start.42) | collective-permute-done | bytes 589856 | tf_op jit(solution)/shard_map/ppermute | solution.py:301
  630.4 5.0 collective-permute-done.41
  635.4 14.1 %collective-permute-done.43 = bf16[384,768]{1,0:T(8,128)(2,1)} collective-permute-done((bf16[384,768]{1,0:T(8,128)(2,1)}, bf16[384,768]{1,0:T(8,128)(2,1)}, u32[]{:S(2)}, u32[]{:S(2)}) %collective-permute-start.43) | collective-permute-done | bytes 589856 | tf_op jit(solution)/shard_map/ppermute | solution.py:301
  652.7 5.2 all-to-all-start.8
  665.3 5.2 convert_reduce_fusion.5
  672.5 18.0 %shard_map.395 = (bf16[1024,384]{1,0:T(8,128)(2,1)S(1)}, f32[1024,384]{1,0:T(8,128)}, f32[1024,384]{1,0:T(8,128)}, f32[2,256,384]{2,1,0:T(8,128)S(1)}, f32[2,256,384]{2,1,0:T(8,128)S(1)}) custom-call(f32[2]{0:T(128)S(1)} %pad_maximum_fusion.36.bias_ref, bf16[1024,1152]{1,0:T(8,128)(2,1)} %copy-done.2, bf16[1024,1152]{1,0:T(8,128)(2,1)} %copy-done.2, ...), custom_call_target="tpu_custom_call" | custom-call | flops 24000000000 | bytes 9000000 | tf_op jit(solution)/shard_map/pallas_call | solution.py:236
  704.4 6.8 collective-permute-done.36
  713.4 4.6 collective-permute-done.37
  746.4 5.1 all-to-all-start.10
  767.5 4.4 all-to-all-start.6
  819.0 9.1 %fusion.14 = f32[2048,768]{1,0:T(8,128)} fusion(bf16[1024,768]{0,1:T(8,128)(2,1)} %collective-permute-done.21, bf16[1024,768]{0,1:T(8,128)(2,1)} %get-tuple-element.202, pred[]{:T(512)S(6)} %eq.36, s32[768]{0:T(1024)S(1)} %copy-done.152), kind=kOutput, calls=%fused_computation.25 | convolution fusion | flops 2430664704 | bytes 9440257 | tf_op jit(solution)/shard_map/dot_general | solution.py:45
  835.9 4.5 add_convert_fusion.2
  861.6 13.3 %collective-permute-done.28 = bf16[1024,768]{0,1:T(8,128)(2,1)} collective-permute-done((bf16[1024,768]{0,1:T(8,128)(2,1)}, bf16[1024,768]{0,1:T(8,128)(2,1)}, u32[]{:S(2)}, u32[]{:S(2)}) %collective-permute-start.28) | collective-permute-done | bytes 1572896 | tf_op jit(solution)/shard_map/ppermute | solution.py:301
  874.9 9.1 %fusion.20 = f32[2048,768]{1,0:T(8,128)} fusion(bf16[1024,768]{0,1:T(8,128)(2,1)} %collective-permute-done.28, bf16[1024,768]{0,1:T(8,128)(2,1)} %add_convert_fusion.2, pred[]{:T(512)S(6)} %eq.36, s32[768]{0:T(1024)S(1)} %copy-done.152), kind=kOutput, calls=%fused_computation.36 | convolution fusion | flops 2430664704 | bytes 9440257 | tf_op jit(solution)/shard_map/dot_general | solution.py:45
  (764 shorter events, 427.3 us)
Async XLA Ops:
  0.7 41.2 %collective-permute-start.3 = (f32[2,6,192]{2,0,1:T(2,128)}, f32[2,6,192]{2,0,1:T(2,128)}, u32[]{:S(2)}, u32[]{:S(2)}) collective-permute-start(f32[2,6,192]{2,0,1:T(2,128)} %param.45), channel_id=1, source_target_pairs={{0,2},{2,0},{1,3},{3,1},{4,6},{6,4},{5,7},{7,5},{8,10},{10,8},{9,1... | collective-permute-start | bytes 27656 | tf_op jit(solution)/shard_map/ppermute | solution.py:301
  8.0 38.7 %all-to-all-start = ((bf16[4,96,768]{2,1,0:T(8,128)(2,1)}), bf16[4,96,768]{2,1,0:T(8,128)(2,1)}, u32[]{:S(2)}, u32[]{:S(2)}) async-start(bf16[4,96,768]{2,1,0:T(8,128)(2,1)} %broadcast_in_dim.38), calls=%async_computation | async-start | bytes 1179648 | tf_op jit(solution)/shard_map/all_to_all | solution.py:317
  25.8 32.1 %collective-permute-start.5 = (bf16[256,768]{1,0:T(8,128)(2,1)S(1)}, bf16[256,768]{1,0:T(8,128)(2,1)}, u32[]{:S(2)}, u32[]{:S(2)}) collective-permute-start(bf16[256,768]{1,0:T(8,128)(2,1)S(1)} %shard_map.391), channel_id=1, source_target_pairs={{0,1},{1,0},{2,3},{3,2},{4,5},{5,4},{6,7},{7,6},{8,9},{9,8},{10,11... | collective-permute-start | bytes 1179656 | tf_op jit(solution)/shard_map/ppermute | solution.py:301
  25.9 18.7 %collective-permute-start.4 = (bf16[2,256,2,192]{1,3,2,0:T(8,128)(2,1)}, bf16[2,256,2,192]{1,3,2,0:T(8,128)(2,1)}, u32[]{:S(2)}, u32[]{:S(2)}) collective-permute-start(bf16[2,256,2,192]{1,3,2,0:T(8,128)(2,1)} %bitcast.13), channel_id=1, source_target_pairs={{0,2},{2,0},{1,3},{3,1},{4,6},{6,4},{5,7},{7,5},{8,10},{10,8},{9,1... | collective-permute-start | bytes 1179656 | tf_op jit(solution)/shard_map/ppermute | solution.py:301
  48.8 71.7 %all-to-all-start.1 = ((bf16[4,96,1536]{2,1,0:T(8,128)(2,1)}), bf16[4,96,1536]{2,1,0:T(8,128)(2,1)}, u32[]{:S(2)}, u32[]{:S(2)}) async-start(bf16[4,96,1536]{2,1,0:T(8,128)(2,1)} %broadcast_in_dim.40), calls=%async_computation.1 | async-start | bytes 2359296 | tf_op jit(solution)/shard_map/all_to_all | solution.py:317
  69.8 17.9 %collective-permute-start.2 = (bf16[384,768]{1,0:T(8,128)(2,1)S(1)}, bf16[384,768]{1,0:T(8,128)(2,1)S(1)}, u32[]{:S(2)}, u32[]{:S(2)}) collective-permute-start(bf16[384,768]{1,0:T(8,128)(2,1)S(1)} %collective-permute-done), channel_id=1, source_target_pairs={{0,2},{2,0},{1,3},{3,1},{4,6},{6,4},{5,7},{7,5},{8,10},{10,8},{9,1... | collective-permute-start | bytes 1769480 | tf_op jit(solution)/shard_map/ppermute | solution.py:301
  111.3 16.6 %collective-permute-start.6 = (bf16[256,768]{1,0:T(8,128)(2,1)}, bf16[256,768]{1,0:T(8,128)(2,1)}, u32[]{:S(2)}, u32[]{:S(2)}) collective-permute-start(bf16[256,768]{1,0:T(8,128)(2,1)} %copy.226), channel_id=1, source_target_pairs={{0,2},{1,3},{4,6},{5,7},{8,10},{9,11},{12,14},{13,15},{16,18},{17,... | collective-permute-start | bytes 1179656 | tf_op jit(solution)/shard_map/ppermute | solution.py:467
  122.2 23.1 %all-to-all-start.2 = ((bf16[4,96,768]{2,1,0:T(8,128)(2,1)}), bf16[4,96,768]{2,1,0:T(8,128)(2,1)}, u32[]{:S(2)}, u32[]{:S(2)}) async-start(bf16[4,96,768]{2,1,0:T(8,128)(2,1)} %broadcast_in_dim.41), calls=%async_computation.2 | async-start | bytes 1179648 | tf_op jit(solution)/shard_map/all_to_all | solution.py:317
  127.3 26.1 %collective-permute-start.9 = (bf16[384,1536]{1,0:T(8,128)(2,1)}, bf16[384,1536]{1,0:T(8,128)(2,1)}, u32[]{:S(2)}, u32[]{:S(2)}) collective-permute-start(bf16[384,1536]{1,0:T(8,128)(2,1)} %bitcast.24), channel_id=1, source_target_pairs={{0,2},{2,0},{1,3},{3,1},{4,6},{6,4},{5,7},{7,5},{8,10},{10,8},{9,1... | collective-permute-start | bytes 3538952 | tf_op jit(solution)/shard_map/ppermute | solution.py:301
  127.3 29.3 %collective-permute-start.8 = (bf16[384,1536]{1,0:T(8,128)(2,1)}, bf16[384,1536]{1,0:T(8,128)(2,1)}, u32[]{:S(2)}, u32[]{:S(2)}) collective-permute-start(bf16[384,1536]{1,0:T(8,128)(2,1)} %bitcast.24), channel_id=1, source_target_pairs={{0,4},{4,0},{1,5},{5,1},{2,6},{6,2},{3,7},{7,3},{8,12},{12,8},{9,1... | collective-permute-start | bytes 3538952 | tf_op jit(solution)/shard_map/ppermute | solution.py:301
  145.3 80.6 %collective-permute-start.12 = (bf16[384,768]{1,0:T(8,128)(2,1)}, bf16[384,768]{1,0:T(8,128)(2,1)}, u32[]{:S(2)}, u32[]{:S(2)}) collective-permute-start(bf16[384,768]{1,0:T(8,128)(2,1)} %bitcast.31), channel_id=1, source_target_pairs={{0,4},{4,0},{1,5},{5,1},{2,6},{6,2},{3,7},{7,3},{8,12},{12,8},{9,1... | collective-permute-start | bytes 1769480 | tf_op jit(solution)/shard_map/ppermute | solution.py:301
  153.4 37.9 %collective-permute-start.10 = (bf16[384,1536]{1,0:T(8,128)(2,1)}, bf16[384,1536]{1,0:T(8,128)(2,1)S(1)}, u32[]{:S(2)}, u32[]{:S(2)}) collective-permute-start(bf16[384,1536]{1,0:T(8,128)(2,1)} %collective-permute-done.9), channel_id=1, source_target_pairs={{0,4},{4,0},{1,5},{5,1},{2,6},{6,2},{3,7},{7,3},{8,12},{12,8},{9,1... | collective-permute-start | bytes 3538952 | tf_op jit(solution)/shard_map/ppermute | solution.py:301
  216.4 41.8 %collective-permute-start.11 = (bf16[1024,768]{0,1:T(8,128)(2,1)}, bf16[1024,768]{0,1:T(8,128)(2,1)}, u32[]{:S(2)}, u32[]{:S(2)}) collective-permute-start(bf16[1024,768]{0,1:T(8,128)(2,1)} %convolution_convert_fusion.5), channel_id=1, source_target_pairs={{0,1},{1,0},{2,3},{3,2},{4,5},{5,4},{6,7},{7,6},{8,9},{9,8},{10,11... | collective-permute-start | bytes 4718600 | tf_op jit(solution)/shard_map/ppermute | solution.py:301
  217.6 67.7 %all-to-all-start.3 = ((bf16[4,96,1536]{2,1,0:T(8,128)(2,1)}), bf16[4,96,1536]{2,1,0:T(8,128)(2,1)}, u32[]{:S(2)}, u32[]{:S(2)}) async-start(bf16[4,96,1536]{2,1,0:T(8,128)(2,1)} %broadcast_in_dim.42), calls=%async_computation.3 | async-start | bytes 2359296 | tf_op jit(solution)/shard_map/all_to_all | solution.py:317
  225.9 25.2 %collective-permute-start.14 = (bf16[384,768]{1,0:T(8,128)(2,1)}, bf16[384,768]{1,0:T(8,128)(2,1)S(1)}, u32[]{:S(2)}, u32[]{:S(2)}) collective-permute-start(bf16[384,768]{1,0:T(8,128)(2,1)} %collective-permute-done.12), channel_id=1, source_target_pairs={{0,2},{2,0},{1,3},{3,1},{4,6},{6,4},{5,7},{7,5},{8,10},{10,8},{9,1... | collective-permute-start | bytes 1769480 | tf_op jit(solution)/shard_map/ppermute | solution.py:301
  285.3 30.9 %collective-permute-start.18 = (bf16[384,1536]{1,0:T(8,128)(2,1)}, bf16[384,1536]{1,0:T(8,128)(2,1)}, u32[]{:S(2)}, u32[]{:S(2)}) collective-permute-start(bf16[384,1536]{1,0:T(8,128)(2,1)} %bitcast.43), channel_id=1, source_target_pairs={{0,2},{2,0},{1,3},{3,1},{4,6},{6,4},{5,7},{7,5},{8,10},{10,8},{9,1... | collective-permute-start | bytes 3538952 | tf_op jit(solution)/shard_map/ppermute | solution.py:301
  285.4 41.8 %collective-permute-start.17 = (bf16[384,1536]{1,0:T(8,128)(2,1)}, bf16[384,1536]{1,0:T(8,128)(2,1)}, u32[]{:S(2)}, u32[]{:S(2)}) collective-permute-start(bf16[384,1536]{1,0:T(8,128)(2,1)} %bitcast.43), channel_id=1, source_target_pairs={{0,4},{4,0},{1,5},{5,1},{2,6},{6,2},{3,7},{7,3},{8,12},{12,8},{9,1... | collective-permute-start | bytes 3538952 | tf_op jit(solution)/shard_map/ppermute | solution.py:301
  309.0 35.4 %collective-permute-start.16 = (bf16[1024,768]{0,1:T(8,128)(2,1)}, bf16[1024,768]{0,1:T(8,128)(2,1)}, u32[]{:S(2)}, u32[]{:S(2)}) collective-permute-start(bf16[1024,768]{0,1:T(8,128)(2,1)} %convolution_convert_fusion), channel_id=1, source_target_pairs={{0,1},{1,0},{2,3},{3,2},{4,5},{5,4},{6,7},{7,6},{8,9},{9,8},{10,11... | collective-permute-start | bytes 4718600 | tf_op jit(solution)/shard_map/ppermute | solution.py:301
  316.2 26.7 %collective-permute-start.19 = (bf16[384,1536]{1,0:T(8,128)(2,1)}, bf16[384,1536]{1,0:T(8,128)(2,1)}, u32[]{:S(2)}, u32[]{:S(2)}) collective-permute-start(bf16[384,1536]{1,0:T(8,128)(2,1)} %collective-permute-done.18), channel_id=1, source_target_pairs={{0,4},{4,0},{1,5},{5,1},{2,6},{6,2},{3,7},{7,3},{8,12},{12,8},{9,1... | collective-permute-start | bytes 3538952 | tf_op jit(solution)/shard_map/ppermute | solution.py:301
  395.4 19.3 %collective-permute-start.51 = (bf16[384,768]{1,0:T(8,128)(2,1)}, bf16[384,768]{1,0:T(8,128)(2,1)}, u32[]{:S(2)}, u32[]{:S(2)}) collective-permute-start(bf16[384,768]{1,0:T(8,128)(2,1)} %fusion.220), channel_id=1, source_target_pairs={{0,2},{2,0},{1,3},{3,1},{4,6},{6,4},{5,7},{7,5},{8,10},{10,8},{9,1... | collective-permute-start | bytes 1769480 | tf_op jit(solution)/shard_map/ppermute | solution.py:301
  399.5 43.8 %collective-permute-start.22 = (bf16[1024,768]{0,1:T(8,128)(2,1)}, bf16[1024,768]{0,1:T(8,128)(2,1)}, u32[]{:S(2)}, u32[]{:S(2)}) collective-permute-start(bf16[1024,768]{0,1:T(8,128)(2,1)} %convolution_convert_fusion.3), channel_id=1, source_target_pairs={{0,1},{1,0},{2,3},{3,2},{4,5},{5,4},{6,7},{7,6},{8,9},{9,8},{10,11... | collective-permute-start | bytes 4718600 | tf_op jit(solution)/shard_map/ppermute | solution.py:301
  399.5 22.8 %collective-permute-start.44 = (bf16[384,768]{1,0:T(8,128)(2,1)S(1)}, bf16[384,768]{1,0:T(8,128)(2,1)S(1)}, u32[]{:S(2)}, u32[]{:S(2)}) collective-permute-start(bf16[384,768]{1,0:T(8,128)(2,1)S(1)} %fusion.154), channel_id=1, source_target_pairs={{0,4},{4,0},{1,5},{5,1},{2,6},{6,2},{3,7},{7,3},{8,12},{12,8},{9,1... | collective-permute-start | bytes 1769480 | tf_op jit(solution)/shard_map/ppermute | solution.py:301
  401.0 39.6 %collective-permute-start.50 = (bf16[384,768]{1,0:T(8,128)(2,1)}, bf16[384,768]{1,0:T(8,128)(2,1)}, u32[]{:S(2)}, u32[]{:S(2)}) collective-permute-start(bf16[384,768]{1,0:T(8,128)(2,1)} %fusion.217), channel_id=1, source_target_pairs={{0,2},{2,0},{1,3},{3,1},{4,6},{6,4},{5,7},{7,5},{8,10},{10,8},{9,1... | collective-permute-start | bytes 1769480 | tf_op jit(solution)/shard_map/ppermute | solution.py:301
  412.1 22.1 %collective-permute-start.46 = (bf16[384,768]{1,0:T(8,128)(2,1)S(1)}, bf16[384,768]{1,0:T(8,128)(2,1)S(1)}, u32[]{:S(2)}, u32[]{:S(2)}) collective-permute-start(bf16[384,768]{1,0:T(8,128)(2,1)S(1)} %fusion.166), channel_id=1, source_target_pairs={{0,2},{2,0},{1,3},{3,1},{4,6},{6,4},{5,7},{7,5},{8,10},{10,8},{9,1... | collective-permute-start | bytes 1769480 | tf_op jit(solution)/shard_map/ppermute | solution.py:301
  417.4 23.3 %collective-permute-start.52 = (bf16[384,768]{1,0:T(8,128)(2,1)}, bf16[384,768]{1,0:T(8,128)(2,1)}, u32[]{:S(2)}, u32[]{:S(2)}) collective-permute-start(bf16[384,768]{1,0:T(8,128)(2,1)} %add_convert_fusion.9), channel_id=1, source_target_pairs={{0,4},{4,0},{1,5},{5,1},{2,6},{6,2},{3,7},{7,3},{8,12},{12,8},{9,1... | collective-permute-start | bytes 1769480 | tf_op jit(solution)/shard_map/ppermute | solution.py:301
  422.3 24.5 %collective-permute-start.20 = (bf16[1024,768]{0,1:T(8,128)(2,1)}, bf16[1024,768]{0,1:T(8,128)(2,1)}, u32[]{:S(2)}, u32[]{:S(2)}) collective-permute-start(bf16[1024,768]{0,1:T(8,128)(2,1)} %convolution_convert_fusion.4), channel_id=1, source_target_pairs={{0,1},{1,0},{2,3},{3,2},{4,5},{5,4},{6,7},{7,6},{8,9},{9,8},{10,11... | collective-permute-start | bytes 4718600 | tf_op jit(solution)/shard_map/ppermute | solution.py:301
  435.8 89.9 %all-to-all-start.9 = ((bf16[4,96,768]{2,1,0:T(8,128)(2,1)}), bf16[4,96,768]{2,1,0:T(8,128)(2,1)}, u32[]{:S(2)}, u32[]{:S(2)}) async-start(bf16[4,96,768]{2,1,0:T(8,128)(2,1)} %bitcast.215), calls=%async_computation.9 | async-start | bytes 1179648 | tf_op jit(solution)/shard_map/all_to_all | solution.py:336
  482.7 23.0 %collective-permute-start.23 = (bf16[256,768]{0,1:T(8,128)(2,1)}, bf16[256,768]{0,1:T(8,128)(2,1)S(1)}, u32[]{:S(2)}, u32[]{:S(2)}) collective-permute-start(bf16[256,768]{0,1:T(8,128)(2,1)} %bitcast.49), channel_id=1, source_target_pairs={{2,0},{3,1},{6,4},{7,5},{10,8},{11,9},{14,12},{15,13},{18,16},{19,... | collective-permute-start | bytes 1179656 | tf_op jit(solution)/shard_map/ppermute | solution.py:559
  519.4 48.7 %collective-permute-start.24 = (bf16[1024,768]{0,1:T(8,128)(2,1)}, bf16[1024,768]{0,1:T(8,128)(2,1)}, u32[]{:S(2)}, u32[]{:S(2)}) collective-permute-start(bf16[1024,768]{0,1:T(8,128)(2,1)} %fusion.59), channel_id=1, source_target_pairs={{0,1},{1,0},{2,3},{3,2},{4,5},{5,4},{6,7},{7,6},{8,9},{9,8},{10,11... | collective-permute-start | bytes 4718600 | tf_op jit(solution)/shard_map/ppermute | solution.py:301
  522.4 37.0 %collective-permute-start.32 = (bf16[384,576]{0,1:T(8,128)(2,1)}, bf16[384,576]{0,1:T(8,128)(2,1)}, u32[]{:S(2)}, u32[]{:S(2)}) collective-permute-start(bf16[384,576]{0,1:T(8,128)(2,1)} %pad_maximum_fusion.9), channel_id=1, source_target_pairs={{0,4},{4,0},{1,5},{5,1},{2,6},{6,2},{3,7},{7,3},{8,12},{12,8},{9,1... | collective-permute-start | bytes 1327112 | tf_op jit(solution)/shard_map/ppermute | solution.py:301
  525.7 20.8 %all-to-all-start.11 = ((bf16[4,96,768]{2,1,0:T(8,128)(2,1)}), bf16[4,96,768]{2,1,0:T(8,128)(2,1)S(1)}, u32[]{:S(2)}, u32[]{:S(2)}) async-start(bf16[4,96,768]{2,1,0:T(8,128)(2,1)} %bitcast.70), calls=%async_computation.11 | async-start | bytes 1179648 | tf_op jit(solution)/shard_map/all_to_all | solution.py:336
  535.4 24.0 %collective-permute-start.34 = (bf16[384,576]{0,1:T(8,128)(2,1)}, bf16[384,576]{0,1:T(8,128)(2,1)}, u32[]{:S(2)}, u32[]{:S(2)}) collective-permute-start(bf16[384,576]{0,1:T(8,128)(2,1)} %add_convert_fusion.11), channel_id=1, source_target_pairs={{0,2},{2,0},{1,3},{3,1},{4,6},{6,4},{5,7},{7,5},{8,10},{10,8},{9,1... | collective-permute-start | bytes 1327112 | tf_op jit(solution)/shard_map/ppermute | solution.py:301
  563.7 63.7 %all-to-all-start.5 = ((bf16[4,96,576]{2,1,0:T(8,128)(2,1)}), bf16[4,96,576]{2,1,0:T(8,128)(2,1)}, u32[]{:S(2)}, u32[]{:S(2)}) async-start(bf16[4,96,576]{2,1,0:T(8,128)(2,1)} %bitcast.200), calls=%async_computation.5 | async-start | bytes 983040 | tf_op jit(solution)/shard_map/all_to_all | solution.py:336
  610.3 51.4 %collective-permute-start.25 = (bf16[1024,768]{0,1:T(8,128)(2,1)}, bf16[1024,768]{0,1:T(8,128)(2,1)}, u32[]{:S(2)}, u32[]{:S(2)}) collective-permute-start(bf16[1024,768]{0,1:T(8,128)(2,1)} %convolution_convert_fusion.2), channel_id=1, source_target_pairs={{0,1},{1,0},{2,3},{3,2},{4,5},{5,4},{6,7},{7,6},{8,9},{9,8},{10,11... | collective-permute-start | bytes 4718600 | tf_op jit(solution)/shard_map/ppermute | solution.py:301
  610.3 25.1 %collective-permute-start.41 = (bf16[384,768]{1,0:T(8,128)(2,1)S(1)}, bf16[384,768]{1,0:T(8,128)(2,1)S(1)}, u32[]{:S(2)}, u32[]{:S(2)}) collective-permute-start(bf16[384,768]{1,0:T(8,128)(2,1)S(1)} %fusion.121), channel_id=1, source_target_pairs={{0,4},{4,0},{1,5},{5,1},{2,6},{6,2},{3,7},{7,3},{8,12},{12,8},{9,1... | collective-permute-start | bytes 1769480 | tf_op jit(solution)/shard_map/ppermute | solution.py:301
  610.9 47.1 %collective-permute-start.47 = (bf16[384,768]{1,0:T(8,128)(2,1)}, bf16[384,768]{1,0:T(8,128)(2,1)}, u32[]{:S(2)}, u32[]{:S(2)}) collective-permute-start(bf16[384,768]{1,0:T(8,128)(2,1)} %fusion.199), channel_id=1, source_target_pairs={{0,2},{2,0},{1,3},{3,1},{4,6},{6,4},{5,7},{7,5},{8,10},{10,8},{9,1... | collective-permute-start | bytes 1769480 | tf_op jit(solution)/shard_map/ppermute | solution.py:301
  624.4 25.1 %collective-permute-start.43 = (bf16[384,768]{1,0:T(8,128)(2,1)}, bf16[384,768]{1,0:T(8,128)(2,1)}, u32[]{:S(2)}, u32[]{:S(2)}) collective-permute-start(bf16[384,768]{1,0:T(8,128)(2,1)} %fusion.133), channel_id=1, source_target_pairs={{0,2},{2,0},{1,3},{3,1},{4,6},{6,4},{5,7},{7,5},{8,10},{10,8},{9,1... | collective-permute-start | bytes 1769480 | tf_op jit(solution)/shard_map/ppermute | solution.py:301
  626.0 32.0 %collective-permute-start.49 = (bf16[384,768]{1,0:T(8,128)(2,1)}, bf16[384,768]{1,0:T(8,128)(2,1)}, u32[]{:S(2)}, u32[]{:S(2)}) collective-permute-start(bf16[384,768]{1,0:T(8,128)(2,1)} %fusion.196), channel_id=1, source_target_pairs={{0,4},{4,0},{1,5},{5,1},{2,6},{6,2},{3,7},{7,3},{8,12},{12,8},{9,1... | collective-permute-start | bytes 1769480 | tf_op jit(solution)/shard_map/ppermute | solution.py:301
  635.4 183.6 %collective-permute-start.21 = (bf16[1024,768]{0,1:T(8,128)(2,1)}, bf16[1024,768]{0,1:T(8,128)(2,1)}, u32[]{:S(2)}, u32[]{:S(2)}) collective-permute-start(bf16[1024,768]{0,1:T(8,128)(2,1)} %get-tuple-element.202), channel_id=1, source_target_pairs={{0,2},{2,0},{1,3},{3,1},{4,6},{6,4},{5,7},{7,5},{8,10},{10,8},{9,1... | collective-permute-start | bytes 4718600 | tf_op jit(solution)/shard_map/ppermute | solution.py:301
  652.7 93.7 %all-to-all-start.8 = ((bf16[4,96,768]{2,1,0:T(8,128)(2,1)}), bf16[4,96,768]{2,1,0:T(8,128)(2,1)}, u32[]{:S(2)}, u32[]{:S(2)}) async-start(bf16[4,96,768]{2,1,0:T(8,128)(2,1)} %bitcast.64), calls=%async_computation.8 | async-start | bytes 1179648 | tf_op jit(solution)/shard_map/all_to_all | solution.py:336
  699.6 21.3 %collective-permute-start.26 = (bf16[256,768]{0,1:T(8,128)(2,1)}, bf16[256,768]{0,1:T(8,128)(2,1)S(1)}, u32[]{:S(2)}, u32[]{:S(2)}) collective-permute-start(bf16[256,768]{0,1:T(8,128)(2,1)} %bitcast.53), channel_id=1, source_target_pairs={{2,0},{3,1},{6,4},{7,5},{10,8},{11,9},{14,12},{15,13},{18,16},{19,... | collective-permute-start | bytes 1179656 | tf_op jit(solution)/shard_map/ppermute | solution.py:559
  734.7 20.7 %collective-permute-start.27 = (bf16[1024,768]{0,1:T(8,128)(2,1)}, bf16[1024,768]{0,1:T(8,128)(2,1)}, u32[]{:S(2)}, u32[]{:S(2)}) collective-permute-start(bf16[1024,768]{0,1:T(8,128)(2,1)} %fusion.56), channel_id=1, source_target_pairs={{0,1},{1,0},{2,3},{3,2},{4,5},{5,4},{6,7},{7,6},{8,9},{9,8},{10,11... | collective-permute-start | bytes 4718600 | tf_op jit(solution)/shard_map/ppermute | solution.py:301
  735.6 17.8 %collective-permute-start.30 = (bf16[384,576]{0,1:T(8,128)(2,1)}, bf16[384,576]{0,1:T(8,128)(2,1)}, u32[]{:S(2)}, u32[]{:S(2)}) collective-permute-start(bf16[384,576]{0,1:T(8,128)(2,1)} %pad_maximum_fusion.8), channel_id=1, source_target_pairs={{0,4},{4,0},{1,5},{5,1},{2,6},{6,2},{3,7},{7,3},{8,12},{12,8},{9,1... | collective-permute-start | bytes 1327112 | tf_op jit(solution)/shard_map/ppermute | solution.py:301
  736.9 35.0 %collective-permute-start.29 = (bf16[384,576]{0,1:T(8,128)(2,1)}, bf16[384,576]{0,1:T(8,128)(2,1)}, u32[]{:S(2)}, u32[]{:S(2)}) collective-permute-start(bf16[384,576]{0,1:T(8,128)(2,1)} %pad_maximum_fusion.7), channel_id=1, source_target_pairs={{0,4},{4,0},{1,5},{5,1},{2,6},{6,2},{3,7},{7,3},{8,12},{12,8},{9,1... | collective-permute-start | bytes 1327112 | tf_op jit(solution)/shard_map/ppermute | solution.py:301
  746.4 21.2 %all-to-all-start.10 = ((bf16[4,96,768]{2,1,0:T(8,128)(2,1)}), bf16[4,96,768]{2,1,0:T(8,128)(2,1)}, u32[]{:S(2)}, u32[]{:S(2)}) async-start(bf16[4,96,768]{2,1,0:T(8,128)(2,1)} %bitcast.214), calls=%async_computation.10 | async-start | bytes 1179648 | tf_op jit(solution)/shard_map/all_to_all | solution.py:336
  764.8 18.0 %collective-permute-start.53 = (f32[11520]{0:T(1024)}, f32[11520]{0:T(1024)}, u32[]{:S(2)}, u32[]{:S(2)}) collective-permute-start(f32[11520]{0:T(1024)} %pad_maximum_fusion.28), channel_id=1, source_target_pairs={{0,2},{2,0},{1,3},{3,1},{4,6},{6,4},{5,7},{7,5},{8,10},{10,8},{9,1... | collective-permute-start | bytes 138248 | tf_op jit(solution)/shard_map/ppermute | solution.py:301
  778.4 17.2 %all-to-all-start.4 = ((bf16[4,96,576]{2,1,0:T(8,128)(2,1)}), bf16[4,96,576]{2,1,0:T(8,128)(2,1)}, u32[]{:S(2)}, u32[]{:S(2)}) async-start(bf16[4,96,576]{2,1,0:T(8,128)(2,1)} %bitcast.201), calls=%async_computation.4 | async-start | bytes 983040 | tf_op jit(solution)/shard_map/all_to_all | solution.py:336
  840.5 34.4 %collective-permute-start.28 = (bf16[1024,768]{0,1:T(8,128)(2,1)}, bf16[1024,768]{0,1:T(8,128)(2,1)}, u32[]{:S(2)}, u32[]{:S(2)}) collective-permute-start(bf16[1024,768]{0,1:T(8,128)(2,1)} %add_convert_fusion.2), channel_id=1, source_target_pairs={{0,2},{2,0},{1,3},{3,1},{4,6},{6,4},{5,7},{7,5},{8,10},{10,8},{9,1... | collective-permute-start | bytes 4718600 | tf_op jit(solution)/shard_map/ppermute | solution.py:301
  (193 other events, 2395.2 us)

commit v2 on v1

v2 whole, which is shorter than its diff:
```python
from functools import partial
from typing import NamedTuple

import jax
import jax.numpy as jnp
from jax import lax
from jax.experimental import pallas as pl
from jax.experimental.pallas import tpu as pltpu
from jax.sharding import Mesh
from jax.sharding import PartitionSpec as P

HEAD_DIM = 64
BASIS = 256
SAMPLES = 256
SEG = 512
SEGS = 4
CRES = 1024
LAYERS = 2
STEP = 10

PRECISE = lax.Precision.HIGHEST
STICKY_RATIO = 0.5
RIDGE_WEIGHT = 0.5
BASIS_WIDTH = 0.01
NORM_EPS = 1e-05
CLIP_LIMIT = 1.0
FIRST_DECAY = 0.9
SECOND_DECAY = 0.95
ADAM_EPS = 1e-08
WEIGHT_DECAY = 0.1
RATE_QKV = 0.05
RATE_OUT = 0.5
RATE_UP = 0.05
RATE_DOWN = 0.03
RATE_VECTOR = 0.5
MASKED = -1e30
GELU_A = 0.7978845608028654
GELU_B = 0.044715
F32 = jnp.float32
BF16 = jnp.bfloat16
SWAP = ((0, 1), (1, 0))
NN = (((1,), (0,)), ((), ()))
NT = (((1,), (1,)), ((), ()))
TN = (((0,), (0,)), ((), ()))


def dot(left, right, dims, precision=None):
    return lax.dot_general(left, right, dims, precision=precision, preferred_element_type=F32)


VMEM_LIMIT = 56 * 2**20
TILE = 256
QT = 256


def cost(micros):
    return pl.CostEstimate(flops=int(micros * 1.1e9), bytes_accessed=10**6, transcendentals=0)


def table_kernel(old_ref, design_ref, out_ref, inv_ref, gram_ref):
    design = design_ref[...]
    eye = (
        lax.broadcasted_iota(jnp.int32, (BASIS, BASIS), 0)
        == lax.broadcasted_iota(jnp.int32, (BASIS, BASIS), 1)
    ).astype(F32)
    gram = dot(design, design, NT, PRECISE) + RIDGE_WEIGHT * eye
    gram_ref[...] = gram
    bound = jnp.max(jnp.sum(jnp.abs(gram), axis=0))
    inv_ref[...] = eye * (1.0 / bound)

    def step(low):
        scale = 2.0 / (1.0 + low)
        now = inv_ref[...]
        inner = dot(gram_ref[...], now, NN, PRECISE)
        inv_ref[...] = scale * (2.0 * now - scale * dot(now, inner, NN, PRECISE))
        return 4.0 * low / ((1.0 + low) * (1.0 + low))

    lax.while_loop(lambda low: low < 0.999, step, 0.99 * RIDGE_WEIGHT / bound)
    for _ in range(2):
        now = inv_ref[...]
        inner = dot(gram_ref[...], now, NN, PRECISE)
        inv_ref[...] = 2.0 * now - dot(now, inner, NN, PRECISE)
    fitted = dot(inv_ref[...], design, NN, PRECISE)
    out_ref[:, BASIS:] = fitted[:, SAMPLES:].astype(BF16)
    out_ref[:, :BASIS] = dot(fitted[:, :SAMPLES], old_ref[...], NT, PRECISE).astype(BF16)


def basis_table(centres, times):
    middle = (centres.astype(F32) + 0.5) / CRES
    offset = (times[None, :] - middle[:, None]) / BASIS_WIDTH
    return jnp.exp(-0.5 * offset * offset)


def make_tables(centres, sticky_row):
    token_times = STICKY_RATIO + (1.0 - STICKY_RATIO) * (jnp.arange(SEG).astype(F32) + 0.5) / SEG
    places = (sticky_row.astype(F32) + 0.5) / CRES
    old_basis = basis_table(centres, places)
    design = basis_table(centres, jnp.concatenate([STICKY_RATIO * places, token_times]))
    return pl.pallas_call(
        table_kernel,
        out_shape=jax.ShapeDtypeStruct((BASIS, BASIS + SEG), BF16),
        scratch_shapes=[pltpu.VMEM((BASIS, BASIS), F32), pltpu.VMEM((BASIS, BASIS), F32)],
        compiler_params=pltpu.CompilerParams(vmem_limit_bytes=VMEM_LIMIT),
        cost_estimate=cost(40),
    )(old_basis, design)


def slab_columns(slab, low, high):
    return slab[:, low:high] if len(slab.shape) == 2 else slab[0, 0, :, low:high]


def project(left, slabs, low, high):
    own, by_x, by_y, by_both = (slab_columns(slab, low, high) for slab in slabs)
    half = own.shape[0]
    first, second = left[:, :half], left[:, half:]
    return (
        dot(first, own, NN) + dot(second, by_x, NN),
        dot(first, by_y, NN) + dot(second, by_both, NN),
    )


def unproject(sides, slabs, low, high):
    own, by_x, by_y, by_both = (slab_columns(slab, low, high) for slab in slabs)
    return jnp.concatenate(
        [
            dot(sides[0], own, NT) + dot(sides[1], by_y, NT),
            dot(sides[0], by_x, NT) + dot(sides[1], by_both, NT),
        ],
        axis=1,
    )


def split_attention(refs, width):
    if len(refs[0].shape) == 2:
        return (refs[:4], 0), (refs[4:8], 0), refs[8:]
    return (refs[:4], 0), (refs[:4], 2 * width), refs[4:]


def split_ffn(refs):
    if len(refs[0].shape) == 2:
        return (refs[:4], 0), (refs[4:8], 0), refs[8:]
    return (refs[:4], 0), (refs[:4], refs[0].shape[-1] // 2), refs[4:]


TURNS = ((0, 0), (0, 1), (1, 0), (1, 1))


def cast_kernel(count, out_ref_index, *refs):
    out_ref = refs[out_ref_index]
    start = 0
    for ref in refs[:count]:
        for index in range(ref.shape[1]):
            columns = ref.shape[3]
            out_ref[:, start : start + columns] = ref[0, index].astype(BF16)
            start += columns


def cast(members, after=()):
    members = [
        (weight if weight.ndim == 4 else weight[:, None], layer) for weight, layer in members
    ]
    rows = members[0][0].shape[2]
    columns = sum(weight.shape[1] * weight.shape[3] for weight, _ in members)
    return pl.pallas_call(
        partial(cast_kernel, len(members), len(members) + len(after)),
        grid=(1,),
        in_specs=[
            pl.BlockSpec((1,) + weight.shape[1:], lambda i, layer=layer: (layer, 0, 0, 0))
            for weight, layer in members
        ]
        + [pl.BlockSpec(memory_space=pl.ANY)] * len(after),
        out_specs=pl.BlockSpec((rows, columns), lambda i: (0, 0)),
        out_shape=array((rows, columns), BF16),
        compiler_params=pltpu.CompilerParams(vmem_limit_bytes=VMEM_LIMIT),
        cost_estimate=cost(1),
    )(*(weight for weight, _ in members), *after)


def split_kernel(count, rows_ref, *refs):
    start = 0
    outs = refs[len(refs) - count - 1 :]
    for out_ref in outs[:count]:
        columns = out_ref.shape[1]
        out_ref[...] = rows_ref[:, start : start + columns]
        start += columns
    outs[count][...] = jnp.zeros_like(outs[count])


def split_columns(rows, widths, after):
    vmem = pl.BlockSpec(memory_space=pltpu.VMEM)
    *groups, zero = pl.pallas_call(
        partial(split_kernel, len(widths)),
        in_specs=[vmem] + [pl.BlockSpec(memory_space=pl.ANY)] * len(after),
        out_specs=[vmem] * (len(widths) + 1),
        out_shape=[array((rows.shape[0], columns), rows.dtype) for columns in widths]
        + [array((8, 128), jnp.int32)],
        compiler_params=pltpu.CompilerParams(vmem_limit_bytes=VMEM_LIMIT),
        cost_estimate=cost(1),
    )(rows, *after)
    return groups, zero[0, 0]


def pass_kernel(keep_a_ref, got_a_ref, keep_b_ref, got_b_ref, *refs):
    for keep_ref, got_ref, out_ref in (
        (keep_a_ref, got_a_ref, refs[-2]),
        (keep_b_ref, got_b_ref, refs[-1]),
    ):
        out_ref[...] = (keep_ref[0].astype(F32) + got_ref[0].astype(F32)).astype(BF16)


def pass_on(keep_a, got_a, keep_b, got_b, after):
    def slab(a):
        return pl.BlockSpec((1,) + a.shape[1:], lambda i: (1, 0, 0))

    def out(a):
        return pl.BlockSpec(a.shape[1:], lambda i: (0, 0))

    return pl.pallas_call(
        pass_kernel,
        grid=(1,),
        in_specs=[slab(a) for a in (keep_a, got_a, keep_b, got_b)]
        + [pl.BlockSpec(memory_space=pl.ANY)] * len(after),
        out_specs=[out(keep_a), out(keep_b)],
        out_shape=[array(keep_a.shape[1:], BF16), array(keep_b.shape[1:], BF16)],
        compiler_params=pltpu.CompilerParams(vmem_limit_bytes=VMEM_LIMIT),
        cost_estimate=cost(2),
    )(keep_a, got_a, keep_b, got_b, *after)


class Gathered(NamedTuple):
    whole: jax.Array
    columns: int
    index: int


def slab_operands(slabs, grid_rank):
    def fixed(shape):
        return pl.BlockSpec(shape, lambda *a: (0,) * len(shape))

    if not isinstance(slabs, Gathered):
        return list(slabs), [fixed(slab.shape) for slab in slabs]
    whole, columns, index = slabs
    specs = []
    for turn_y, turn_x in TURNS:
        specs.append(
            pl.BlockSpec(
                (1, 1, whole.shape[2], columns),
                lambda *a, turn_y=turn_y, turn_x=turn_x: (
                    a[grid_rank][0] ^ turn_y,
                    a[grid_rank][1] ^ turn_x,
                    0,
                    index,
                ),
            )
        )
    return [whole] * 4, specs


def norm_stats(inputs):
    centred = inputs - jnp.mean(inputs, axis=-1, keepdims=True)
    variance = jnp.mean(centred * centred, axis=-1, keepdims=True)
    rstd = lax.rsqrt(variance + NORM_EPS)
    return centred * rstd, rstd


def norm_backward(inputs, grad, gain_row):
    unit, rstd = norm_stats(inputs)
    scaled = grad * gain_row
    back = rstd * (
        scaled
        - jnp.mean(scaled, axis=-1, keepdims=True)
        - unit * jnp.mean(scaled * unit, axis=-1, keepdims=True)
    )
    return back, grad * unit


def both_parts(own_ref, got_ref):
    return own_ref[...].astype(F32) + got_ref[...].astype(F32)


def add_rows(ref, rows):
    @pl.when(pl.program_id(0) == 0)
    def _():
        ref[...] = jnp.zeros_like(ref)

    for index, row in rows:
        ref[index : index + 1, :] += jnp.sum(row, axis=0, keepdims=True)


def rows_call(
    kernel, place, tiled, whole, slabs, more, tiled_outs, whole_outs, micros, scratch=(), after=()
):
    rows = tiled[0].shape[-2]

    def tile_spec(shape):
        if len(shape) == 2:
            return pl.BlockSpec((TILE, shape[1]), lambda i, p: (i, 0))
        return pl.BlockSpec((shape[0], TILE, shape[2]), lambda i, p: (0, i, 0))

    def whole_spec(shape):
        return pl.BlockSpec(shape, lambda i, p: (0,) * len(shape))

    slab_arrays, slab_specs = slab_operands(slabs, 1) if slabs is not None else ([], [])

    taken = len(tiled) + len(whole) + len(slab_arrays) + len(more)

    def body(place_ref, *refs):
        kernel(*refs[:taken], *refs[taken + len(after) :])

    return pl.pallas_call(
        body,
        grid_spec=pltpu.PrefetchScalarGridSpec(
            num_scalar_prefetch=1,
            grid=(rows // TILE,),
            in_specs=[tile_spec(a.shape) for a in tiled]
            + [whole_spec(a.shape) for a in whole]
            + slab_specs
            + [whole_spec(a.shape) for a in more]
            + [pl.BlockSpec(memory_space=pl.ANY)] * len(after),
            out_specs=[tile_spec(a.shape) for a in tiled_outs]
            + [whole_spec(a.shape) for a in whole_outs],
            scratch_shapes=list(scratch),
        ),
        out_shape=[*tiled_outs, *whole_outs],
        compiler_params=pltpu.CompilerParams(vmem_limit_bytes=VMEM_LIMIT),
        cost_estimate=cost(micros),
    )(place, *tiled, *whole, *slab_arrays, *more, *after)


def array(shape, dtype):
    return jax.ShapeDtypeStruct(shape, dtype)


def enter_kernel(layer, *refs):
    if layer == 0:
        h_ref, order_ref, gains_ref, bias_ref, *refs = refs
        stream = dot(h_ref[...], order_ref[...], NN)
    else:
        middle_ref, own_ref, got_ref, gains_ref, bias_ref, *refs = refs
        stream = middle_ref[...] + (both_parts(own_ref, got_ref) + gains_ref[layer - 1, 5:6, :])
    width = refs[-4].shape[2] // 3
    slabs_qk, slabs_vo, refs = split_attention(refs, width)
    near_ref, far_ref, start_ref, *refs = refs
    stream_ref, normed_ref, qkv_ref, fit_ref, ahead_ref, signal_ref = refs
    step = pl.program_id(0)
    stream_ref[...] = stream
    unit, _ = norm_stats(stream)
    normed = (unit * gains_ref[layer, 0:1, :] + gains_ref[layer, 1:2, :]).astype(BF16)
    normed_ref[...] = normed
    rows = pl.ds(pl.multiple_of(step * TILE, TILE), TILE)
    low = slabs_qk[1]
    queries_keys = project(normed, slabs_qk[0], low, low + 2 * width)
    low = slabs_vo[1]
    values = project(normed, slabs_vo[0], low, low + width)
    for side in range(2):
        result = jnp.concatenate([queries_keys[side], values[side]], axis=1)
        result = (result + bias_ref[layer, side : side + 1, :]).astype(BF16)
        qkv_ref[side] = result
        signal_ref[side, rows, :] = result[:, width:]

    @pl.when(step == pl.num_programs(0) - 1)
    def _():
        for side in range(2):
            fit_near = dot(near_ref[:, BASIS:], signal_ref[side, :SEG, :], NN)
            fit_far = dot(far_ref[:, BASIS:], signal_ref[side, SEG:, :], NN)
            fit_ref[side] = fit_near
            ahead = dot(near_ref[:, :BASIS], start_ref[layer, side], NN) + fit_near
            ahead = dot(far_ref[:, :BASIS], ahead.astype(BF16), NN) + fit_far
            ahead_ref[side] = ahead.astype(BF16)


def ffn_forward_kernel(layer, stream_ref, own_ref, got_ref, gains_ref, bias_ref, *refs):
    (up, up_low), (down, down_low), refs = split_ffn(refs)
    middle_ref, normed_ref, active_ref, slope_ref, part_ref = refs
    hidden_own = active_ref.shape[2]
    middle = stream_ref[...] + (both_parts(own_ref, got_ref) + gains_ref[layer, 4:5, :])
    middle_ref[...] = middle
    unit, _ = norm_stats(middle)
    normed = (unit * gains_ref[layer, 2:3, :] + gains_ref[layer, 3:4, :]).astype(BF16)
    normed_ref[...] = normed
    sides = []
    for side, hidden in enumerate(project(normed, up, up_low, up_low + hidden_own)):
        hidden = hidden + bias_ref[layer, side : side + 1, :]
        square = hidden * hidden
        bend = jnp.tanh(hidden * (GELU_A + (GELU_A * GELU_B) * square))
        half_more = 0.5 + 0.5 * bend
        active = (hidden * half_more).astype(BF16)
        slope = half_more + (0.5 - 0.5 * bend * bend) * hidden * (
            GELU_A + (3.0 * GELU_A * GELU_B) * square
        )
        active_ref[side] = active
        slope_ref[side] = slope.astype(BF16)
        sides.append(active)
    part_ref[...] = unproject(sides, down, down_low, down_low + hidden_own).astype(BF16)


def ffn_backward_kernel(layer, *refs):
    if layer == LAYERS - 1:
        cot_ref, slope_ref, order_ref, *refs = refs
        (up_slabs, up_low), (down_slabs, down_low), refs = split_ffn(refs)
        stream_grad = dot(cot_ref[...], order_ref[...], NN)
        grad_ref, down_ref, hidden_ref, part_ref, sums_ref = refs
        sums = []
    else:
        before_ref, stream_ref, own_ref, got_ref, slope_ref, gains_ref, *refs = refs
        (up_slabs, up_low), (down_slabs, down_low), refs = split_ffn(refs)
        grad_ref, down_ref, hidden_ref, part_ref, sums_ref = refs
        normed_grad = both_parts(own_ref, got_ref)
        back, gain_rows = norm_backward(
            stream_ref[...], normed_grad, gains_ref[layer + 1, 0:1, :]
        )
        stream_grad = before_ref[...] + back
        sums = [(0, gain_rows), (1, normed_grad)]
    hidden_own = slope_ref.shape[2]
    grad_ref[...] = stream_grad
    down = stream_grad.astype(BF16)
    down_ref[...] = down
    sums.append((2, down.astype(F32)))
    sides = []
    for side, active_grad in enumerate(project(down, down_slabs, down_low, down_low + hidden_own)):
        hidden_grad = (active_grad * slope_ref[side].astype(F32)).astype(BF16)
        hidden_ref[side] = hidden_grad
        sums.append((3 + side, hidden_grad.astype(F32)))
        sides.append(hidden_grad)
    part_ref[...] = unproject(sides, up_slabs, up_low, up_low + hidden_own).astype(BF16)
    add_rows(sums_ref, sums)


def mix_backward_kernel(layer, before_ref, middle_ref, own_ref, got_ref, gains_ref, *refs):
    width = refs[-2].shape[2]
    slabs_qk, (slabs, low), refs = split_attention(refs, width)
    grad_ref, branch_ref, attended_ref, sums_ref = refs
    normed_grad = both_parts(own_ref, got_ref)
    back, gain_rows = norm_backward(middle_ref[...], normed_grad, gains_ref[layer, 2:3, :])
    stream_grad = before_ref[...] + back
    grad_ref[...] = stream_grad
    branch = stream_grad.astype(BF16)
    branch_ref[...] = branch
    for side, result in enumerate(project(branch, slabs, low + width, low + 2 * width)):
        attended_ref[side] = result.astype(BF16)
    add_rows(sums_ref, [(0, gain_rows), (1, normed_grad), (2, branch.astype(F32))])


def leave_kernel(before_ref, stream_ref, own_ref, got_ref, gains_ref, grad_ref, sums_ref):
    normed_grad = both_parts(own_ref, got_ref)
    back, gain_rows = norm_backward(stream_ref[...], normed_grad, gains_ref[0, 0:1, :])
    grad_ref[...] = (before_ref[...] + back).astype(BF16)
    add_rows(sums_ref, [(0, gain_rows), (1, normed_grad)])


def restore_kernel(context_ref, own_ref, got_ref, order_ref, *refs):
    out_ref = refs[-1]
    mine = (pl.program_id(0) // (pl.num_programs(0) // 2)) == context_ref[0]
    rows = jnp.where(mine, own_ref[...].astype(F32), got_ref[...].astype(F32)).astype(BF16)
    out_ref[...] = dot(rows, order_ref[...], NN)


def restore(own, got, order, context, after=()):
    rows, features = own.shape
    tiles = rows // TILE
    block = pl.BlockSpec((TILE, features), lambda i: (i % tiles, 0))
    return pl.pallas_call(
        restore_kernel,
        grid=(2 * tiles,),
        in_specs=[
            pl.BlockSpec(memory_space=pltpu.SMEM),
            block,
            block,
            pl.BlockSpec(order.shape, lambda i: (0, 0)),
            *(pl.BlockSpec(memory_space=pl.ANY) for _ in after),
        ],
        out_specs=pl.BlockSpec((TILE, features), lambda i: (i, 0)),
        out_shape=array((2 * rows, features), F32),
        compiler_params=pltpu.CompilerParams(vmem_limit_bytes=VMEM_LIMIT),
        cost_estimate=cost(4),
    )(context, own, got, order, *after)


def causal(shape):
    return lax.broadcasted_iota(jnp.int32, shape, 0) <= lax.broadcasted_iota(jnp.int32, shape, 1)


def head_lanes(kind, head, heads):
    low = (kind * heads + head) * HEAD_DIM
    return slice(low, low + HEAD_DIM)


def attention_forward_kernel(
    place_ref,
    bias_ref,
    qkv_ref,
    start_ref,
    got_ref,
    fit_ref,
    near_ref,
    *refs,
):
    slabs = refs[:4]
    out_ref, lse_ref, memory_ref, part_ref, rows_ref, total_ref = refs[-6:]
    segment, side = pl.program_id(0), pl.program_id(1)
    heads = qkv_ref.shape[2] // (3 * HEAD_DIM)
    width = heads * HEAD_DIM

    @pl.when(segment == 0)
    def _():
        @pl.when(place_ref[0] == 0)
        def _():
            rows_ref[side, 0] = start_ref[0, 0]

        @pl.when(place_ref[0] != 0)
        def _():
            rows_ref[side, 0] = got_ref[0]

        second = dot(near_ref[:, :BASIS], rows_ref[side, 0], NN) + fit_ref[0]
        rows_ref[side, 1] = second.astype(BF16)

    memory_ref[0, 0] = rows_ref[side, segment]
    memory_bias = bias_ref[segment]
    for tile in range(SEG // QT):
        rows = slice(tile * QT, (tile + 1) * QT)
        stacked = []
        for head in range(heads):
            lanes_q, lanes_k, lanes_v = (head_lanes(kind, head, heads) for kind in range(3))
            query = qkv_ref[0, rows, lanes_q] * HEAD_DIM ** (-0.5)
            scores = []
            values = []
            for part in range(tile + 1):
                keys = slice(part * QT, (part + 1) * QT)
                score = dot(qkv_ref[0, keys, lanes_k], query, NT)
                if part == tile:
                    score = jnp.where(causal(score.shape), score, MASKED)
                scores.append(score)
                values.append(qkv_ref[0, keys, lanes_v])
            memory_key = rows_ref[side, segment, :, head_lanes(0, head, heads)]
            scores.append(dot(memory_key, query, NT) + memory_bias)
            values.append(rows_ref[side, segment, :, head_lanes(1, head, heads)])
            top = scores[0].max(axis=0, keepdims=True)
            for score in scores[1:]:
                top = jnp.maximum(top, score.max(axis=0, keepdims=True))
            total = jnp.zeros_like(top)
            result = jnp.zeros((HEAD_DIM, QT), F32)
            for score, value in zip(scores, values):
                weight = jnp.exp(score - top)
                total = total + weight.sum(axis=0, keepdims=True)
                result = result + dot(value, weight.astype(BF16), TN)
            stacked.append(result / total)
            lse_ref[0, 0, head : head + 1, rows] = top + jnp.log(total)
        out_ref[0, rows, :] = jnp.concatenate(stacked, axis=0).T.astype(BF16)
    attended = out_ref[0]
    low = slabs[0].shape[-1] - width
    own, by_x, by_y, by_both = (slab_columns(slab, low, low + width) for slab in slabs)

    @pl.when(side == 0)
    def _():
        total_ref[...] = jnp.concatenate(
            [dot(attended, own, NT), dot(attended, by_x, NT)], axis=1
        )

    @pl.when(side == 1)
    def _():
        part = total_ref[...] + jnp.concatenate(
            [dot(attended, by_y, NT), dot(attended, by_both, NT)],
            axis=1,
        )
        part_ref[...] = part.astype(BF16)


def attention_forward(layer, place, memory_bias, qkv, starts, got, fit, near, slabs, after=()):
    rows = qkv.shape[1]
    width = qkv.shape[2] // 3
    heads = width // HEAD_DIM
    segs = rows // SEG
    slab_arrays, slab_specs = slab_operands(slabs, 2)
    features = 2 * slab_arrays[0].shape[-2]
    return pl.pallas_call(
        attention_forward_kernel,
        grid_spec=pltpu.PrefetchScalarGridSpec(
            num_scalar_prefetch=1,
            grid=(segs, 2),
            in_specs=[
                pl.BlockSpec(memory_space=pltpu.SMEM),
                pl.BlockSpec((1, SEG, 3 * width), lambda g, s, p: (s, g, 0)),
                pl.BlockSpec((1, 1, BASIS, 2 * width), lambda g, s, p: (layer, s, 0, 0)),
                pl.BlockSpec((1, BASIS, 2 * width), lambda g, s, p: (1 - s, 0, 0)),
                pl.BlockSpec((1, BASIS, 2 * width), lambda g, s, p: (s, 0, 0)),
                pl.BlockSpec(near.shape, lambda g, s, p: (0, 0)),
                *slab_specs,
                *(pl.BlockSpec(memory_space=pl.ANY) for _ in after),
            ],
            out_specs=[
                pl.BlockSpec((1, SEG, width), lambda g, s, p: (s, g, 0)),
                pl.BlockSpec((1, 1, heads, SEG), lambda g, s, p: (g, s, 0, 0)),
                pl.BlockSpec((1, 1, BASIS, 2 * width), lambda g, s, p: (g, s, 0, 0)),
                pl.BlockSpec((SEG, features), lambda g, s, p: (g, 0)),
            ],
            scratch_shapes=[
                pltpu.VMEM((2, segs, BASIS, 2 * width), BF16),
                pltpu.VMEM((SEG, features), F32),
            ],
        ),
        out_shape=[
            array((2, rows, width), BF16),
            array((segs, 2, heads, SEG), F32),
            array((segs, 2, BASIS, 2 * width), BF16),
            array((rows, features), BF16),
        ],
        compiler_params=pltpu.CompilerParams(vmem_limit_bytes=VMEM_LIMIT),
        cost_estimate=cost(13),
    )(place, memory_bias, qkv, starts, got, fit, near, *slab_arrays, *after)


def attention_backward_kernel(
    bias_ref,
    qkv_ref,
    memory_ref,
    lse_ref,
    out_ref,
    grad_ref,
    near_ref,
    *refs,
):
    dq_ref, dkv_ref, last_ref, back_ref, first_ref = refs[-5:]
    segment = pl.program_id(1)
    memory_bias = bias_ref[segment]
    heads = out_ref.shape[2] // HEAD_DIM
    scale = HEAD_DIM ** (-0.5)
    tiles = SEG // QT
    product = (out_ref[0].astype(F32) * grad_ref[0].astype(F32)).T
    query_grads = []
    for head in range(heads):
        lanes = head_lanes(0, head, heads)
        lanes_k, lanes_v = head_lanes(1, head, heads), head_lanes(2, head, heads)
        query = qkv_ref[0, :, lanes] * scale
        grad = grad_ref[0, :, lanes]
        dots = product[lanes, :].sum(axis=0, keepdims=True)
        log_total = lse_ref[0, 0, head : head + 1, :]
        head_grads = [jnp.zeros((HEAD_DIM, QT), F32) for _ in range(tiles)]
        for part in range(tiles + 1):
            if part < tiles:
                keys = slice(part * QT, (part + 1) * QT)
                key, value = qkv_ref[0, keys, lanes_k], qkv_ref[0, keys, lanes_v]
            else:
                key = memory_ref[0, 0, :, head_lanes(0, head, heads)]
                value = memory_ref[0, 0, :, head_lanes(1, head, heads)]
            key_grad = jnp.zeros((QT, HEAD_DIM), F32)
            value_grad = jnp.zeros((QT, HEAD_DIM), F32)
            for tile in range(part if part < tiles else 0, tiles):
                rows = slice(tile * QT, (tile + 1) * QT)
                score = dot(key, query[rows], NT)
                if part == tile:
                    score = jnp.where(causal(score.shape), score, MASKED)
                if part == tiles:
                    score = score + memory_bias
                weight = jnp.exp(score - log_total[:, rows])
                weight_grad = dot(value, grad[rows], NT)
                score_grad = (weight * (weight_grad - dots[:, rows])).astype(BF16)
                value_grad = value_grad + dot(weight.astype(BF16), grad[rows], NN)
                key_grad = key_grad + dot(score_grad, query[rows], NN)
                head_grads[tile] = head_grads[tile] + dot(key, score_grad, TN)
            if part < tiles:
                dkv_ref[0, keys, head_lanes(0, head, heads)] = key_grad
                dkv_ref[0, keys, head_lanes(1, head, heads)] = value_grad
            else:
                last_ref[0, :, head_lanes(0, head, heads)] = key_grad
                last_ref[0, :, head_lanes(1, head, heads)] = value_grad
        query_grads.append(jnp.concatenate(head_grads, axis=1) * scale)
    dq_ref[0] = jnp.concatenate(query_grads, axis=0).T.astype(BF16)

    @pl.when(segment == 0)
    def _():
        first_ref[...] = last_ref[0]

    @pl.when(segment == 1)
    def _():
        back = first_ref[...] + dot(near_ref[:, :BASIS], last_ref[0].astype(BF16), TN)
        back_ref[0] = back.astype(BF16)


def attention_backward(memory_bias, qkv, memory, log_totals, attended, grad, near, after):
    rows, width = attended.shape[1:]
    heads = width // HEAD_DIM
    segs = rows // SEG
    narrow = pl.BlockSpec((1, SEG, width), lambda s, g: (s, g, 0))
    side_block = pl.BlockSpec((1, BASIS, 2 * width), lambda s, g: (s, 0, 0))
    return pl.pallas_call(
        attention_backward_kernel,
        grid=(2, segs),
        in_specs=[
            pl.BlockSpec(memory_space=pltpu.SMEM),
            pl.BlockSpec((1, SEG, 3 * width), lambda s, g: (s, g, 0)),
            pl.BlockSpec((1, 1, BASIS, 2 * width), lambda s, g: (g, s, 0, 0)),
            pl.BlockSpec((1, 1, heads, SEG), lambda s, g: (g, s, 0, 0)),
            narrow,
            narrow,
            pl.BlockSpec(near.shape, lambda s, g: (0, 0)),
            *(pl.BlockSpec(memory_space=pl.ANY) for _ in after),
        ],
        out_specs=[
            narrow,
            pl.BlockSpec((1, SEG, 2 * width), lambda s, g: (s, g, 0)),
            side_block,
            side_block,
        ],
        out_shape=[
            array((2, rows, width), BF16),
            array((2, rows, 2 * width), F32),
            array((2, BASIS, 2 * width), F32),
            array((2, BASIS, 2 * width), BF16),
        ],
        scratch_shapes=[pltpu.VMEM((BASIS, 2 * width), F32)],
        compiler_params=pltpu.CompilerParams(vmem_limit_bytes=VMEM_LIMIT),
        cost_estimate=cost(18),
    )(memory_bias, qkv, memory, log_totals, attended, grad, near, *after)


def memory_backward_kernel(
    place_ref,
    dq_ref,
    dkv_ref,
    last_ref,
    got_ref,
    near_ref,
    far_ref,
    *refs,
):
    width = dq_ref.shape[2]
    slabs_qk, slabs_vo, refs = split_attention(refs, width)
    grads_ref, part_ref, sums_ref, signal_ref = refs[-4:]
    segment = pl.program_id(0)

    @pl.when(segment == 0)
    def _():
        for side in range(2):
            carry = last_ref[side] + dot(far_ref[:, :BASIS], got_ref[1 - side], TN)
            signal_ref[side] = dot(near_ref[:, BASIS:], carry.astype(BF16), TN)

    @pl.when(segment == 1)
    def _():
        for side in range(2):
            signal_ref[side] = dot(far_ref[:, BASIS:], got_ref[1 - side], TN)

    sides = []
    for side in range(2):
        grads_ref[side, :, :width] = dq_ref[side]
        grads_ref[side, :, width:] = (dkv_ref[side] + signal_ref[side]).astype(BF16)
        sides.append(grads_ref[side])
    slabs, low = slabs_qk
    part = unproject([side[:, : 2 * width] for side in sides], slabs, low, low + 2 * width)
    slabs, low = slabs_vo
    part = part + unproject([side[:, 2 * width :] for side in sides], slabs, low, low + width)
    part_ref[...] = part.astype(BF16)
    add_rows(sums_ref, [(side, sides[side].astype(F32)) for side in range(2)])


def memory_backward(place, dq, dkv, last, got, near, far, slabs, after):
    rows, width = dq.shape[1:]
    slab_arrays, slab_specs = slab_operands(slabs, 1)
    features = 2 * slab_arrays[0].shape[-2]
    whole = lambda a: pl.BlockSpec(a.shape, lambda g, p: (0,) * a.ndim)
    return pl.pallas_call(
        memory_backward_kernel,
        grid_spec=pltpu.PrefetchScalarGridSpec(
            num_scalar_prefetch=1,
            grid=(rows // SEG,),
            in_specs=[
                pl.BlockSpec((2, SEG, width), lambda g, p: (0, g, 0)),
                pl.BlockSpec((2, SEG, 2 * width), lambda g, p: (0, g, 0)),
                *(whole(a) for a in (last, got, near, far)),
                *slab_specs,
                *(pl.BlockSpec(memory_space=pl.ANY) for _ in after),
            ],
            out_specs=[
                pl.BlockSpec((2, SEG, 3 * width), lambda g, p: (0, g, 0)),
                pl.BlockSpec((SEG, features), lambda g, p: (g, 0)),
                pl.BlockSpec((8, 3 * width), lambda g, p: (0, 0)),
            ],
            scratch_shapes=[pltpu.VMEM((2, SEG, 2 * width), F32)],
        ),
        out_shape=[
            array((2, rows, 3 * width), BF16),
            array((rows, features), BF16),
            array((8, 3 * width), F32),
        ],
        compiler_params=pltpu.CompilerParams(vmem_limit_bytes=VMEM_LIMIT),
        cost_estimate=cost(5),
    )(place, dq, dkv, last, got, near, far, *slab_arrays, *after)


def weight_grads_kernel(plan, *refs):
    outs = refs[len(refs) - len(plan) :]
    for out_ref, slabs in zip(outs, plan):
        half = out_ref.shape[1]
        for index, products in enumerate(slabs):
            start = 0
            for left, turn, right, side, low, high in products:
                columns = slice(turn * half, (turn + 1) * half)
                result = dot(refs[left][:, columns], refs[right][side, :, low:high], TN)
                out_ref[index, :, start : start + high - low] = result.astype(BF16)
                start += high - low


def weight_grads(operands, plan, half, after=()):
    shapes = [
        array((2, half, sum(high - low for *_, low, high in slabs[0])), BF16) for slabs in plan
    ]
    vmem = pl.BlockSpec(memory_space=pltpu.VMEM)
    return pl.pallas_call(
        partial(weight_grads_kernel, plan),
        in_specs=[vmem] * len(operands) + [pl.BlockSpec(memory_space=pl.ANY)] * len(after),
        out_specs=[vmem] * len(plan),
        out_shape=shapes,
        compiler_params=pltpu.CompilerParams(vmem_limit_bytes=VMEM_LIMIT),
        cost_estimate=cost(6),
    )(*operands, *after)


GIVE_X = ((1, 0), (1, 1))
GIVE_Y = ((0, 1), (1, 1))
KEEP_X = ((0, 0), (0, 1))
KEEP_Y = ((0, 0), (1, 0))


def flip(array, axis):
    return lax.ppermute(array, axis, SWAP)


ALL_BUT_CORE = ("cy", "tx", "tz")


def gather_blocks(shard):
    whole = lax.all_gather(shard, ALL_BUT_CORE, axis=0, tiled=True)
    return whole.reshape(2, 2, -1, shard.shape[1])


def gather_z(shard):
    size = lax.axis_size("tz")
    spread = jnp.broadcast_to(shard[None], (size,) + shard.shape)
    return lax.all_to_all(spread, "tz", 0, 0, tiled=True).reshape(-1, shard.shape[1])


def gather_z_soon(shard):
    size = lax.axis_size("tz")
    here = lax.axis_index("tz")
    rows = jnp.zeros((size,) + shard.shape, shard.dtype)
    for bit in range(size):
        piece = shift(shard, "tz", bit) if bit else shard
        rows = lax.dynamic_update_index_in_dim(rows, piece, here ^ bit, 0)
    return rows.reshape(-1, shard.shape[1])


def shift(array, axis, bit):
    return lax.ppermute(array, axis, [(i, i ^ bit) for i in range(lax.axis_size(axis))])


def gather_second(two, axis):
    own, near = two
    far, both = flip(own, axis), flip(near, axis)
    return (own, far, near, both) if axis == "tx" else (own, near, far, both)


def pieces_of(parts, block_rows):
    total = jnp.concatenate(
        [sum(piece.astype(F32) for piece in three).astype(BF16) for three in parts], axis=1
    )
    return total.reshape(-1, block_rows, total.shape[-1])


def spread_pieces(pieces):
    return lax.all_to_all(pieces, "tz", 0, 0, tiled=True)


def butterfly(array, axes):
    for axis in axes:
        bit = 1
        while bit < lax.axis_size(axis):
            array = array + shift(array, axis, bit)
            bit *= 2
    return array


def adamw(weight, first, second, grad, rate, decay):
    first_new = FIRST_DECAY * first + (1.0 - FIRST_DECAY) * grad
    second_new = SECOND_DECAY * second + (1.0 - SECOND_DECAY) * grad * grad
    first_hat = first_new / (1.0 - FIRST_DECAY**STEP)
    second_hat = second_new / (1.0 - SECOND_DECAY**STEP)
    weight_new = weight * (1.0 - rate * decay) - rate * first_hat / (
        jnp.sqrt(second_hat) + ADAM_EPS
    )
    return (weight_new, first_new, second_new)


def shards(
    h_in,
    cotangent,
    carried,
    centres,
    sticky,
    flags,
    w_qkv,
    w_qkv_first,
    w_qkv_second,
    w_out_t,
    w_out_first,
    w_out_second,
    w_up,
    w_up_first,
    w_up_second,
    w_down_t,
    w_down_first,
    w_down_second,
    vec_d,
    vec_d_first,
    vec_d_second,
    vec_c,
    vec_c_first,
    vec_c_second,
):
    depth = lax.axis_size("tz")
    tok_count = depth * 2
    ch_count = 2 * lax.axis_size("cc")
    context = lax.axis_index("cy")
    core = lax.axis_index("cc")
    x_place = lax.axis_index("tx")
    block_rows = w_qkv.shape[2]
    width = w_qkv.shape[1 + 2] * 1
    features = h_in.shape[1]
    half = features // 2
    rows = h_in.shape[0] // 2
    hidden_own = w_up.shape[2]

    table_index = jnp.where(context == 0, core, 2)
    sticky_row = lax.dynamic_index_in_dim(sticky[0], table_index, 0, keepdims=False)
    table_own = make_tables(centres, sticky_row)
    table_other = flip(table_own, "cc")
    table_near = jnp.where(core == 0, table_own, table_other)
    table_far = jnp.where(core == 0, table_other, table_own)

    def attention_members(layer):
        return [(w_qkv, layer), (w_out_t, layer)]

    def ffn_members(layer):
        return [(w_up, layer), (w_down_t, layer)]

    attn_shard = cast(attention_members(0))
    attn_rows = gather_z_soon(attn_shard)
    more_rows = gather_z(cast(ffn_members(0) + attention_members(1), (attn_shard,)))
    (qk_own, vo_own), zero = split_columns(attn_rows, (2 * width, 2 * width), (table_own,))
    qk_two, vo_two = (qk_own, flip(qk_own, "tx")), (vo_own, flip(vo_own, "cy"))
    (up_own, down_own, qk_above, vo_above), _ = split_columns(
        more_rows, (hidden_own, hidden_own, 2 * width, 2 * width), (qk_own,)
    )
    up_two, down_two = (up_own, flip(up_own, "tx")), (down_own, flip(down_own, "cy"))
    above_two = (qk_above, flip(qk_above, "tx")), (vo_above, flip(vo_above, "cy"))
    attn_slabs = [
        gather_second(qk_two, "cy") + gather_second(vo_two, "tx"),
        gather_second(above_two[0], "cy") + gather_second(above_two[1], "tx"),
    ]
    ffn_slabs = [
        gather_second(up_two, "cy") + gather_second(down_two, "tx"),
        Gathered(gather_blocks(cast(ffn_members(1), (up_own,))), 2 * hidden_own, 0),
    ]

    x_place = x_place + zero
    late_context = context + zero
    spot = jnp.arange(features)
    turned = spot // half
    block_z = (spot % half) // block_rows
    source = block_z * (2 * block_rows) + jnp.where(
        turned == 0, x_place, 1 - x_place
    ) * block_rows + spot % block_rows
    order = (jnp.arange(features)[:, None] == source[None, :]).astype(BF16)
    order_wide = order.astype(F32)
    order_back = (source[:, None] == jnp.arange(features)[None, :]).astype(BF16)
    place = jnp.stack([context, x_place]).astype(jnp.int32)

    vec_c_other = flip(vec_c, "cy")
    gains = jnp.dot(
        vec_d.reshape(-1, features), order_wide, precision=PRECISE
    ).reshape(vec_d.shape)
    both_c = jnp.stack([vec_c, vec_c_other], axis=1)
    in_bias = jnp.concatenate(
        [both_c[:, :, 0], jnp.zeros_like(both_c[:, :, 0]), both_c[:, :, 1]], axis=-1
    )
    up_bias = both_c[:, :, 2:6].transpose(0, 1, 3, 2).reshape(LAYERS, 2, hidden_own)
    flag_on = flags[0] + zero > 0
    carried_own = carried[:, 0].reshape(LAYERS, BASIS, 2 * width)
    starts = jnp.stack([carried_own, flip(carried_own, "cy")], axis=1)
    starts = jnp.where(flag_on, starts, jnp.zeros_like(starts))
    memory_bias = jnp.stack(
        [jnp.where((context == 0) & ~flag_on, MASKED, 0.0), jnp.float32(0.0)]
    ).astype(F32)
    own_h = lax.dynamic_slice_in_dim(h_in, late_context * rows, rows, axis=0)
    own_cot = lax.dynamic_slice_in_dim(cotangent, late_context * rows, rows, axis=0)

    row_f32 = array((rows, features), F32)
    row_b16 = array((rows, features), BF16)
    side_hidden = array((2, rows, hidden_own), BF16)
    side_width = array((2, rows, width), BF16)
    sums_shape = array((8, features), F32)

    saved = []
    for layer in range(LAYERS):
        stream, normed, qkv, fit, ahead = rows_call(
            partial(enter_kernel, layer),
            place,
            (own_h,) if layer == 0 else (middle, part, got),
            ((order,) if layer == 0 else ()) + (gains, in_bias),
            attn_slabs[layer],
            (table_near, table_far, starts),
            (row_f32, row_b16, array((2, rows, 3 * width), BF16)),
            (array((2, BASIS, 2 * width), F32), array((2, BASIS, 2 * width), BF16)),
            7,
            [pltpu.VMEM((2, rows, 2 * width), BF16)],
            after=(up_two[1], down_two[1]) if layer == 0 else (),
        )
        received = lax.ppermute(ahead, "cy", ((0, 1),))
        out_slabs = attn_slabs[layer][4:]
        attended, log_totals, memory, part = attention_forward(
            layer, place, memory_bias, qkv, starts, received, fit, table_near, out_slabs,
            after=ffn_slabs[0][1:4] + ffn_slabs[0][5:8] + (above_two[0][1], above_two[1][1])
            if layer == 0
            else (),
        )
        got = flip(part, "cc")
        middle, normed_two, active, slope, part = rows_call(
            partial(ffn_forward_kernel, layer),
            place,
            (stream, part, got),
            (gains, up_bias),
            ffn_slabs[layer],
            (),
            (row_f32, row_b16, side_hidden, side_hidden, row_b16),
            (),
            11,
        )
        got = flip(part, "cc")
        saved.append(
            (
                stream,
                normed,
                qkv,
                memory,
                log_totals,
                attended,
                middle,
                normed_two,
                active,
                slope,
            )
        )
    final = middle + (part.astype(F32) + got.astype(F32) + gains[LAYERS - 1, 5])
    final = lax.optimization_barrier(final.astype(BF16))
    outputs = final, flip(final, "cy")

    sums_ffn = [None] * (LAYERS + 1)
    sums_mix = [None] * LAYERS
    sums_in = [None] * LAYERS
    reduced = [None] * LAYERS

    def second_hop(keep_x, got_x, keep_y, got_y, after):
        pass_x, pass_y = pass_on(keep_x, got_x, keep_y, got_y, after)
        all_x = (keep_x[0], got_x[0], flip(pass_x, "cy"))
        all_y = (keep_y[0], got_y[0], flip(pass_y, "tx"))
        return pass_x, pieces_of((all_x, all_y), block_rows)

    zero_first = ()
    zero_mix = ()
    zero_attention = ()
    zero_memory = ()
    above_attention = None
    for layer in reversed(range(LAYERS)):
        (
            stream,
            normed,
            qkv,
            memory,
            log_totals,
            attended,
            middle,
            normed_two,
            active,
            slope,
        ) = saved[layer]
        top = layer == LAYERS - 1
        stream_grad, down, hidden_grad, part, sums_ffn[layer] = rows_call(
            partial(ffn_backward_kernel, layer),
            place,
            (own_cot, slope) if top else (stream_grad, stream_above, part, got, slope),
            (order if top else gains,),
            ffn_slabs[layer],
            (),
            (row_f32, row_b16, side_hidden, row_b16),
            (sums_shape,),
            9,
            after=zero_first,
        )
        got = flip(part, "cc")
        if above_attention is not None:
            qk_give, qk_keep, qk_got, vo_keep, vo_got = above_attention
            passed, attn_pieces = second_hop(qk_keep, qk_got, vo_keep, vo_got, (down,))
            zero_mix, zero_attention = (passed,), (attn_pieces,)
            reduced[layer + 1] = (spread_pieces(attn_pieces), spread_ffn)
            zero_memory = (spread_ffn,)
        ffn_operands = (normed_two, down, hidden_grad, active)
        ffn_plans = [
            [
                [[(0, x, 2, y, 0, hidden_own)] for x, y in pair_x],
                [[(1, x, 3, y, 0, hidden_own)] for x, y in pair_y],
            ]
            for pair_x, pair_y in ((GIVE_X, GIVE_Y), (KEEP_X, KEEP_Y))
        ]
        up_give, down_give = weight_grads(ffn_operands, ffn_plans[0], half)
        up_got, down_got = flip(up_give, "tx"), flip(down_give, "cy")
        stream_grad, branch_grad, attended_grad, sums_mix[layer] = rows_call(
            partial(mix_backward_kernel, layer),
            place,
            (stream_grad, middle, part, got),
            (gains,),
            attn_slabs[layer],
            (),
            (row_f32, row_b16, side_width),
            (sums_shape,),
            6,
            after=(up_give, *zero_mix),
        )
        dq, dkv, last, back = attention_backward(
            memory_bias, qkv, memory, log_totals, attended, attended_grad, table_near, zero_attention
        )
        received = lax.ppermute(back, "cy", ((1, 0),))
        up_keep, down_keep = weight_grads(ffn_operands, ffn_plans[1], half, (dq,))
        passed, ffn_pieces = second_hop(up_keep, up_got, down_keep, down_got, (dq,))
        grads_in, part, sums_in[layer] = memory_backward(
            place, dq, dkv, last, received, table_near, table_far, attn_slabs[layer],
            (passed, *zero_memory),
        )
        got = flip(part, "cc")
        spread_ffn = spread_pieces(ffn_pieces)
        attn_plans = [
            [
                [[(0, x, 2, y, 0, 2 * width)] for x, y in pair_x],
                [
                    [(0, x, 2, y, 2 * width, 3 * width), (1, x, 3, y, 0, width)]
                    for x, y in pair_y
                ],
            ]
            for pair_x, pair_y in ((GIVE_X, GIVE_Y), (KEEP_X, KEEP_Y))
        ]
        attn_operands = (normed, branch_grad, grads_in, attended)
        qk_give, vo_give = weight_grads(attn_operands, attn_plans[0], half)
        qk_got, vo_got = flip(qk_give, "tx"), flip(vo_give, "cy")
        if layer > 0:
            qk_keep, vo_keep = weight_grads(attn_operands, attn_plans[1], half)
            above_attention = qk_give, qk_keep, qk_got, vo_keep, vo_got
            zero_first = (qk_give, ffn_pieces)
        stream_above = stream
    final, sums_ffn[LAYERS] = rows_call(
        leave_kernel,
        place,
        (stream_grad, stream, part, got),
        (gains,),
        None,
        (),
        (row_b16,),
        (sums_shape,),
        5,
        after=(qk_give, ffn_pieces),
    )
    qk_keep, vo_keep = weight_grads(attn_operands, attn_plans[1], half, (final,))
    passed, attn_pieces = second_hop(qk_keep, qk_got, vo_keep, vo_got, (final,))
    reduced[0] = (spread_pieces(attn_pieces), spread_ffn)
    reduced = [[piece.astype(F32).sum(axis=0) for piece in pair] for pair in reduced]
    activations = restore(*outputs, order_back, place, (passed,))
    input_grad = restore(final, flip(final, "cy"), order_back, place)

    vector_d = []
    vector_own = []
    vector_other = []
    for layer in range(LAYERS):
        below = sums_ffn[layer - 1] if layer > 0 else sums_ffn[LAYERS]
        vector_d.append(
            jnp.concatenate(
                [below[:2], sums_mix[layer][:3], sums_ffn[layer][2:3]], axis=0
            )
        )
        ups = sums_ffn[layer][3:5].reshape(2, width, 4).transpose(0, 2, 1)
        for side, out in enumerate((vector_own, vector_other)):
            sums = sums_in[layer][side]
            out.append(
                jnp.concatenate(
                    [sums[None, :width], sums[None, 2 * width :], ups[side]], axis=0
                )
            )
    qkv_grads = [
        jnp.stack([r[0][:, i * width : (i + 1) * width] for i in range(3)]) for r in reduced
    ]
    matrix_grads = (
        jnp.stack(qkv_grads),
        jnp.stack([r[0][:, 3 * width :] for r in reduced]),
        jnp.stack([r[1][:, :hidden_own] for r in reduced]),
        jnp.stack([r[1][:, hidden_own:] for r in reduced]),
    )
    vec_d_grad = jnp.dot(
        jnp.stack(vector_d).reshape(-1, features), order_wide.T, precision=PRECISE
    ).reshape(-1)
    own_c = jnp.stack(vector_own).reshape(-1)
    other_c = jnp.stack(vector_other).reshape(-1)
    arrived = flip(jnp.concatenate([vec_d_grad, other_c]), "cy")
    vector = butterfly(jnp.concatenate([vec_d_grad, own_c]) + arrived, ("tx", "tz"))
    vec_d_grad = vector[: vec_d.size].reshape(vec_d.shape)
    vec_c_grad = vector[vec_d.size :].reshape(vec_c.shape)

    square = sum(jnp.sum(grad * grad) for grad in matrix_grads)
    square = (
        square
        + jnp.sum(vec_d_grad * vec_d_grad) / (tok_count * ch_count)
        + jnp.sum(vec_c_grad * vec_c_grad) / tok_count
    )
    everywhere = ("tz", "tx", "cy", "cc")
    squares = lax.all_to_all(
        jnp.full((tok_count * ch_count, 128), square), everywhere, 0, 0, tiled=True
    )
    total_square = jnp.sum(squares[:, 0])
    grad_norm = jnp.sqrt(total_square)
    factor = CLIP_LIMIT / jnp.maximum(grad_norm, CLIP_LIMIT)
    attention_update = adamw(
        w_qkv, w_qkv_first, w_qkv_second, matrix_grads[0] * factor, RATE_QKV, WEIGHT_DECAY
    )
    output_update = adamw(
        w_out_t, w_out_first, w_out_second, matrix_grads[1] * factor, RATE_OUT, WEIGHT_DECAY
    )
    expand_update = adamw(
        w_up, w_up_first, w_up_second, matrix_grads[2] * factor, RATE_UP, WEIGHT_DECAY
    )
    reduce_update = adamw(
        w_down_t, w_down_first, w_down_second, matrix_grads[3] * factor, RATE_DOWN, WEIGHT_DECAY
    )
    width_update = adamw(vec_d, vec_d_first, vec_d_second, vec_d_grad * factor, RATE_VECTOR, 0.0)
    channel_update = adamw(vec_c, vec_c_first, vec_c_second, vec_c_grad * factor, RATE_VECTOR, 0.0)
    return (
        activations,
        input_grad,
        grad_norm,
        *attention_update,
        *output_update,
        *expand_update,
        *reduce_update,
        *width_update,
        *channel_update,
    )


def solution(mesh):
    tok, ch = mesh.shape["tok"], mesh.shape["ch"]
    fine = Mesh(mesh.devices.reshape(tok // 2, 2, 2, ch // 2), ("tz", "tx", "cy", "cc"))
    t, c = ("tz", "tx"), ("cy", "cc")
    cube = P(None, None, t, c)
    matrix = P(None, t, c)
    channel = P(None, None, c)
    return jax.shard_map(
        shards,
        mesh=fine,
        in_specs=(
            P(t, None),
            P(t, None),
            P(None, t, None, None, c),
            P(),
            P(t, None, None),
            P(t),
            *(cube,) * 3,
            *(matrix,) * 9,
            *(P(),) * 3,
            *(channel,) * 3,
        ),
        out_specs=(
            P(t, None),
            P(t, None),
            P(),
            *(cube,) * 3,
            *(matrix,) * 9,
            *(P(),) * 3,
            *(channel,) * 3,
        ),
        check_vma=False,
    )
```

time: 896 us -> 616 us (0.69)
  Pallas kernels: 72.2 us -> 312 us
  matrix products: 228 us -> 2.54 us
  waiting for transfers between devices: 219 us -> 93.3 us
  other arithmetic: 117 us -> 36.7 us
  local copies, waits for them, and re-layouts: 119 us -> 41.8 us
  starting transfers between devices: 121 us -> 95 us
  between operations: 9.94 us -> 23.8 us
    pallas_call x4 -> x34, Pallas kernels: 60.3 us -> 298 us  [the longest x9 114 us: rows_call(): pl.pallas_call(body, grid_spec=pltpu.PrefetchScalarGridSpec(num_scalar_pr...]
    dot_general x82 -> x0, matrix products: 224 us -> none  [the longest x80 217 us: dot(): lax.dot_general(left, right, dims, precision=precision, preferred_element...]
    ppermute x50 -> x48, waiting for transfers between devices: 189 us -> 54 us  [flip(): return lax.ppermute(array, axis, SWAP)]
    reduce_sum x26 -> x5, other arithmetic: 60.1 us -> 1.08 us  [the longest x1 0.6 us: shards(): total_square = jnp.sum(squares[:, 0])]
    all_to_all x12 -> x6, starting transfers between devices: 57.4 us -> 27.7 us  [the longest x4 19.9 us: spread_pieces(): return lax.all_to_all(pieces, 'tz', 0, 0, tiled=True)]
    slice x27 -> x11, local copies, waits for them, and re-layouts: 27.6 us -> 5.9 us  [the longest x2 1.71 us: shards(): sums[None, :width]]
    unnamed x355 -> x137, local copies, waits for them, and re-layouts: 36.4 us -> 14.7 us
    ppermute x12 -> x10, waiting for transfers between devices: 11.1 us -> 23.2 us  [the longest x2 15.4 us: shards(): received = lax.ppermute(ahead, 'cy', ((0, 1),))]
  transfers between devices with their start and end apart: 74 -> 65, of which waited for: 29 -> 18; matrix products, arithmetic and copies ran while one was open for 44% -> 12% of each run, Pallas kernels for 8% -> 45%
where the time goes in v2:
time: 616 us; the launch traced here: 605 us
  Pallas kernels  312 us (51%)
  starting transfers between devices  95 us (15%)
  waiting for transfers between devices  93.3 us (15%)
  local copies, waits for them, and re-layouts  41.8 us (7%)
  other arithmetic  36.7 us (6%)
  between operations  23.8 us (4%)
    pallas_call x9, Pallas kernels, rows_call(): pl.pallas_call(body, grid_spec=pltpu.PrefetchScalarGridSpec(num_scalar_pr...  114 us
    ppermute x48, waiting for transfers between devices, flip(): return lax.ppermute(array, axis, SWAP)  54 us
    pallas_call x8, Pallas kernels, weight_grads(): pl.pallas_call(partial(weight_grads_kernel, plan), in_specs=[vmem] * len(...  52.6 us
    ppermute x48, starting transfers between devices, flip(): return lax.ppermute(array, axis, SWAP)  43.2 us
    pallas_call x2, Pallas kernels, attention_backward(): pl.pallas_call(attention_backward_kernel, grid=(2, segs), in_specs=[pl.Bl...  36.5 us
    pallas_call x2, Pallas kernels, attention_forward(): pl.pallas_call(attention_forward_kernel, grid_spec=pltpu.PrefetchScalarGr...  35.2 us
    pallas_call x2, Pallas kernels, memory_backward(): pl.pallas_call(memory_backward_kernel, grid_spec=pltpu.PrefetchScalarGrid...  21 us
    all_to_all x4, starting transfers between devices, spread_pieces(): return lax.all_to_all(pieces, 'tz', 0, 0, tiled=True)  19.9 us
  transfers between devices with their start and end apart: 65, of which 18 were waited for; matrix products, arithmetic and copies ran while one was open for 12% of the time, Pallas kernels for 45%

profile of v2, /device:TPU:0, one launch (start us, length us, event | category | flops | bytes accessed | tf_op | source)
XLA Modules:
  0.0 605.3 jit_solution(7169763896050731443)
XLA Ops:
  9.1 3.0 collective-permute-start
  19.1 5.2 all-to-all-start
  29.9 13.8 %shard_map.392.refs_0_ = bf16[256,768]{1,0:T(8,128)(2,1)} custom-call(f32[256,256]{1,0:T(8,128)} %fusion.21.old_ref, f32[256,768]{1,0:T(8,128)} %fusion.12.design_ref), custom_call_target="tpu_custom_call" | custom-call | flops 44000002048 | bytes 1000000 | tf_op jit(solution)/shard_map/pallas_call | solution.py:99
  85.2 10.9 %collective-permute-done.9.refs_11_.refs_3_.refs_12_.refs_7_ = bf16[384,384]{1,0:T(8,128)(2,1)S(1)} collective-permute-done((bf16[384,384]{1,0:T(8,128)(2,1)}, bf16[384,384]{1,0:T(8,128)(2,1)S(1)}, u32[]{:S(2)}, u32[]{:S(2)}) %collective-permute-start.9) | collective-permute-done | bytes 294944 | tf_op jit(solution)/shard_map/ppermute | solution.py:824
  99.1 4.8 collective-permute-done.20.refs_11_.refs_2_.refs_6_
  106.7 13.3 %shard_map.396 = (f32[1024,768]{1,0:T(8,128)}, bf16[1024,768]{1,0:T(8,128)(2,1)}, bf16[2,1024,576]{2,1,0:T(8,128)(2,1)}, f32[2,256,384]{2,1,0:T(8,128)}, bf16[2,256,384]{2,1,0:T(8,128)(2,1)}) custom-call(s32[2]{0:T(128)} %pad_add_fusion.place_ref.context_ref, bf16[1024,768]{1,0:T(8,128)(2,1)} %constant_dynamic-slice_fusion.1.refs_0_, ...), custom_call_target="tpu_custom_call" | custom-call | flops 7699999744 | bytes 1000000 | tf_op jit(solution)/shard_map/pallas_call | solution.py:310
  120.9 3.3 collective-permute-start.14
  126.8 7.7 %collective-permute-done.14.got_ref = bf16[2,256,384]{2,1,0:T(8,128)(2,1)S(1)} collective-permute-done((bf16[2,256,384]{2,1,0:T(8,128)(2,1)}, bf16[2,256,384]{2,1,0:T(8,128)(2,1)S(1)}, u32[]{:S(2)}, u32[]{:S(2)}) %collective-permute-start.14) | collective-permute-done | bytes 393248 | tf_op jit(solution)/shard_map/ppermute | solution.py:1016
  135.4 17.6 %shard_map.397 = (bf16[2,1024,192]{2,1,0:T(8,128)(2,1)}, f32[2,2,3,512]{3,2,1,0:T(4,128)}, bf16[2,2,256,384]{3,2,1,0:T(8,128)(2,1)}, bf16[1024,768]{1,0:T(8,128)(2,1)}) custom-call(s32[2]{0:T(128)} %pad_add_fusion.place_ref.context_ref, f32[2]{0:T(128)} %pad_maximum_fusion.16.bias_ref, bf16[2,1024,576]{2,1,0:T(8,128)(2,1)} %get-tuple-element.120.qkv_ref, ...), custom_call_target="tpu_custom_call" | custom-call | flops 14300000256 | bytes 1000000 | tf_op jit(solution)/shard_map/pallas_call | solution.py:575
  157.8 15.3 %shard_map.398 = (f32[1024,768]{1,0:T(8,128)}, bf16[1024,768]{1,0:T(8,128)(2,1)}, bf16[2,1024,768]{2,1,0:T(8,128)(2,1)}, bf16[2,1024,768]{2,1,0:T(8,128)(2,1)}, bf16[1024,768]{1,0:T(8,128)(2,1)}) custom-call(s32[2]{0:T(128)} %pad_add_fusion.place_ref.context_ref, f32[1024,768]{1,0:T(8,128)} %get-tuple-element.119.refs_0_.refs_1_, ...), custom_call_target="tpu_custom_call" | custom-call | flops 12099999744 | bytes 1000000 | tf_op jit(solution)/shard_map/pallas_call | solution.py:310
  177.8 10.2 %collective-permute-done.25.refs_10_.refs_1_.refs_5_ = bf16[384,384]{1,0:T(8,128)(2,1)S(1)} collective-permute-done((bf16[384,384]{1,0:T(8,128)(2,1)S(1)}, bf16[384,384]{1,0:T(8,128)(2,1)S(1)}, u32[]{:S(2)}, u32[]{:S(2)}) %collective-permute-start.25) | collective-permute-done | bytes 294944 | tf_op jit(solution)/shard_map/ppermute | solution.py:824
  188.0 3.2 collective-permute-done.23.refs_7_.refs_2_
  191.2 8.9 %collective-permute-done.26.refs_12_.refs_3_.refs_7_ = bf16[384,384]{1,0:T(8,128)(2,1)S(1)} collective-permute-done((bf16[384,384]{1,0:T(8,128)(2,1)S(1)}, bf16[384,384]{1,0:T(8,128)(2,1)S(1)}, u32[]{:S(2)}, u32[]{:S(2)}) %collective-permute-start.26) | collective-permute-done | bytes 294944 | tf_op jit(solution)/shard_map/ppermute | solution.py:824
  200.0 3.3 collective-permute-done.24.refs_8_.refs_3_
  204.6 12.3 %shard_map.399 = (f32[1024,768]{1,0:T(8,128)}, bf16[1024,768]{1,0:T(8,128)(2,1)}, bf16[2,1024,576]{2,1,0:T(8,128)(2,1)}, f32[2,256,384]{2,1,0:T(8,128)}, bf16[2,256,384]{2,1,0:T(8,128)(2,1)}) custom-call(s32[2]{0:T(128)} %pad_add_fusion.place_ref.context_ref, f32[1024,768]{1,0:T(8,128)} %get-tuple-element.126.refs_0_.refs_1_, ...), custom_call_target="tpu_custom_call" | custom-call | flops 7699999744 | bytes 1000000 | tf_op jit(solution)/shard_map/pallas_call | solution.py:310
  216.9 4.4 collective-permute-start.27
  221.3 7.7 %collective-permute-done.27.got_ref = bf16[2,256,384]{2,1,0:T(8,128)(2,1)S(1)} collective-permute-done((bf16[2,256,384]{2,1,0:T(8,128)(2,1)}, bf16[2,256,384]{2,1,0:T(8,128)(2,1)S(1)}, u32[]{:S(2)}, u32[]{:S(2)}) %collective-permute-start.27) | collective-permute-done | bytes 393248 | tf_op jit(solution)/shard_map/ppermute | solution.py:1016
  229.7 17.6 %shard_map.400 = (bf16[2,1024,192]{2,1,0:T(8,128)(2,1)}, f32[2,2,3,512]{3,2,1,0:T(4,128)}, bf16[2,2,256,384]{3,2,1,0:T(8,128)(2,1)}, bf16[1024,768]{1,0:T(8,128)(2,1)}) custom-call(s32[2]{0:T(128)} %pad_add_fusion.place_ref.context_ref, f32[2]{0:T(128)} %pad_maximum_fusion.16.bias_ref, bf16[2,1024,576]{2,1,0:T(8,128)(2,1)} %get-tuple-element.129.qkv_ref, ...), custom_call_target="tpu_custom_call" | custom-call | flops 14300000256 | bytes 1000000 | tf_op jit(solution)/shard_map/pallas_call | solution.py:575
  251.1 15.2 %shard_map.402 = (f32[1024,768]{1,0:T(8,128)}, bf16[1024,768]{1,0:T(8,128)(2,1)}, bf16[2,1024,768]{2,1,0:T(8,128)(2,1)}, bf16[2,1024,768]{2,1,0:T(8,128)(2,1)}, bf16[1024,768]{1,0:T(8,128)(2,1)}) custom-call(s32[2]{0:T(128)} %pad_add_fusion.place_ref.context_ref, f32[1024,768]{1,0:T(8,128)} %get-tuple-element.128.refs_0_.refs_1_, ...), custom_call_target="tpu_custom_call" | custom-call | flops 12099999744 | bytes 1000000 | tf_op jit(solution)/shard_map/pallas_call | solution.py:310
  266.3 14.7 %shard_map.403 = (f32[1024,768]{1,0:T(8,128)}, bf16[1024,768]{1,0:T(8,128)(2,1)}, bf16[2,1024,768]{2,1,0:T(8,128)(2,1)}, bf16[1024,768]{1,0:T(8,128)(2,1)}, f32[8,768]{1,0:T(8,128)}) custom-call(s32[2]{0:T(128)} %pad_add_fusion.place_ref.context_ref, bf16[1024,768]{1,0:T(8,128)(2,1)} %constant_dynamic-slice_fusion.refs_0_, ...), custom_call_target="tpu_custom_call" | custom-call | flops 9900000256 | bytes 1000000 | tf_op jit(solution)/shard_map/pallas_call | solution.py:310
  283.4 7.4 %shard_map.404 = (bf16[2,384,768]{2,1,0:T(8,128)(2,1)}, bf16[2,384,768]{2,1,0:T(8,128)(2,1)}) custom-call(bf16[1024,768]{1,0:T(8,128)(2,1)} %get-tuple-element.139.refs_0_, bf16[1024,768]{1,0:T(8,128)(2,1)} %get-tuple-element.140.refs_1_, bf16[2,1024,768]{2,1,0:T(8,128)(2,1)} %get-tuple-element.141.refs_2_, bf16[2,1024,768]{2,1,0:T(8,128)(2,1)} %get-tuple-element.142.refs_3_), custom_call_target="tpu_custom_call" | custom-call | flops 6600000000 | bytes 1000000 | tf_op jit(solution)/shard_map/pallas_call | solution.py:807
  294.1 10.2 %shard_map.405 = (f32[1024,768]{1,0:T(8,128)}, bf16[1024,768]{1,0:T(8,128)(2,1)}, bf16[2,1024,192]{2,1,0:T(8,128)(2,1)}, f32[8,768]{1,0:T(8,128)}) custom-call(s32[2]{0:T(128)} %pad_add_fusion.place_ref.context_ref, f32[1024,768]{1,0:T(8,128)} %get-tuple-element.137.refs_0_, f32[1024,768]{1,0:T(8,128)} %get-tuple-element.133.refs_1_, ...), custom_call_target="tpu_custom_call" | custom-call | flops 6600000000 | bytes 1000000 | tf_op jit(solution)/shard_map/pallas_call | solution.py:310
  304.2 18.4 %shard_map.406 = (bf16[2,1024,192]{2,1,0:T(8,128)(2,1)}, f32[2,1024,384]{2,1,0:T(8,128)}, f32[2,256,384]{2,1,0:T(8,128)}, bf16[2,256,384]{2,1,0:T(8,128)(2,1)}) custom-call(f32[2]{0:T(128)} %pad_maximum_fusion.16.bias_ref, bf16[2,1024,576]{2,1,0:T(8,128)(2,1)} %get-tuple-element.129.qkv_ref, bf16[2,2,256,384]{3,2,1,0:T(8,128)(2,1)} %get-tuple-element.145.memory_ref, ...), custom_call_target="tpu_custom_call" | custom-call | flops 19800000512 | bytes 1000000 | tf_op jit(solution)/shard_map/pallas_call | solution.py:685
  323.9 7.5 %shard_map.407 = (bf16[2,384,768]{2,1,0:T(8,128)(2,1)}, bf16[2,384,768]{2,1,0:T(8,128)(2,1)}) custom-call(bf16[1024,768]{1,0:T(8,128)(2,1)} %get-tuple-element.139.refs_0_, bf16[1024,768]{1,0:T(8,128)(2,1)} %get-tuple-element.140.refs_1_, bf16[2,1024,768]{2,1,0:T(8,128)(2,1)} %get-tuple-element.141.refs_2_, ...), custom_call_target="tpu_custom_call" | custom-call | flops 6600000000 | bytes 1000000 | tf_op jit(solution)/shard_map/pallas_call | solution.py:807
  340.1 3.1 add_convert_fusion.own_ref
  344.0 10.7 %shard_map.409 = (bf16[2,1024,576]{2,1,0:T(8,128)(2,1)}, bf16[1024,768]{1,0:T(8,128)(2,1)}, f32[8,576]{1,0:T(8,128)}) custom-call(s32[2]{0:T(128)} %pad_add_fusion.place_ref.context_ref, bf16[2,1024,192]{2,1,0:T(8,128)(2,1)} %get-tuple-element.149.refs_4_.refs_0_.dq_ref, f32[2,1024,384]{2,1,0:T(8,128)} %get-tuple-element.150.dkv_ref, ...), custom_call_target="tpu_custom_call" | custom-call | flops 5500000256 | bytes 1000000 | tf_op jit(solution)/shard_map/pallas_call | solution.py:760
  354.8 5.7 shard_map.413
  360.4 5.8 shard_map.410
  371.3 5.6 all-to-all-start.1
  376.9 15.6 %shard_map.411 = (f32[1024,768]{1,0:T(8,128)}, bf16[1024,768]{1,0:T(8,128)(2,1)}, bf16[2,1024,768]{2,1,0:T(8,128)(2,1)}, bf16[1024,768]{1,0:T(8,128)(2,1)}, f32[8,768]{1,0:T(8,128)}) custom-call(s32[2]{0:T(128)} %pad_add_fusion.place_ref.context_ref, f32[1024,768]{1,0:T(8,128)} %get-tuple-element.144.refs_0_, ...), custom_call_target="tpu_custom_call" | custom-call | flops 9900000256 | bytes 1000000 | tf_op jit(solution)/shard_map/pallas_call | solution.py:310
  392.5 6.3 %collective-permute-done.40.got_b_ref = bf16[2,384,384]{2,1,0:T(8,128)(2,1)} collective-permute-done((bf16[2,384,384]{2,1,0:T(8,128)(2,1)}, bf16[2,384,384]{2,1,0:T(8,128)(2,1)}, u32[]{:S(2)}, u32[]{:S(2)}) %collective-permute-start.40) | collective-permute-done | bytes 589856 | tf_op jit(solution)/shard_map/ppermute | solution.py:824
  404.3 7.5 %shard_map.412 = (bf16[2,384,768]{2,1,0:T(8,128)(2,1)}, bf16[2,384,768]{2,1,0:T(8,128)(2,1)}) custom-call(bf16[1024,768]{1,0:T(8,128)(2,1)} %get-tuple-element.166.refs_0_, bf16[1024,768]{1,0:T(8,128)(2,1)} %get-tuple-element.167.refs_1_.refs_0_, bf16[2,1024,768]{2,1,0:T(8,128)(2,1)} %get-tuple-element.168.refs_2_, ...), custom_call_target="tpu_custom_call" | custom-call | flops 6600000000 | bytes 1000000 | tf_op jit(solution)/shard_map/pallas_call | solution.py:807
  416.0 5.5 all-to-all-start.3
  421.7 10.1 %shard_map.415 = (f32[1024,768]{1,0:T(8,128)}, bf16[1024,768]{1,0:T(8,128)(2,1)}, bf16[2,1024,192]{2,1,0:T(8,128)(2,1)}, f32[8,768]{1,0:T(8,128)}) custom-call(s32[2]{0:T(128)} %pad_add_fusion.place_ref.context_ref, f32[1024,768]{1,0:T(8,128)} %get-tuple-element.164.refs_0_, f32[1024,768]{1,0:T(8,128)} %get-tuple-element.126.refs_0_.refs_1_, ...), custom_call_target="tpu_custom_call" | custom-call | flops 6600000000 | bytes 1000000 | tf_op jit(solution)/shard_map/pallas_call | solution.py:310
  431.8 18.1 %shard_map.416 = (bf16[2,1024,192]{2,1,0:T(8,128)(2,1)}, f32[2,1024,384]{2,1,0:T(8,128)}, f32[2,256,384]{2,1,0:T(8,128)}, bf16[2,256,384]{2,1,0:T(8,128)(2,1)}) custom-call(f32[2]{0:T(128)} %pad_maximum_fusion.16.bias_ref, bf16[2,1024,576]{2,1,0:T(8,128)(2,1)} %get-tuple-element.120.qkv_ref, bf16[2,2,256,384]{3,2,1,0:T(8,128)(2,1)} %get-tuple-element.176.memory_ref, ...), custom_call_target="tpu_custom_call" | custom-call | flops 19800000512 | bytes 1000000 | tf_op jit(solution)/shard_map/pallas_call | solution.py:685
  451.5 7.4 %shard_map.417 = (bf16[2,384,768]{2,1,0:T(8,128)(2,1)}, bf16[2,384,768]{2,1,0:T(8,128)(2,1)}) custom-call(bf16[1024,768]{1,0:T(8,128)(2,1)} %get-tuple-element.166.refs_0_, bf16[1024,768]{1,0:T(8,128)(2,1)} %get-tuple-element.167.refs_1_.refs_0_, bf16[2,1024,768]{2,1,0:T(8,128)(2,1)} %get-tuple-element.168.refs_2_, ...), custom_call_target="tpu_custom_call" | custom-call | flops 6600000000 | bytes 1000000 | tf_op jit(solution)/shard_map/pallas_call | solution.py:807
  466.3 10.3 %shard_map.419 = (bf16[2,1024,576]{2,1,0:T(8,128)(2,1)}, bf16[1024,768]{1,0:T(8,128)(2,1)}, f32[8,576]{1,0:T(8,128)}) custom-call(s32[2]{0:T(128)} %pad_add_fusion.place_ref.context_ref, bf16[2,1024,192]{2,1,0:T(8,128)(2,1)} %get-tuple-element.181.refs_4_.refs_0_.dq_ref, f32[2,1024,384]{2,1,0:T(8,128)} %get-tuple-element.182.dkv_ref, ...), custom_call_target="tpu_custom_call" | custom-call | flops 5500000256 | bytes 1000000 | tf_op jit(solution)/shard_map/pallas_call | solution.py:760
  476.7 5.7 shard_map.420
  488.1 7.4 %shard_map.421 = (bf16[1024,768]{1,0:T(8,128)(2,1)}, f32[8,768]{1,0:T(8,128)}) custom-call(s32[2]{0:T(128)} %pad_add_fusion.place_ref.context_ref, f32[1024,768]{1,0:T(8,128)} %get-tuple-element.190.refs_0_, f32[1024,768]{1,0:T(8,128)} %get-tuple-element.119.refs_0_.refs_1_, bf16[1024,768]{1,0:T(8,128)(2,1)} %get-tuple-element.191.refs_2_, ...), custom_call_target="tpu_custom_call" | custom-call | flops 5500000256 | bytes 1000000 | tf_op jit(solution)/shard_map/pallas_call | solution.py:310
  499.6 5.3 all-to-all-start.4
  505.0 5.7 shard_map.422
  519.6 5.4 collective-permute-done.56
  525.0 4.7 collective-permute-start.57
  534.9 3.5 all-to-all-start.2
  543.1 10.1 %all-to-all-done.2 = bf16[4,96,768]{2,1,0:T(8,128)(2,1)S(1)} async-done(((bf16[4,96,768]{2,1,0:T(8,128)(2,1)}), bf16[4,96,768]{2,1,0:T(8,128)(2,1)S(1)}, u32[]{:S(2)}, u32[]{:S(2)}) %all-to-all-start.2) | async-done | bytes 589856 | tf_op jit(solution)/shard_map/all_to_all | solution.py:869
  560.7 9.4 %shard_map.424 = f32[2048,768]{1,0:T(8,128)} custom-call(s32[2]{0:T(128)} %pad_add_fusion.place_ref.context_ref, bf16[1024,768]{1,0:T(8,128)(2,1)} %add_convert_fusion.own_ref, bf16[1024,768]{1,0:T(8,128)(2,1)} %collective-permute-done.30.got_ref, bf16[768,768]{1,0:T(8,128)(2,1)} %get-tuple-element.339.order_ref, bf16[384,384]{1,0:T(8,128)(2,1)} %get-tuple-element.198.refs_0_), custom_call_target="tpu_custom_call" | custom-call | flops 4400000000 | bytes 1000000 | tf_op jit(solution)/shard_map/pallas_call | solution.py:462
  570.1 3.8 all-to-all-done.5
  587.4 9.5 %shard_map.425 = f32[2048,768]{1,0:T(8,128)} custom-call(s32[2]{0:T(128)} %pad_add_fusion.place_ref.context_ref, bf16[1024,768]{1,0:T(8,128)(2,1)} %get-tuple-element.194.refs_4_.refs_0_.own_ref, bf16[1024,768]{1,0:T(8,128)(2,1)} %collective-permute-done.51.got_ref, bf16[768,768]{1,0:T(8,128)(2,1)} %get-tuple-element.339.order_ref), custom_call_target="tpu_custom_call" | custom-call | flops 4400000000 | bytes 1000000 | tf_op jit(solution)/shard_map/pallas_call | solution.py:462
  (364 shorter events, 163.6 us)
Async XLA Ops:
  9.1 44.2 %collective-permute-start = (bf16[96,768]{1,0:T(8,128)(2,1)}, bf16[96,768]{1,0:T(8,128)(2,1)}, u32[]{:S(2)}, u32[]{:S(2)}) collective-permute-start(bf16[96,768]{1,0:T(8,128)(2,1)} %shard_map.391.refs_4_), channel_id=1, source_target_pairs={{0,8},{8,0},{16,24},{24,16},{1,9},{9,1},{17,25},{25,17},{2,10},{10... | collective-permute-start | bytes 442376 | tf_op jit(solution)/shard_map/ppermute | solution.py:852
  12.1 42.8 %collective-permute-start.1 = (bf16[96,768]{1,0:T(8,128)(2,1)}, bf16[96,768]{1,0:T(8,128)(2,1)}, u32[]{:S(2)}, u32[]{:S(2)}) collective-permute-start(bf16[96,768]{1,0:T(8,128)(2,1)} %shard_map.391.refs_4_), channel_id=1, source_target_pairs={{0,16},{8,24},{16,0},{24,8},{1,17},{9,25},{17,1},{25,9},{2,18},{10... | collective-permute-start | bytes 442376 | tf_op jit(solution)/shard_map/ppermute | solution.py:852
  14.7 41.8 %collective-permute-start.2 = (bf16[96,768]{1,0:T(8,128)(2,1)}, bf16[96,768]{1,0:T(8,128)(2,1)}, u32[]{:S(2)}, u32[]{:S(2)}) collective-permute-start(bf16[96,768]{1,0:T(8,128)(2,1)} %shard_map.391.refs_4_), channel_id=1, source_target_pairs={{0,24},{8,16},{16,8},{24,0},{1,25},{9,17},{17,9},{25,1},{2,26},{10... | collective-permute-start | bytes 442376 | tf_op jit(solution)/shard_map/ppermute | solution.py:852
  19.1 50.0 %all-to-all-start = ((bf16[4,96,2304]{2,1,0:T(8,128)(2,1)}), bf16[4,96,2304]{2,1,0:T(8,128)(2,1)}, u32[]{:S(2)}, u32[]{:S(2)}) async-start(bf16[4,96,2304]{2,1,0:T(8,128)(2,1)} %broadcast_in_dim.79), calls=%async_computation | async-start | bytes 3538944 | tf_op jit(solution)/shard_map/all_to_all | solution.py:838
  24.3 226.8 %all-gather.2.cloned.1.call-start = ((), (), s32[]{:S(2)}) async-start(), calls=%async_computation.6 | async-start | bytes 5013504 | tf_op jit(solution)/shard_map/all_gather | solution.py:831
  25.2 43.3 %collective-permute-start.11 = (bf16[2,256,384]{2,1,0:T(8,128)(2,1)}, bf16[2,256,384]{2,1,0:T(8,128)(2,1)}, u32[]{:S(2)}, u32[]{:S(2)}) collective-permute-start(bf16[2,256,384]{2,1,0:T(8,128)(2,1)} %copy.129), channel_id=1, source_target_pairs={{0,2},{2,0},{1,3},{3,1},{4,6},{6,4},{5,7},{7,5},{8,10},{10,8},{9,1... | collective-permute-start | bytes 1179656 | tf_op jit(solution)/shard_map/ppermute | solution.py:824
  26.7 24.6 %collective-permute-start.3 = (f32[2,6,192]{2,0,1:T(2,128)}, f32[2,6,192]{2,0,1:T(2,128)}, u32[]{:S(2)}, u32[]{:S(2)}) collective-permute-start(f32[2,6,192]{2,0,1:T(2,128)} %param.45), channel_id=1, source_target_pairs={{0,2},{2,0},{1,3},{3,1},{4,6},{6,4},{5,7},{7,5},{8,10},{10,8},{9,1... | collective-permute-start | bytes 27656 | tf_op jit(solution)/shard_map/ppermute | solution.py:824
  51.3 20.5 %collective-permute-start.10 = (bf16[256,768]{1,0:T(8,128)(2,1)}, bf16[256,768]{1,0:T(8,128)(2,1)S(1)}, u32[]{:S(2)}, u32[]{:S(2)}) collective-permute-start(bf16[256,768]{1,0:T(8,128)(2,1)} %shard_map.392.refs_0_), channel_id=1, source_target_pairs={{0,1},{1,0},{2,3},{3,2},{4,5},{5,4},{6,7},{7,6},{8,9},{9,8},{10,11... | collective-permute-start | bytes 1179656 | tf_op jit(solution)/shard_map/ppermute | solution.py:824
  61.5 18.5 %collective-permute-start.7 = (bf16[384,384]{1,0:T(8,128)(2,1)}, bf16[384,384]{1,0:T(8,128)(2,1)}, u32[]{:S(2)}, u32[]{:S(2)}) collective-permute-start(bf16[384,384]{1,0:T(8,128)(2,1)} %get-tuple-element.116.refs_8_.refs_0_.refs_9_.refs_4_), channel_id=1, source_target_pairs={{0,4},{4,0},{1,5},{5,1},{2,6},{6,2},{3,7},{7,3},{8,12},{12,8},{9,1... | collective-permute-start | bytes 884744 | tf_op jit(solution)/shard_map/ppermute | solution.py:824
  71.8 33.7 %collective-permute-start.12 = (bf16[384,768]{1,0:T(8,128)(2,1)}, bf16[384,768]{1,0:T(8,128)(2,1)}, u32[]{:S(2)}, u32[]{:S(2)}) collective-permute-start(bf16[384,768]{1,0:T(8,128)(2,1)} %get-tuple-element.117.refs_5_.refs_2_.refs_6_), channel_id=1, source_target_pairs={{0,4},{4,0},{1,5},{5,1},{2,6},{6,2},{3,7},{7,3},{8,12},{12,8},{9,1... | collective-permute-start | bytes 1769480 | tf_op jit(solution)/shard_map/ppermute | solution.py:824
  73.3 32.7 %collective-permute-start.13 = (bf16[384,768]{1,0:T(8,128)(2,1)}, bf16[384,768]{1,0:T(8,128)(2,1)}, u32[]{:S(2)}, u32[]{:S(2)}) collective-permute-start(bf16[384,768]{1,0:T(8,128)(2,1)} %get-tuple-element.118.refs_9_.refs_10_), channel_id=1, source_target_pairs={{0,2},{2,0},{1,3},{3,1},{4,6},{6,4},{5,7},{7,5},{8,10},{10,8},{9,1... | collective-permute-start | bytes 1769480 | tf_op jit(solution)/shard_map/ppermute | solution.py:824
  79.5 16.6 %collective-permute-start.9 = (bf16[384,384]{1,0:T(8,128)(2,1)}, bf16[384,384]{1,0:T(8,128)(2,1)S(1)}, u32[]{:S(2)}, u32[]{:S(2)}) collective-permute-start(bf16[384,384]{1,0:T(8,128)(2,1)} %collective-permute-done.8.refs_10_.refs_2_.refs_11_.refs_6_), channel_id=1, source_target_pairs={{0,4},{4,0},{1,5},{5,1},{2,6},{6,2},{3,7},{7,3},{8,12},{12,8},{9,1... | collective-permute-start | bytes 884744 | tf_op jit(solution)/shard_map/ppermute | solution.py:824
  80.0 17.6 %collective-permute-start.6 = (bf16[384,384]{1,0:T(8,128)(2,1)}, bf16[384,384]{1,0:T(8,128)(2,1)S(1)}, u32[]{:S(2)}, u32[]{:S(2)}) collective-permute-start(bf16[384,384]{1,0:T(8,128)(2,1)} %collective-permute-done.4.refs_5_.refs_6_.refs_1_), channel_id=1, source_target_pairs={{0,2},{2,0},{1,3},{3,1},{4,6},{6,4},{5,7},{7,5},{8,10},{10,8},{9,1... | collective-permute-start | bytes 884744 | tf_op jit(solution)/shard_map/ppermute | solution.py:824
  80.5 23.4 %collective-permute-start.20 = (bf16[384,384]{1,0:T(8,128)(2,1)S(1)}, bf16[384,384]{1,0:T(8,128)(2,1)S(1)}, u32[]{:S(2)}, u32[]{:S(2)}) collective-permute-start(bf16[384,384]{1,0:T(8,128)(2,1)S(1)} %copy-done.55), channel_id=1, source_target_pairs={{0,2},{2,0},{1,3},{3,1},{4,6},{6,4},{5,7},{7,5},{8,10},{10,8},{9,1... | collective-permute-start | bytes 884744 | tf_op jit(solution)/shard_map/ppermute | solution.py:824
  96.1 30.6 %collective-permute-start.15 = (bf16[384,768]{1,0:T(8,128)(2,1)S(1)}, bf16[384,768]{1,0:T(8,128)(2,1)S(1)}, u32[]{:S(2)}, u32[]{:S(2)}) collective-permute-start(bf16[384,768]{1,0:T(8,128)(2,1)S(1)} %copy-done.42), channel_id=1, source_target_pairs={{0,2},{2,0},{1,3},{3,1},{4,6},{6,4},{5,7},{7,5},{8,10},{10,8},{9,1... | collective-permute-start | bytes 1769480 | tf_op jit(solution)/shard_map/ppermute | solution.py:824
  97.7 29.1 %collective-permute-start.17 = (bf16[384,768]{1,0:T(8,128)(2,1)S(1)}, bf16[384,768]{1,0:T(8,128)(2,1)S(1)}, u32[]{:S(2)}, u32[]{:S(2)}) collective-permute-start(bf16[384,768]{1,0:T(8,128)(2,1)S(1)} %copy-done.43), channel_id=1, source_target_pairs={{0,4},{4,0},{1,5},{5,1},{2,6},{6,2},{3,7},{7,3},{8,12},{12,8},{9,1... | collective-permute-start | bytes 1769480 | tf_op jit(solution)/shard_map/ppermute | solution.py:824
  104.0 16.3 %collective-permute-start.19 = (bf16[384,384]{1,0:T(8,128)(2,1)S(1)}, bf16[384,384]{1,0:T(8,128)(2,1)S(1)}, u32[]{:S(2)}, u32[]{:S(2)}) collective-permute-start(bf16[384,384]{1,0:T(8,128)(2,1)S(1)} %copy-done.53), channel_id=1, source_target_pairs={{0,4},{4,0},{1,5},{5,1},{2,6},{6,2},{3,7},{7,3},{8,12},{12,8},{9,1... | collective-permute-start | bytes 884744 | tf_op jit(solution)/shard_map/ppermute | solution.py:824
  105.5 29.0 %collective-permute-start.16 = (bf16[384,768]{1,0:T(8,128)(2,1)}, bf16[384,768]{1,0:T(8,128)(2,1)S(1)}, u32[]{:S(2)}, u32[]{:S(2)}) collective-permute-start(bf16[384,768]{1,0:T(8,128)(2,1)} %collective-permute-done.12.refs_15_.refs_4_.refs_6_.refs_7_), channel_id=1, source_target_pairs={{0,2},{2,0},{1,3},{3,1},{4,6},{6,4},{5,7},{7,5},{8,10},{10,8},{9,1... | collective-permute-start | bytes 1769480 | tf_op jit(solution)/shard_map/ppermute | solution.py:824
  106.0 28.5 %collective-permute-start.18 = (bf16[384,768]{1,0:T(8,128)(2,1)}, bf16[384,768]{1,0:T(8,128)(2,1)}, u32[]{:S(2)}, u32[]{:S(2)}) collective-permute-start(bf16[384,768]{1,0:T(8,128)(2,1)} %collective-permute-done.13.refs_16_.refs_8_.refs_11_.refs_12_), channel_id=1, source_target_pairs={{0,4},{4,0},{1,5},{5,1},{2,6},{6,2},{3,7},{7,3},{8,12},{12,8},{9,1... | collective-permute-start | bytes 1769480 | tf_op jit(solution)/shard_map/ppermute | solution.py:824
  173.1 30.3 %collective-permute-start.22 = (bf16[1024,768]{1,0:T(8,128)(2,1)}, bf16[1024,768]{1,0:T(8,128)(2,1)S(1)}, u32[]{:S(2)}, u32[]{:S(2)}) collective-permute-start(bf16[1024,768]{1,0:T(8,128)(2,1)} %get-tuple-element.127.refs_1_), channel_id=1, source_target_pairs={{0,1},{1,0},{2,3},{3,2},{4,5},{5,4},{6,7},{7,6},{8,9},{9,8},{10,11... | collective-permute-start | bytes 4718600 | tf_op jit(solution)/shard_map/ppermute | solution.py:824
  174.8 16.3 %collective-permute-start.23 = (bf16[384,384]{1,0:T(8,128)(2,1)S(1)}, bf16[384,384]{1,0:T(8,128)(2,1)S(1)}, u32[]{:S(2)}, u32[]{:S(2)}) collective-permute-start(bf16[384,384]{1,0:T(8,128)(2,1)S(1)} %copy-done.54), channel_id=1, source_target_pairs={{0,2},{2,0},{1,3},{3,1},{4,6},{6,4},{5,7},{7,5},{8,10},{10,8},{9,1... | collective-permute-start | bytes 884744 | tf_op jit(solution)/shard_map/ppermute | solution.py:824
  177.1 22.9 %collective-permute-start.26 = (bf16[384,384]{1,0:T(8,128)(2,1)S(1)}, bf16[384,384]{1,0:T(8,128)(2,1)S(1)}, u32[]{:S(2)}, u32[]{:S(2)}) collective-permute-start(bf16[384,384]{1,0:T(8,128)(2,1)S(1)} %copy-done.58), channel_id=1, source_target_pairs={{0,4},{4,0},{1,5},{5,1},{2,6},{6,2},{3,7},{7,3},{8,12},{12,8},{9,1... | collective-permute-start | bytes 884744 | tf_op jit(solution)/shard_map/ppermute | solution.py:824
  177.7 25.7 %collective-permute-start.24 = (bf16[384,384]{1,0:T(8,128)(2,1)S(1)}, bf16[384,384]{1,0:T(8,128)(2,1)S(1)}, u32[]{:S(2)}, u32[]{:S(2)}) collective-permute-start(bf16[384,384]{1,0:T(8,128)(2,1)S(1)} %copy-done.60), channel_id=1, source_target_pairs={{0,2},{2,0},{1,3},{3,1},{4,6},{6,4},{5,7},{7,5},{8,10},{10,8},{9,1... | collective-permute-start | bytes 884744 | tf_op jit(solution)/shard_map/ppermute | solution.py:824
  290.9 40.6 %collective-permute-start.33 = (bf16[2,384,768]{2,1,0:T(8,128)(2,1)}, bf16[2,384,768]{2,1,0:T(8,128)(2,1)S(1)}, u32[]{:S(2)}, u32[]{:S(2)}) collective-permute-start(bf16[2,384,768]{2,1,0:T(8,128)(2,1)} %get-tuple-element.143.refs_13_), channel_id=1, source_target_pairs={{0,4},{4,0},{1,5},{5,1},{2,6},{6,2},{3,7},{7,3},{8,12},{12,8},{9,1... | collective-permute-start | bytes 3538952 | tf_op jit(solution)/shard_map/ppermute | solution.py:824
  291.2 40.2 %collective-permute-start.34 = (bf16[2,384,768]{2,1,0:T(8,128)(2,1)}, bf16[2,384,768]{2,1,0:T(8,128)(2,1)S(1)}, u32[]{:S(2)}, u32[]{:S(2)}) collective-permute-start(bf16[2,384,768]{2,1,0:T(8,128)(2,1)} %get-tuple-element.155), channel_id=1, source_target_pairs={{0,2},{2,0},{1,3},{3,1},{4,6},{6,4},{5,7},{7,5},{8,10},{10,8},{9,1... | collective-permute-start | bytes 3538952 | tf_op jit(solution)/shard_map/ppermute | solution.py:824
  294.0 46.1 %collective-permute-start.29 = (bf16[1024,768]{1,0:T(8,128)(2,1)}, bf16[1024,768]{1,0:T(8,128)(2,1)S(1)}, u32[]{:S(2)}, u32[]{:S(2)}) collective-permute-start(bf16[1024,768]{1,0:T(8,128)(2,1)} %get-tuple-element.134), channel_id=1, source_target_pairs={{0,1},{1,0},{2,3},{3,2},{4,5},{5,4},{6,7},{7,6},{8,9},{9,8},{10,11... | collective-permute-start | bytes 4718600 | tf_op jit(solution)/shard_map/ppermute | solution.py:824
  322.6 20.6 %collective-permute-start.32 = (bf16[2,256,384]{2,1,0:T(8,128)(2,1)}, bf16[2,256,384]{2,1,0:T(8,128)(2,1)S(1)}, u32[]{:S(2)}, u32[]{:S(2)}) collective-permute-start(bf16[2,256,384]{2,1,0:T(8,128)(2,1)} %get-tuple-element.152), channel_id=1, source_target_pairs={{2,0},{3,1},{6,4},{7,5},{10,8},{11,9},{14,12},{15,13},{18,16},{19,... | collective-permute-start | bytes 1179656 | tf_op jit(solution)/shard_map/ppermute | solution.py:1129
  335.8 31.8 %collective-permute-start.36 = (bf16[384,768]{1,0:T(8,128)(2,1)}, bf16[384,768]{1,0:T(8,128)(2,1)S(1)}, u32[]{:S(2)}, u32[]{:S(2)}) collective-permute-start(bf16[384,768]{1,0:T(8,128)(2,1)} %get-tuple-element.156.refs_8_), channel_id=1, source_target_pairs={{0,2},{2,0},{1,3},{3,1},{4,6},{6,4},{5,7},{7,5},{8,10},{10,8},{9,1... | collective-permute-start | bytes 1769480 | tf_op jit(solution)/shard_map/ppermute | solution.py:824
  338.4 31.4 %collective-permute-start.37 = (bf16[384,768]{1,0:T(8,128)(2,1)}, bf16[384,768]{1,0:T(8,128)(2,1)S(1)}, u32[]{:S(2)}, u32[]{:S(2)}) collective-permute-start(bf16[384,768]{1,0:T(8,128)(2,1)} %get-tuple-element.163), channel_id=1, source_target_pairs={{0,4},{4,0},{1,5},{5,1},{2,6},{6,2},{3,7},{7,3},{8,12},{12,8},{9,1... | collective-permute-start | bytes 1769480 | tf_op jit(solution)/shard_map/ppermute | solution.py:824
  343.2 217.4 %collective-permute-start.30 = (bf16[1024,768]{1,0:T(8,128)(2,1)}, bf16[1024,768]{1,0:T(8,128)(2,1)}, u32[]{:S(2)}, u32[]{:S(2)}) collective-permute-start(bf16[1024,768]{1,0:T(8,128)(2,1)} %add_convert_fusion.own_ref), channel_id=1, source_target_pairs={{0,2},{2,0},{1,3},{3,1},{4,6},{6,4},{5,7},{7,5},{8,10},{10,8},{9,1... | collective-permute-start | bytes 4718600 | tf_op jit(solution)/shard_map/ppermute | solution.py:824
  354.7 22.2 %collective-permute-start.35 = (bf16[1024,768]{1,0:T(8,128)(2,1)}, bf16[1024,768]{1,0:T(8,128)(2,1)}, u32[]{:S(2)}, u32[]{:S(2)}) collective-permute-start(bf16[1024,768]{1,0:T(8,128)(2,1)} %get-tuple-element.157.refs_2_), channel_id=1, source_target_pairs={{0,1},{1,0},{2,3},{3,2},{4,5},{5,4},{6,7},{7,6},{8,9},{9,8},{10,11... | collective-permute-start | bytes 4718600 | tf_op jit(solution)/shard_map/ppermute | solution.py:824
  366.2 26.2 %collective-permute-start.39 = (bf16[2,384,384]{2,1,0:T(8,128)(2,1)}, bf16[2,384,384]{2,1,0:T(8,128)(2,1)S(1)}, u32[]{:S(2)}, u32[]{:S(2)}) collective-permute-start(bf16[2,384,384]{2,1,0:T(8,128)(2,1)} %get-tuple-element.162.refs_14_), channel_id=1, source_target_pairs={{0,4},{4,0},{1,5},{5,1},{2,6},{6,2},{3,7},{7,3},{8,12},{12,8},{9,1... | collective-permute-start | bytes 1769480 | tf_op jit(solution)/shard_map/ppermute | solution.py:824
  367.5 31.2 %collective-permute-start.40 = (bf16[2,384,384]{2,1,0:T(8,128)(2,1)}, bf16[2,384,384]{2,1,0:T(8,128)(2,1)}, u32[]{:S(2)}, u32[]{:S(2)}) collective-permute-start(bf16[2,384,384]{2,1,0:T(8,128)(2,1)} %get-tuple-element.173), channel_id=1, source_target_pairs={{0,2},{2,0},{1,3},{3,1},{4,6},{6,4},{5,7},{7,5},{8,10},{10,8},{9,1... | collective-permute-start | bytes 1769480 | tf_op jit(solution)/shard_map/ppermute | solution.py:824
  371.3 44.7 %all-to-all-start.1 = ((bf16[4,96,1536]{2,1,0:T(8,128)(2,1)}), bf16[4,96,1536]{2,1,0:T(8,128)(2,1)S(1)}, u32[]{:S(2)}, u32[]{:S(2)}) async-start(bf16[4,96,1536]{2,1,0:T(8,128)(2,1)} %bitcast.26.refs_15_), calls=%async_computation.1 | async-start | bytes 2359296 | tf_op jit(solution)/shard_map/all_to_all | solution.py:869
  404.3 17.4 %collective-permute-start.38 = (bf16[1024,768]{1,0:T(8,128)(2,1)}, bf16[1024,768]{1,0:T(8,128)(2,1)}, u32[]{:S(2)}, u32[]{:S(2)}) collective-permute-start(bf16[1024,768]{1,0:T(8,128)(2,1)} %get-tuple-element.165.refs_2_), channel_id=1, source_target_pairs={{0,1},{1,0},{2,3},{3,2},{4,5},{5,4},{6,7},{7,6},{8,9},{9,8},{10,11... | collective-permute-start | bytes 4718600 | tf_op jit(solution)/shard_map/ppermute | solution.py:824
  411.8 47.1 %collective-permute-start.44 = (bf16[2,384,768]{2,1,0:T(8,128)(2,1)}, bf16[2,384,768]{2,1,0:T(8,128)(2,1)}, u32[]{:S(2)}, u32[]{:S(2)}) collective-permute-start(bf16[2,384,768]{2,1,0:T(8,128)(2,1)} %get-tuple-element.170.refs_13_), channel_id=1, source_target_pairs={{0,4},{4,0},{1,5},{5,1},{2,6},{6,2},{3,7},{7,3},{8,12},{12,8},{9,1... | collective-permute-start | bytes 3538952 | tf_op jit(solution)/shard_map/ppermute | solution.py:824
  412.5 46.4 %collective-permute-start.45 = (bf16[2,384,768]{2,1,0:T(8,128)(2,1)}, bf16[2,384,768]{2,1,0:T(8,128)(2,1)}, u32[]{:S(2)}, u32[]{:S(2)}) collective-permute-start(bf16[2,384,768]{2,1,0:T(8,128)(2,1)} %get-tuple-element.187), channel_id=1, source_target_pairs={{0,2},{2,0},{1,3},{3,1},{4,6},{6,4},{5,7},{7,5},{8,10},{10,8},{9,1... | collective-permute-start | bytes 3538952 | tf_op jit(solution)/shard_map/ppermute | solution.py:824
  416.0 83.6 %all-to-all-start.3 = ((bf16[4,96,768]{2,1,0:T(8,128)(2,1)}), bf16[4,96,768]{2,1,0:T(8,128)(2,1)S(1)}, u32[]{:S(2)}, u32[]{:S(2)}) async-start(bf16[4,96,768]{2,1,0:T(8,128)(2,1)} %bitcast.29.refs_0_), calls=%async_computation.3 | async-start | bytes 1179648 | tf_op jit(solution)/shard_map/all_to_all | solution.py:869
  461.7 22.4 %collective-permute-start.47 = (bf16[384,768]{1,0:T(8,128)(2,1)}, bf16[384,768]{1,0:T(8,128)(2,1)S(1)}, u32[]{:S(2)}, u32[]{:S(2)}) collective-permute-start(bf16[384,768]{1,0:T(8,128)(2,1)} %get-tuple-element.188.refs_8_), channel_id=1, source_target_pairs={{0,2},{2,0},{1,3},{3,1},{4,6},{6,4},{5,7},{7,5},{8,10},{10,8},{9,1... | collective-permute-start | bytes 1769480 | tf_op jit(solution)/shard_map/ppermute | solution.py:824
  464.3 21.2 %collective-permute-start.48 = (bf16[384,768]{1,0:T(8,128)(2,1)}, bf16[384,768]{1,0:T(8,128)(2,1)S(1)}, u32[]{:S(2)}, u32[]{:S(2)}) collective-permute-start(bf16[384,768]{1,0:T(8,128)(2,1)} %get-tuple-element.193), channel_id=1, source_target_pairs={{0,4},{4,0},{1,5},{5,1},{2,6},{6,2},{3,7},{7,3},{8,12},{12,8},{9,1... | collective-permute-start | bytes 1769480 | tf_op jit(solution)/shard_map/ppermute | solution.py:824
  483.3 27.3 %collective-permute-start.49 = (bf16[2,384,384]{2,1,0:T(8,128)(2,1)}, bf16[2,384,384]{2,1,0:T(8,128)(2,1)}, u32[]{:S(2)}, u32[]{:S(2)}) collective-permute-start(bf16[2,384,384]{2,1,0:T(8,128)(2,1)} %get-tuple-element.192.refs_5_), channel_id=1, source_target_pairs={{0,4},{4,0},{1,5},{5,1},{2,6},{6,2},{3,7},{7,3},{8,12},{12,8},{9,1... | collective-permute-start | bytes 1769480 | tf_op jit(solution)/shard_map/ppermute | solution.py:824
  484.1 26.6 %collective-permute-start.50 = (bf16[2,384,384]{2,1,0:T(8,128)(2,1)}, bf16[2,384,384]{2,1,0:T(8,128)(2,1)}, u32[]{:S(2)}, u32[]{:S(2)}) collective-permute-start(bf16[2,384,384]{2,1,0:T(8,128)(2,1)} %get-tuple-element.197), channel_id=1, source_target_pairs={{0,2},{2,0},{1,3},{3,1},{4,6},{6,4},{5,7},{7,5},{8,10},{10,8},{9,1... | collective-permute-start | bytes 1769480 | tf_op jit(solution)/shard_map/ppermute | solution.py:824
  499.6 35.3 %all-to-all-start.4 = ((bf16[4,96,1536]{2,1,0:T(8,128)(2,1)}), bf16[4,96,1536]{2,1,0:T(8,128)(2,1)S(1)}, u32[]{:S(2)}, u32[]{:S(2)}) async-start(bf16[4,96,1536]{2,1,0:T(8,128)(2,1)} %bitcast.32.refs_6_), calls=%async_computation.4 | async-start | bytes 2359296 | tf_op jit(solution)/shard_map/all_to_all | solution.py:869
  512.8 16.9 %collective-permute-start.52 = (bf16[384,384]{1,0:T(8,128)(2,1)}, bf16[384,384]{1,0:T(8,128)(2,1)S(1)}, u32[]{:S(2)}, u32[]{:S(2)}) collective-permute-start(bf16[384,384]{1,0:T(8,128)(2,1)} %get-tuple-element.198.refs_0_), channel_id=1, source_target_pairs={{0,2},{2,0},{1,3},{3,1},{4,6},{6,4},{5,7},{7,5},{8,10},{10,8},{9,1... | collective-permute-start | bytes 884744 | tf_op jit(solution)/shard_map/ppermute | solution.py:824
  514.2 16.6 %collective-permute-start.53 = (bf16[384,384]{1,0:T(8,128)(2,1)}, bf16[384,384]{1,0:T(8,128)(2,1)S(1)}, u32[]{:S(2)}, u32[]{:S(2)}) collective-permute-start(bf16[384,384]{1,0:T(8,128)(2,1)} %get-tuple-element.199), channel_id=1, source_target_pairs={{0,4},{4,0},{1,5},{5,1},{2,6},{6,2},{3,7},{7,3},{8,12},{12,8},{9,1... | collective-permute-start | bytes 884744 | tf_op jit(solution)/shard_map/ppermute | solution.py:824
  534.9 18.3 %all-to-all-start.2 = ((bf16[4,96,768]{2,1,0:T(8,128)(2,1)}), bf16[4,96,768]{2,1,0:T(8,128)(2,1)S(1)}, u32[]{:S(2)}, u32[]{:S(2)}) async-start(bf16[4,96,768]{2,1,0:T(8,128)(2,1)} %bitcast.35), calls=%async_computation.2 | async-start | bytes 1179648 | tf_op jit(solution)/shard_map/all_to_all | solution.py:869
  538.5 48.9 %collective-permute-start.51 = (bf16[1024,768]{1,0:T(8,128)(2,1)}, bf16[1024,768]{1,0:T(8,128)(2,1)}, u32[]{:S(2)}, u32[]{:S(2)}) collective-permute-start(bf16[1024,768]{1,0:T(8,128)(2,1)} %get-tuple-element.194.refs_4_.refs_0_.own_ref), channel_id=1, source_target_pairs={{0,2},{2,0},{1,3},{3,1},{4,6},{6,4},{5,7},{7,5},{8,10},{10,8},{9,1... | collective-permute-start | bytes 4718600 | tf_op jit(solution)/shard_map/ppermute | solution.py:824
  558.1 15.8 %all-to-all-start.5 = ((f32[32,1,128]{2,1,0:T(1,128)}), f32[32,1,128]{2,1,0:T(1,128)S(1)}, u32[]{:S(2)}, u32[]{:S(2)}) async-start(f32[32,1,128]{2,1,0:T(1,128)} %broadcast_in_dim.80), calls=%async_computation.5 | async-start | bytes 32768 | tf_op jit(solution)/shard_map/all_to_all | solution.py:1219
  (82 other events, 766.7 us)
Sparse Core Ops, SparseCore 0:
  126.8 93.8 all-gather.1

commit v3 on v2

--- a/solution.py
+++ b/solution.py
@@ -48,7 +48,7 @@
     return lax.dot_general(left, right, dims, precision=precision, preferred_element_type=F32)
 
 
-VMEM_LIMIT = 56 * 2**20
+VMEM_LIMIT = 24 * 2**20
 TILE = 256
 QT = 256
 
@@ -91,18 +91,29 @@
     return jnp.exp(-0.5 * offset * offset)
 
 
-def make_tables(centres, sticky_row):
+def table_inputs(centres, sticky_row):
     token_times = STICKY_RATIO + (1.0 - STICKY_RATIO) * (jnp.arange(SEG).astype(F32) + 0.5) / SEG
     places = (sticky_row.astype(F32) + 0.5) / CRES
-    old_basis = basis_table(centres, places)
-    design = basis_table(centres, jnp.concatenate([STICKY_RATIO * places, token_times]))
+    return (
+        basis_table(centres, places),
+        basis_table(centres, jnp.concatenate([STICKY_RATIO * places, token_times])),
+    )
+
+
+def make_tables(old_basis, design, after):
+    def body(old_ref, design_ref, *refs):
+        table_kernel(old_ref, design_ref, *refs[len(after) :])
+
+    vmem = pl.BlockSpec(memory_space=pltpu.VMEM)
     return pl.pallas_call(
-        table_kernel,
+        body,
+        in_specs=[vmem, vmem] + [pl.BlockSpec(memory_space=pl.ANY)] * len(after),
+        out_specs=vmem,
         out_shape=jax.ShapeDtypeStruct((BASIS, BASIS + SEG), BF16),
         scratch_shapes=[pltpu.VMEM((BASIS, BASIS), F32), pltpu.VMEM((BASIS, BASIS), F32)],
         compiler_params=pltpu.CompilerParams(vmem_limit_bytes=VMEM_LIMIT),
-        cost_estimate=cost(40),
-    )(old_basis, design)
+        cost_estimate=cost(14),
+    )(old_basis, design, *after)
 
 
 def slab_columns(slab, low, high):
@@ -238,7 +249,7 @@
         return pl.BlockSpec(shape, lambda *a: (0,) * len(shape))
 
     if not isinstance(slabs, Gathered):
-        return list(slabs), [fixed(slab.shape) for slab in slabs]
+        return [in_hbm(slab) for slab in slabs], [fixed(slab.shape) for slab in slabs]
     whole, columns, index = slabs
     specs = []
     for turn_y, turn_x in TURNS:
@@ -253,7 +264,7 @@
                 ),
             )
         )
-    return [whole] * 4, specs
+    return [in_hbm(whole)] * 4, specs
 
 
 def norm_stats(inputs):
@@ -325,6 +336,14 @@
         compiler_params=pltpu.CompilerParams(vmem_limit_bytes=VMEM_LIMIT),
         cost_estimate=cost(micros),
     )(place, *tiled, *whole, *slab_arrays, *more, *after)
+
+
+def in_hbm(operand):
+    return pltpu.with_memory_space_constraint(operand, pltpu.HBM)
+
+
+def kept(shape, dtype):
+    return pltpu.HBM(shape, dtype)
 
 
 def array(shape, dtype):
@@ -449,7 +468,8 @@
 
 
 def restore_kernel(context_ref, own_ref, got_ref, order_ref, *refs):
-    out_ref = refs[-1]
+    out_ref, zero_ref = refs[-2:]
+    zero_ref[...] = jnp.zeros_like(zero_ref)
     mine = (pl.program_id(0) // (pl.num_programs(0) // 2)) == context_ref[0]
     rows = jnp.where(mine, own_ref[...].astype(F32), got_ref[...].astype(F32)).astype(BF16)
     out_ref[...] = dot(rows, order_ref[...], NN)
@@ -469,8 +489,11 @@
             pl.BlockSpec(order.shape, lambda i: (0, 0)),
             *(pl.BlockSpec(memory_space=pl.ANY) for _ in after),
         ],
-        out_specs=pl.BlockSpec((TILE, features), lambda i: (i, 0)),
-        out_shape=array((2 * rows, features), F32),
+        out_specs=[
+            pl.BlockSpec((TILE, features), lambda i: (i, 0)),
+            pl.BlockSpec((8, 128), lambda i: (0, 0)),
+        ],
+        out_shape=[kept((2 * rows, features), F32), array((8, 128), F32)],
         compiler_params=pltpu.CompilerParams(vmem_limit_bytes=VMEM_LIMIT),
         cost_estimate=cost(4),
     )(context, own, got, order, *after)
@@ -599,14 +622,14 @@
             ],
         ),
         out_shape=[
-            array((2, rows, width), BF16),
-            array((segs, 2, heads, SEG), F32),
-            array((segs, 2, BASIS, 2 * width), BF16),
+            kept((2, rows, width), BF16),
+            kept((segs, 2, heads, SEG), F32),
+            kept((segs, 2, BASIS, 2 * width), BF16),
             array((rows, features), BF16),
         ],
         compiler_params=pltpu.CompilerParams(vmem_limit_bytes=VMEM_LIMIT),
         cost_estimate=cost(13),
-    )(place, memory_bias, qkv, starts, got, fit, near, *slab_arrays, *after)
+    )(place, memory_bias, in_hbm(qkv), starts, got, fit, near, *slab_arrays, *after)
 
 
 def attention_backward_kernel(
@@ -728,16 +751,20 @@
     grads_ref, part_ref, sums_ref, signal_ref = refs[-4:]
     segment = pl.program_id(0)
 
+    def arrived(side):
+        got = got_ref[1 - side]
+        return jnp.where(place_ref[0] == 0, got.astype(F32), 0.0).astype(BF16)
+
     @pl.when(segment == 0)
     def _():
         for side in range(2):
-            carry = last_ref[side] + dot(far_ref[:, :BASIS], got_ref[1 - side], TN)
+            carry = last_ref[side] + dot(far_ref[:, :BASIS], arrived(side), TN)
             signal_ref[side] = dot(near_ref[:, BASIS:], carry.astype(BF16), TN)
 
     @pl.when(segment == 1)
     def _():
         for side in range(2):
-            signal_ref[side] = dot(far_ref[:, BASIS:], got_ref[1 - side], TN)
+            signal_ref[side] = dot(far_ref[:, BASIS:], arrived(side), TN)
 
     sides = []
     for side in range(2):
@@ -838,14 +865,37 @@
     return lax.all_to_all(spread, "tz", 0, 0, tiled=True).reshape(-1, shard.shape[1])
 
 
-def gather_z_soon(shard):
+def join_kernel(here_ref, *refs):
+    *pieces, first_ref, second_ref, zero_ref = refs
+    rows = pieces[0].shape[0]
+    columns = first_ref.shape[1]
+    for bit, piece_ref in enumerate(pieces):
+        place = pl.ds(pl.multiple_of((here_ref[0] ^ bit) * rows, rows), rows)
+        first_ref[place, :] = piece_ref[:, :columns]
+        second_ref[place, :] = piece_ref[:, columns:]
+    zero_ref[...] = jnp.zeros_like(zero_ref)
+
+
+def gather_split(shard, widths):
     size = lax.axis_size("tz")
     here = lax.axis_index("tz")
-    rows = jnp.zeros((size,) + shard.shape, shard.dtype)
-    for bit in range(size):
-        piece = shift(shard, "tz", bit) if bit else shard
-        rows = lax.dynamic_update_index_in_dim(rows, piece, here ^ bit, 0)
-    return rows.reshape(-1, shard.shape[1])
+    pieces = [shift(shard, "tz", bit) if bit else shard for bit in range(size)]
+    if shard.shape[0] % 16:
+        rows = jnp.zeros((size,) + shard.shape, shard.dtype)
+        for bit, piece in enumerate(pieces):
+            rows = lax.dynamic_update_index_in_dim(rows, piece, here ^ bit, 0)
+        return split_columns(rows.reshape(-1, shard.shape[1]), widths, ())
+    vmem = pl.BlockSpec(memory_space=pltpu.VMEM)
+    first, second, zero = pl.pallas_call(
+        join_kernel,
+        in_specs=[pl.BlockSpec(memory_space=pltpu.SMEM)] + [vmem] * size,
+        out_specs=[vmem] * 3,
+        out_shape=[array((size * shard.shape[0], columns), BF16) for columns in widths]
+        + [array((8, 128), jnp.int32)],
+        compiler_params=pltpu.CompilerParams(vmem_limit_bytes=VMEM_LIMIT),
+        cost_estimate=cost(1),
+    )(here.reshape(1).astype(jnp.int32), *pieces)
+    return (first, second), zero[0, 0]
 
 
 def shift(array, axis, bit):
@@ -930,10 +980,7 @@
 
     table_index = jnp.where(context == 0, core, 2)
     sticky_row = lax.dynamic_index_in_dim(sticky[0], table_index, 0, keepdims=False)
-    table_own = make_tables(centres, sticky_row)
-    table_other = flip(table_own, "cc")
-    table_near = jnp.where(core == 0, table_own, table_other)
-    table_far = jnp.where(core == 0, table_other, table_own)
+    old_basis, design = table_inputs(centres, sticky_row)
 
     def attention_members(layer):
         return [(w_qkv, layer), (w_out_t, layer)]
@@ -942,23 +989,24 @@
         return [(w_up, layer), (w_down_t, layer)]
 
     attn_shard = cast(attention_members(0))
-    attn_rows = gather_z_soon(attn_shard)
-    more_rows = gather_z(cast(ffn_members(0) + attention_members(1), (attn_shard,)))
-    (qk_own, vo_own), zero = split_columns(attn_rows, (2 * width, 2 * width), (table_own,))
+    (qk_own, vo_own), zero = gather_split(attn_shard, (2 * width, 2 * width))
     qk_two, vo_two = (qk_own, flip(qk_own, "tx")), (vo_own, flip(vo_own, "cy"))
-    (up_own, down_own, qk_above, vo_above), _ = split_columns(
-        more_rows, (hidden_own, hidden_own, 2 * width, 2 * width), (qk_own,)
-    )
+    ffn_rows = gather_z(cast(ffn_members(0), (attn_shard,)))
+    (up_own, down_own), _ = split_columns(ffn_rows, (hidden_own, hidden_own), (qk_own,))
     up_two, down_two = (up_own, flip(up_own, "tx")), (down_own, flip(down_own, "cy"))
-    above_two = (qk_above, flip(qk_above, "tx")), (vo_above, flip(vo_above, "cy"))
+    above = cast(attention_members(1), (qk_own,))
     attn_slabs = [
         gather_second(qk_two, "cy") + gather_second(vo_two, "tx"),
-        gather_second(above_two[0], "cy") + gather_second(above_two[1], "tx"),
+        Gathered(gather_blocks(above), 4 * width, 0),
     ]
     ffn_slabs = [
         gather_second(up_two, "cy") + gather_second(down_two, "tx"),
         Gathered(gather_blocks(cast(ffn_members(1), (up_own,))), 2 * hidden_own, 0),
     ]
+    table_own = make_tables(old_basis, design, (qk_own,))
+    table_other = flip(table_own, "cc")
+    table_near = jnp.where(core == 0, table_own, table_other)
+    table_far = jnp.where(core == 0, table_other, table_own)
 
     x_place = x_place + zero
     late_context = context + zero
@@ -993,6 +1041,9 @@
     own_cot = lax.dynamic_slice_in_dim(cotangent, late_context * rows, rows, axis=0)
 
     row_f32 = array((rows, features), F32)
+    kept_f32 = kept((rows, features), F32)
+    kept_b16 = kept((rows, features), BF16)
+    kept_hidden = kept((2, rows, hidden_own), BF16)
     row_b16 = array((rows, features), BF16)
     side_hidden = array((2, rows, hidden_own), BF16)
     side_width = array((2, rows, width), BF16)
@@ -1003,39 +1054,37 @@
         stream, normed, qkv, fit, ahead = rows_call(
             partial(enter_kernel, layer),
             place,
-            (own_h,) if layer == 0 else (middle, part, got),
+            (in_hbm(own_h),) if layer == 0 else (in_hbm(middle), part, got),
             ((order,) if layer == 0 else ()) + (gains, in_bias),
             attn_slabs[layer],
             (table_near, table_far, starts),
-            (row_f32, row_b16, array((2, rows, 3 * width), BF16)),
+            (kept_f32, kept_b16, kept((2, rows, 3 * width), BF16)),
             (array((2, BASIS, 2 * width), F32), array((2, BASIS, 2 * width), BF16)),
             7,
             [pltpu.VMEM((2, rows, 2 * width), BF16)],
             after=(up_two[1], down_two[1]) if layer == 0 else (),
         )
-        received = lax.ppermute(ahead, "cy", ((0, 1),))
-        out_slabs = attn_slabs[layer][4:]
+        received = flip(ahead, "cy")
+        out_slabs = attn_slabs[layer][4:] if layer == 0 else attn_slabs[layer]
         attended, log_totals, memory, part = attention_forward(
             layer, place, memory_bias, qkv, starts, received, fit, table_near, out_slabs,
-            after=ffn_slabs[0][1:4] + ffn_slabs[0][5:8] + (above_two[0][1], above_two[1][1])
-            if layer == 0
-            else (),
+            after=ffn_slabs[0][1:4] + ffn_slabs[0][5:8] if layer == 0 else (),
         )
         got = flip(part, "cc")
         middle, normed_two, active, slope, part = rows_call(
             partial(ffn_forward_kernel, layer),
             place,
-            (stream, part, got),
+            (in_hbm(stream), part, got),
             (gains, up_bias),
             ffn_slabs[layer],
             (),
-            (row_f32, row_b16, side_hidden, side_hidden, row_b16),
+            (kept_f32, kept_b16, kept_hidden, kept_hidden, row_b16),
             (),
             11,
         )
         got = flip(part, "cc")
         saved.append(
-            (
+            tuple(in_hbm(member) for member in (
                 stream,
                 normed,
                 qkv,
@@ -1046,7 +1095,7 @@
                 normed_two,
                 active,
                 slope,
-            )
+            ))
         )
     final = middle + (part.astype(F32) + got.astype(F32) + gains[LAYERS - 1, 5])
     final = lax.optimization_barrier(final.astype(BF16))
@@ -1085,7 +1134,7 @@
         stream_grad, down, hidden_grad, part, sums_ffn[layer] = rows_call(
             partial(ffn_backward_kernel, layer),
             place,
-            (own_cot, slope) if top else (stream_grad, stream_above, part, got, slope),
+            (in_hbm(own_cot), slope) if top else (stream_grad, stream_above, part, got, slope),
             (order if top else gains,),
             ffn_slabs[layer],
             (),
@@ -1126,7 +1175,7 @@
         dq, dkv, last, back = attention_backward(
             memory_bias, qkv, memory, log_totals, attended, attended_grad, table_near, zero_attention
         )
-        received = lax.ppermute(back, "cy", ((1, 0),))
+        received = flip(back, "cy")
         up_keep, down_keep = weight_grads(ffn_operands, ffn_plans[1], half, (dq,))
         passed, ffn_pieces = second_hop(up_keep, up_got, down_keep, down_got, (dq,))
         grads_in, part, sums_in[layer] = memory_backward(
@@ -1169,8 +1218,8 @@
     passed, attn_pieces = second_hop(qk_keep, qk_got, vo_keep, vo_got, (final,))
     reduced[0] = (spread_pieces(attn_pieces), spread_ffn)
     reduced = [[piece.astype(F32).sum(axis=0) for piece in pair] for pair in reduced]
-    activations = restore(*outputs, order_back, place, (passed,))
-    input_grad = restore(final, flip(final, "cy"), order_back, place)
+    activations, zero_act = restore(*outputs, order_back, place, (passed,))
+    input_grad, zero_in = restore(final, flip(final, "cy"), order_back, place)
 
     vector_d = []
     vector_own = []
@@ -1212,6 +1261,8 @@
     square = sum(jnp.sum(grad * grad) for grad in matrix_grads)
     square = (
         square
+        + zero_act[0, 0]
+        + zero_in[0, 0]
         + jnp.sum(vec_d_grad * vec_d_grad) / (tok_count * ch_count)
         + jnp.sum(vec_c_grad * vec_c_grad) / tok_count
     )

time: 616 us -> 581 us (0.943)
  Pallas kernels: 312 us -> 272 us
  local copies, waits for them, and re-layouts: 41.8 us -> 60.4 us
  starting transfers between devices: 95 us -> 76.8 us
  blocking collectives: 0 us -> 12.6 us
  waiting for transfers between devices: 93.3 us -> 83.4 us
    unnamed x137 -> x217, local copies, waits for them, and re-layouts: 14.7 us -> 36.5 us
    ppermute x48 -> x46, waiting for transfers between devices: 54 us -> 73.6 us  [flip(): return lax.ppermute(array, axis, SWAP)]
    ppermute x4 -> x0, waiting for transfers between devices: 15.4 us -> none  [the longest x2 15.4 us: shards(): received = lax.ppermute(ahead, 'cy', ((0, 1),))]
    pallas_call x8, Pallas kernels: 52.6 us -> 38.2 us  [weight_grads(): pl.pallas_call(partial(weight_grads_kernel, plan), in_specs=[vmem] * len(...]
    all_to_all x0 -> x1, blocking collectives: none -> 12.6 us  [shards(): lax.all_to_all(jnp.full((tok_count * ch_count, 128), square), everywhere,...]
    ppermute x4 -> x0, starting transfers between devices: 10.5 us -> none  [the longest x2 7.71 us: shards(): received = lax.ppermute(ahead, 'cy', ((0, 1),))]
    all_to_all x4, waiting for transfers between devices: 12.3 us -> 1.88 us  [spread_pieces(): return lax.all_to_all(pieces, 'tz', 0, 0, tiled=True)]
    pallas_call x9, Pallas kernels: 114 us -> 104 us  [rows_call(): pl.pallas_call(body, grid_spec=pltpu.PrefetchScalarGridSpec(num_scalar_pr...]
  transfers between devices with their start and end apart: 65 -> 59, of which waited for: 18 -> 15; matrix products, arithmetic and copies ran while one was open for 12% -> 10% of each run, Pallas kernels for 45% -> 41%
where the time goes in v3:
time: 581 us; the launch traced here: 572 us
  Pallas kernels  272 us (47%)
  waiting for transfers between devices  83.4 us (14%)
  starting transfers between devices  76.8 us (13%)
  local copies, waits for them, and re-layouts  60.4 us (10%)
  other arithmetic  38.4 us (7%)
  between operations  25.5 us (4%)
  blocking collectives  12.6 us (2%)
    pallas_call x9, Pallas kernels, rows_call(): pl.pallas_call(body, grid_spec=pltpu.PrefetchScalarGridSpec(num_scalar_pr...  104 us
    ppermute x46, waiting for transfers between devices, flip(): return lax.ppermute(array, axis, SWAP)  73.6 us
    ppermute x46, starting transfers between devices, flip(): return lax.ppermute(array, axis, SWAP)  38.5 us
    pallas_call x8, Pallas kernels, weight_grads(): pl.pallas_call(partial(weight_grads_kernel, plan), in_specs=[vmem] * len(...  38.2 us
    unnamed x217, local copies, waits for them, and re-layouts  36.5 us
    pallas_call x2, Pallas kernels, attention_backward(): pl.pallas_call(attention_backward_kernel, grid=(2, segs), in_specs=[pl.Bl...  35.5 us
    pallas_call x2, Pallas kernels, attention_forward(): pl.pallas_call(attention_forward_kernel, grid_spec=pltpu.PrefetchScalarGr...  33.9 us
    all_to_all x4, starting transfers between devices, spread_pieces(): return lax.all_to_all(pieces, 'tz', 0, 0, tiled=True)  18.6 us
  transfers between devices with their start and end apart: 59, of which 15 were waited for; matrix products, arithmetic and copies ran while one was open for 10% of the time, Pallas kernels for 41%

profile of v3, /device:TPU:0, one launch (start us, length us, event | category | flops | bytes accessed | tf_op | source)
XLA Modules:
  0.0 572.2 jit_solution(11876950851702881833)
XLA Ops:
  9.5 3.1 collective-permute-start
  12.5 2.6 collective-permute-start.1
  16.3 5.2 all-to-all-start
  27.3 5.2 collective-permute-done.1.refs_2_
  47.2 11.8 %shard_map.393 = bf16[256,768]{1,0:T(8,128)(2,1)S(1)} custom-call(f32[256,256]{1,0:T(8,128)S(1)} %copy-done.30, f32[256,768]{1,0:T(8,128)S(1)} %copy-done.6, bf16[384,384]{1,0:T(8,128)(2,1)} %get-tuple-element.117.refs_0_.refs_4_.refs_2_.refs_5_), custom_call_target="tpu_custom_call" | custom-call | flops 15399999488 | bytes 1000000 | tf_op jit(solution)/shard_map/pallas_call | solution.py:108
  63.9 2.3 shard_map.395
  72.4 3.3 collective-permute-done.8.refs_10_.refs_2_.refs_11_.refs_6_
  80.5 12.7 %collective-permute-done.7.refs_9_.refs_1_.refs_10_.refs_5_ = bf16[384,384]{1,0:T(8,128)(2,1)S(1)} collective-permute-done((bf16[384,384]{1,0:T(8,128)(2,1)}, bf16[384,384]{1,0:T(8,128)(2,1)S(1)}, u32[]{:S(2)}, u32[]{:S(2)}) %collective-permute-start.7) | collective-permute-done | bytes 294944 | tf_op jit(solution)/shard_map/ppermute | solution.py:851
  94.6 5.1 collective-permute-done.6.refs_7_.refs_8_.refs_3_
  102.4 3.4 collective-permute-done.9.refs_11_.refs_3_.refs_12_.refs_7_
  106.5 12.1 %shard_map.396 = (f32[1024,768]{1,0:T(8,128)}, bf16[1024,768]{1,0:T(8,128)(2,1)}, bf16[2,1024,576]{2,1,0:T(8,128)(2,1)}, f32[2,256,384]{2,1,0:T(8,128)S(1)}, bf16[2,256,384]{2,1,0:T(8,128)(2,1)}) custom-call(s32[2]{0:T(128)S(1)} %pad_add_fusion.place_ref.context_ref, bf16[1024,768]{1,0:T(8,128)(2,1)} %constant_dynamic-slice_fusion.1.refs_0_, ...), custom_call_target="tpu_custom_call" | custom-call | flops 7699999744 | bytes 1000000 | tf_op jit(solution)/shard_map/pallas_call | solution.py:321
  121.9 16.5 %collective-permute-done.14.got_ref = bf16[2,256,384]{2,1,0:T(8,128)(2,1)} collective-permute-done((bf16[2,256,384]{2,1,0:T(8,128)(2,1)}, bf16[2,256,384]{2,1,0:T(8,128)(2,1)}, u32[]{:S(2)}, u32[]{:S(2)}) %collective-permute-start.14) | collective-permute-done | bytes 393248 | tf_op jit(solution)/shard_map/ppermute | solution.py:851
  140.6 16.8 %shard_map.397 = (bf16[2,1024,192]{2,1,0:T(8,128)(2,1)}, f32[2,2,3,512]{3,2,1,0:T(4,128)}, bf16[2,2,256,384]{3,2,1,0:T(8,128)(2,1)}, bf16[1024,768]{1,0:T(8,128)(2,1)}) custom-call(s32[2]{0:T(128)S(1)} %pad_add_fusion.place_ref.context_ref, f32[2]{0:T(128)S(1)} %pad_maximum_fusion.16.bias_ref, bf16[2,1024,576]{2,1,0:T(8,128)(2,1)} %get-tuple-element.122.qkv_ref, ...), custom_call_target="tpu_custom_call" | custom-call | flops 14300000256 | bytes 1000000 | tf_op jit(solution)/shard_map/pallas_call | solution.py:598
  157.9 3.2 collective-permute-done.19.refs_2_
  161.2 15.0 %shard_map.398 = (f32[1024,768]{1,0:T(8,128)}, bf16[1024,768]{1,0:T(8,128)(2,1)}, bf16[2,1024,768]{2,1,0:T(8,128)(2,1)}, bf16[2,1024,768]{2,1,0:T(8,128)(2,1)}, bf16[1024,768]{1,0:T(8,128)(2,1)}) custom-call(s32[2]{0:T(128)S(1)} %pad_add_fusion.place_ref.context_ref, f32[1024,768]{1,0:T(8,128)} %get-tuple-element.121.refs_0_.refs_1_, ...), custom_call_target="tpu_custom_call" | custom-call | flops 12099999744 | bytes 1000000 | tf_op jit(solution)/shard_map/pallas_call | solution.py:321
  176.3 3.6 collective-permute-done.20.refs_2_
  179.9 11.4 %shard_map.400 = (f32[1024,768]{1,0:T(8,128)}, bf16[1024,768]{1,0:T(8,128)(2,1)}, bf16[2,1024,576]{2,1,0:T(8,128)(2,1)}, f32[2,256,384]{2,1,0:T(8,128)S(1)}, bf16[2,256,384]{2,1,0:T(8,128)(2,1)S(1)}) custom-call(s32[2]{0:T(128)S(1)} %pad_add_fusion.place_ref.context_ref, f32[1024,768]{1,0:T(8,128)} %get-tuple-element.126.refs_0_.refs_1_, ...), custom_call_target="tpu_custom_call" | custom-call | flops 7699999744 | bytes 1000000 | tf_op jit(solution)/shard_map/pallas_call | solution.py:321
  191.8 10.7 %collective-permute-done.21.got_ref = bf16[2,256,384]{2,1,0:T(8,128)(2,1)S(1)} collective-permute-done((bf16[2,256,384]{2,1,0:T(8,128)(2,1)S(1)}, bf16[2,256,384]{2,1,0:T(8,128)(2,1)S(1)}, u32[]{:S(2)}, u32[]{:S(2)}) %collective-permute-start.21) | collective-permute-done | bytes 393248 | tf_op jit(solution)/shard_map/ppermute | solution.py:851
  202.5 17.2 %shard_map.401 = (bf16[2,1024,192]{2,1,0:T(8,128)(2,1)}, f32[2,2,3,512]{3,2,1,0:T(4,128)}, bf16[2,2,256,384]{3,2,1,0:T(8,128)(2,1)}, bf16[1024,768]{1,0:T(8,128)(2,1)S(1)}) custom-call(s32[2]{0:T(128)S(1)} %pad_add_fusion.place_ref.context_ref, f32[2]{0:T(128)S(1)} %pad_maximum_fusion.16.bias_ref, bf16[2,1024,576]{2,1,0:T(8,128)(2,1)} %get-tuple-element.129.qkv_ref, ...), custom_call_target="tpu_custom_call" | custom-call | flops 14300000256 | bytes 1000000 | tf_op jit(solution)/shard_map/pallas_call | solution.py:598
  227.1 14.6 %shard_map.403 = (f32[1024,768]{1,0:T(8,128)}, bf16[1024,768]{1,0:T(8,128)(2,1)}, bf16[2,1024,768]{2,1,0:T(8,128)(2,1)}, bf16[2,1024,768]{2,1,0:T(8,128)(2,1)}, bf16[1024,768]{1,0:T(8,128)(2,1)S(1)}) custom-call(s32[2]{0:T(128)S(1)} %pad_add_fusion.place_ref.context_ref, f32[1024,768]{1,0:T(8,128)} %get-tuple-element.128.refs_0_.refs_1_, ...), custom_call_target="tpu_custom_call" | custom-call | flops 12099999744 | bytes 1000000 | tf_op jit(solution)/shard_map/pallas_call | solution.py:321
  241.7 13.9 %shard_map.404 = (f32[1024,768]{1,0:T(8,128)S(1)}, bf16[1024,768]{1,0:T(8,128)(2,1)S(1)}, bf16[2,1024,768]{2,1,0:T(8,128)(2,1)S(1)}, bf16[1024,768]{1,0:T(8,128)(2,1)}, f32[8,768]{1,0:T(8,128)S(1)}) custom-call(s32[2]{0:T(128)S(1)} %pad_add_fusion.place_ref.context_ref, bf16[1024,768]{1,0:T(8,128)(2,1)} %constant_dynamic-slice_fusion.refs_0_, ...), custom_call_target="tpu_custom_call" | custom-call | flops 9900000256 | bytes 1000000 | tf_op jit(solution)/shard_map/pallas_call | solution.py:321
  258.1 6.8 %shard_map.405 = (bf16[2,384,768]{2,1,0:T(8,128)(2,1)}, bf16[2,384,768]{2,1,0:T(8,128)(2,1)}) custom-call(bf16[1024,768]{1,0:T(8,128)(2,1)} %get-tuple-element.139.refs_0_, bf16[1024,768]{1,0:T(8,128)(2,1)S(1)} %get-tuple-element.140.refs_1_, bf16[2,1024,768]{2,1,0:T(8,128)(2,1)S(1)} %get-tuple-element.141.refs_2_, ...), custom_call_target="tpu_custom_call" | custom-call | flops 6600000000 | bytes 1000000 | tf_op jit(solution)/shard_map/pallas_call | solution.py:834
  271.4 8.0 %shard_map.406 = (f32[1024,768]{1,0:T(8,128)S(1)}, bf16[1024,768]{1,0:T(8,128)(2,1)S(1)}, bf16[2,1024,192]{2,1,0:T(8,128)(2,1)S(1)}, f32[8,768]{1,0:T(8,128)S(1)}) custom-call(s32[2]{0:T(128)S(1)} %pad_add_fusion.place_ref.context_ref, f32[1024,768]{1,0:T(8,128)S(1)} %copy-done.53, f32[1024,768]{1,0:T(8,128)} %get-tuple-element.133.refs_1_, ...), custom_call_target="tpu_custom_call" | custom-call | flops 6600000000 | bytes 1000000 | tf_op jit(solution)/shard_map/pallas_call | solution.py:321
  279.5 18.4 %shard_map.407 = (bf16[2,1024,192]{2,1,0:T(8,128)(2,1)S(1)}, f32[2,1024,384]{2,1,0:T(8,128)S(1)}, f32[2,256,384]{2,1,0:T(8,128)S(1)}, bf16[2,256,384]{2,1,0:T(8,128)(2,1)S(1)}) custom-call(f32[2]{0:T(128)S(1)} %pad_maximum_fusion.16.bias_ref, bf16[2,1024,576]{2,1,0:T(8,128)(2,1)} %get-tuple-element.129.qkv_ref, ...), custom_call_target="tpu_custom_call" | custom-call | flops 19800000512 | bytes 1000000 | tf_op jit(solution)/shard_map/pallas_call | solution.py:708
  299.4 5.0 shard_map.408
  310.7 9.1 %shard_map.410 = (bf16[2,1024,576]{2,1,0:T(8,128)(2,1)S(1)}, bf16[1024,768]{1,0:T(8,128)(2,1)}, f32[8,576]{1,0:T(8,128)S(1)}) custom-call(s32[2]{0:T(128)S(1)} %pad_add_fusion.place_ref.context_ref, bf16[2,1024,192]{2,1,0:T(8,128)(2,1)S(1)} %get-tuple-element.149.refs_4_.refs_0_.dq_ref, f32[2,1024,384]{2,1,0:T(8,128)S(1)} %get-tuple-element.150.dkv_ref, ...), custom_call_target="tpu_custom_call" | custom-call | flops 5500000256 | bytes 1000000 | tf_op jit(solution)/shard_map/pallas_call | solution.py:787
  319.9 3.7 shard_map.414
  324.4 4.7 shard_map.411
  334.0 4.4 all-to-all-start.1
  340.4 14.9 %shard_map.412 = (f32[1024,768]{1,0:T(8,128)S(1)}, bf16[1024,768]{1,0:T(8,128)(2,1)S(1)}, bf16[2,1024,768]{2,1,0:T(8,128)(2,1)S(1)}, bf16[1024,768]{1,0:T(8,128)(2,1)}, f32[8,768]{1,0:T(8,128)S(1)}) custom-call(s32[2]{0:T(128)S(1)} %pad_add_fusion.place_ref.context_ref, f32[1024,768]{1,0:T(8,128)S(1)} %copy-done.51, ...), custom_call_target="tpu_custom_call" | custom-call | flops 9900000256 | bytes 1000000 | tf_op jit(solution)/shard_map/pallas_call | solution.py:321
  355.3 13.2 %collective-permute-done.34.got_b_ref = bf16[2,384,384]{2,1,0:T(8,128)(2,1)} collective-permute-done((bf16[2,384,384]{2,1,0:T(8,128)(2,1)}, bf16[2,384,384]{2,1,0:T(8,128)(2,1)}, u32[]{:S(2)}, u32[]{:S(2)}) %collective-permute-start.34) | collective-permute-done | bytes 589856 | tf_op jit(solution)/shard_map/ppermute | solution.py:851
  374.7 5.0 shard_map.413
  388.7 4.9 all-to-all-start.3
  396.6 8.0 %shard_map.416 = (f32[1024,768]{1,0:T(8,128)S(1)}, bf16[1024,768]{1,0:T(8,128)(2,1)S(1)}, bf16[2,1024,192]{2,1,0:T(8,128)(2,1)S(1)}, f32[8,768]{1,0:T(8,128)S(1)}) custom-call(s32[2]{0:T(128)S(1)} %pad_add_fusion.place_ref.context_ref, f32[1024,768]{1,0:T(8,128)S(1)} %copy-done.61, f32[1024,768]{1,0:T(8,128)} %get-tuple-element.126.refs_0_.refs_1_, ...), custom_call_target="tpu_custom_call" | custom-call | flops 6600000000 | bytes 1000000 | tf_op jit(solution)/shard_map/pallas_call | solution.py:321
  406.2 17.2 %shard_map.417 = (bf16[2,1024,192]{2,1,0:T(8,128)(2,1)S(1)}, f32[2,1024,384]{2,1,0:T(8,128)S(1)}, f32[2,256,384]{2,1,0:T(8,128)S(1)}, bf16[2,256,384]{2,1,0:T(8,128)(2,1)S(1)}) custom-call(f32[2]{0:T(128)S(1)} %pad_maximum_fusion.16.bias_ref, bf16[2,1024,576]{2,1,0:T(8,128)(2,1)} %get-tuple-element.122.qkv_ref, ...), custom_call_target="tpu_custom_call" | custom-call | flops 19800000512 | bytes 1000000 | tf_op jit(solution)/shard_map/pallas_call | solution.py:708
  425.0 5.0 shard_map.418
  430.0 3.2 shard_map.419
  435.1 9.1 %shard_map.420 = (bf16[2,1024,576]{2,1,0:T(8,128)(2,1)S(1)}, bf16[1024,768]{1,0:T(8,128)(2,1)}, f32[8,576]{1,0:T(8,128)S(1)}) custom-call(s32[2]{0:T(128)S(1)} %pad_add_fusion.place_ref.context_ref, bf16[2,1024,192]{2,1,0:T(8,128)(2,1)S(1)} %get-tuple-element.181.refs_4_.refs_0_.dq_ref, f32[2,1024,384]{2,1,0:T(8,128)S(1)} %get-tuple-element.182.dkv_ref, ...), custom_call_target="tpu_custom_call" | custom-call | flops 5500000256 | bytes 1000000 | tf_op jit(solution)/shard_map/pallas_call | solution.py:787
  444.3 4.5 shard_map.421
  457.5 6.2 %shard_map.422 = (bf16[1024,768]{1,0:T(8,128)(2,1)}, f32[8,768]{1,0:T(8,128)S(1)}) custom-call(s32[2]{0:T(128)S(1)} %pad_add_fusion.place_ref.context_ref, f32[1024,768]{1,0:T(8,128)S(1)} %copy-done.57, f32[1024,768]{1,0:T(8,128)} %get-tuple-element.121.refs_0_.refs_1_, bf16[1024,768]{1,0:T(8,128)(2,1)} %get-tuple-element.191.refs_2_, ...), custom_call_target="tpu_custom_call" | custom-call | flops 5500000256 | bytes 1000000 | tf_op jit(solution)/shard_map/pallas_call | solution.py:321
  465.7 5.1 all-to-all-start.4
  473.9 3.6 shard_map.423
  489.9 5.2 collective-permute-start.51
  499.9 4.2 all-to-all-start.2
  505.1 8.3 %shard_map.425 = (f32[2048,768]{1,0:T(8,128)}, f32[8,128]{1,0:T(8,128)S(1)}) custom-call(s32[2]{0:T(128)S(1)} %pad_add_fusion.place_ref.context_ref, bf16[1024,768]{1,0:T(8,128)(2,1)S(1)} %add_convert_fusion.own_ref, bf16[1024,768]{1,0:T(8,128)(2,1)} %collective-permute-done.24.got_ref, bf16[768,768]{1,0:T(8,128)(2,1)S(1)} %copy-done.4, ...), custom_call_target="tpu_custom_call" | custom-call | flops 4400000000 | bytes 1000000 | tf_op jit(solution)/shard_map/pallas_call | solution.py:482
  526.7 9.0 %shard_map.426 = (f32[2048,768]{1,0:T(8,128)}, f32[8,128]{1,0:T(8,128)S(1)}) custom-call(s32[2]{0:T(128)S(1)} %pad_add_fusion.place_ref.context_ref, bf16[1024,768]{1,0:T(8,128)(2,1)} %get-tuple-element.194.refs_4_.refs_0_.own_ref, bf16[1024,768]{1,0:T(8,128)(2,1)} %collective-permute-done.45.got_ref, bf16[768,768]{1,0:T(8,128)(2,1)S(1)} %copy-done.4), custom_call_target="tpu_custom_call" | custom-call | flops 4400000000 | bytes 1000000 | tf_op jit(solution)/shard_map/pallas_call | solution.py:482
  536.9 12.6 %all_to_all.34 = f32[32,1,128]{2,1,0:T(1,128)S(1)} all-to-all(f32[32,1,128]{2,1,0:T(1,128)S(1)} %broadcast_in_dim.30), channel_id=1, replica_groups=mesh['tz'=4,'tx'=2,'cy'=2,'cc'=2] {'tz','tx','cy','cc'}, dimensions={0} | all-to-all | bytes 32768 | tf_op jit(solution)/shard_map/all_to_all | solution.py:1270
  556.3 2.9 divide_subtract_fusion
  (431 shorter events, 155.0 us)
Async XLA Ops:
  9.5 17.8 %collective-permute-start = (bf16[96,768]{1,0:T(8,128)(2,1)S(1)}, bf16[96,768]{1,0:T(8,128)(2,1)S(1)}, u32[]{:S(2)}, u32[]{:S(2)}) collective-permute-start(bf16[96,768]{1,0:T(8,128)(2,1)S(1)} %shard_map.391.refs_0_.refs_2_), channel_id=1, source_target_pairs={{0,8},{8,0},{16,24},{24,16},{1,9},{9,1},{17,25},{25,17},{2,10},{10... | collective-permute-start | bytes 442376 | tf_op jit(solution)/shard_map/ppermute | solution.py:902
  12.5 19.9 %collective-permute-start.1 = (bf16[96,768]{1,0:T(8,128)(2,1)S(1)}, bf16[96,768]{1,0:T(8,128)(2,1)}, u32[]{:S(2)}, u32[]{:S(2)}) collective-permute-start(bf16[96,768]{1,0:T(8,128)(2,1)S(1)} %shard_map.391.refs_0_.refs_2_), channel_id=1, source_target_pairs={{0,16},{8,24},{16,0},{24,8},{1,17},{9,25},{17,1},{25,9},{2,18},{10... | collective-permute-start | bytes 442376 | tf_op jit(solution)/shard_map/ppermute | solution.py:902
  15.1 17.3 %collective-permute-start.2 = (bf16[96,768]{1,0:T(8,128)(2,1)S(1)}, bf16[96,768]{1,0:T(8,128)(2,1)}, u32[]{:S(2)}, u32[]{:S(2)}) collective-permute-start(bf16[96,768]{1,0:T(8,128)(2,1)S(1)} %shard_map.391.refs_0_.refs_2_), channel_id=1, source_target_pairs={{0,24},{8,16},{16,8},{24,0},{1,25},{9,17},{17,9},{25,1},{2,26},{10... | collective-permute-start | bytes 442376 | tf_op jit(solution)/shard_map/ppermute | solution.py:902
  16.3 47.7 %all-to-all-start = ((bf16[4,96,1536]{2,1,0:T(8,128)(2,1)}), bf16[4,96,1536]{2,1,0:T(8,128)(2,1)}, u32[]{:S(2)}, u32[]{:S(2)}) async-start(bf16[4,96,1536]{2,1,0:T(8,128)(2,1)} %broadcast_in_dim.29), calls=%async_computation | async-start | bytes 2359296 | tf_op jit(solution)/shard_map/all_to_all | solution.py:865
  21.5 154.8 %all-gather.3.cloned.1.call-start = ((), (), s32[]{:S(2)}) async-start(), calls=%async_computation.6 | async-start | bytes 2506752 | tf_op jit(solution)/shard_map/all_gather | solution.py:858
  23.4 42.8 %collective-permute-start.11 = (bf16[2,256,384]{2,1,0:T(8,128)(2,1)}, bf16[2,256,384]{2,1,0:T(8,128)(2,1)}, u32[]{:S(2)}, u32[]{:S(2)}) collective-permute-start(bf16[2,256,384]{2,1,0:T(8,128)(2,1)} %copy.129), channel_id=1, source_target_pairs={{0,2},{2,0},{1,3},{3,1},{4,6},{6,4},{5,7},{7,5},{8,10},{10,8},{9,1... | collective-permute-start | bytes 1179656 | tf_op jit(solution)/shard_map/ppermute | solution.py:851
  24.9 16.3 %collective-permute-start.3 = (f32[2,6,192]{2,0,1:T(2,128)}, f32[2,6,192]{2,0,1:T(2,128)}, u32[]{:S(2)}, u32[]{:S(2)}) collective-permute-start(f32[2,6,192]{2,0,1:T(2,128)} %param.45), channel_id=1, source_target_pairs={{0,2},{2,0},{1,3},{3,1},{4,6},{6,4},{5,7},{7,5},{8,10},{10,8},{9,1... | collective-permute-start | bytes 27656 | tf_op jit(solution)/shard_map/ppermute | solution.py:851
  35.2 189.1 %all-gather.5.cloned.1.call-start = ((), (), s32[]{:S(2)}) async-start(), calls=%async_computation.7 | async-start | bytes 5013504 | tf_op jit(solution)/shard_map/all_gather | solution.py:858
  42.0 24.8 %collective-permute-start.4 = (bf16[384,384]{1,0:T(8,128)(2,1)}, bf16[384,384]{1,0:T(8,128)(2,1)}, u32[]{:S(2)}, u32[]{:S(2)}) collective-permute-start(bf16[384,384]{1,0:T(8,128)(2,1)} %get-tuple-element.117.refs_0_.refs_4_.refs_2_.refs_5_), channel_id=1, source_target_pairs={{0,4},{4,0},{1,5},{5,1},{2,6},{6,2},{3,7},{7,3},{8,12},{12,8},{9,1... | collective-permute-start | bytes 884744 | tf_op jit(solution)/shard_map/ppermute | solution.py:851
  43.6 32.6 %collective-permute-start.5 = (bf16[384,384]{1,0:T(8,128)(2,1)}, bf16[384,384]{1,0:T(8,128)(2,1)}, u32[]{:S(2)}, u32[]{:S(2)}) collective-permute-start(bf16[384,384]{1,0:T(8,128)(2,1)} %get-tuple-element.117.refs_0_.refs_4_.refs_2_.refs_5_), channel_id=1, source_target_pairs={{0,2},{2,0},{1,3},{3,1},{4,6},{6,4},{5,7},{7,5},{8,10},{10,8},{9,1... | collective-permute-start | bytes 884744 | tf_op jit(solution)/shard_map/ppermute | solution.py:851
  59.1 17.6 %collective-permute-start.10 = (bf16[256,768]{1,0:T(8,128)(2,1)S(1)}, bf16[256,768]{1,0:T(8,128)(2,1)}, u32[]{:S(2)}, u32[]{:S(2)}) collective-permute-start(bf16[256,768]{1,0:T(8,128)(2,1)S(1)} %shard_map.393), channel_id=1, source_target_pairs={{0,1},{1,0},{2,3},{3,2},{4,5},{5,4},{6,7},{7,6},{8,9},{9,8},{10,11... | collective-permute-start | bytes 1179656 | tf_op jit(solution)/shard_map/ppermute | solution.py:851
  66.3 33.4 %collective-permute-start.12 = (bf16[384,768]{1,0:T(8,128)(2,1)}, bf16[384,768]{1,0:T(8,128)(2,1)}, u32[]{:S(2)}, u32[]{:S(2)}) collective-permute-start(bf16[384,768]{1,0:T(8,128)(2,1)} %get-tuple-element.119.refs_5_.refs_2_.refs_6_), channel_id=1, source_target_pairs={{0,4},{4,0},{1,5},{5,1},{2,6},{6,2},{3,7},{7,3},{8,12},{12,8},{9,1... | collective-permute-start | bytes 1769480 | tf_op jit(solution)/shard_map/ppermute | solution.py:851
  66.8 33.6 %collective-permute-start.13 = (bf16[384,768]{1,0:T(8,128)(2,1)}, bf16[384,768]{1,0:T(8,128)(2,1)}, u32[]{:S(2)}, u32[]{:S(2)}) collective-permute-start(bf16[384,768]{1,0:T(8,128)(2,1)} %get-tuple-element.120.refs_9_.refs_10_), channel_id=1, source_target_pairs={{0,2},{2,0},{1,3},{3,1},{4,6},{6,4},{5,7},{7,5},{8,10},{10,8},{9,1... | collective-permute-start | bytes 1769480 | tf_op jit(solution)/shard_map/ppermute | solution.py:851
  75.7 17.5 %collective-permute-start.7 = (bf16[384,384]{1,0:T(8,128)(2,1)}, bf16[384,384]{1,0:T(8,128)(2,1)S(1)}, u32[]{:S(2)}, u32[]{:S(2)}) collective-permute-start(bf16[384,384]{1,0:T(8,128)(2,1)} %get-tuple-element.118.refs_8_.refs_0_.refs_9_.refs_4_), channel_id=1, source_target_pairs={{0,4},{4,0},{1,5},{5,1},{2,6},{6,2},{3,7},{7,3},{8,12},{12,8},{9,1... | collective-permute-start | bytes 884744 | tf_op jit(solution)/shard_map/ppermute | solution.py:851
  76.2 23.5 %collective-permute-start.6 = (bf16[384,384]{1,0:T(8,128)(2,1)}, bf16[384,384]{1,0:T(8,128)(2,1)S(1)}, u32[]{:S(2)}, u32[]{:S(2)}) collective-permute-start(bf16[384,384]{1,0:T(8,128)(2,1)} %collective-permute-done.4.refs_5_.refs_6_.refs_1_), channel_id=1, source_target_pairs={{0,2},{2,0},{1,3},{3,1},{4,6},{6,4},{5,7},{7,5},{8,10},{10,8},{9,1... | collective-permute-start | bytes 884744 | tf_op jit(solution)/shard_map/ppermute | solution.py:851
  76.7 29.1 %collective-permute-start.9 = (bf16[384,384]{1,0:T(8,128)(2,1)}, bf16[384,384]{1,0:T(8,128)(2,1)S(1)}, u32[]{:S(2)}, u32[]{:S(2)}) collective-permute-start(bf16[384,384]{1,0:T(8,128)(2,1)} %collective-permute-done.8.refs_10_.refs_2_.refs_11_.refs_6_), channel_id=1, source_target_pairs={{0,4},{4,0},{1,5},{5,1},{2,6},{6,2},{3,7},{7,3},{8,12},{12,8},{9,1... | collective-permute-start | bytes 884744 | tf_op jit(solution)/shard_map/ppermute | solution.py:851
  93.2 28.8 %collective-permute-start.15 = (bf16[384,768]{1,0:T(8,128)(2,1)}, bf16[384,768]{1,0:T(8,128)(2,1)}, u32[]{:S(2)}, u32[]{:S(2)}) collective-permute-start(bf16[384,768]{1,0:T(8,128)(2,1)} %get-tuple-element.119.refs_5_.refs_2_.refs_6_), channel_id=1, source_target_pairs={{0,2},{2,0},{1,3},{3,1},{4,6},{6,4},{5,7},{7,5},{8,10},{10,8},{9,1... | collective-permute-start | bytes 1769480 | tf_op jit(solution)/shard_map/ppermute | solution.py:851
  99.7 22.2 %collective-permute-start.17 = (bf16[384,768]{1,0:T(8,128)(2,1)}, bf16[384,768]{1,0:T(8,128)(2,1)}, u32[]{:S(2)}, u32[]{:S(2)}) collective-permute-start(bf16[384,768]{1,0:T(8,128)(2,1)} %get-tuple-element.120.refs_9_.refs_10_), channel_id=1, source_target_pairs={{0,4},{4,0},{1,5},{5,1},{2,6},{6,2},{3,7},{7,3},{8,12},{12,8},{9,1... | collective-permute-start | bytes 1769480 | tf_op jit(solution)/shard_map/ppermute | solution.py:851
  99.7 38.8 %collective-permute-start.16 = (bf16[384,768]{1,0:T(8,128)(2,1)}, bf16[384,768]{1,0:T(8,128)(2,1)}, u32[]{:S(2)}, u32[]{:S(2)}) collective-permute-start(bf16[384,768]{1,0:T(8,128)(2,1)} %collective-permute-done.12.refs_15_.refs_4_.refs_6_.refs_7_), channel_id=1, source_target_pairs={{0,2},{2,0},{1,3},{3,1},{4,6},{6,4},{5,7},{7,5},{8,10},{10,8},{9,1... | collective-permute-start | bytes 1769480 | tf_op jit(solution)/shard_map/ppermute | solution.py:851
  100.4 38.0 %collective-permute-start.18 = (bf16[384,768]{1,0:T(8,128)(2,1)}, bf16[384,768]{1,0:T(8,128)(2,1)}, u32[]{:S(2)}, u32[]{:S(2)}) collective-permute-start(bf16[384,768]{1,0:T(8,128)(2,1)} %collective-permute-done.13.refs_16_.refs_8_.refs_11_.refs_12_), channel_id=1, source_target_pairs={{0,4},{4,0},{1,5},{5,1},{2,6},{6,2},{3,7},{7,3},{8,12},{12,8},{9,1... | collective-permute-start | bytes 1769480 | tf_op jit(solution)/shard_map/ppermute | solution.py:851
  119.6 18.9 %collective-permute-start.14 = (bf16[2,256,384]{2,1,0:T(8,128)(2,1)}, bf16[2,256,384]{2,1,0:T(8,128)(2,1)}, u32[]{:S(2)}, u32[]{:S(2)}) collective-permute-start(bf16[2,256,384]{2,1,0:T(8,128)(2,1)} %get-tuple-element.123), channel_id=1, source_target_pairs={{0,2},{2,0},{1,3},{3,1},{4,6},{6,4},{5,7},{7,5},{8,10},{10,8},{9,1... | collective-permute-start | bytes 1179656 | tf_op jit(solution)/shard_map/ppermute | solution.py:851
  264.9 39.5 %collective-permute-start.27 = (bf16[2,384,768]{2,1,0:T(8,128)(2,1)}, bf16[2,384,768]{2,1,0:T(8,128)(2,1)}, u32[]{:S(2)}, u32[]{:S(2)}) collective-permute-start(bf16[2,384,768]{2,1,0:T(8,128)(2,1)} %get-tuple-element.143.refs_9_), channel_id=1, source_target_pairs={{0,4},{4,0},{1,5},{5,1},{2,6},{6,2},{3,7},{7,3},{8,12},{12,8},{9,1... | collective-permute-start | bytes 3538952 | tf_op jit(solution)/shard_map/ppermute | solution.py:851
  265.4 39.0 %collective-permute-start.28 = (bf16[2,384,768]{2,1,0:T(8,128)(2,1)}, bf16[2,384,768]{2,1,0:T(8,128)(2,1)S(1)}, u32[]{:S(2)}, u32[]{:S(2)}) collective-permute-start(bf16[2,384,768]{2,1,0:T(8,128)(2,1)} %get-tuple-element.155), channel_id=1, source_target_pairs={{0,2},{2,0},{1,3},{3,1},{4,6},{6,4},{5,7},{7,5},{8,10},{10,8},{9,1... | collective-permute-start | bytes 3538952 | tf_op jit(solution)/shard_map/ppermute | solution.py:851
  269.4 39.0 %collective-permute-start.23 = (bf16[1024,768]{1,0:T(8,128)(2,1)S(1)}, bf16[1024,768]{1,0:T(8,128)(2,1)S(1)}, u32[]{:S(2)}, u32[]{:S(2)}) collective-permute-start(bf16[1024,768]{1,0:T(8,128)(2,1)S(1)} %get-tuple-element.134), channel_id=1, source_target_pairs={{0,1},{1,0},{2,3},{3,2},{4,5},{5,4},{6,7},{7,6},{8,9},{9,8},{10,11... | collective-permute-start | bytes 4718600 | tf_op jit(solution)/shard_map/ppermute | solution.py:851
  306.3 23.3 %collective-permute-start.30 = (bf16[384,768]{1,0:T(8,128)(2,1)S(1)}, bf16[384,768]{1,0:T(8,128)(2,1)S(1)}, u32[]{:S(2)}, u32[]{:S(2)}) collective-permute-start(bf16[384,768]{1,0:T(8,128)(2,1)S(1)} %get-tuple-element.156.refs_4_), channel_id=1, source_target_pairs={{0,2},{2,0},{1,3},{3,1},{4,6},{6,4},{5,7},{7,5},{8,10},{10,8},{9,1... | collective-permute-start | bytes 1769480 | tf_op jit(solution)/shard_map/ppermute | solution.py:851
  306.9 25.8 %collective-permute-start.31 = (bf16[384,768]{1,0:T(8,128)(2,1)S(1)}, bf16[384,768]{1,0:T(8,128)(2,1)S(1)}, u32[]{:S(2)}, u32[]{:S(2)}) collective-permute-start(bf16[384,768]{1,0:T(8,128)(2,1)S(1)} %get-tuple-element.163), channel_id=1, source_target_pairs={{0,4},{4,0},{1,5},{5,1},{2,6},{6,2},{3,7},{7,3},{8,12},{12,8},{9,1... | collective-permute-start | bytes 1769480 | tf_op jit(solution)/shard_map/ppermute | solution.py:851
  309.1 194.9 %collective-permute-start.24 = (bf16[1024,768]{1,0:T(8,128)(2,1)S(1)}, bf16[1024,768]{1,0:T(8,128)(2,1)}, u32[]{:S(2)}, u32[]{:S(2)}) collective-permute-start(bf16[1024,768]{1,0:T(8,128)(2,1)S(1)} %add_convert_fusion.own_ref), channel_id=1, source_target_pairs={{0,2},{2,0},{1,3},{3,1},{4,6},{6,4},{5,7},{7,5},{8,10},{10,8},{9,1... | collective-permute-start | bytes 4718600 | tf_op jit(solution)/shard_map/ppermute | solution.py:851
  319.8 18.7 %collective-permute-start.29 = (bf16[1024,768]{1,0:T(8,128)(2,1)}, bf16[1024,768]{1,0:T(8,128)(2,1)}, u32[]{:S(2)}, u32[]{:S(2)}) collective-permute-start(bf16[1024,768]{1,0:T(8,128)(2,1)} %get-tuple-element.157.refs_2_), channel_id=1, source_target_pairs={{0,1},{1,0},{2,3},{3,2},{4,5},{5,4},{6,7},{7,6},{8,9},{9,8},{10,11... | collective-permute-start | bytes 4718600 | tf_op jit(solution)/shard_map/ppermute | solution.py:851
  329.1 26.2 %collective-permute-start.33 = (bf16[2,384,384]{2,1,0:T(8,128)(2,1)}, bf16[2,384,384]{2,1,0:T(8,128)(2,1)}, u32[]{:S(2)}, u32[]{:S(2)}) collective-permute-start(bf16[2,384,384]{2,1,0:T(8,128)(2,1)} %get-tuple-element.162.refs_14_), channel_id=1, source_target_pairs={{0,4},{4,0},{1,5},{5,1},{2,6},{6,2},{3,7},{7,3},{8,12},{12,8},{9,1... | collective-permute-start | bytes 1769480 | tf_op jit(solution)/shard_map/ppermute | solution.py:851
  329.6 38.9 %collective-permute-start.34 = (bf16[2,384,384]{2,1,0:T(8,128)(2,1)}, bf16[2,384,384]{2,1,0:T(8,128)(2,1)}, u32[]{:S(2)}, u32[]{:S(2)}) collective-permute-start(bf16[2,384,384]{2,1,0:T(8,128)(2,1)} %get-tuple-element.173), channel_id=1, source_target_pairs={{0,2},{2,0},{1,3},{3,1},{4,6},{6,4},{5,7},{7,5},{8,10},{10,8},{9,1... | collective-permute-start | bytes 1769480 | tf_op jit(solution)/shard_map/ppermute | solution.py:851
  334.0 54.7 %all-to-all-start.1 = ((bf16[4,96,1536]{2,1,0:T(8,128)(2,1)}), bf16[4,96,1536]{2,1,0:T(8,128)(2,1)S(1)}, u32[]{:S(2)}, u32[]{:S(2)}) async-start(bf16[4,96,1536]{2,1,0:T(8,128)(2,1)} %bitcast.23.refs_15_), calls=%async_computation.1 | async-start | bytes 2359296 | tf_op jit(solution)/shard_map/all_to_all | solution.py:919
  370.5 14.3 %collective-permute-start.35 = (bf16[384,384]{1,0:T(8,128)(2,1)}, bf16[384,384]{1,0:T(8,128)(2,1)}, u32[]{:S(2)}, u32[]{:S(2)}) collective-permute-start(bf16[384,384]{1,0:T(8,128)(2,1)} %get-tuple-element.174.refs_14_), channel_id=1, source_target_pairs={{0,2},{2,0},{1,3},{3,1},{4,6},{6,4},{5,7},{7,5},{8,10},{10,8},{9,1... | collective-permute-start | bytes 884744 | tf_op jit(solution)/shard_map/ppermute | solution.py:851
  372.0 14.6 %collective-permute-start.36 = (bf16[384,384]{1,0:T(8,128)(2,1)}, bf16[384,384]{1,0:T(8,128)(2,1)}, u32[]{:S(2)}, u32[]{:S(2)}) collective-permute-start(bf16[384,384]{1,0:T(8,128)(2,1)} %get-tuple-element.180), channel_id=1, source_target_pairs={{0,4},{4,0},{1,5},{5,1},{2,6},{6,2},{3,7},{7,3},{8,12},{12,8},{9,1... | collective-permute-start | bytes 884744 | tf_op jit(solution)/shard_map/ppermute | solution.py:851
  373.5 21.1 %collective-permute-start.32 = (bf16[1024,768]{1,0:T(8,128)(2,1)}, bf16[1024,768]{1,0:T(8,128)(2,1)}, u32[]{:S(2)}, u32[]{:S(2)}) collective-permute-start(bf16[1024,768]{1,0:T(8,128)(2,1)} %get-tuple-element.165.refs_2_), channel_id=1, source_target_pairs={{0,1},{1,0},{2,3},{3,2},{4,5},{5,4},{6,7},{7,6},{8,9},{9,8},{10,11... | collective-permute-start | bytes 4718600 | tf_op jit(solution)/shard_map/ppermute | solution.py:851
  380.8 49.2 %collective-permute-start.38 = (bf16[2,384,768]{2,1,0:T(8,128)(2,1)}, bf16[2,384,768]{2,1,0:T(8,128)(2,1)}, u32[]{:S(2)}, u32[]{:S(2)}) collective-permute-start(bf16[2,384,768]{2,1,0:T(8,128)(2,1)} %get-tuple-element.170.refs_13_), channel_id=1, source_target_pairs={{0,4},{4,0},{1,5},{5,1},{2,6},{6,2},{3,7},{7,3},{8,12},{12,8},{9,1... | collective-permute-start | bytes 3538952 | tf_op jit(solution)/shard_map/ppermute | solution.py:851
  384.8 45.2 %collective-permute-start.39 = (bf16[2,384,768]{2,1,0:T(8,128)(2,1)}, bf16[2,384,768]{2,1,0:T(8,128)(2,1)}, u32[]{:S(2)}, u32[]{:S(2)}) collective-permute-start(bf16[2,384,768]{2,1,0:T(8,128)(2,1)} %copy-done.44), channel_id=1, source_target_pairs={{0,2},{2,0},{1,3},{3,1},{4,6},{6,4},{5,7},{7,5},{8,10},{10,8},{9,1... | collective-permute-start | bytes 3538952 | tf_op jit(solution)/shard_map/ppermute | solution.py:851
  388.7 77.0 %all-to-all-start.3 = ((bf16[4,96,768]{2,1,0:T(8,128)(2,1)}), bf16[4,96,768]{2,1,0:T(8,128)(2,1)}, u32[]{:S(2)}, u32[]{:S(2)}) async-start(bf16[4,96,768]{2,1,0:T(8,128)(2,1)} %bitcast.26.refs_0_), calls=%async_computation.3 | async-start | bytes 1179648 | tf_op jit(solution)/shard_map/all_to_all | solution.py:919
  433.3 18.1 %collective-permute-start.41 = (bf16[384,768]{1,0:T(8,128)(2,1)}, bf16[384,768]{1,0:T(8,128)(2,1)}, u32[]{:S(2)}, u32[]{:S(2)}) collective-permute-start(bf16[384,768]{1,0:T(8,128)(2,1)} %get-tuple-element.188.refs_8_), channel_id=1, source_target_pairs={{0,2},{2,0},{1,3},{3,1},{4,6},{6,4},{5,7},{7,5},{8,10},{10,8},{9,1... | collective-permute-start | bytes 1769480 | tf_op jit(solution)/shard_map/ppermute | solution.py:851
  433.8 20.6 %collective-permute-start.42 = (bf16[384,768]{1,0:T(8,128)(2,1)}, bf16[384,768]{1,0:T(8,128)(2,1)}, u32[]{:S(2)}, u32[]{:S(2)}) collective-permute-start(bf16[384,768]{1,0:T(8,128)(2,1)} %get-tuple-element.193), channel_id=1, source_target_pairs={{0,4},{4,0},{1,5},{5,1},{2,6},{6,2},{3,7},{7,3},{8,12},{12,8},{9,1... | collective-permute-start | bytes 1769480 | tf_op jit(solution)/shard_map/ppermute | solution.py:851
  450.6 26.8 %collective-permute-start.43 = (bf16[2,384,384]{2,1,0:T(8,128)(2,1)}, bf16[2,384,384]{2,1,0:T(8,128)(2,1)}, u32[]{:S(2)}, u32[]{:S(2)}) collective-permute-start(bf16[2,384,384]{2,1,0:T(8,128)(2,1)} %copy-done.46), channel_id=1, source_target_pairs={{0,4},{4,0},{1,5},{5,1},{2,6},{6,2},{3,7},{7,3},{8,12},{12,8},{9,1... | collective-permute-start | bytes 1769480 | tf_op jit(solution)/shard_map/ppermute | solution.py:851
  451.4 26.1 %collective-permute-start.44 = (bf16[2,384,384]{2,1,0:T(8,128)(2,1)}, bf16[2,384,384]{2,1,0:T(8,128)(2,1)}, u32[]{:S(2)}, u32[]{:S(2)}) collective-permute-start(bf16[2,384,384]{2,1,0:T(8,128)(2,1)} %copy-done.45), channel_id=1, source_target_pairs={{0,2},{2,0},{1,3},{3,1},{4,6},{6,4},{5,7},{7,5},{8,10},{10,8},{9,1... | collective-permute-start | bytes 1769480 | tf_op jit(solution)/shard_map/ppermute | solution.py:851
  465.0 15.2 %collective-permute-start.48 = (f32[11520]{0:T(1024)S(1)}, f32[11520]{0:T(1024)S(1)}, u32[]{:S(2)}, u32[]{:S(2)}) collective-permute-start(f32[11520]{0:T(1024)S(1)} %pad_maximum_fusion.8), channel_id=1, source_target_pairs={{0,2},{2,0},{1,3},{3,1},{4,6},{6,4},{5,7},{7,5},{8,10},{10,8},{9,1... | collective-permute-start | bytes 138248 | tf_op jit(solution)/shard_map/ppermute | solution.py:851
  465.7 34.2 %all-to-all-start.4 = ((bf16[4,96,1536]{2,1,0:T(8,128)(2,1)}), bf16[4,96,1536]{2,1,0:T(8,128)(2,1)}, u32[]{:S(2)}, u32[]{:S(2)}) async-start(bf16[4,96,1536]{2,1,0:T(8,128)(2,1)} %bitcast.29.refs_6_), calls=%async_computation.4 | async-start | bytes 2359296 | tf_op jit(solution)/shard_map/all_to_all | solution.py:919
  478.7 16.4 %collective-permute-start.46 = (bf16[384,384]{1,0:T(8,128)(2,1)S(1)}, bf16[384,384]{1,0:T(8,128)(2,1)S(1)}, u32[]{:S(2)}, u32[]{:S(2)}) collective-permute-start(bf16[384,384]{1,0:T(8,128)(2,1)S(1)} %get-tuple-element.198.refs_0_), channel_id=1, source_target_pairs={{0,2},{2,0},{1,3},{3,1},{4,6},{6,4},{5,7},{7,5},{8,10},{10,8},{9,1... | collective-permute-start | bytes 884744 | tf_op jit(solution)/shard_map/ppermute | solution.py:851
  482.9 13.3 %collective-permute-start.47 = (bf16[384,384]{1,0:T(8,128)(2,1)S(1)}, bf16[384,384]{1,0:T(8,128)(2,1)S(1)}, u32[]{:S(2)}, u32[]{:S(2)}) collective-permute-start(bf16[384,384]{1,0:T(8,128)(2,1)S(1)} %get-tuple-element.201), channel_id=1, source_target_pairs={{0,4},{4,0},{1,5},{5,1},{2,6},{6,2},{3,7},{7,3},{8,12},{12,8},{9,1... | collective-permute-start | bytes 884744 | tf_op jit(solution)/shard_map/ppermute | solution.py:851
  487.8 38.9 %collective-permute-start.45 = (bf16[1024,768]{1,0:T(8,128)(2,1)}, bf16[1024,768]{1,0:T(8,128)(2,1)}, u32[]{:S(2)}, u32[]{:S(2)}) collective-permute-start(bf16[1024,768]{1,0:T(8,128)(2,1)} %get-tuple-element.194.refs_4_.refs_0_.own_ref), channel_id=1, source_target_pairs={{0,2},{2,0},{1,3},{3,1},{4,6},{6,4},{5,7},{7,5},{8,10},{10,8},{9,1... | collective-permute-start | bytes 4718600 | tf_op jit(solution)/shard_map/ppermute | solution.py:851
  489.9 24.0 %collective-permute-start.51 = (f32[11520]{0:T(1024)S(1)}, f32[11520]{0:T(1024)S(1)}, u32[]{:S(2)}, u32[]{:S(2)}) collective-permute-start(f32[11520]{0:T(1024)S(1)} %add.337), channel_id=1, source_target_pairs={{0,16},{8,24},{16,0},{24,8},{1,17},{9,25},{17,1},{25,9},{2,18},{10... | collective-permute-start | bytes 138248 | tf_op jit(solution)/shard_map/ppermute | solution.py:902
  499.9 19.1 %all-to-all-start.2 = ((bf16[4,96,768]{2,1,0:T(8,128)(2,1)}), bf16[4,96,768]{2,1,0:T(8,128)(2,1)}, u32[]{:S(2)}, u32[]{:S(2)}) async-start(bf16[4,96,768]{2,1,0:T(8,128)(2,1)} %bitcast.129), calls=%async_computation.2 | async-start | bytes 1179648 | tf_op jit(solution)/shard_map/all_to_all | solution.py:919
  (116 other events, 1048.6 us)
Sparse Core Ops, SparseCore 0:
  35.3 78.8 all-gather.2
  122.0 78.6 all-gather.4

commit v4 on v3

--- a/solution.py
+++ b/solution.py
@@ -48,8 +48,8 @@
     return lax.dot_general(left, right, dims, precision=precision, preferred_element_type=F32)
 
 
-VMEM_LIMIT = 24 * 2**20
-TILE = 256
+VMEM_LIMIT = 40 * 2**20
+TILE = 512
 QT = 256
 
 
@@ -122,16 +122,20 @@
 
 def project(left, slabs, low, high):
     own, by_x, by_y, by_both = (slab_columns(slab, low, high) for slab in slabs)
-    half = own.shape[0]
-    first, second = left[:, :half], left[:, half:]
     return (
-        dot(first, own, NN) + dot(second, by_x, NN),
-        dot(first, by_y, NN) + dot(second, by_both, NN),
+        dot(left, jnp.concatenate([own, by_x], axis=0), NN),
+        dot(left, jnp.concatenate([by_y, by_both], axis=0), NN),
     )
 
 
 def unproject(sides, slabs, low, high):
     own, by_x, by_y, by_both = (slab_columns(slab, low, high) for slab in slabs)
+    if (high - low) % 128 == 0:
+        both = jnp.concatenate(sides, axis=1)
+        weights = jnp.concatenate(
+            [jnp.concatenate([own, by_y], axis=1), jnp.concatenate([by_x, by_both], axis=1)], axis=0
+        )
+        return dot(both, weights, NT)
     return jnp.concatenate(
         [
             dot(sides[0], own, NT) + dot(sides[1], by_y, NT),
@@ -467,6 +471,20 @@
     add_rows(sums_ref, [(0, gain_rows), (1, normed_grad)])
 
 
+def zero_kernel(_, zero_ref):
+    zero_ref[...] = jnp.zeros_like(zero_ref)
+
+
+def zero_after(operand):
+    return pl.pallas_call(
+        zero_kernel,
+        in_specs=[pl.BlockSpec(memory_space=pl.ANY)],
+        out_specs=pl.BlockSpec(memory_space=pltpu.VMEM),
+        out_shape=array((8, 128), F32),
+        cost_estimate=cost(1),
+    )(operand)[0, 0]
+
+
 def restore_kernel(context_ref, own_ref, got_ref, order_ref, *refs):
     out_ref, zero_ref = refs[-2:]
     zero_ref[...] = jnp.zeros_like(zero_ref)
@@ -545,27 +563,22 @@
         for head in range(heads):
             lanes_q, lanes_k, lanes_v = (head_lanes(kind, head, heads) for kind in range(3))
             query = qkv_ref[0, rows, lanes_q] * HEAD_DIM ** (-0.5)
-            scores = []
-            values = []
-            for part in range(tile + 1):
-                keys = slice(part * QT, (part + 1) * QT)
-                score = dot(qkv_ref[0, keys, lanes_k], query, NT)
-                if part == tile:
-                    score = jnp.where(causal(score.shape), score, MASKED)
-                scores.append(score)
-                values.append(qkv_ref[0, keys, lanes_v])
+            keys = (tile + 1) * QT
             memory_key = rows_ref[side, segment, :, head_lanes(0, head, heads)]
-            scores.append(dot(memory_key, query, NT) + memory_bias)
-            values.append(rows_ref[side, segment, :, head_lanes(1, head, heads)])
-            top = scores[0].max(axis=0, keepdims=True)
-            for score in scores[1:]:
-                top = jnp.maximum(top, score.max(axis=0, keepdims=True))
-            total = jnp.zeros_like(top)
-            result = jnp.zeros((HEAD_DIM, QT), F32)
-            for score, value in zip(scores, values):
-                weight = jnp.exp(score - top)
-                total = total + weight.sum(axis=0, keepdims=True)
-                result = result + dot(value, weight.astype(BF16), TN)
+            memory_value = rows_ref[side, segment, :, head_lanes(1, head, heads)]
+            all_keys = jnp.concatenate([qkv_ref[0, :keys, lanes_k], memory_key], axis=0)
+            all_values = jnp.concatenate([qkv_ref[0, :keys, lanes_v], memory_value], axis=0)
+            score = dot(all_keys, query, NT)
+            parts = [score[:keys - QT]] if tile else []
+            parts.append(jnp.where(causal((QT, QT)), score[keys - QT : keys], MASKED))
+            parts.append(score[keys:] + memory_bias)
+            top = parts[0].max(axis=0, keepdims=True)
+            for part in parts[1:]:
+                top = jnp.maximum(top, part.max(axis=0, keepdims=True))
+            weights = [jnp.exp(part - top) for part in parts]
+            total = sum(weight.sum(axis=0, keepdims=True) for weight in weights)
+            weights = jnp.concatenate([weight.astype(BF16) for weight in weights], axis=0)
+            result = dot(all_values, weights, TN)
             stacked.append(result / total)
             lse_ref[0, 0, head : head + 1, rows] = top + jnp.log(total)
         out_ref[0, rows, :] = jnp.concatenate(stacked, axis=0).T.astype(BF16)
@@ -657,35 +670,48 @@
         grad = grad_ref[0, :, lanes]
         dots = product[lanes, :].sum(axis=0, keepdims=True)
         log_total = lse_ref[0, 0, head : head + 1, :]
-        head_grads = [jnp.zeros((HEAD_DIM, QT), F32) for _ in range(tiles)]
+        all_keys = []
+        score_grads = []
         for part in range(tiles + 1):
+            start = part * QT if part < tiles else 0
             if part < tiles:
-                keys = slice(part * QT, (part + 1) * QT)
+                keys = slice(start, start + QT)
                 key, value = qkv_ref[0, keys, lanes_k], qkv_ref[0, keys, lanes_v]
             else:
                 key = memory_ref[0, 0, :, head_lanes(0, head, heads)]
                 value = memory_ref[0, 0, :, head_lanes(1, head, heads)]
-            key_grad = jnp.zeros((QT, HEAD_DIM), F32)
-            value_grad = jnp.zeros((QT, HEAD_DIM), F32)
-            for tile in range(part if part < tiles else 0, tiles):
-                rows = slice(tile * QT, (tile + 1) * QT)
-                score = dot(key, query[rows], NT)
-                if part == tile:
-                    score = jnp.where(causal(score.shape), score, MASKED)
-                if part == tiles:
-                    score = score + memory_bias
-                weight = jnp.exp(score - log_total[:, rows])
-                weight_grad = dot(value, grad[rows], NT)
-                score_grad = (weight * (weight_grad - dots[:, rows])).astype(BF16)
-                value_grad = value_grad + dot(weight.astype(BF16), grad[rows], NN)
-                key_grad = key_grad + dot(score_grad, query[rows], NN)
-                head_grads[tile] = head_grads[tile] + dot(key, score_grad, TN)
+            score = dot(key, query[start:], NT)
+            if part < tiles:
+                score = jnp.where(causal(score.shape), score, MASKED)
+            else:
+                score = score + memory_bias
+            weight = jnp.exp(score - log_total[:, start:])
+            weight_grad = dot(value, grad[start:], NT)
+            score_grad = (weight * (weight_grad - dots[:, start:])).astype(BF16)
+            value_grad = dot(weight.astype(BF16), grad[start:], NN)
+            key_grad = dot(score_grad, query[start:], NN)
+            all_keys.append(key)
+            score_grads.append(score_grad)
             if part < tiles:
                 dkv_ref[0, keys, head_lanes(0, head, heads)] = key_grad
                 dkv_ref[0, keys, head_lanes(1, head, heads)] = value_grad
             else:
                 last_ref[0, :, head_lanes(0, head, heads)] = key_grad
                 last_ref[0, :, head_lanes(1, head, heads)] = value_grad
+        head_grads = []
+        for tile in range(tiles):
+            members = [part for part in range(tiles + 1) if part <= tile or part == tiles]
+            columns = [tile * QT - (part * QT if part < tiles else 0) for part in members]
+            head_grads.append(
+                dot(
+                    jnp.concatenate([all_keys[part] for part in members], axis=0),
+                    jnp.concatenate(
+                        [score_grads[p][:, low : low + QT] for p, low in zip(members, columns)],
+                        axis=0,
+                    ),
+                    TN,
+                )
+            )
         query_grads.append(jnp.concatenate(head_grads, axis=1) * scale)
     dq_ref[0] = jnp.concatenate(query_grads, axis=0).T.astype(BF16)
 
@@ -1219,7 +1245,8 @@
     reduced[0] = (spread_pieces(attn_pieces), spread_ffn)
     reduced = [[piece.astype(F32).sum(axis=0) for piece in pair] for pair in reduced]
     activations, zero_act = restore(*outputs, order_back, place, (passed,))
-    input_grad, zero_in = restore(final, flip(final, "cy"), order_back, place)
+    final_got = flip(final, "cy")
+    input_grad, _ = restore(final, final_got, order_back, place)
 
     vector_d = []
     vector_own = []
@@ -1262,7 +1289,7 @@
     square = (
         square
         + zero_act[0, 0]
-        + zero_in[0, 0]
+        + zero_after(final_got)
         + jnp.sum(vec_d_grad * vec_d_grad) / (tok_count * ch_count)
         + jnp.sum(vec_c_grad * vec_c_grad) / tok_count
     )

time: 581 us -> 567 us (0.976)
  Pallas kernels: 272 us -> 259 us
  blocking collectives: 12.6 us -> 0 us
    all_to_all x1 -> x0, blocking collectives: 12.6 us -> none  [shards(): lax.all_to_all(jnp.full((tok_count * ch_count, 128), square), everywhere,...]
    pallas_call x9, Pallas kernels: 104 us -> 96.8 us  [rows_call(): pl.pallas_call(body, grid_spec=pltpu.PrefetchScalarGridSpec(num_scalar_pr...]
    pallas_call x2, Pallas kernels: 35.5 us -> 28.9 us  [attention_backward(): pl.pallas_call(attention_backward_kernel, grid=(2, segs), in_specs=[pl.Bl...]
    unnamed x217 -> x221, local copies, waits for them, and re-layouts: 36.5 us -> 37.2 us
  transfers between devices with their start and end apart: 59 -> 60, of which waited for: 15 -> 15; matrix products, arithmetic and copies ran while one was open for 10% -> 11% of each run, Pallas kernels for 41% -> 42%
where the time goes in v4:
time: 567 us; the launch traced here: 558 us
  Pallas kernels  259 us (46%)
  waiting for transfers between devices  88.1 us (16%)
  starting transfers between devices  80.1 us (14%)
  local copies, waits for them, and re-layouts  62.4 us (11%)
  other arithmetic  40.7 us (7%)
  between operations  25.6 us (5%)
    pallas_call x9, Pallas kernels, rows_call(): pl.pallas_call(body, grid_spec=pltpu.PrefetchScalarGridSpec(num_scalar_pr...  96.8 us
    ppermute x46, waiting for transfers between devices, flip(): return lax.ppermute(array, axis, SWAP)  76.2 us
    pallas_call x8, Pallas kernels, weight_grads(): pl.pallas_call(partial(weight_grads_kernel, plan), in_specs=[vmem] * len(...  38.4 us
    pallas_call x2, Pallas kernels, attention_forward(): pl.pallas_call(attention_forward_kernel, grid_spec=pltpu.PrefetchScalarGr...  38 us
    ppermute x46, starting transfers between devices, flip(): return lax.ppermute(array, axis, SWAP)  37.5 us
    unnamed x221, local copies, waits for them, and re-layouts  37.2 us
    pallas_call x2, Pallas kernels, attention_backward(): pl.pallas_call(attention_backward_kernel, grid=(2, segs), in_specs=[pl.Bl...  28.9 us
    all_to_all x4, starting transfers between devices, spread_pieces(): return lax.all_to_all(pieces, 'tz', 0, 0, tiled=True)  19.1 us
  transfers between devices with their start and end apart: 60, of which 15 were waited for; matrix products, arithmetic and copies ran while one was open for 11% of the time, Pallas kernels for 42%

profile of v4, /device:TPU:0, one launch (start us, length us, event | category | flops | bytes accessed | tf_op | source)
XLA Modules:
  0.0 558.3 jit_solution(15891886344822979922)
XLA Ops:
  9.5 3.1 collective-permute-start
  12.5 2.6 collective-permute-start.1
  16.3 5.2 all-to-all-start
  27.3 5.2 collective-permute-done.1.refs_2_
  47.2 11.8 %shard_map.393 = bf16[256,768]{1,0:T(8,128)(2,1)S(1)} custom-call(f32[256,256]{1,0:T(8,128)S(1)} %copy-done.30, f32[256,768]{1,0:T(8,128)S(1)} %copy-done.6, bf16[384,384]{1,0:T(8,128)(2,1)} %get-tuple-element.116.refs_0_.refs_4_.refs_2_.refs_5_), custom_call_target="tpu_custom_call" | custom-call | flops 15399999488 | bytes 1000000 | tf_op jit(solution)/shard_map/pallas_call | solution.py:108
  72.4 3.3 collective-permute-done.8.refs_10_.refs_2_.refs_11_.refs_6_
  80.5 12.7 %collective-permute-done.7.refs_9_.refs_1_.refs_10_.refs_5_ = bf16[384,384]{1,0:T(8,128)(2,1)S(1)} collective-permute-done((bf16[384,384]{1,0:T(8,128)(2,1)}, bf16[384,384]{1,0:T(8,128)(2,1)S(1)}, u32[]{:S(2)}, u32[]{:S(2)}) %collective-permute-start.7) | collective-permute-done | bytes 294944 | tf_op jit(solution)/shard_map/ppermute | solution.py:877
  94.6 5.1 collective-permute-done.6.refs_7_.refs_8_.refs_3_
  102.4 3.4 collective-permute-done.9.refs_11_.refs_3_.refs_12_.refs_7_
  106.5 11.5 %shard_map.396 = (f32[1024,768]{1,0:T(8,128)}, bf16[1024,768]{1,0:T(8,128)(2,1)}, bf16[2,1024,576]{2,1,0:T(8,128)(2,1)}, f32[2,256,384]{2,1,0:T(8,128)S(1)}, bf16[2,256,384]{2,1,0:T(8,128)(2,1)}) custom-call(s32[2]{0:T(128)S(1)} %pad_add_fusion.place_ref.context_ref, bf16[1024,768]{1,0:T(8,128)(2,1)} %constant_dynamic-slice_fusion.1.refs_0_, ...), custom_call_target="tpu_custom_call" | custom-call | flops 7699999744 | bytes 1000000 | tf_op jit(solution)/shard_map/pallas_call | solution.py:325
  121.3 17.2 %collective-permute-done.14.got_ref = bf16[2,256,384]{2,1,0:T(8,128)(2,1)} collective-permute-done((bf16[2,256,384]{2,1,0:T(8,128)(2,1)}, bf16[2,256,384]{2,1,0:T(8,128)(2,1)}, u32[]{:S(2)}, u32[]{:S(2)}) %collective-permute-start.14) | collective-permute-done | bytes 393248 | tf_op jit(solution)/shard_map/ppermute | solution.py:877
  140.6 18.8 %shard_map.397 = (bf16[2,1024,192]{2,1,0:T(8,128)(2,1)}, f32[2,2,3,512]{3,2,1,0:T(4,128)}, bf16[2,2,256,384]{3,2,1,0:T(8,128)(2,1)}, bf16[1024,768]{1,0:T(8,128)(2,1)}) custom-call(s32[2]{0:T(128)S(1)} %pad_add_fusion.place_ref.context_ref, f32[2]{0:T(128)S(1)} %pad_maximum_fusion.16.bias_ref, bf16[2,1024,576]{2,1,0:T(8,128)(2,1)} %get-tuple-element.121.qkv_ref, ...), custom_call_target="tpu_custom_call" | custom-call | flops 14300000256 | bytes 1000000 | tf_op jit(solution)/shard_map/pallas_call | solution.py:611
  160.0 3.2 collective-permute-done.19.refs_2_
  163.3 13.6 %shard_map.398 = (f32[1024,768]{1,0:T(8,128)}, bf16[1024,768]{1,0:T(8,128)(2,1)}, bf16[2,1024,768]{2,1,0:T(8,128)(2,1)}, bf16[2,1024,768]{2,1,0:T(8,128)(2,1)}, bf16[1024,768]{1,0:T(8,128)(2,1)}) custom-call(s32[2]{0:T(128)S(1)} %pad_add_fusion.place_ref.context_ref, f32[1024,768]{1,0:T(8,128)} %get-tuple-element.120.refs_0_.refs_1_, ...), custom_call_target="tpu_custom_call" | custom-call | flops 12099999744 | bytes 1000000 | tf_op jit(solution)/shard_map/pallas_call | solution.py:325
  177.0 3.6 collective-permute-done.20.refs_2_
  180.7 10.9 %shard_map.400 = (f32[1024,768]{1,0:T(8,128)}, bf16[1024,768]{1,0:T(8,128)(2,1)}, bf16[2,1024,576]{2,1,0:T(8,128)(2,1)}, f32[2,256,384]{2,1,0:T(8,128)S(1)}, bf16[2,256,384]{2,1,0:T(8,128)(2,1)S(1)}) custom-call(s32[2]{0:T(128)S(1)} %pad_add_fusion.place_ref.context_ref, f32[1024,768]{1,0:T(8,128)} %get-tuple-element.125.refs_0_.refs_1_, ...), custom_call_target="tpu_custom_call" | custom-call | flops 7699999744 | bytes 1000000 | tf_op jit(solution)/shard_map/pallas_call | solution.py:325
  192.0 10.6 %collective-permute-done.21.got_ref = bf16[2,256,384]{2,1,0:T(8,128)(2,1)S(1)} collective-permute-done((bf16[2,256,384]{2,1,0:T(8,128)(2,1)S(1)}, bf16[2,256,384]{2,1,0:T(8,128)(2,1)S(1)}, u32[]{:S(2)}, u32[]{:S(2)}) %collective-permute-start.21) | collective-permute-done | bytes 393248 | tf_op jit(solution)/shard_map/ppermute | solution.py:877
  202.7 19.2 %shard_map.401 = (bf16[2,1024,192]{2,1,0:T(8,128)(2,1)}, f32[2,2,3,512]{3,2,1,0:T(4,128)}, bf16[2,2,256,384]{3,2,1,0:T(8,128)(2,1)}, bf16[1024,768]{1,0:T(8,128)(2,1)S(1)}) custom-call(s32[2]{0:T(128)S(1)} %pad_add_fusion.place_ref.context_ref, f32[2]{0:T(128)S(1)} %pad_maximum_fusion.16.bias_ref, bf16[2,1024,576]{2,1,0:T(8,128)(2,1)} %get-tuple-element.128.qkv_ref, ...), custom_call_target="tpu_custom_call" | custom-call | flops 14300000256 | bytes 1000000 | tf_op jit(solution)/shard_map/pallas_call | solution.py:611
  229.3 12.8 %shard_map.403 = (f32[1024,768]{1,0:T(8,128)}, bf16[1024,768]{1,0:T(8,128)(2,1)}, bf16[2,1024,768]{2,1,0:T(8,128)(2,1)}, bf16[2,1024,768]{2,1,0:T(8,128)(2,1)}, bf16[1024,768]{1,0:T(8,128)(2,1)S(1)}) custom-call(s32[2]{0:T(128)S(1)} %pad_add_fusion.place_ref.context_ref, f32[1024,768]{1,0:T(8,128)} %get-tuple-element.127.refs_0_.refs_1_, ...), custom_call_target="tpu_custom_call" | custom-call | flops 12099999744 | bytes 1000000 | tf_op jit(solution)/shard_map/pallas_call | solution.py:325
  242.1 13.1 %shard_map.404 = (f32[1024,768]{1,0:T(8,128)S(1)}, bf16[1024,768]{1,0:T(8,128)(2,1)S(1)}, bf16[2,1024,768]{2,1,0:T(8,128)(2,1)S(1)}, bf16[1024,768]{1,0:T(8,128)(2,1)}, f32[8,768]{1,0:T(8,128)S(1)}) custom-call(s32[2]{0:T(128)S(1)} %pad_add_fusion.place_ref.context_ref, bf16[1024,768]{1,0:T(8,128)(2,1)} %constant_dynamic-slice_fusion.refs_0_, ...), custom_call_target="tpu_custom_call" | custom-call | flops 9900000256 | bytes 1000000 | tf_op jit(solution)/shard_map/pallas_call | solution.py:325
  257.8 6.8 %shard_map.405 = (bf16[2,384,768]{2,1,0:T(8,128)(2,1)}, bf16[2,384,768]{2,1,0:T(8,128)(2,1)}) custom-call(bf16[1024,768]{1,0:T(8,128)(2,1)} %get-tuple-element.138.refs_0_, bf16[1024,768]{1,0:T(8,128)(2,1)S(1)} %get-tuple-element.139.refs_1_, bf16[2,1024,768]{2,1,0:T(8,128)(2,1)S(1)} %get-tuple-element.140.refs_2_, ...), custom_call_target="tpu_custom_call" | custom-call | flops 6600000000 | bytes 1000000 | tf_op jit(solution)/shard_map/pallas_call | solution.py:860
  271.1 7.3 %shard_map.406 = (f32[1024,768]{1,0:T(8,128)S(1)}, bf16[1024,768]{1,0:T(8,128)(2,1)S(1)}, bf16[2,1024,192]{2,1,0:T(8,128)(2,1)S(1)}, f32[8,768]{1,0:T(8,128)S(1)}) custom-call(s32[2]{0:T(128)S(1)} %pad_add_fusion.place_ref.context_ref, f32[1024,768]{1,0:T(8,128)S(1)} %copy-done.52, f32[1024,768]{1,0:T(8,128)} %get-tuple-element.132.refs_1_, ...), custom_call_target="tpu_custom_call" | custom-call | flops 6600000000 | bytes 1000000 | tf_op jit(solution)/shard_map/pallas_call | solution.py:325
  278.5 15.2 %shard_map.407 = (bf16[2,1024,192]{2,1,0:T(8,128)(2,1)S(1)}, f32[2,1024,384]{2,1,0:T(8,128)S(1)}, f32[2,256,384]{2,1,0:T(8,128)S(1)}, bf16[2,256,384]{2,1,0:T(8,128)(2,1)S(1)}) custom-call(f32[2]{0:T(128)S(1)} %pad_maximum_fusion.16.bias_ref, bf16[2,1024,576]{2,1,0:T(8,128)(2,1)} %get-tuple-element.128.qkv_ref, ...), custom_call_target="tpu_custom_call" | custom-call | flops 19800000512 | bytes 1000000 | tf_op jit(solution)/shard_map/pallas_call | solution.py:734
  295.3 5.0 shard_map.408
  304.2 3.0 add_convert_fusion.own_ref
  308.8 8.4 %shard_map.410 = (bf16[2,1024,576]{2,1,0:T(8,128)(2,1)S(1)}, bf16[1024,768]{1,0:T(8,128)(2,1)}, f32[8,576]{1,0:T(8,128)S(1)}) custom-call(s32[2]{0:T(128)S(1)} %pad_add_fusion.place_ref.context_ref, bf16[2,1024,192]{2,1,0:T(8,128)(2,1)S(1)} %get-tuple-element.148.refs_4_.refs_0_.dq_ref, f32[2,1024,384]{2,1,0:T(8,128)S(1)} %get-tuple-element.149.dkv_ref, ...), custom_call_target="tpu_custom_call" | custom-call | flops 5500000256 | bytes 1000000 | tf_op jit(solution)/shard_map/pallas_call | solution.py:813
  317.2 3.7 shard_map.414
  320.9 4.9 shard_map.411
  329.7 4.9 all-to-all-start.1
  334.6 14.3 %shard_map.412 = (f32[1024,768]{1,0:T(8,128)S(1)}, bf16[1024,768]{1,0:T(8,128)(2,1)S(1)}, bf16[2,1024,768]{2,1,0:T(8,128)(2,1)S(1)}, bf16[1024,768]{1,0:T(8,128)(2,1)}, f32[8,768]{1,0:T(8,128)S(1)}) custom-call(s32[2]{0:T(128)S(1)} %pad_add_fusion.place_ref.context_ref, f32[1024,768]{1,0:T(8,128)} %copy-done.50, ...), custom_call_target="tpu_custom_call" | custom-call | flops 9900000256 | bytes 1000000 | tf_op jit(solution)/shard_map/pallas_call | solution.py:325
  349.0 15.3 %collective-permute-done.34.got_b_ref = bf16[2,384,384]{2,1,0:T(8,128)(2,1)} collective-permute-done((bf16[2,384,384]{2,1,0:T(8,128)(2,1)}, bf16[2,384,384]{2,1,0:T(8,128)(2,1)}, u32[]{:S(2)}, u32[]{:S(2)}) %collective-permute-start.34) | collective-permute-done | bytes 589856 | tf_op jit(solution)/shard_map/ppermute | solution.py:877
  370.5 5.0 shard_map.413
  384.5 5.0 all-to-all-start.3
  392.4 7.3 %shard_map.416 = (f32[1024,768]{1,0:T(8,128)S(1)}, bf16[1024,768]{1,0:T(8,128)(2,1)S(1)}, bf16[2,1024,192]{2,1,0:T(8,128)(2,1)S(1)}, f32[8,768]{1,0:T(8,128)S(1)}) custom-call(s32[2]{0:T(128)S(1)} %pad_add_fusion.place_ref.context_ref, f32[1024,768]{1,0:T(8,128)S(1)} %copy-done.60, f32[1024,768]{1,0:T(8,128)} %get-tuple-element.125.refs_0_.refs_1_, ...), custom_call_target="tpu_custom_call" | custom-call | flops 6600000000 | bytes 1000000 | tf_op jit(solution)/shard_map/pallas_call | solution.py:325
  404.8 13.7 %shard_map.417 = (bf16[2,1024,192]{2,1,0:T(8,128)(2,1)S(1)}, f32[2,1024,384]{2,1,0:T(8,128)S(1)}, f32[2,256,384]{2,1,0:T(8,128)S(1)}, bf16[2,256,384]{2,1,0:T(8,128)(2,1)S(1)}) custom-call(f32[2]{0:T(128)S(1)} %pad_maximum_fusion.16.bias_ref, bf16[2,1024,576]{2,1,0:T(8,128)(2,1)} %get-tuple-element.121.qkv_ref, ...), custom_call_target="tpu_custom_call" | custom-call | flops 19800000512 | bytes 1000000 | tf_op jit(solution)/shard_map/pallas_call | solution.py:734
  420.1 5.0 shard_map.418
  425.1 3.2 shard_map.419
  430.2 8.6 %shard_map.420 = (bf16[2,1024,576]{2,1,0:T(8,128)(2,1)S(1)}, bf16[1024,768]{1,0:T(8,128)(2,1)}, f32[8,576]{1,0:T(8,128)S(1)}) custom-call(s32[2]{0:T(128)S(1)} %pad_add_fusion.place_ref.context_ref, bf16[2,1024,192]{2,1,0:T(8,128)(2,1)S(1)} %get-tuple-element.180.refs_4_.refs_0_.dq_ref, f32[2,1024,384]{2,1,0:T(8,128)S(1)} %get-tuple-element.181.dkv_ref, ...), custom_call_target="tpu_custom_call" | custom-call | flops 5500000256 | bytes 1000000 | tf_op jit(solution)/shard_map/pallas_call | solution.py:813
  439.0 4.4 shard_map.421
  452.2 5.9 %shard_map.422 = (bf16[1024,768]{1,0:T(8,128)(2,1)}, f32[8,768]{1,0:T(8,128)S(1)}) custom-call(s32[2]{0:T(128)S(1)} %pad_add_fusion.place_ref.context_ref, f32[1024,768]{1,0:T(8,128)S(1)} %copy-done.56, f32[1024,768]{1,0:T(8,128)} %get-tuple-element.120.refs_0_.refs_1_, bf16[1024,768]{1,0:T(8,128)(2,1)} %get-tuple-element.190.refs_2_, ...), custom_call_target="tpu_custom_call" | custom-call | flops 5500000256 | bytes 1000000 | tf_op jit(solution)/shard_map/pallas_call | solution.py:325
  460.0 5.1 all-to-all-start.4
  468.3 3.6 shard_map.423
  484.3 5.2 collective-permute-start.51
  494.3 4.1 all-to-all-start.2
  499.4 6.4 %shard_map.425 = (f32[2048,768]{1,0:T(8,128)}, f32[8,128]{1,0:T(8,128)S(1)}) custom-call(s32[2]{0:T(128)S(1)} %pad_add_fusion.place_ref.context_ref, bf16[1024,768]{1,0:T(8,128)(2,1)S(1)} %add_convert_fusion.own_ref, bf16[1024,768]{1,0:T(8,128)(2,1)} %collective-permute-done.24.got_ref, bf16[768,768]{1,0:T(8,128)(2,1)S(1)} %copy-done.4, ...), custom_call_target="tpu_custom_call" | custom-call | flops 4400000000 | bytes 1000000 | tf_op jit(solution)/shard_map/pallas_call | solution.py:500
  524.1 4.0 all-to-all-start.5
  528.1 7.5 %shard_map.426 = (f32[2048,768]{1,0:T(8,128)}, f32[8,128]{1,0:T(8,128)}) custom-call(s32[2]{0:T(128)S(1)} %pad_add_fusion.place_ref.context_ref, bf16[1024,768]{1,0:T(8,128)(2,1)} %get-tuple-element.193.refs_4_.refs_0_.own_ref, bf16[1024,768]{1,0:T(8,128)(2,1)} %collective-permute-done.45.got_ref._, bf16[768,768]{1,0:T(8,128)(2,1)S(1)} %copy-done.4), custom_call_target="tpu_custom_call" | custom-call | flops 4400000000 | bytes 1000000 | tf_op jit(solution)/shard_map/pallas_call | solution.py:500
  542.4 2.9 divide_subtract_fusion
  (437 shorter events, 160.1 us)
Async XLA Ops:
  9.5 17.8 %collective-permute-start = (bf16[96,768]{1,0:T(8,128)(2,1)S(1)}, bf16[96,768]{1,0:T(8,128)(2,1)S(1)}, u32[]{:S(2)}, u32[]{:S(2)}) collective-permute-start(bf16[96,768]{1,0:T(8,128)(2,1)S(1)} %shard_map.391.refs_0_.refs_2_), channel_id=1, source_target_pairs={{0,8},{8,0},{16,24},{24,16},{1,9},{9,1},{17,25},{25,17},{2,10},{10... | collective-permute-start | bytes 442376 | tf_op jit(solution)/shard_map/ppermute | solution.py:928
  12.5 19.9 %collective-permute-start.1 = (bf16[96,768]{1,0:T(8,128)(2,1)S(1)}, bf16[96,768]{1,0:T(8,128)(2,1)}, u32[]{:S(2)}, u32[]{:S(2)}) collective-permute-start(bf16[96,768]{1,0:T(8,128)(2,1)S(1)} %shard_map.391.refs_0_.refs_2_), channel_id=1, source_target_pairs={{0,16},{8,24},{16,0},{24,8},{1,17},{9,25},{17,1},{25,9},{2,18},{10... | collective-permute-start | bytes 442376 | tf_op jit(solution)/shard_map/ppermute | solution.py:928
  15.1 17.3 %collective-permute-start.2 = (bf16[96,768]{1,0:T(8,128)(2,1)S(1)}, bf16[96,768]{1,0:T(8,128)(2,1)}, u32[]{:S(2)}, u32[]{:S(2)}) collective-permute-start(bf16[96,768]{1,0:T(8,128)(2,1)S(1)} %shard_map.391.refs_0_.refs_2_), channel_id=1, source_target_pairs={{0,24},{8,16},{16,8},{24,0},{1,25},{9,17},{17,9},{25,1},{2,26},{10... | collective-permute-start | bytes 442376 | tf_op jit(solution)/shard_map/ppermute | solution.py:928
  16.3 47.7 %all-to-all-start = ((bf16[4,96,1536]{2,1,0:T(8,128)(2,1)}), bf16[4,96,1536]{2,1,0:T(8,128)(2,1)}, u32[]{:S(2)}, u32[]{:S(2)}) async-start(bf16[4,96,1536]{2,1,0:T(8,128)(2,1)} %broadcast_in_dim.29), calls=%async_computation | async-start | bytes 2359296 | tf_op jit(solution)/shard_map/all_to_all | solution.py:891
  21.5 155.5 %all-gather.3.cloned.1.call-start = ((), (), s32[]{:S(2)}) async-start(), calls=%async_computation.6 | async-start | bytes 2506752 | tf_op jit(solution)/shard_map/all_gather | solution.py:884
  23.4 42.9 %collective-permute-start.11 = (bf16[2,256,384]{2,1,0:T(8,128)(2,1)}, bf16[2,256,384]{2,1,0:T(8,128)(2,1)}, u32[]{:S(2)}, u32[]{:S(2)}) collective-permute-start(bf16[2,256,384]{2,1,0:T(8,128)(2,1)} %copy.129), channel_id=1, source_target_pairs={{0,2},{2,0},{1,3},{3,1},{4,6},{6,4},{5,7},{7,5},{8,10},{10,8},{9,1... | collective-permute-start | bytes 1179656 | tf_op jit(solution)/shard_map/ppermute | solution.py:877
  24.9 16.3 %collective-permute-start.3 = (f32[2,6,192]{2,0,1:T(2,128)}, f32[2,6,192]{2,0,1:T(2,128)}, u32[]{:S(2)}, u32[]{:S(2)}) collective-permute-start(f32[2,6,192]{2,0,1:T(2,128)} %param.45), channel_id=1, source_target_pairs={{0,2},{2,0},{1,3},{3,1},{4,6},{6,4},{5,7},{7,5},{8,10},{10,8},{9,1... | collective-permute-start | bytes 27656 | tf_op jit(solution)/shard_map/ppermute | solution.py:877
  35.2 191.3 %all-gather.5.cloned.1.call-start = ((), (), s32[]{:S(2)}) async-start(), calls=%async_computation.7 | async-start | bytes 5013504 | tf_op jit(solution)/shard_map/all_gather | solution.py:884
  42.1 24.8 %collective-permute-start.4 = (bf16[384,384]{1,0:T(8,128)(2,1)}, bf16[384,384]{1,0:T(8,128)(2,1)}, u32[]{:S(2)}, u32[]{:S(2)}) collective-permute-start(bf16[384,384]{1,0:T(8,128)(2,1)} %get-tuple-element.116.refs_0_.refs_4_.refs_2_.refs_5_), channel_id=1, source_target_pairs={{0,4},{4,0},{1,5},{5,1},{2,6},{6,2},{3,7},{7,3},{8,12},{12,8},{9,1... | collective-permute-start | bytes 884744 | tf_op jit(solution)/shard_map/ppermute | solution.py:877
  43.6 32.6 %collective-permute-start.5 = (bf16[384,384]{1,0:T(8,128)(2,1)}, bf16[384,384]{1,0:T(8,128)(2,1)}, u32[]{:S(2)}, u32[]{:S(2)}) collective-permute-start(bf16[384,384]{1,0:T(8,128)(2,1)} %get-tuple-element.116.refs_0_.refs_4_.refs_2_.refs_5_), channel_id=1, source_target_pairs={{0,2},{2,0},{1,3},{3,1},{4,6},{6,4},{5,7},{7,5},{8,10},{10,8},{9,1... | collective-permute-start | bytes 884744 | tf_op jit(solution)/shard_map/ppermute | solution.py:877
  59.1 17.6 %collective-permute-start.10 = (bf16[256,768]{1,0:T(8,128)(2,1)S(1)}, bf16[256,768]{1,0:T(8,128)(2,1)}, u32[]{:S(2)}, u32[]{:S(2)}) collective-permute-start(bf16[256,768]{1,0:T(8,128)(2,1)S(1)} %shard_map.393), channel_id=1, source_target_pairs={{0,1},{1,0},{2,3},{3,2},{4,5},{5,4},{6,7},{7,6},{8,9},{9,8},{10,11... | collective-permute-start | bytes 1179656 | tf_op jit(solution)/shard_map/ppermute | solution.py:877
  66.3 33.4 %collective-permute-start.12 = (bf16[384,768]{1,0:T(8,128)(2,1)}, bf16[384,768]{1,0:T(8,128)(2,1)}, u32[]{:S(2)}, u32[]{:S(2)}) collective-permute-start(bf16[384,768]{1,0:T(8,128)(2,1)} %get-tuple-element.118.refs_5_.refs_2_.refs_6_), channel_id=1, source_target_pairs={{0,4},{4,0},{1,5},{5,1},{2,6},{6,2},{3,7},{7,3},{8,12},{12,8},{9,1... | collective-permute-start | bytes 1769480 | tf_op jit(solution)/shard_map/ppermute | solution.py:877
  66.8 33.6 %collective-permute-start.13 = (bf16[384,768]{1,0:T(8,128)(2,1)}, bf16[384,768]{1,0:T(8,128)(2,1)}, u32[]{:S(2)}, u32[]{:S(2)}) collective-permute-start(bf16[384,768]{1,0:T(8,128)(2,1)} %get-tuple-element.119.refs_9_.refs_10_), channel_id=1, source_target_pairs={{0,2},{2,0},{1,3},{3,1},{4,6},{6,4},{5,7},{7,5},{8,10},{10,8},{9,1... | collective-permute-start | bytes 1769480 | tf_op jit(solution)/shard_map/ppermute | solution.py:877
  75.7 17.5 %collective-permute-start.7 = (bf16[384,384]{1,0:T(8,128)(2,1)}, bf16[384,384]{1,0:T(8,128)(2,1)S(1)}, u32[]{:S(2)}, u32[]{:S(2)}) collective-permute-start(bf16[384,384]{1,0:T(8,128)(2,1)} %get-tuple-element.117.refs_8_.refs_0_.refs_9_.refs_4_), channel_id=1, source_target_pairs={{0,4},{4,0},{1,5},{5,1},{2,6},{6,2},{3,7},{7,3},{8,12},{12,8},{9,1... | collective-permute-start | bytes 884744 | tf_op jit(solution)/shard_map/ppermute | solution.py:877
  76.2 23.5 %collective-permute-start.6 = (bf16[384,384]{1,0:T(8,128)(2,1)}, bf16[384,384]{1,0:T(8,128)(2,1)S(1)}, u32[]{:S(2)}, u32[]{:S(2)}) collective-permute-start(bf16[384,384]{1,0:T(8,128)(2,1)} %collective-permute-done.4.refs_5_.refs_6_.refs_1_), channel_id=1, source_target_pairs={{0,2},{2,0},{1,3},{3,1},{4,6},{6,4},{5,7},{7,5},{8,10},{10,8},{9,1... | collective-permute-start | bytes 884744 | tf_op jit(solution)/shard_map/ppermute | solution.py:877
  76.7 29.1 %collective-permute-start.9 = (bf16[384,384]{1,0:T(8,128)(2,1)}, bf16[384,384]{1,0:T(8,128)(2,1)S(1)}, u32[]{:S(2)}, u32[]{:S(2)}) collective-permute-start(bf16[384,384]{1,0:T(8,128)(2,1)} %collective-permute-done.8.refs_10_.refs_2_.refs_11_.refs_6_), channel_id=1, source_target_pairs={{0,4},{4,0},{1,5},{5,1},{2,6},{6,2},{3,7},{7,3},{8,12},{12,8},{9,1... | collective-permute-start | bytes 884744 | tf_op jit(solution)/shard_map/ppermute | solution.py:877
  93.2 28.1 %collective-permute-start.15 = (bf16[384,768]{1,0:T(8,128)(2,1)}, bf16[384,768]{1,0:T(8,128)(2,1)}, u32[]{:S(2)}, u32[]{:S(2)}) collective-permute-start(bf16[384,768]{1,0:T(8,128)(2,1)} %get-tuple-element.118.refs_5_.refs_2_.refs_6_), channel_id=1, source_target_pairs={{0,2},{2,0},{1,3},{3,1},{4,6},{6,4},{5,7},{7,5},{8,10},{10,8},{9,1... | collective-permute-start | bytes 1769480 | tf_op jit(solution)/shard_map/ppermute | solution.py:877
  99.7 21.6 %collective-permute-start.17 = (bf16[384,768]{1,0:T(8,128)(2,1)}, bf16[384,768]{1,0:T(8,128)(2,1)}, u32[]{:S(2)}, u32[]{:S(2)}) collective-permute-start(bf16[384,768]{1,0:T(8,128)(2,1)} %get-tuple-element.119.refs_9_.refs_10_), channel_id=1, source_target_pairs={{0,4},{4,0},{1,5},{5,1},{2,6},{6,2},{3,7},{7,3},{8,12},{12,8},{9,1... | collective-permute-start | bytes 1769480 | tf_op jit(solution)/shard_map/ppermute | solution.py:877
  99.7 38.8 %collective-permute-start.16 = (bf16[384,768]{1,0:T(8,128)(2,1)}, bf16[384,768]{1,0:T(8,128)(2,1)}, u32[]{:S(2)}, u32[]{:S(2)}) collective-permute-start(bf16[384,768]{1,0:T(8,128)(2,1)} %collective-permute-done.12.refs_15_.refs_4_.refs_6_.refs_7_), channel_id=1, source_target_pairs={{0,2},{2,0},{1,3},{3,1},{4,6},{6,4},{5,7},{7,5},{8,10},{10,8},{9,1... | collective-permute-start | bytes 1769480 | tf_op jit(solution)/shard_map/ppermute | solution.py:877
  100.5 38.0 %collective-permute-start.18 = (bf16[384,768]{1,0:T(8,128)(2,1)}, bf16[384,768]{1,0:T(8,128)(2,1)}, u32[]{:S(2)}, u32[]{:S(2)}) collective-permute-start(bf16[384,768]{1,0:T(8,128)(2,1)} %collective-permute-done.13.refs_16_.refs_8_.refs_11_.refs_12_), channel_id=1, source_target_pairs={{0,4},{4,0},{1,5},{5,1},{2,6},{6,2},{3,7},{7,3},{8,12},{12,8},{9,1... | collective-permute-start | bytes 1769480 | tf_op jit(solution)/shard_map/ppermute | solution.py:877
  119.0 19.5 %collective-permute-start.14 = (bf16[2,256,384]{2,1,0:T(8,128)(2,1)}, bf16[2,256,384]{2,1,0:T(8,128)(2,1)}, u32[]{:S(2)}, u32[]{:S(2)}) collective-permute-start(bf16[2,256,384]{2,1,0:T(8,128)(2,1)} %get-tuple-element.122), channel_id=1, source_target_pairs={{0,2},{2,0},{1,3},{3,1},{4,6},{6,4},{5,7},{7,5},{8,10},{10,8},{9,1... | collective-permute-start | bytes 1179656 | tf_op jit(solution)/shard_map/ppermute | solution.py:877
  264.6 35.6 %collective-permute-start.27 = (bf16[2,384,768]{2,1,0:T(8,128)(2,1)}, bf16[2,384,768]{2,1,0:T(8,128)(2,1)}, u32[]{:S(2)}, u32[]{:S(2)}) collective-permute-start(bf16[2,384,768]{2,1,0:T(8,128)(2,1)} %get-tuple-element.142.refs_9_), channel_id=1, source_target_pairs={{0,4},{4,0},{1,5},{5,1},{2,6},{6,2},{3,7},{7,3},{8,12},{12,8},{9,1... | collective-permute-start | bytes 3538952 | tf_op jit(solution)/shard_map/ppermute | solution.py:877
  265.2 35.1 %collective-permute-start.28 = (bf16[2,384,768]{2,1,0:T(8,128)(2,1)}, bf16[2,384,768]{2,1,0:T(8,128)(2,1)S(1)}, u32[]{:S(2)}, u32[]{:S(2)}) collective-permute-start(bf16[2,384,768]{2,1,0:T(8,128)(2,1)} %get-tuple-element.154), channel_id=1, source_target_pairs={{0,2},{2,0},{1,3},{3,1},{4,6},{6,4},{5,7},{7,5},{8,10},{10,8},{9,1... | collective-permute-start | bytes 3538952 | tf_op jit(solution)/shard_map/ppermute | solution.py:877
  269.2 35.0 %collective-permute-start.23 = (bf16[1024,768]{1,0:T(8,128)(2,1)S(1)}, bf16[1024,768]{1,0:T(8,128)(2,1)}, u32[]{:S(2)}, u32[]{:S(2)}) collective-permute-start(bf16[1024,768]{1,0:T(8,128)(2,1)S(1)} %get-tuple-element.133), channel_id=1, source_target_pairs={{0,1},{1,0},{2,3},{3,2},{4,5},{5,4},{6,7},{7,6},{8,9},{9,8},{10,11... | collective-permute-start | bytes 4718600 | tf_op jit(solution)/shard_map/ppermute | solution.py:877
  293.7 15.1 %collective-permute-start.26 = (bf16[2,256,384]{2,1,0:T(8,128)(2,1)S(1)}, bf16[2,256,384]{2,1,0:T(8,128)(2,1)S(1)}, u32[]{:S(2)}, u32[]{:S(2)}) collective-permute-start(bf16[2,256,384]{2,1,0:T(8,128)(2,1)S(1)} %get-tuple-element.151), channel_id=1, source_target_pairs={{0,2},{2,0},{1,3},{3,1},{4,6},{6,4},{5,7},{7,5},{8,10},{10,8},{9,1... | collective-permute-start | bytes 1179656 | tf_op jit(solution)/shard_map/ppermute | solution.py:877
  302.1 24.3 %collective-permute-start.30 = (bf16[384,768]{1,0:T(8,128)(2,1)S(1)}, bf16[384,768]{1,0:T(8,128)(2,1)S(1)}, u32[]{:S(2)}, u32[]{:S(2)}) collective-permute-start(bf16[384,768]{1,0:T(8,128)(2,1)S(1)} %get-tuple-element.155.refs_4_), channel_id=1, source_target_pairs={{0,2},{2,0},{1,3},{3,1},{4,6},{6,4},{5,7},{7,5},{8,10},{10,8},{9,1... | collective-permute-start | bytes 1769480 | tf_op jit(solution)/shard_map/ppermute | solution.py:877
  302.7 25.6 %collective-permute-start.31 = (bf16[384,768]{1,0:T(8,128)(2,1)S(1)}, bf16[384,768]{1,0:T(8,128)(2,1)S(1)}, u32[]{:S(2)}, u32[]{:S(2)}) collective-permute-start(bf16[384,768]{1,0:T(8,128)(2,1)S(1)} %get-tuple-element.162), channel_id=1, source_target_pairs={{0,4},{4,0},{1,5},{5,1},{2,6},{6,2},{3,7},{7,3},{8,12},{12,8},{9,1... | collective-permute-start | bytes 1769480 | tf_op jit(solution)/shard_map/ppermute | solution.py:877
  307.2 191.2 %collective-permute-start.24 = (bf16[1024,768]{1,0:T(8,128)(2,1)S(1)}, bf16[1024,768]{1,0:T(8,128)(2,1)}, u32[]{:S(2)}, u32[]{:S(2)}) collective-permute-start(bf16[1024,768]{1,0:T(8,128)(2,1)S(1)} %add_convert_fusion.own_ref), channel_id=1, source_target_pairs={{0,2},{2,0},{1,3},{3,1},{4,6},{6,4},{5,7},{7,5},{8,10},{10,8},{9,1... | collective-permute-start | bytes 4718600 | tf_op jit(solution)/shard_map/ppermute | solution.py:877
  317.2 17.4 %collective-permute-start.29 = (bf16[1024,768]{1,0:T(8,128)(2,1)}, bf16[1024,768]{1,0:T(8,128)(2,1)}, u32[]{:S(2)}, u32[]{:S(2)}) collective-permute-start(bf16[1024,768]{1,0:T(8,128)(2,1)} %get-tuple-element.156.refs_2_), channel_id=1, source_target_pairs={{0,1},{1,0},{2,3},{3,2},{4,5},{5,4},{6,7},{7,6},{8,9},{9,8},{10,11... | collective-permute-start | bytes 4718600 | tf_op jit(solution)/shard_map/ppermute | solution.py:877
  325.8 23.2 %collective-permute-start.33 = (bf16[2,384,384]{2,1,0:T(8,128)(2,1)}, bf16[2,384,384]{2,1,0:T(8,128)(2,1)}, u32[]{:S(2)}, u32[]{:S(2)}) collective-permute-start(bf16[2,384,384]{2,1,0:T(8,128)(2,1)} %get-tuple-element.161.refs_14_), channel_id=1, source_target_pairs={{0,4},{4,0},{1,5},{5,1},{2,6},{6,2},{3,7},{7,3},{8,12},{12,8},{9,1... | collective-permute-start | bytes 1769480 | tf_op jit(solution)/shard_map/ppermute | solution.py:877
  326.4 37.9 %collective-permute-start.34 = (bf16[2,384,384]{2,1,0:T(8,128)(2,1)}, bf16[2,384,384]{2,1,0:T(8,128)(2,1)}, u32[]{:S(2)}, u32[]{:S(2)}) collective-permute-start(bf16[2,384,384]{2,1,0:T(8,128)(2,1)} %get-tuple-element.172), channel_id=1, source_target_pairs={{0,2},{2,0},{1,3},{3,1},{4,6},{6,4},{5,7},{7,5},{8,10},{10,8},{9,1... | collective-permute-start | bytes 1769480 | tf_op jit(solution)/shard_map/ppermute | solution.py:877
  329.7 54.9 %all-to-all-start.1 = ((bf16[4,96,1536]{2,1,0:T(8,128)(2,1)}), bf16[4,96,1536]{2,1,0:T(8,128)(2,1)S(1)}, u32[]{:S(2)}, u32[]{:S(2)}) async-start(bf16[4,96,1536]{2,1,0:T(8,128)(2,1)} %bitcast.23.refs_15_), calls=%async_computation.1 | async-start | bytes 2359296 | tf_op jit(solution)/shard_map/all_to_all | solution.py:945
  366.3 14.3 %collective-permute-start.35 = (bf16[384,384]{1,0:T(8,128)(2,1)}, bf16[384,384]{1,0:T(8,128)(2,1)}, u32[]{:S(2)}, u32[]{:S(2)}) collective-permute-start(bf16[384,384]{1,0:T(8,128)(2,1)} %get-tuple-element.173.refs_14_), channel_id=1, source_target_pairs={{0,2},{2,0},{1,3},{3,1},{4,6},{6,4},{5,7},{7,5},{8,10},{10,8},{9,1... | collective-permute-start | bytes 884744 | tf_op jit(solution)/shard_map/ppermute | solution.py:877
  367.8 14.6 %collective-permute-start.36 = (bf16[384,384]{1,0:T(8,128)(2,1)}, bf16[384,384]{1,0:T(8,128)(2,1)}, u32[]{:S(2)}, u32[]{:S(2)}) collective-permute-start(bf16[384,384]{1,0:T(8,128)(2,1)} %get-tuple-element.179), channel_id=1, source_target_pairs={{0,4},{4,0},{1,5},{5,1},{2,6},{6,2},{3,7},{7,3},{8,12},{12,8},{9,1... | collective-permute-start | bytes 884744 | tf_op jit(solution)/shard_map/ppermute | solution.py:877
  369.3 21.2 %collective-permute-start.32 = (bf16[1024,768]{1,0:T(8,128)(2,1)}, bf16[1024,768]{1,0:T(8,128)(2,1)}, u32[]{:S(2)}, u32[]{:S(2)}) collective-permute-start(bf16[1024,768]{1,0:T(8,128)(2,1)} %get-tuple-element.164.refs_2_), channel_id=1, source_target_pairs={{0,1},{1,0},{2,3},{3,2},{4,5},{5,4},{6,7},{7,6},{8,9},{9,8},{10,11... | collective-permute-start | bytes 4718600 | tf_op jit(solution)/shard_map/ppermute | solution.py:877
  376.6 48.6 %collective-permute-start.38 = (bf16[2,384,768]{2,1,0:T(8,128)(2,1)}, bf16[2,384,768]{2,1,0:T(8,128)(2,1)}, u32[]{:S(2)}, u32[]{:S(2)}) collective-permute-start(bf16[2,384,768]{2,1,0:T(8,128)(2,1)} %get-tuple-element.169.refs_13_), channel_id=1, source_target_pairs={{0,4},{4,0},{1,5},{5,1},{2,6},{6,2},{3,7},{7,3},{8,12},{12,8},{9,1... | collective-permute-start | bytes 3538952 | tf_op jit(solution)/shard_map/ppermute | solution.py:877
  380.6 44.5 %collective-permute-start.39 = (bf16[2,384,768]{2,1,0:T(8,128)(2,1)}, bf16[2,384,768]{2,1,0:T(8,128)(2,1)}, u32[]{:S(2)}, u32[]{:S(2)}) collective-permute-start(bf16[2,384,768]{2,1,0:T(8,128)(2,1)} %copy-done.44), channel_id=1, source_target_pairs={{0,2},{2,0},{1,3},{3,1},{4,6},{6,4},{5,7},{7,5},{8,10},{10,8},{9,1... | collective-permute-start | bytes 3538952 | tf_op jit(solution)/shard_map/ppermute | solution.py:877
  384.5 75.5 %all-to-all-start.3 = ((bf16[4,96,768]{2,1,0:T(8,128)(2,1)}), bf16[4,96,768]{2,1,0:T(8,128)(2,1)}, u32[]{:S(2)}, u32[]{:S(2)}) async-start(bf16[4,96,768]{2,1,0:T(8,128)(2,1)} %bitcast.26.refs_0_), calls=%async_computation.3 | async-start | bytes 1179648 | tf_op jit(solution)/shard_map/all_to_all | solution.py:945
  428.4 17.6 %collective-permute-start.41 = (bf16[384,768]{1,0:T(8,128)(2,1)}, bf16[384,768]{1,0:T(8,128)(2,1)}, u32[]{:S(2)}, u32[]{:S(2)}) collective-permute-start(bf16[384,768]{1,0:T(8,128)(2,1)} %get-tuple-element.187.refs_8_), channel_id=1, source_target_pairs={{0,2},{2,0},{1,3},{3,1},{4,6},{6,4},{5,7},{7,5},{8,10},{10,8},{9,1... | collective-permute-start | bytes 1769480 | tf_op jit(solution)/shard_map/ppermute | solution.py:877
  429.0 20.2 %collective-permute-start.42 = (bf16[384,768]{1,0:T(8,128)(2,1)}, bf16[384,768]{1,0:T(8,128)(2,1)}, u32[]{:S(2)}, u32[]{:S(2)}) collective-permute-start(bf16[384,768]{1,0:T(8,128)(2,1)} %get-tuple-element.192), channel_id=1, source_target_pairs={{0,4},{4,0},{1,5},{5,1},{2,6},{6,2},{3,7},{7,3},{8,12},{12,8},{9,1... | collective-permute-start | bytes 1769480 | tf_op jit(solution)/shard_map/ppermute | solution.py:877
  445.2 26.6 %collective-permute-start.43 = (bf16[2,384,384]{2,1,0:T(8,128)(2,1)}, bf16[2,384,384]{2,1,0:T(8,128)(2,1)}, u32[]{:S(2)}, u32[]{:S(2)}) collective-permute-start(bf16[2,384,384]{2,1,0:T(8,128)(2,1)} %copy-done.46), channel_id=1, source_target_pairs={{0,4},{4,0},{1,5},{5,1},{2,6},{6,2},{3,7},{7,3},{8,12},{12,8},{9,1... | collective-permute-start | bytes 1769480 | tf_op jit(solution)/shard_map/ppermute | solution.py:877
  446.0 25.8 %collective-permute-start.44 = (bf16[2,384,384]{2,1,0:T(8,128)(2,1)}, bf16[2,384,384]{2,1,0:T(8,128)(2,1)}, u32[]{:S(2)}, u32[]{:S(2)}) collective-permute-start(bf16[2,384,384]{2,1,0:T(8,128)(2,1)} %copy-done.45), channel_id=1, source_target_pairs={{0,2},{2,0},{1,3},{3,1},{4,6},{6,4},{5,7},{7,5},{8,10},{10,8},{9,1... | collective-permute-start | bytes 1769480 | tf_op jit(solution)/shard_map/ppermute | solution.py:877
  459.4 15.2 %collective-permute-start.48 = (f32[11520]{0:T(1024)S(1)}, f32[11520]{0:T(1024)S(1)}, u32[]{:S(2)}, u32[]{:S(2)}) collective-permute-start(f32[11520]{0:T(1024)S(1)} %pad_maximum_fusion.8), channel_id=1, source_target_pairs={{0,2},{2,0},{1,3},{3,1},{4,6},{6,4},{5,7},{7,5},{8,10},{10,8},{9,1... | collective-permute-start | bytes 138248 | tf_op jit(solution)/shard_map/ppermute | solution.py:877
  460.0 34.3 %all-to-all-start.4 = ((bf16[4,96,1536]{2,1,0:T(8,128)(2,1)}), bf16[4,96,1536]{2,1,0:T(8,128)(2,1)}, u32[]{:S(2)}, u32[]{:S(2)}) async-start(bf16[4,96,1536]{2,1,0:T(8,128)(2,1)} %bitcast.29.refs_6_), calls=%async_computation.4 | async-start | bytes 2359296 | tf_op jit(solution)/shard_map/all_to_all | solution.py:945
  473.1 16.4 %collective-permute-start.46 = (bf16[384,384]{1,0:T(8,128)(2,1)S(1)}, bf16[384,384]{1,0:T(8,128)(2,1)S(1)}, u32[]{:S(2)}, u32[]{:S(2)}) collective-permute-start(bf16[384,384]{1,0:T(8,128)(2,1)S(1)} %get-tuple-element.197.refs_0_), channel_id=1, source_target_pairs={{0,2},{2,0},{1,3},{3,1},{4,6},{6,4},{5,7},{7,5},{8,10},{10,8},{9,1... | collective-permute-start | bytes 884744 | tf_op jit(solution)/shard_map/ppermute | solution.py:877
  482.1 38.9 %collective-permute-start.45 = (bf16[1024,768]{1,0:T(8,128)(2,1)}, bf16[1024,768]{1,0:T(8,128)(2,1)}, u32[]{:S(2)}, u32[]{:S(2)}) collective-permute-start(bf16[1024,768]{1,0:T(8,128)(2,1)} %get-tuple-element.193.refs_4_.refs_0_.own_ref), channel_id=1, source_target_pairs={{0,2},{2,0},{1,3},{3,1},{4,6},{6,4},{5,7},{7,5},{8,10},{10,8},{9,1... | collective-permute-start | bytes 4718600 | tf_op jit(solution)/shard_map/ppermute | solution.py:877
  484.3 22.1 %collective-permute-start.51 = (f32[11520]{0:T(1024)S(1)}, f32[11520]{0:T(1024)S(1)}, u32[]{:S(2)}, u32[]{:S(2)}) collective-permute-start(f32[11520]{0:T(1024)S(1)} %add.337), channel_id=1, source_target_pairs={{0,16},{8,24},{16,0},{24,8},{1,17},{9,25},{17,1},{25,9},{2,18},{10... | collective-permute-start | bytes 138248 | tf_op jit(solution)/shard_map/ppermute | solution.py:928
  494.3 19.1 %all-to-all-start.2 = ((bf16[4,96,768]{2,1,0:T(8,128)(2,1)}), bf16[4,96,768]{2,1,0:T(8,128)(2,1)}, u32[]{:S(2)}, u32[]{:S(2)}) async-start(bf16[4,96,768]{2,1,0:T(8,128)(2,1)} %bitcast.129), calls=%async_computation.2 | async-start | bytes 1179648 | tf_op jit(solution)/shard_map/all_to_all | solution.py:945
  (119 other events, 986.4 us)
Sparse Core Ops, SparseCore 0:
  35.3 78.8 all-gather.2
  121.4 79.0 all-gather.4

commit v5 on v4

--- a/solution.py
+++ b/solution.py
@@ -48,7 +48,7 @@
     return lax.dot_general(left, right, dims, precision=precision, preferred_element_type=F32)
 
 
-VMEM_LIMIT = 40 * 2**20
+VMEM_LIMIT = 32 * 2**20
 TILE = 512
 QT = 256
 
@@ -1172,7 +1172,7 @@
         got = flip(part, "cc")
         if above_attention is not None:
             qk_give, qk_keep, qk_got, vo_keep, vo_got = above_attention
-            passed, attn_pieces = second_hop(qk_keep, qk_got, vo_keep, vo_got, (down,))
+            passed, attn_pieces = second_hop(qk_keep, qk_got, vo_keep, vo_got, (hidden_grad, slope))
             zero_mix, zero_attention = (passed,), (attn_pieces,)
             reduced[layer + 1] = (spread_pieces(attn_pieces), spread_ffn)
             zero_memory = (spread_ffn,)

time: 567 us -> 560 us (0.988)
    unnamed x221 -> x211, local copies, waits for them, and re-layouts: 37.2 us -> 34.5 us
  transfers between devices with their start and end apart: 60 -> 60, of which waited for: 15 -> 15; matrix products, arithmetic and copies ran while one was open for 11% -> 9% of each run, Pallas kernels for 42% -> 42%
where the time goes in v5:
time: 560 us; the launch traced here: 551 us
  Pallas kernels  259 us (46%)
  waiting for transfers between devices  89.7 us (16%)
  starting transfers between devices  80.9 us (14%)
  local copies, waits for them, and re-layouts  56.8 us (10%)
  other arithmetic  36.3 us (6%)
  between operations  25.6 us (5%)
    pallas_call x9, Pallas kernels, rows_call(): pl.pallas_call(body, grid_spec=pltpu.PrefetchScalarGridSpec(num_scalar_pr...  96.3 us
    ppermute x46, waiting for transfers between devices, flip(): return lax.ppermute(array, axis, SWAP)  76 us
    pallas_call x8, Pallas kernels, weight_grads(): pl.pallas_call(partial(weight_grads_kernel, plan), in_specs=[vmem] * len(...  38.8 us
    ppermute x46, starting transfers between devices, flip(): return lax.ppermute(array, axis, SWAP)  38.6 us
    pallas_call x2, Pallas kernels, attention_forward(): pl.pallas_call(attention_forward_kernel, grid_spec=pltpu.PrefetchScalarGr...  38.1 us
    unnamed x211, local copies, waits for them, and re-layouts  34.5 us
    pallas_call x2, Pallas kernels, attention_backward(): pl.pallas_call(attention_backward_kernel, grid=(2, segs), in_specs=[pl.Bl...  29.4 us
    all_to_all x4, starting transfers between devices, spread_pieces(): return lax.all_to_all(pieces, 'tz', 0, 0, tiled=True)  18.9 us
  transfers between devices with their start and end apart: 60, of which 15 were waited for; matrix products, arithmetic and copies ran while one was open for 9% of the time, Pallas kernels for 42%

profile of v5, /device:TPU:0, one launch (start us, length us, event | category | flops | bytes accessed | tf_op | source)
XLA Modules:
  0.0 551.1 jit_solution(17143160234140835811)
XLA Ops:
  9.5 3.1 collective-permute-start
  16.3 5.2 all-to-all-start
  27.3 5.2 collective-permute-done.1.refs_2_
  47.2 11.8 %shard_map.393 = bf16[256,768]{1,0:T(8,128)(2,1)S(1)} custom-call(f32[256,256]{1,0:T(8,128)S(1)} %copy-done.33, f32[256,768]{1,0:T(8,128)S(1)} %copy-done.10, bf16[384,384]{1,0:T(8,128)(2,1)} %get-tuple-element.116.refs_0_.refs_4_.refs_2_.refs_5_), custom_call_target="tpu_custom_call" | custom-call | flops 15399999488 | bytes 1000000 | tf_op jit(solution)/shard_map/pallas_call | solution.py:108
  72.4 3.3 collective-permute-done.8.refs_10_.refs_2_.refs_11_.refs_6_
  80.5 12.7 %collective-permute-done.7.refs_9_.refs_1_.refs_10_.refs_5_ = bf16[384,384]{1,0:T(8,128)(2,1)S(1)} collective-permute-done((bf16[384,384]{1,0:T(8,128)(2,1)}, bf16[384,384]{1,0:T(8,128)(2,1)S(1)}, u32[]{:S(2)}, u32[]{:S(2)}) %collective-permute-start.7) | collective-permute-done | bytes 294944 | tf_op jit(solution)/shard_map/ppermute | solution.py:877
  94.6 5.1 collective-permute-done.6.refs_7_.refs_8_.refs_3_
  102.4 3.4 collective-permute-done.9.refs_11_.refs_3_.refs_12_.refs_7_
  106.5 11.5 %shard_map.396 = (f32[1024,768]{1,0:T(8,128)}, bf16[1024,768]{1,0:T(8,128)(2,1)}, bf16[2,1024,576]{2,1,0:T(8,128)(2,1)}, f32[2,256,384]{2,1,0:T(8,128)S(1)}, bf16[2,256,384]{2,1,0:T(8,128)(2,1)}) custom-call(s32[2]{0:T(128)S(1)} %pad_add_fusion.place_ref.context_ref, bf16[1024,768]{1,0:T(8,128)(2,1)} %constant_dynamic-slice_fusion.1.refs_0_, ...), custom_call_target="tpu_custom_call" | custom-call | flops 7699999744 | bytes 1000000 | tf_op jit(solution)/shard_map/pallas_call | solution.py:325
  121.3 17.1 %collective-permute-done.14.got_ref = bf16[2,256,384]{2,1,0:T(8,128)(2,1)} collective-permute-done((bf16[2,256,384]{2,1,0:T(8,128)(2,1)}, bf16[2,256,384]{2,1,0:T(8,128)(2,1)}, u32[]{:S(2)}, u32[]{:S(2)}) %collective-permute-start.14) | collective-permute-done | bytes 393248 | tf_op jit(solution)/shard_map/ppermute | solution.py:877
  140.6 18.9 %shard_map.397 = (bf16[2,1024,192]{2,1,0:T(8,128)(2,1)}, f32[2,2,3,512]{3,2,1,0:T(4,128)}, bf16[2,2,256,384]{3,2,1,0:T(8,128)(2,1)}, bf16[1024,768]{1,0:T(8,128)(2,1)}) custom-call(s32[2]{0:T(128)S(1)} %pad_add_fusion.place_ref.context_ref, f32[2]{0:T(128)S(1)} %pad_maximum_fusion.16.bias_ref, bf16[2,1024,576]{2,1,0:T(8,128)(2,1)} %get-tuple-element.121.qkv_ref, ...), custom_call_target="tpu_custom_call" | custom-call | flops 14300000256 | bytes 1000000 | tf_op jit(solution)/shard_map/pallas_call | solution.py:611
  160.0 3.2 collective-permute-done.19.refs_2_
  163.2 13.7 %shard_map.398 = (f32[1024,768]{1,0:T(8,128)}, bf16[1024,768]{1,0:T(8,128)(2,1)}, bf16[2,1024,768]{2,1,0:T(8,128)(2,1)}, bf16[2,1024,768]{2,1,0:T(8,128)(2,1)}, bf16[1024,768]{1,0:T(8,128)(2,1)}) custom-call(s32[2]{0:T(128)S(1)} %pad_add_fusion.place_ref.context_ref, f32[1024,768]{1,0:T(8,128)} %get-tuple-element.120.refs_0_.refs_1_, ...), custom_call_target="tpu_custom_call" | custom-call | flops 12099999744 | bytes 1000000 | tf_op jit(solution)/shard_map/pallas_call | solution.py:325
  177.1 3.6 collective-permute-done.20.refs_2_
  180.7 10.8 %shard_map.400 = (f32[1024,768]{1,0:T(8,128)}, bf16[1024,768]{1,0:T(8,128)(2,1)}, bf16[2,1024,576]{2,1,0:T(8,128)(2,1)}, f32[2,256,384]{2,1,0:T(8,128)S(1)}, bf16[2,256,384]{2,1,0:T(8,128)(2,1)S(1)}) custom-call(s32[2]{0:T(128)S(1)} %pad_add_fusion.place_ref.context_ref, f32[1024,768]{1,0:T(8,128)} %get-tuple-element.125.refs_0_.refs_1_, ...), custom_call_target="tpu_custom_call" | custom-call | flops 7699999744 | bytes 1000000 | tf_op jit(solution)/shard_map/pallas_call | solution.py:325
  192.1 10.6 %collective-permute-done.21.got_ref = bf16[2,256,384]{2,1,0:T(8,128)(2,1)S(1)} collective-permute-done((bf16[2,256,384]{2,1,0:T(8,128)(2,1)S(1)}, bf16[2,256,384]{2,1,0:T(8,128)(2,1)S(1)}, u32[]{:S(2)}, u32[]{:S(2)}) %collective-permute-start.21) | collective-permute-done | bytes 393248 | tf_op jit(solution)/shard_map/ppermute | solution.py:877
  202.7 19.2 %shard_map.401 = (bf16[2,1024,192]{2,1,0:T(8,128)(2,1)}, f32[2,2,3,512]{3,2,1,0:T(4,128)}, bf16[2,2,256,384]{3,2,1,0:T(8,128)(2,1)}, bf16[1024,768]{1,0:T(8,128)(2,1)S(1)}) custom-call(s32[2]{0:T(128)S(1)} %pad_add_fusion.place_ref.context_ref, f32[2]{0:T(128)S(1)} %pad_maximum_fusion.16.bias_ref, bf16[2,1024,576]{2,1,0:T(8,128)(2,1)} %get-tuple-element.128.qkv_ref, ...), custom_call_target="tpu_custom_call" | custom-call | flops 14300000256 | bytes 1000000 | tf_op jit(solution)/shard_map/pallas_call | solution.py:611
  229.4 12.8 %shard_map.403 = (f32[1024,768]{1,0:T(8,128)}, bf16[1024,768]{1,0:T(8,128)(2,1)}, bf16[2,1024,768]{2,1,0:T(8,128)(2,1)}, bf16[2,1024,768]{2,1,0:T(8,128)(2,1)}, bf16[1024,768]{1,0:T(8,128)(2,1)S(1)}) custom-call(s32[2]{0:T(128)S(1)} %pad_add_fusion.place_ref.context_ref, f32[1024,768]{1,0:T(8,128)} %get-tuple-element.127.refs_0_.refs_1_, ...), custom_call_target="tpu_custom_call" | custom-call | flops 12099999744 | bytes 1000000 | tf_op jit(solution)/shard_map/pallas_call | solution.py:325
  242.2 13.1 %shard_map.404 = (f32[1024,768]{1,0:T(8,128)S(1)}, bf16[1024,768]{1,0:T(8,128)(2,1)S(1)}, bf16[2,1024,768]{2,1,0:T(8,128)(2,1)S(1)}, bf16[1024,768]{1,0:T(8,128)(2,1)}, f32[8,768]{1,0:T(8,128)S(1)}) custom-call(s32[2]{0:T(128)S(1)} %pad_add_fusion.place_ref.context_ref, bf16[1024,768]{1,0:T(8,128)(2,1)} %constant_dynamic-slice_fusion.refs_0_, ...), custom_call_target="tpu_custom_call" | custom-call | flops 9900000256 | bytes 1000000 | tf_op jit(solution)/shard_map/pallas_call | solution.py:325
  257.2 7.6 %shard_map.405 = (bf16[2,384,768]{2,1,0:T(8,128)(2,1)}, bf16[2,384,768]{2,1,0:T(8,128)(2,1)}) custom-call(bf16[1024,768]{1,0:T(8,128)(2,1)} %get-tuple-element.138.refs_0_, bf16[1024,768]{1,0:T(8,128)(2,1)S(1)} %get-tuple-element.139.refs_1_, bf16[2,1024,768]{2,1,0:T(8,128)(2,1)S(1)} %get-tuple-element.140.refs_2_, ...), custom_call_target="tpu_custom_call" | custom-call | flops 6600000000 | bytes 1000000 | tf_op jit(solution)/shard_map/pallas_call | solution.py:860
  269.7 7.3 %shard_map.406 = (f32[1024,768]{1,0:T(8,128)S(1)}, bf16[1024,768]{1,0:T(8,128)(2,1)S(1)}, bf16[2,1024,192]{2,1,0:T(8,128)(2,1)S(1)}, f32[8,768]{1,0:T(8,128)S(1)}) custom-call(s32[2]{0:T(128)S(1)} %pad_add_fusion.place_ref.context_ref, f32[1024,768]{1,0:T(8,128)S(1)} %copy-done.52, f32[1024,768]{1,0:T(8,128)} %get-tuple-element.132.refs_1_, ...), custom_call_target="tpu_custom_call" | custom-call | flops 6600000000 | bytes 1000000 | tf_op jit(solution)/shard_map/pallas_call | solution.py:325
  277.0 15.2 %shard_map.407 = (bf16[2,1024,192]{2,1,0:T(8,128)(2,1)S(1)}, f32[2,1024,384]{2,1,0:T(8,128)S(1)}, f32[2,256,384]{2,1,0:T(8,128)S(1)}, bf16[2,256,384]{2,1,0:T(8,128)(2,1)S(1)}) custom-call(f32[2]{0:T(128)S(1)} %pad_maximum_fusion.16.bias_ref, bf16[2,1024,576]{2,1,0:T(8,128)(2,1)} %get-tuple-element.128.qkv_ref, ...), custom_call_target="tpu_custom_call" | custom-call | flops 19800000512 | bytes 1000000 | tf_op jit(solution)/shard_map/pallas_call | solution.py:734
  293.9 5.0 shard_map.408
  305.1 8.4 %shard_map.410 = (bf16[2,1024,576]{2,1,0:T(8,128)(2,1)S(1)}, bf16[1024,768]{1,0:T(8,128)(2,1)}, f32[8,576]{1,0:T(8,128)S(1)}) custom-call(s32[2]{0:T(128)S(1)} %pad_add_fusion.place_ref.context_ref, bf16[2,1024,192]{2,1,0:T(8,128)(2,1)S(1)} %get-tuple-element.148.refs_4_.refs_0_.dq_ref, f32[2,1024,384]{2,1,0:T(8,128)S(1)} %get-tuple-element.149.dkv_ref, ...), custom_call_target="tpu_custom_call" | custom-call | flops 5500000256 | bytes 1000000 | tf_op jit(solution)/shard_map/pallas_call | solution.py:813
  313.5 3.7 shard_map.414
  318.0 4.5 shard_map.411
  327.4 4.7 all-to-all-start.1
  334.0 13.8 %shard_map.412 = (f32[1024,768]{1,0:T(8,128)S(1)}, bf16[1024,768]{1,0:T(8,128)(2,1)S(1)}, bf16[2,1024,768]{2,1,0:T(8,128)(2,1)S(1)}, bf16[1024,768]{1,0:T(8,128)(2,1)}, f32[8,768]{1,0:T(8,128)S(1)}) custom-call(s32[2]{0:T(128)S(1)} %pad_add_fusion.place_ref.context_ref, f32[1024,768]{1,0:T(8,128)S(1)} %copy-done.50, ...), custom_call_target="tpu_custom_call" | custom-call | flops 9900000256 | bytes 1000000 | tf_op jit(solution)/shard_map/pallas_call | solution.py:325
  347.9 15.0 %collective-permute-done.34.got_b_ref = bf16[2,384,384]{2,1,0:T(8,128)(2,1)} collective-permute-done((bf16[2,384,384]{2,1,0:T(8,128)(2,1)}, bf16[2,384,384]{2,1,0:T(8,128)(2,1)}, u32[]{:S(2)}, u32[]{:S(2)}) %collective-permute-start.34) | collective-permute-done | bytes 589856 | tf_op jit(solution)/shard_map/ppermute | solution.py:877
  368.5 5.0 shard_map.413
  382.4 5.0 all-to-all-start.3
  390.4 7.3 %shard_map.416 = (f32[1024,768]{1,0:T(8,128)S(1)}, bf16[1024,768]{1,0:T(8,128)(2,1)S(1)}, bf16[2,1024,192]{2,1,0:T(8,128)(2,1)S(1)}, f32[8,768]{1,0:T(8,128)S(1)}) custom-call(s32[2]{0:T(128)S(1)} %pad_add_fusion.place_ref.context_ref, f32[1024,768]{1,0:T(8,128)S(1)} %copy-done.58, f32[1024,768]{1,0:T(8,128)} %get-tuple-element.125.refs_0_.refs_1_, ...), custom_call_target="tpu_custom_call" | custom-call | flops 6600000000 | bytes 1000000 | tf_op jit(solution)/shard_map/pallas_call | solution.py:325
  399.4 14.2 %shard_map.417 = (bf16[2,1024,192]{2,1,0:T(8,128)(2,1)S(1)}, f32[2,1024,384]{2,1,0:T(8,128)S(1)}, f32[2,256,384]{2,1,0:T(8,128)S(1)}, bf16[2,256,384]{2,1,0:T(8,128)(2,1)S(1)}) custom-call(f32[2]{0:T(128)S(1)} %pad_maximum_fusion.16.bias_ref, bf16[2,1024,576]{2,1,0:T(8,128)(2,1)} %get-tuple-element.121.qkv_ref, ...), custom_call_target="tpu_custom_call" | custom-call | flops 19800000512 | bytes 1000000 | tf_op jit(solution)/shard_map/pallas_call | solution.py:734
  415.1 5.0 shard_map.418
  420.1 3.2 shard_map.419
  425.2 8.6 %shard_map.420 = (bf16[2,1024,576]{2,1,0:T(8,128)(2,1)S(1)}, bf16[1024,768]{1,0:T(8,128)(2,1)}, f32[8,576]{1,0:T(8,128)S(1)}) custom-call(s32[2]{0:T(128)S(1)} %pad_add_fusion.place_ref.context_ref, bf16[2,1024,192]{2,1,0:T(8,128)(2,1)S(1)} %get-tuple-element.180.refs_4_.refs_0_.dq_ref, f32[2,1024,384]{2,1,0:T(8,128)S(1)} %get-tuple-element.181.dkv_ref, ...), custom_call_target="tpu_custom_call" | custom-call | flops 5500000256 | bytes 1000000 | tf_op jit(solution)/shard_map/pallas_call | solution.py:813
  433.9 4.5 shard_map.421
  447.0 5.9 %shard_map.422 = (bf16[1024,768]{1,0:T(8,128)(2,1)}, f32[8,768]{1,0:T(8,128)S(1)}) custom-call(s32[2]{0:T(128)S(1)} %pad_add_fusion.place_ref.context_ref, f32[1024,768]{1,0:T(8,128)S(1)} %copy-done.54, f32[1024,768]{1,0:T(8,128)} %get-tuple-element.120.refs_0_.refs_1_, bf16[1024,768]{1,0:T(8,128)(2,1)} %get-tuple-element.190.refs_2_, ...), custom_call_target="tpu_custom_call" | custom-call | flops 5500000256 | bytes 1000000 | tf_op jit(solution)/shard_map/pallas_call | solution.py:325
  454.7 5.1 all-to-all-start.4
  463.0 3.6 shard_map.423
  479.0 5.2 collective-permute-start.51
  486.4 2.6 all-to-all-done.4
  489.0 4.2 all-to-all-start.2
  493.2 6.5 %shard_map.425 = (f32[2048,768]{1,0:T(8,128)}, f32[8,128]{1,0:T(8,128)S(1)}) custom-call(s32[2]{0:T(128)S(1)} %pad_add_fusion.place_ref.context_ref, bf16[1024,768]{1,0:T(8,128)(2,1)S(1)} %add_convert_fusion.own_ref, bf16[1024,768]{1,0:T(8,128)(2,1)} %collective-permute-done.24.got_ref, bf16[768,768]{1,0:T(8,128)(2,1)S(1)} %copy-done.8, ...), custom_call_target="tpu_custom_call" | custom-call | flops 4400000000 | bytes 1000000 | tf_op jit(solution)/shard_map/pallas_call | solution.py:500
  505.0 3.0 all-to-all-done.2
  517.2 3.8 all-to-all-start.5
  521.0 7.5 %shard_map.426 = (f32[2048,768]{1,0:T(8,128)}, f32[8,128]{1,0:T(8,128)}) custom-call(s32[2]{0:T(128)S(1)} %pad_add_fusion.place_ref.context_ref, bf16[1024,768]{1,0:T(8,128)(2,1)} %get-tuple-element.193.refs_4_.refs_0_.own_ref, bf16[1024,768]{1,0:T(8,128)(2,1)} %collective-permute-done.45.got_ref._, bf16[768,768]{1,0:T(8,128)(2,1)S(1)} %copy-done.8), custom_call_target="tpu_custom_call" | custom-call | flops 4400000000 | bytes 1000000 | tf_op jit(solution)/shard_map/pallas_call | solution.py:500
  535.3 2.8 divide_subtract_fusion
  (427 shorter events, 153.1 us)
Async XLA Ops:
  9.5 17.8 %collective-permute-start = (bf16[96,768]{1,0:T(8,128)(2,1)S(1)}, bf16[96,768]{1,0:T(8,128)(2,1)S(1)}, u32[]{:S(2)}, u32[]{:S(2)}) collective-permute-start(bf16[96,768]{1,0:T(8,128)(2,1)S(1)} %shard_map.391.refs_0_.refs_2_), channel_id=1, source_target_pairs={{0,8},{8,0},{16,24},{24,16},{1,9},{9,1},{17,25},{25,17},{2,10},{10... | collective-permute-start | bytes 442376 | tf_op jit(solution)/shard_map/ppermute | solution.py:928
  12.5 19.9 %collective-permute-start.1 = (bf16[96,768]{1,0:T(8,128)(2,1)S(1)}, bf16[96,768]{1,0:T(8,128)(2,1)}, u32[]{:S(2)}, u32[]{:S(2)}) collective-permute-start(bf16[96,768]{1,0:T(8,128)(2,1)S(1)} %shard_map.391.refs_0_.refs_2_), channel_id=1, source_target_pairs={{0,16},{8,24},{16,0},{24,8},{1,17},{9,25},{17,1},{25,9},{2,18},{10... | collective-permute-start | bytes 442376 | tf_op jit(solution)/shard_map/ppermute | solution.py:928
  15.1 17.3 %collective-permute-start.2 = (bf16[96,768]{1,0:T(8,128)(2,1)S(1)}, bf16[96,768]{1,0:T(8,128)(2,1)}, u32[]{:S(2)}, u32[]{:S(2)}) collective-permute-start(bf16[96,768]{1,0:T(8,128)(2,1)S(1)} %shard_map.391.refs_0_.refs_2_), channel_id=1, source_target_pairs={{0,24},{8,16},{16,8},{24,0},{1,25},{9,17},{17,9},{25,1},{2,26},{10... | collective-permute-start | bytes 442376 | tf_op jit(solution)/shard_map/ppermute | solution.py:928
  16.3 47.7 %all-to-all-start = ((bf16[4,96,1536]{2,1,0:T(8,128)(2,1)}), bf16[4,96,1536]{2,1,0:T(8,128)(2,1)}, u32[]{:S(2)}, u32[]{:S(2)}) async-start(bf16[4,96,1536]{2,1,0:T(8,128)(2,1)} %broadcast_in_dim.29), calls=%async_computation | async-start | bytes 2359296 | tf_op jit(solution)/shard_map/all_to_all | solution.py:891
  21.5 155.6 %all-gather.3.cloned.1.call-start = ((), (), s32[]{:S(2)}) async-start(), calls=%async_computation.6 | async-start | bytes 2506752 | tf_op jit(solution)/shard_map/all_gather | solution.py:884
  23.4 42.9 %collective-permute-start.11 = (bf16[2,256,384]{2,1,0:T(8,128)(2,1)}, bf16[2,256,384]{2,1,0:T(8,128)(2,1)}, u32[]{:S(2)}, u32[]{:S(2)}) collective-permute-start(bf16[2,256,384]{2,1,0:T(8,128)(2,1)} %copy.129), channel_id=1, source_target_pairs={{0,2},{2,0},{1,3},{3,1},{4,6},{6,4},{5,7},{7,5},{8,10},{10,8},{9,1... | collective-permute-start | bytes 1179656 | tf_op jit(solution)/shard_map/ppermute | solution.py:877
  24.9 16.3 %collective-permute-start.3 = (f32[2,6,192]{2,0,1:T(2,128)}, f32[2,6,192]{2,0,1:T(2,128)}, u32[]{:S(2)}, u32[]{:S(2)}) collective-permute-start(f32[2,6,192]{2,0,1:T(2,128)} %param.45), channel_id=1, source_target_pairs={{0,2},{2,0},{1,3},{3,1},{4,6},{6,4},{5,7},{7,5},{8,10},{10,8},{9,1... | collective-permute-start | bytes 27656 | tf_op jit(solution)/shard_map/ppermute | solution.py:877
  35.2 191.4 %all-gather.5.cloned.1.call-start = ((), (), s32[]{:S(2)}) async-start(), calls=%async_computation.7 | async-start | bytes 5013504 | tf_op jit(solution)/shard_map/all_gather | solution.py:884
  42.0 24.8 %collective-permute-start.4 = (bf16[384,384]{1,0:T(8,128)(2,1)}, bf16[384,384]{1,0:T(8,128)(2,1)}, u32[]{:S(2)}, u32[]{:S(2)}) collective-permute-start(bf16[384,384]{1,0:T(8,128)(2,1)} %get-tuple-element.116.refs_0_.refs_4_.refs_2_.refs_5_), channel_id=1, source_target_pairs={{0,4},{4,0},{1,5},{5,1},{2,6},{6,2},{3,7},{7,3},{8,12},{12,8},{9,1... | collective-permute-start | bytes 884744 | tf_op jit(solution)/shard_map/ppermute | solution.py:877
  43.6 32.6 %collective-permute-start.5 = (bf16[384,384]{1,0:T(8,128)(2,1)}, bf16[384,384]{1,0:T(8,128)(2,1)}, u32[]{:S(2)}, u32[]{:S(2)}) collective-permute-start(bf16[384,384]{1,0:T(8,128)(2,1)} %get-tuple-element.116.refs_0_.refs_4_.refs_2_.refs_5_), channel_id=1, source_target_pairs={{0,2},{2,0},{1,3},{3,1},{4,6},{6,4},{5,7},{7,5},{8,10},{10,8},{9,1... | collective-permute-start | bytes 884744 | tf_op jit(solution)/shard_map/ppermute | solution.py:877
  59.1 17.6 %collective-permute-start.10 = (bf16[256,768]{1,0:T(8,128)(2,1)S(1)}, bf16[256,768]{1,0:T(8,128)(2,1)}, u32[]{:S(2)}, u32[]{:S(2)}) collective-permute-start(bf16[256,768]{1,0:T(8,128)(2,1)S(1)} %shard_map.393), channel_id=1, source_target_pairs={{0,1},{1,0},{2,3},{3,2},{4,5},{5,4},{6,7},{7,6},{8,9},{9,8},{10,11... | collective-permute-start | bytes 1179656 | tf_op jit(solution)/shard_map/ppermute | solution.py:877
  66.3 33.4 %collective-permute-start.12 = (bf16[384,768]{1,0:T(8,128)(2,1)}, bf16[384,768]{1,0:T(8,128)(2,1)}, u32[]{:S(2)}, u32[]{:S(2)}) collective-permute-start(bf16[384,768]{1,0:T(8,128)(2,1)} %get-tuple-element.118.refs_5_.refs_2_.refs_6_), channel_id=1, source_target_pairs={{0,4},{4,0},{1,5},{5,1},{2,6},{6,2},{3,7},{7,3},{8,12},{12,8},{9,1... | collective-permute-start | bytes 1769480 | tf_op jit(solution)/shard_map/ppermute | solution.py:877
  66.8 33.6 %collective-permute-start.13 = (bf16[384,768]{1,0:T(8,128)(2,1)}, bf16[384,768]{1,0:T(8,128)(2,1)}, u32[]{:S(2)}, u32[]{:S(2)}) collective-permute-start(bf16[384,768]{1,0:T(8,128)(2,1)} %get-tuple-element.119.refs_9_.refs_10_), channel_id=1, source_target_pairs={{0,2},{2,0},{1,3},{3,1},{4,6},{6,4},{5,7},{7,5},{8,10},{10,8},{9,1... | collective-permute-start | bytes 1769480 | tf_op jit(solution)/shard_map/ppermute | solution.py:877
  75.7 17.5 %collective-permute-start.7 = (bf16[384,384]{1,0:T(8,128)(2,1)}, bf16[384,384]{1,0:T(8,128)(2,1)S(1)}, u32[]{:S(2)}, u32[]{:S(2)}) collective-permute-start(bf16[384,384]{1,0:T(8,128)(2,1)} %get-tuple-element.117.refs_8_.refs_0_.refs_9_.refs_4_), channel_id=1, source_target_pairs={{0,4},{4,0},{1,5},{5,1},{2,6},{6,2},{3,7},{7,3},{8,12},{12,8},{9,1... | collective-permute-start | bytes 884744 | tf_op jit(solution)/shard_map/ppermute | solution.py:877
  76.2 23.5 %collective-permute-start.6 = (bf16[384,384]{1,0:T(8,128)(2,1)}, bf16[384,384]{1,0:T(8,128)(2,1)S(1)}, u32[]{:S(2)}, u32[]{:S(2)}) collective-permute-start(bf16[384,384]{1,0:T(8,128)(2,1)} %collective-permute-done.4.refs_5_.refs_6_.refs_1_), channel_id=1, source_target_pairs={{0,2},{2,0},{1,3},{3,1},{4,6},{6,4},{5,7},{7,5},{8,10},{10,8},{9,1... | collective-permute-start | bytes 884744 | tf_op jit(solution)/shard_map/ppermute | solution.py:877
  76.7 29.1 %collective-permute-start.9 = (bf16[384,384]{1,0:T(8,128)(2,1)}, bf16[384,384]{1,0:T(8,128)(2,1)S(1)}, u32[]{:S(2)}, u32[]{:S(2)}) collective-permute-start(bf16[384,384]{1,0:T(8,128)(2,1)} %collective-permute-done.8.refs_10_.refs_2_.refs_11_.refs_6_), channel_id=1, source_target_pairs={{0,4},{4,0},{1,5},{5,1},{2,6},{6,2},{3,7},{7,3},{8,12},{12,8},{9,1... | collective-permute-start | bytes 884744 | tf_op jit(solution)/shard_map/ppermute | solution.py:877
  93.2 28.2 %collective-permute-start.15 = (bf16[384,768]{1,0:T(8,128)(2,1)}, bf16[384,768]{1,0:T(8,128)(2,1)}, u32[]{:S(2)}, u32[]{:S(2)}) collective-permute-start(bf16[384,768]{1,0:T(8,128)(2,1)} %get-tuple-element.118.refs_5_.refs_2_.refs_6_), channel_id=1, source_target_pairs={{0,2},{2,0},{1,3},{3,1},{4,6},{6,4},{5,7},{7,5},{8,10},{10,8},{9,1... | collective-permute-start | bytes 1769480 | tf_op jit(solution)/shard_map/ppermute | solution.py:877
  99.7 21.6 %collective-permute-start.17 = (bf16[384,768]{1,0:T(8,128)(2,1)}, bf16[384,768]{1,0:T(8,128)(2,1)}, u32[]{:S(2)}, u32[]{:S(2)}) collective-permute-start(bf16[384,768]{1,0:T(8,128)(2,1)} %get-tuple-element.119.refs_9_.refs_10_), channel_id=1, source_target_pairs={{0,4},{4,0},{1,5},{5,1},{2,6},{6,2},{3,7},{7,3},{8,12},{12,8},{9,1... | collective-permute-start | bytes 1769480 | tf_op jit(solution)/shard_map/ppermute | solution.py:877
  99.7 38.8 %collective-permute-start.16 = (bf16[384,768]{1,0:T(8,128)(2,1)}, bf16[384,768]{1,0:T(8,128)(2,1)}, u32[]{:S(2)}, u32[]{:S(2)}) collective-permute-start(bf16[384,768]{1,0:T(8,128)(2,1)} %collective-permute-done.12.refs_15_.refs_4_.refs_6_.refs_7_), channel_id=1, source_target_pairs={{0,2},{2,0},{1,3},{3,1},{4,6},{6,4},{5,7},{7,5},{8,10},{10,8},{9,1... | collective-permute-start | bytes 1769480 | tf_op jit(solution)/shard_map/ppermute | solution.py:877
  100.4 38.0 %collective-permute-start.18 = (bf16[384,768]{1,0:T(8,128)(2,1)}, bf16[384,768]{1,0:T(8,128)(2,1)}, u32[]{:S(2)}, u32[]{:S(2)}) collective-permute-start(bf16[384,768]{1,0:T(8,128)(2,1)} %collective-permute-done.13.refs_16_.refs_8_.refs_11_.refs_12_), channel_id=1, source_target_pairs={{0,4},{4,0},{1,5},{5,1},{2,6},{6,2},{3,7},{7,3},{8,12},{12,8},{9,1... | collective-permute-start | bytes 1769480 | tf_op jit(solution)/shard_map/ppermute | solution.py:877
  119.0 19.5 %collective-permute-start.14 = (bf16[2,256,384]{2,1,0:T(8,128)(2,1)}, bf16[2,256,384]{2,1,0:T(8,128)(2,1)}, u32[]{:S(2)}, u32[]{:S(2)}) collective-permute-start(bf16[2,256,384]{2,1,0:T(8,128)(2,1)} %get-tuple-element.122), channel_id=1, source_target_pairs={{0,2},{2,0},{1,3},{3,1},{4,6},{6,4},{5,7},{7,5},{8,10},{10,8},{9,1... | collective-permute-start | bytes 1179656 | tf_op jit(solution)/shard_map/ppermute | solution.py:877
  264.8 34.1 %collective-permute-start.27 = (bf16[2,384,768]{2,1,0:T(8,128)(2,1)}, bf16[2,384,768]{2,1,0:T(8,128)(2,1)}, u32[]{:S(2)}, u32[]{:S(2)}) collective-permute-start(bf16[2,384,768]{2,1,0:T(8,128)(2,1)} %get-tuple-element.142.refs_9_), channel_id=1, source_target_pairs={{0,4},{4,0},{1,5},{5,1},{2,6},{6,2},{3,7},{7,3},{8,12},{12,8},{9,1... | collective-permute-start | bytes 3538952 | tf_op jit(solution)/shard_map/ppermute | solution.py:877
  265.3 33.5 %collective-permute-start.28 = (bf16[2,384,768]{2,1,0:T(8,128)(2,1)}, bf16[2,384,768]{2,1,0:T(8,128)(2,1)S(1)}, u32[]{:S(2)}, u32[]{:S(2)}) collective-permute-start(bf16[2,384,768]{2,1,0:T(8,128)(2,1)} %get-tuple-element.154), channel_id=1, source_target_pairs={{0,2},{2,0},{1,3},{3,1},{4,6},{6,4},{5,7},{7,5},{8,10},{10,8},{9,1... | collective-permute-start | bytes 3538952 | tf_op jit(solution)/shard_map/ppermute | solution.py:877
  267.7 35.0 %collective-permute-start.23 = (bf16[1024,768]{1,0:T(8,128)(2,1)S(1)}, bf16[1024,768]{1,0:T(8,128)(2,1)S(1)}, u32[]{:S(2)}, u32[]{:S(2)}) collective-permute-start(bf16[1024,768]{1,0:T(8,128)(2,1)S(1)} %get-tuple-element.133), channel_id=1, source_target_pairs={{0,1},{1,0},{2,3},{3,2},{4,5},{5,4},{6,7},{7,6},{8,9},{9,8},{10,11... | collective-permute-start | bytes 4718600 | tf_op jit(solution)/shard_map/ppermute | solution.py:877
  300.7 22.3 %collective-permute-start.30 = (bf16[384,768]{1,0:T(8,128)(2,1)S(1)}, bf16[384,768]{1,0:T(8,128)(2,1)S(1)}, u32[]{:S(2)}, u32[]{:S(2)}) collective-permute-start(bf16[384,768]{1,0:T(8,128)(2,1)S(1)} %get-tuple-element.155.refs_4_), channel_id=1, source_target_pairs={{0,2},{2,0},{1,3},{3,1},{4,6},{6,4},{5,7},{7,5},{8,10},{10,8},{9,1... | collective-permute-start | bytes 1769480 | tf_op jit(solution)/shard_map/ppermute | solution.py:877
  301.3 24.8 %collective-permute-start.31 = (bf16[384,768]{1,0:T(8,128)(2,1)S(1)}, bf16[384,768]{1,0:T(8,128)(2,1)S(1)}, u32[]{:S(2)}, u32[]{:S(2)}) collective-permute-start(bf16[384,768]{1,0:T(8,128)(2,1)S(1)} %get-tuple-element.162), channel_id=1, source_target_pairs={{0,4},{4,0},{1,5},{5,1},{2,6},{6,2},{3,7},{7,3},{8,12},{12,8},{9,1... | collective-permute-start | bytes 1769480 | tf_op jit(solution)/shard_map/ppermute | solution.py:877
  303.5 189.7 %collective-permute-start.24 = (bf16[1024,768]{1,0:T(8,128)(2,1)S(1)}, bf16[1024,768]{1,0:T(8,128)(2,1)}, u32[]{:S(2)}, u32[]{:S(2)}) collective-permute-start(bf16[1024,768]{1,0:T(8,128)(2,1)S(1)} %add_convert_fusion.own_ref), channel_id=1, source_target_pairs={{0,2},{2,0},{1,3},{3,1},{4,6},{6,4},{5,7},{7,5},{8,10},{10,8},{9,1... | collective-permute-start | bytes 4718600 | tf_op jit(solution)/shard_map/ppermute | solution.py:877
  313.5 18.6 %collective-permute-start.29 = (bf16[1024,768]{1,0:T(8,128)(2,1)}, bf16[1024,768]{1,0:T(8,128)(2,1)}, u32[]{:S(2)}, u32[]{:S(2)}) collective-permute-start(bf16[1024,768]{1,0:T(8,128)(2,1)} %get-tuple-element.156.refs_2_), channel_id=1, source_target_pairs={{0,1},{1,0},{2,3},{3,2},{4,5},{5,4},{6,7},{7,6},{8,9},{9,8},{10,11... | collective-permute-start | bytes 4718600 | tf_op jit(solution)/shard_map/ppermute | solution.py:877
  322.5 25.4 %collective-permute-start.33 = (bf16[2,384,384]{2,1,0:T(8,128)(2,1)}, bf16[2,384,384]{2,1,0:T(8,128)(2,1)}, u32[]{:S(2)}, u32[]{:S(2)}) collective-permute-start(bf16[2,384,384]{2,1,0:T(8,128)(2,1)} %get-tuple-element.161.refs_14_), channel_id=1, source_target_pairs={{0,4},{4,0},{1,5},{5,1},{2,6},{6,2},{3,7},{7,3},{8,12},{12,8},{9,1... | collective-permute-start | bytes 1769480 | tf_op jit(solution)/shard_map/ppermute | solution.py:877
  323.0 39.9 %collective-permute-start.34 = (bf16[2,384,384]{2,1,0:T(8,128)(2,1)}, bf16[2,384,384]{2,1,0:T(8,128)(2,1)}, u32[]{:S(2)}, u32[]{:S(2)}) collective-permute-start(bf16[2,384,384]{2,1,0:T(8,128)(2,1)} %get-tuple-element.172), channel_id=1, source_target_pairs={{0,2},{2,0},{1,3},{3,1},{4,6},{6,4},{5,7},{7,5},{8,10},{10,8},{9,1... | collective-permute-start | bytes 1769480 | tf_op jit(solution)/shard_map/ppermute | solution.py:877
  327.4 55.0 %all-to-all-start.1 = ((bf16[4,96,1536]{2,1,0:T(8,128)(2,1)}), bf16[4,96,1536]{2,1,0:T(8,128)(2,1)S(1)}, u32[]{:S(2)}, u32[]{:S(2)}) async-start(bf16[4,96,1536]{2,1,0:T(8,128)(2,1)} %bitcast.23.refs_15_), calls=%async_computation.1 | async-start | bytes 2359296 | tf_op jit(solution)/shard_map/all_to_all | solution.py:945
  364.9 13.8 %collective-permute-start.35 = (bf16[384,384]{1,0:T(8,128)(2,1)}, bf16[384,384]{1,0:T(8,128)(2,1)}, u32[]{:S(2)}, u32[]{:S(2)}) collective-permute-start(bf16[384,384]{1,0:T(8,128)(2,1)} %get-tuple-element.173.refs_14_), channel_id=1, source_target_pairs={{0,2},{2,0},{1,3},{3,1},{4,6},{6,4},{5,7},{7,5},{8,10},{10,8},{9,1... | collective-permute-start | bytes 884744 | tf_op jit(solution)/shard_map/ppermute | solution.py:877
  366.4 14.0 %collective-permute-start.36 = (bf16[384,384]{1,0:T(8,128)(2,1)}, bf16[384,384]{1,0:T(8,128)(2,1)}, u32[]{:S(2)}, u32[]{:S(2)}) collective-permute-start(bf16[384,384]{1,0:T(8,128)(2,1)} %get-tuple-element.179), channel_id=1, source_target_pairs={{0,4},{4,0},{1,5},{5,1},{2,6},{6,2},{3,7},{7,3},{8,12},{12,8},{9,1... | collective-permute-start | bytes 884744 | tf_op jit(solution)/shard_map/ppermute | solution.py:877
  367.9 20.6 %collective-permute-start.32 = (bf16[1024,768]{1,0:T(8,128)(2,1)}, bf16[1024,768]{1,0:T(8,128)(2,1)}, u32[]{:S(2)}, u32[]{:S(2)}) collective-permute-start(bf16[1024,768]{1,0:T(8,128)(2,1)} %get-tuple-element.164.refs_2_), channel_id=1, source_target_pairs={{0,1},{1,0},{2,3},{3,2},{4,5},{5,4},{6,7},{7,6},{8,9},{9,8},{10,11... | collective-permute-start | bytes 4718600 | tf_op jit(solution)/shard_map/ppermute | solution.py:877
  374.6 45.5 %collective-permute-start.38 = (bf16[2,384,768]{2,1,0:T(8,128)(2,1)}, bf16[2,384,768]{2,1,0:T(8,128)(2,1)}, u32[]{:S(2)}, u32[]{:S(2)}) collective-permute-start(bf16[2,384,768]{2,1,0:T(8,128)(2,1)} %get-tuple-element.169.refs_13_), channel_id=1, source_target_pairs={{0,4},{4,0},{1,5},{5,1},{2,6},{6,2},{3,7},{7,3},{8,12},{12,8},{9,1... | collective-permute-start | bytes 3538952 | tf_op jit(solution)/shard_map/ppermute | solution.py:877
  378.6 41.5 %collective-permute-start.39 = (bf16[2,384,768]{2,1,0:T(8,128)(2,1)}, bf16[2,384,768]{2,1,0:T(8,128)(2,1)}, u32[]{:S(2)}, u32[]{:S(2)}) collective-permute-start(bf16[2,384,768]{2,1,0:T(8,128)(2,1)} %copy-done.43), channel_id=1, source_target_pairs={{0,2},{2,0},{1,3},{3,1},{4,6},{6,4},{5,7},{7,5},{8,10},{10,8},{9,1... | collective-permute-start | bytes 3538952 | tf_op jit(solution)/shard_map/ppermute | solution.py:877
  382.4 72.3 %all-to-all-start.3 = ((bf16[4,96,768]{2,1,0:T(8,128)(2,1)}), bf16[4,96,768]{2,1,0:T(8,128)(2,1)}, u32[]{:S(2)}, u32[]{:S(2)}) async-start(bf16[4,96,768]{2,1,0:T(8,128)(2,1)} %bitcast.26.refs_0_), calls=%async_computation.3 | async-start | bytes 1179648 | tf_op jit(solution)/shard_map/all_to_all | solution.py:945
  423.4 17.4 %collective-permute-start.41 = (bf16[384,768]{1,0:T(8,128)(2,1)}, bf16[384,768]{1,0:T(8,128)(2,1)}, u32[]{:S(2)}, u32[]{:S(2)}) collective-permute-start(bf16[384,768]{1,0:T(8,128)(2,1)} %get-tuple-element.187.refs_8_), channel_id=1, source_target_pairs={{0,2},{2,0},{1,3},{3,1},{4,6},{6,4},{5,7},{7,5},{8,10},{10,8},{9,1... | collective-permute-start | bytes 1769480 | tf_op jit(solution)/shard_map/ppermute | solution.py:877
  423.9 20.0 %collective-permute-start.42 = (bf16[384,768]{1,0:T(8,128)(2,1)}, bf16[384,768]{1,0:T(8,128)(2,1)}, u32[]{:S(2)}, u32[]{:S(2)}) collective-permute-start(bf16[384,768]{1,0:T(8,128)(2,1)} %get-tuple-element.192), channel_id=1, source_target_pairs={{0,4},{4,0},{1,5},{5,1},{2,6},{6,2},{3,7},{7,3},{8,12},{12,8},{9,1... | collective-permute-start | bytes 1769480 | tf_op jit(solution)/shard_map/ppermute | solution.py:877
  433.8 12.9 %collective-permute-start.40 = (bf16[1024,768]{1,0:T(8,128)(2,1)}, bf16[1024,768]{1,0:T(8,128)(2,1)}, u32[]{:S(2)}, u32[]{:S(2)}) collective-permute-start(bf16[1024,768]{1,0:T(8,128)(2,1)} %get-tuple-element.190.refs_2_), channel_id=1, source_target_pairs={{0,1},{1,0},{2,3},{3,2},{4,5},{5,4},{6,7},{7,6},{8,9},{9,8},{10,11... | collective-permute-start | bytes 4718600 | tf_op jit(solution)/shard_map/ppermute | solution.py:877
  440.1 26.5 %collective-permute-start.43 = (bf16[2,384,384]{2,1,0:T(8,128)(2,1)}, bf16[2,384,384]{2,1,0:T(8,128)(2,1)S(1)}, u32[]{:S(2)}, u32[]{:S(2)}) collective-permute-start(bf16[2,384,384]{2,1,0:T(8,128)(2,1)} %copy-done.45), channel_id=1, source_target_pairs={{0,4},{4,0},{1,5},{5,1},{2,6},{6,2},{3,7},{7,3},{8,12},{12,8},{9,1... | collective-permute-start | bytes 1769480 | tf_op jit(solution)/shard_map/ppermute | solution.py:877
  440.8 25.8 %collective-permute-start.44 = (bf16[2,384,384]{2,1,0:T(8,128)(2,1)}, bf16[2,384,384]{2,1,0:T(8,128)(2,1)}, u32[]{:S(2)}, u32[]{:S(2)}) collective-permute-start(bf16[2,384,384]{2,1,0:T(8,128)(2,1)} %copy-done.44), channel_id=1, source_target_pairs={{0,2},{2,0},{1,3},{3,1},{4,6},{6,4},{5,7},{7,5},{8,10},{10,8},{9,1... | collective-permute-start | bytes 1769480 | tf_op jit(solution)/shard_map/ppermute | solution.py:877
  454.1 15.1 %collective-permute-start.48 = (f32[11520]{0:T(1024)S(1)}, f32[11520]{0:T(1024)S(1)}, u32[]{:S(2)}, u32[]{:S(2)}) collective-permute-start(f32[11520]{0:T(1024)S(1)} %pad_maximum_fusion.8), channel_id=1, source_target_pairs={{0,2},{2,0},{1,3},{3,1},{4,6},{6,4},{5,7},{7,5},{8,10},{10,8},{9,1... | collective-permute-start | bytes 138248 | tf_op jit(solution)/shard_map/ppermute | solution.py:877
  454.7 34.3 %all-to-all-start.4 = ((bf16[4,96,1536]{2,1,0:T(8,128)(2,1)}), bf16[4,96,1536]{2,1,0:T(8,128)(2,1)}, u32[]{:S(2)}, u32[]{:S(2)}) async-start(bf16[4,96,1536]{2,1,0:T(8,128)(2,1)} %bitcast.29.refs_6_), calls=%async_computation.4 | async-start | bytes 2359296 | tf_op jit(solution)/shard_map/all_to_all | solution.py:945
  467.7 16.5 %collective-permute-start.46 = (bf16[384,384]{1,0:T(8,128)(2,1)S(1)}, bf16[384,384]{1,0:T(8,128)(2,1)S(1)}, u32[]{:S(2)}, u32[]{:S(2)}) collective-permute-start(bf16[384,384]{1,0:T(8,128)(2,1)S(1)} %get-tuple-element.197.refs_0_), channel_id=1, source_target_pairs={{0,2},{2,0},{1,3},{3,1},{4,6},{6,4},{5,7},{7,5},{8,10},{10,8},{9,1... | collective-permute-start | bytes 884744 | tf_op jit(solution)/shard_map/ppermute | solution.py:877
  476.8 37.3 %collective-permute-start.45 = (bf16[1024,768]{1,0:T(8,128)(2,1)}, bf16[1024,768]{1,0:T(8,128)(2,1)}, u32[]{:S(2)}, u32[]{:S(2)}) collective-permute-start(bf16[1024,768]{1,0:T(8,128)(2,1)} %get-tuple-element.193.refs_4_.refs_0_.own_ref), channel_id=1, source_target_pairs={{0,2},{2,0},{1,3},{3,1},{4,6},{6,4},{5,7},{7,5},{8,10},{10,8},{9,1... | collective-permute-start | bytes 4718600 | tf_op jit(solution)/shard_map/ppermute | solution.py:877
  479.0 21.2 %collective-permute-start.51 = (f32[11520]{0:T(1024)S(1)}, f32[11520]{0:T(1024)S(1)}, u32[]{:S(2)}, u32[]{:S(2)}) collective-permute-start(f32[11520]{0:T(1024)S(1)} %add.337), channel_id=1, source_target_pairs={{0,16},{8,24},{16,0},{24,8},{1,17},{9,25},{17,1},{25,9},{2,18},{10... | collective-permute-start | bytes 138248 | tf_op jit(solution)/shard_map/ppermute | solution.py:928
  489.0 19.1 %all-to-all-start.2 = ((bf16[4,96,768]{2,1,0:T(8,128)(2,1)}), bf16[4,96,768]{2,1,0:T(8,128)(2,1)}, u32[]{:S(2)}, u32[]{:S(2)}) async-start(bf16[4,96,768]{2,1,0:T(8,128)(2,1)} %bitcast.129), calls=%async_computation.2 | async-start | bytes 1179648 | tf_op jit(solution)/shard_map/all_to_all | solution.py:945
  (114 other events, 941.2 us)
Sparse Core Ops, SparseCore 0:
  35.3 78.8 all-gather.2
  121.4 79.2 all-gather.4

commit v6 on v5

--- a/solution.py
+++ b/solution.py
@@ -563,22 +563,27 @@
         for head in range(heads):
             lanes_q, lanes_k, lanes_v = (head_lanes(kind, head, heads) for kind in range(3))
             query = qkv_ref[0, rows, lanes_q] * HEAD_DIM ** (-0.5)
-            keys = (tile + 1) * QT
+            scores = []
+            values = []
+            for part in range(tile + 1):
+                keys = slice(part * QT, (part + 1) * QT)
+                score = dot(qkv_ref[0, keys, lanes_k], query, NT)
+                if part == tile:
+                    score = jnp.where(causal(score.shape), score, MASKED)
+                scores.append(score)
+                values.append(qkv_ref[0, keys, lanes_v])
             memory_key = rows_ref[side, segment, :, head_lanes(0, head, heads)]
-            memory_value = rows_ref[side, segment, :, head_lanes(1, head, heads)]
-            all_keys = jnp.concatenate([qkv_ref[0, :keys, lanes_k], memory_key], axis=0)
-            all_values = jnp.concatenate([qkv_ref[0, :keys, lanes_v], memory_value], axis=0)
-            score = dot(all_keys, query, NT)
-            parts = [score[:keys - QT]] if tile else []
-            parts.append(jnp.where(causal((QT, QT)), score[keys - QT : keys], MASKED))
-            parts.append(score[keys:] + memory_bias)
-            top = parts[0].max(axis=0, keepdims=True)
-            for part in parts[1:]:
-                top = jnp.maximum(top, part.max(axis=0, keepdims=True))
-            weights = [jnp.exp(part - top) for part in parts]
-            total = sum(weight.sum(axis=0, keepdims=True) for weight in weights)
-            weights = jnp.concatenate([weight.astype(BF16) for weight in weights], axis=0)
-            result = dot(all_values, weights, TN)
+            scores.append(dot(memory_key, query, NT) + memory_bias)
+            values.append(rows_ref[side, segment, :, head_lanes(1, head, heads)])
+            top = scores[0].max(axis=0, keepdims=True)
+            for score in scores[1:]:
+                top = jnp.maximum(top, score.max(axis=0, keepdims=True))
+            total = jnp.zeros_like(top)
+            result = jnp.zeros((HEAD_DIM, QT), F32)
+            for score, value in zip(scores, values):
+                weight = jnp.exp(score - top)
+                total = total + weight.sum(axis=0, keepdims=True)
+                result = result + dot(value, weight.astype(BF16), TN)
             stacked.append(result / total)
             lse_ref[0, 0, head : head + 1, rows] = top + jnp.log(total)
         out_ref[0, rows, :] = jnp.concatenate(stacked, axis=0).T.astype(BF16)

time: 560 us -> 556 us (level)
  no operation moved by 1% of the time
where the time goes in v6:
time: 556 us; the launch traced here: 547 us
  Pallas kernels  255 us (46%)
  waiting for transfers between devices  89.7 us (16%)
  starting transfers between devices  80.9 us (15%)
  local copies, waits for them, and re-layouts  56.8 us (10%)
  other arithmetic  36.3 us (7%)
  between operations  25.6 us (5%)
    pallas_call x9, Pallas kernels, rows_call(): pl.pallas_call(body, grid_spec=pltpu.PrefetchScalarGridSpec(num_scalar_pr...  96.3 us
    ppermute x46, waiting for transfers between devices, flip(): return lax.ppermute(array, axis, SWAP)  76 us
    pallas_call x8, Pallas kernels, weight_grads(): pl.pallas_call(partial(weight_grads_kernel, plan), in_specs=[vmem] * len(...  38.8 us
    ppermute x46, starting transfers between devices, flip(): return lax.ppermute(array, axis, SWAP)  38.5 us
    unnamed x211, local copies, waits for them, and re-layouts  34.5 us
    pallas_call x2, Pallas kernels, attention_forward(): pl.pallas_call(attention_forward_kernel, grid_spec=pltpu.PrefetchScalarGr...  33.9 us
    pallas_call x2, Pallas kernels, attention_backward(): pl.pallas_call(attention_backward_kernel, grid=(2, segs), in_specs=[pl.Bl...  29.4 us
    all_to_all x4, starting transfers between devices, spread_pieces(): return lax.all_to_all(pieces, 'tz', 0, 0, tiled=True)  18.9 us
  transfers between devices with their start and end apart: 60, of which 15 were waited for; matrix products, arithmetic and copies ran while one was open for 9% of the time, Pallas kernels for 42%

profile of v6, /device:TPU:0, one launch (start us, length us, event | category | flops | bytes accessed | tf_op | source)
XLA Modules:
  0.0 546.9 jit_solution(9629213761616651069)
XLA Ops:
  9.5 3.1 collective-permute-start
  16.3 5.2 all-to-all-start
  27.3 5.2 collective-permute-done.1.refs_2_
  47.2 11.8 %shard_map.393 = bf16[256,768]{1,0:T(8,128)(2,1)S(1)} custom-call(f32[256,256]{1,0:T(8,128)S(1)} %copy-done.33, f32[256,768]{1,0:T(8,128)S(1)} %copy-done.10, bf16[384,384]{1,0:T(8,128)(2,1)} %get-tuple-element.116.refs_0_.refs_4_.refs_2_.refs_5_), custom_call_target="tpu_custom_call" | custom-call | flops 15399999488 | bytes 1000000 | tf_op jit(solution)/shard_map/pallas_call | solution.py:108
  72.4 3.3 collective-permute-done.8.refs_10_.refs_2_.refs_11_.refs_6_
  80.5 12.7 %collective-permute-done.7.refs_9_.refs_1_.refs_10_.refs_5_ = bf16[384,384]{1,0:T(8,128)(2,1)S(1)} collective-permute-done((bf16[384,384]{1,0:T(8,128)(2,1)}, bf16[384,384]{1,0:T(8,128)(2,1)S(1)}, u32[]{:S(2)}, u32[]{:S(2)}) %collective-permute-start.7) | collective-permute-done | bytes 294944 | tf_op jit(solution)/shard_map/ppermute | solution.py:882
  94.6 5.1 collective-permute-done.6.refs_7_.refs_8_.refs_3_
  102.4 3.4 collective-permute-done.9.refs_11_.refs_3_.refs_12_.refs_7_
  106.5 11.5 %shard_map.396 = (f32[1024,768]{1,0:T(8,128)}, bf16[1024,768]{1,0:T(8,128)(2,1)}, bf16[2,1024,576]{2,1,0:T(8,128)(2,1)}, f32[2,256,384]{2,1,0:T(8,128)S(1)}, bf16[2,256,384]{2,1,0:T(8,128)(2,1)}) custom-call(s32[2]{0:T(128)S(1)} %pad_add_fusion.place_ref.context_ref, bf16[1024,768]{1,0:T(8,128)(2,1)} %constant_dynamic-slice_fusion.1.refs_0_, ...), custom_call_target="tpu_custom_call" | custom-call | flops 7699999744 | bytes 1000000 | tf_op jit(solution)/shard_map/pallas_call | solution.py:325
  121.3 17.1 %collective-permute-done.14.got_ref = bf16[2,256,384]{2,1,0:T(8,128)(2,1)} collective-permute-done((bf16[2,256,384]{2,1,0:T(8,128)(2,1)}, bf16[2,256,384]{2,1,0:T(8,128)(2,1)}, u32[]{:S(2)}, u32[]{:S(2)}) %collective-permute-start.14) | collective-permute-done | bytes 393248 | tf_op jit(solution)/shard_map/ppermute | solution.py:882
  140.6 16.8 %shard_map.397 = (bf16[2,1024,192]{2,1,0:T(8,128)(2,1)}, f32[2,2,3,512]{3,2,1,0:T(4,128)}, bf16[2,2,256,384]{3,2,1,0:T(8,128)(2,1)}, bf16[1024,768]{1,0:T(8,128)(2,1)}) custom-call(s32[2]{0:T(128)S(1)} %pad_add_fusion.place_ref.context_ref, f32[2]{0:T(128)S(1)} %pad_maximum_fusion.16.bias_ref, bf16[2,1024,576]{2,1,0:T(8,128)(2,1)} %get-tuple-element.121.qkv_ref, ...), custom_call_target="tpu_custom_call" | custom-call | flops 14300000256 | bytes 1000000 | tf_op jit(solution)/shard_map/pallas_call | solution.py:616
  157.9 3.2 collective-permute-done.19.refs_2_
  161.2 13.7 %shard_map.398 = (f32[1024,768]{1,0:T(8,128)}, bf16[1024,768]{1,0:T(8,128)(2,1)}, bf16[2,1024,768]{2,1,0:T(8,128)(2,1)}, bf16[2,1024,768]{2,1,0:T(8,128)(2,1)}, bf16[1024,768]{1,0:T(8,128)(2,1)}) custom-call(s32[2]{0:T(128)S(1)} %pad_add_fusion.place_ref.context_ref, f32[1024,768]{1,0:T(8,128)} %get-tuple-element.120.refs_0_.refs_1_, ...), custom_call_target="tpu_custom_call" | custom-call | flops 12099999744 | bytes 1000000 | tf_op jit(solution)/shard_map/pallas_call | solution.py:325
  175.0 3.6 collective-permute-done.20.refs_2_
  178.6 10.9 %shard_map.400 = (f32[1024,768]{1,0:T(8,128)}, bf16[1024,768]{1,0:T(8,128)(2,1)}, bf16[2,1024,576]{2,1,0:T(8,128)(2,1)}, f32[2,256,384]{2,1,0:T(8,128)S(1)}, bf16[2,256,384]{2,1,0:T(8,128)(2,1)S(1)}) custom-call(s32[2]{0:T(128)S(1)} %pad_add_fusion.place_ref.context_ref, f32[1024,768]{1,0:T(8,128)} %get-tuple-element.125.refs_0_.refs_1_, ...), custom_call_target="tpu_custom_call" | custom-call | flops 7699999744 | bytes 1000000 | tf_op jit(solution)/shard_map/pallas_call | solution.py:325
  189.9 10.7 %collective-permute-done.21.got_ref = bf16[2,256,384]{2,1,0:T(8,128)(2,1)S(1)} collective-permute-done((bf16[2,256,384]{2,1,0:T(8,128)(2,1)S(1)}, bf16[2,256,384]{2,1,0:T(8,128)(2,1)S(1)}, u32[]{:S(2)}, u32[]{:S(2)}) %collective-permute-start.21) | collective-permute-done | bytes 393248 | tf_op jit(solution)/shard_map/ppermute | solution.py:882
  200.6 17.1 %shard_map.401 = (bf16[2,1024,192]{2,1,0:T(8,128)(2,1)}, f32[2,2,3,512]{3,2,1,0:T(4,128)}, bf16[2,2,256,384]{3,2,1,0:T(8,128)(2,1)}, bf16[1024,768]{1,0:T(8,128)(2,1)S(1)}) custom-call(s32[2]{0:T(128)S(1)} %pad_add_fusion.place_ref.context_ref, f32[2]{0:T(128)S(1)} %pad_maximum_fusion.16.bias_ref, bf16[2,1024,576]{2,1,0:T(8,128)(2,1)} %get-tuple-element.128.qkv_ref, ...), custom_call_target="tpu_custom_call" | custom-call | flops 14300000256 | bytes 1000000 | tf_op jit(solution)/shard_map/pallas_call | solution.py:616
  225.2 12.8 %shard_map.403 = (f32[1024,768]{1,0:T(8,128)}, bf16[1024,768]{1,0:T(8,128)(2,1)}, bf16[2,1024,768]{2,1,0:T(8,128)(2,1)}, bf16[2,1024,768]{2,1,0:T(8,128)(2,1)}, bf16[1024,768]{1,0:T(8,128)(2,1)S(1)}) custom-call(s32[2]{0:T(128)S(1)} %pad_add_fusion.place_ref.context_ref, f32[1024,768]{1,0:T(8,128)} %get-tuple-element.127.refs_0_.refs_1_, ...), custom_call_target="tpu_custom_call" | custom-call | flops 12099999744 | bytes 1000000 | tf_op jit(solution)/shard_map/pallas_call | solution.py:325
  238.0 13.1 %shard_map.404 = (f32[1024,768]{1,0:T(8,128)S(1)}, bf16[1024,768]{1,0:T(8,128)(2,1)S(1)}, bf16[2,1024,768]{2,1,0:T(8,128)(2,1)S(1)}, bf16[1024,768]{1,0:T(8,128)(2,1)}, f32[8,768]{1,0:T(8,128)S(1)}) custom-call(s32[2]{0:T(128)S(1)} %pad_add_fusion.place_ref.context_ref, bf16[1024,768]{1,0:T(8,128)(2,1)} %constant_dynamic-slice_fusion.refs_0_, ...), custom_call_target="tpu_custom_call" | custom-call | flops 9900000256 | bytes 1000000 | tf_op jit(solution)/shard_map/pallas_call | solution.py:325
  253.0 7.6 %shard_map.405 = (bf16[2,384,768]{2,1,0:T(8,128)(2,1)}, bf16[2,384,768]{2,1,0:T(8,128)(2,1)}) custom-call(bf16[1024,768]{1,0:T(8,128)(2,1)} %get-tuple-element.138.refs_0_, bf16[1024,768]{1,0:T(8,128)(2,1)S(1)} %get-tuple-element.139.refs_1_, bf16[2,1024,768]{2,1,0:T(8,128)(2,1)S(1)} %get-tuple-element.140.refs_2_, ...), custom_call_target="tpu_custom_call" | custom-call | flops 6600000000 | bytes 1000000 | tf_op jit(solution)/shard_map/pallas_call | solution.py:865
  265.5 7.3 %shard_map.406 = (f32[1024,768]{1,0:T(8,128)S(1)}, bf16[1024,768]{1,0:T(8,128)(2,1)S(1)}, bf16[2,1024,192]{2,1,0:T(8,128)(2,1)S(1)}, f32[8,768]{1,0:T(8,128)S(1)}) custom-call(s32[2]{0:T(128)S(1)} %pad_add_fusion.place_ref.context_ref, f32[1024,768]{1,0:T(8,128)S(1)} %copy-done.52, f32[1024,768]{1,0:T(8,128)} %get-tuple-element.132.refs_1_, ...), custom_call_target="tpu_custom_call" | custom-call | flops 6600000000 | bytes 1000000 | tf_op jit(solution)/shard_map/pallas_call | solution.py:325
  272.8 15.2 %shard_map.407 = (bf16[2,1024,192]{2,1,0:T(8,128)(2,1)S(1)}, f32[2,1024,384]{2,1,0:T(8,128)S(1)}, f32[2,256,384]{2,1,0:T(8,128)S(1)}, bf16[2,256,384]{2,1,0:T(8,128)(2,1)S(1)}) custom-call(f32[2]{0:T(128)S(1)} %pad_maximum_fusion.16.bias_ref, bf16[2,1024,576]{2,1,0:T(8,128)(2,1)} %get-tuple-element.128.qkv_ref, ...), custom_call_target="tpu_custom_call" | custom-call | flops 19800000512 | bytes 1000000 | tf_op jit(solution)/shard_map/pallas_call | solution.py:739
  289.7 5.0 shard_map.408
  300.9 8.4 %shard_map.410 = (bf16[2,1024,576]{2,1,0:T(8,128)(2,1)S(1)}, bf16[1024,768]{1,0:T(8,128)(2,1)}, f32[8,576]{1,0:T(8,128)S(1)}) custom-call(s32[2]{0:T(128)S(1)} %pad_add_fusion.place_ref.context_ref, bf16[2,1024,192]{2,1,0:T(8,128)(2,1)S(1)} %get-tuple-element.148.refs_4_.refs_0_.dq_ref, f32[2,1024,384]{2,1,0:T(8,128)S(1)} %get-tuple-element.149.dkv_ref, ...), custom_call_target="tpu_custom_call" | custom-call | flops 5500000256 | bytes 1000000 | tf_op jit(solution)/shard_map/pallas_call | solution.py:818
  309.3 3.7 shard_map.414
  313.8 4.5 shard_map.411
  323.3 4.7 all-to-all-start.1
  329.9 13.8 %shard_map.412 = (f32[1024,768]{1,0:T(8,128)S(1)}, bf16[1024,768]{1,0:T(8,128)(2,1)S(1)}, bf16[2,1024,768]{2,1,0:T(8,128)(2,1)S(1)}, bf16[1024,768]{1,0:T(8,128)(2,1)}, f32[8,768]{1,0:T(8,128)S(1)}) custom-call(s32[2]{0:T(128)S(1)} %pad_add_fusion.place_ref.context_ref, f32[1024,768]{1,0:T(8,128)S(1)} %copy-done.50, ...), custom_call_target="tpu_custom_call" | custom-call | flops 9900000256 | bytes 1000000 | tf_op jit(solution)/shard_map/pallas_call | solution.py:325
  343.7 15.0 %collective-permute-done.34.got_b_ref = bf16[2,384,384]{2,1,0:T(8,128)(2,1)} collective-permute-done((bf16[2,384,384]{2,1,0:T(8,128)(2,1)}, bf16[2,384,384]{2,1,0:T(8,128)(2,1)}, u32[]{:S(2)}, u32[]{:S(2)}) %collective-permute-start.34) | collective-permute-done | bytes 589856 | tf_op jit(solution)/shard_map/ppermute | solution.py:882
  364.3 5.0 shard_map.413
  378.2 5.0 all-to-all-start.3
  386.2 7.3 %shard_map.416 = (f32[1024,768]{1,0:T(8,128)S(1)}, bf16[1024,768]{1,0:T(8,128)(2,1)S(1)}, bf16[2,1024,192]{2,1,0:T(8,128)(2,1)S(1)}, f32[8,768]{1,0:T(8,128)S(1)}) custom-call(s32[2]{0:T(128)S(1)} %pad_add_fusion.place_ref.context_ref, f32[1024,768]{1,0:T(8,128)S(1)} %copy-done.58, f32[1024,768]{1,0:T(8,128)} %get-tuple-element.125.refs_0_.refs_1_, ...), custom_call_target="tpu_custom_call" | custom-call | flops 6600000000 | bytes 1000000 | tf_op jit(solution)/shard_map/pallas_call | solution.py:325
  395.2 14.2 %shard_map.417 = (bf16[2,1024,192]{2,1,0:T(8,128)(2,1)S(1)}, f32[2,1024,384]{2,1,0:T(8,128)S(1)}, f32[2,256,384]{2,1,0:T(8,128)S(1)}, bf16[2,256,384]{2,1,0:T(8,128)(2,1)S(1)}) custom-call(f32[2]{0:T(128)S(1)} %pad_maximum_fusion.16.bias_ref, bf16[2,1024,576]{2,1,0:T(8,128)(2,1)} %get-tuple-element.121.qkv_ref, ...), custom_call_target="tpu_custom_call" | custom-call | flops 19800000512 | bytes 1000000 | tf_op jit(solution)/shard_map/pallas_call | solution.py:739
  410.9 5.0 shard_map.418
  416.0 3.2 shard_map.419
  421.1 8.6 %shard_map.420 = (bf16[2,1024,576]{2,1,0:T(8,128)(2,1)S(1)}, bf16[1024,768]{1,0:T(8,128)(2,1)}, f32[8,576]{1,0:T(8,128)S(1)}) custom-call(s32[2]{0:T(128)S(1)} %pad_add_fusion.place_ref.context_ref, bf16[2,1024,192]{2,1,0:T(8,128)(2,1)S(1)} %get-tuple-element.180.refs_4_.refs_0_.dq_ref, f32[2,1024,384]{2,1,0:T(8,128)S(1)} %get-tuple-element.181.dkv_ref, ...), custom_call_target="tpu_custom_call" | custom-call | flops 5500000256 | bytes 1000000 | tf_op jit(solution)/shard_map/pallas_call | solution.py:818
  429.8 4.5 shard_map.421
  442.8 5.9 %shard_map.422 = (bf16[1024,768]{1,0:T(8,128)(2,1)}, f32[8,768]{1,0:T(8,128)S(1)}) custom-call(s32[2]{0:T(128)S(1)} %pad_add_fusion.place_ref.context_ref, f32[1024,768]{1,0:T(8,128)S(1)} %copy-done.54, f32[1024,768]{1,0:T(8,128)} %get-tuple-element.120.refs_0_.refs_1_, bf16[1024,768]{1,0:T(8,128)(2,1)} %get-tuple-element.190.refs_2_, ...), custom_call_target="tpu_custom_call" | custom-call | flops 5500000256 | bytes 1000000 | tf_op jit(solution)/shard_map/pallas_call | solution.py:325
  450.5 5.1 all-to-all-start.4
  458.8 3.6 shard_map.423
  474.8 5.2 collective-permute-start.51
  482.2 2.6 all-to-all-done.4
  484.8 4.2 all-to-all-start.2
  489.0 6.5 %shard_map.425 = (f32[2048,768]{1,0:T(8,128)}, f32[8,128]{1,0:T(8,128)S(1)}) custom-call(s32[2]{0:T(128)S(1)} %pad_add_fusion.place_ref.context_ref, bf16[1024,768]{1,0:T(8,128)(2,1)S(1)} %add_convert_fusion.own_ref, bf16[1024,768]{1,0:T(8,128)(2,1)} %collective-permute-done.24.got_ref, bf16[768,768]{1,0:T(8,128)(2,1)S(1)} %copy-done.8, ...), custom_call_target="tpu_custom_call" | custom-call | flops 4400000000 | bytes 1000000 | tf_op jit(solution)/shard_map/pallas_call | solution.py:500
  500.9 3.0 all-to-all-done.2
  513.0 3.8 all-to-all-start.5
  516.8 7.5 %shard_map.426 = (f32[2048,768]{1,0:T(8,128)}, f32[8,128]{1,0:T(8,128)}) custom-call(s32[2]{0:T(128)S(1)} %pad_add_fusion.place_ref.context_ref, bf16[1024,768]{1,0:T(8,128)(2,1)} %get-tuple-element.193.refs_4_.refs_0_.own_ref, bf16[1024,768]{1,0:T(8,128)(2,1)} %collective-permute-done.45.got_ref._, bf16[768,768]{1,0:T(8,128)(2,1)S(1)} %copy-done.8), custom_call_target="tpu_custom_call" | custom-call | flops 4400000000 | bytes 1000000 | tf_op jit(solution)/shard_map/pallas_call | solution.py:500
  531.1 2.8 divide_subtract_fusion
  (427 shorter events, 153.0 us)
Async XLA Ops:
  9.5 17.8 %collective-permute-start = (bf16[96,768]{1,0:T(8,128)(2,1)S(1)}, bf16[96,768]{1,0:T(8,128)(2,1)S(1)}, u32[]{:S(2)}, u32[]{:S(2)}) collective-permute-start(bf16[96,768]{1,0:T(8,128)(2,1)S(1)} %shard_map.391.refs_0_.refs_2_), channel_id=1, source_target_pairs={{0,8},{8,0},{16,24},{24,16},{1,9},{9,1},{17,25},{25,17},{2,10},{10... | collective-permute-start | bytes 442376 | tf_op jit(solution)/shard_map/ppermute | solution.py:933
  12.5 19.9 %collective-permute-start.1 = (bf16[96,768]{1,0:T(8,128)(2,1)S(1)}, bf16[96,768]{1,0:T(8,128)(2,1)}, u32[]{:S(2)}, u32[]{:S(2)}) collective-permute-start(bf16[96,768]{1,0:T(8,128)(2,1)S(1)} %shard_map.391.refs_0_.refs_2_), channel_id=1, source_target_pairs={{0,16},{8,24},{16,0},{24,8},{1,17},{9,25},{17,1},{25,9},{2,18},{10... | collective-permute-start | bytes 442376 | tf_op jit(solution)/shard_map/ppermute | solution.py:933
  15.1 17.3 %collective-permute-start.2 = (bf16[96,768]{1,0:T(8,128)(2,1)S(1)}, bf16[96,768]{1,0:T(8,128)(2,1)}, u32[]{:S(2)}, u32[]{:S(2)}) collective-permute-start(bf16[96,768]{1,0:T(8,128)(2,1)S(1)} %shard_map.391.refs_0_.refs_2_), channel_id=1, source_target_pairs={{0,24},{8,16},{16,8},{24,0},{1,25},{9,17},{17,9},{25,1},{2,26},{10... | collective-permute-start | bytes 442376 | tf_op jit(solution)/shard_map/ppermute | solution.py:933
  16.3 47.7 %all-to-all-start = ((bf16[4,96,1536]{2,1,0:T(8,128)(2,1)}), bf16[4,96,1536]{2,1,0:T(8,128)(2,1)}, u32[]{:S(2)}, u32[]{:S(2)}) async-start(bf16[4,96,1536]{2,1,0:T(8,128)(2,1)} %broadcast_in_dim.29), calls=%async_computation | async-start | bytes 2359296 | tf_op jit(solution)/shard_map/all_to_all | solution.py:896
  21.5 153.5 %all-gather.3.cloned.1.call-start = ((), (), s32[]{:S(2)}) async-start(), calls=%async_computation.6 | async-start | bytes 2506752 | tf_op jit(solution)/shard_map/all_gather | solution.py:889
  23.4 42.9 %collective-permute-start.11 = (bf16[2,256,384]{2,1,0:T(8,128)(2,1)}, bf16[2,256,384]{2,1,0:T(8,128)(2,1)}, u32[]{:S(2)}, u32[]{:S(2)}) collective-permute-start(bf16[2,256,384]{2,1,0:T(8,128)(2,1)} %copy.129), channel_id=1, source_target_pairs={{0,2},{2,0},{1,3},{3,1},{4,6},{6,4},{5,7},{7,5},{8,10},{10,8},{9,1... | collective-permute-start | bytes 1179656 | tf_op jit(solution)/shard_map/ppermute | solution.py:882
  24.9 16.3 %collective-permute-start.3 = (f32[2,6,192]{2,0,1:T(2,128)}, f32[2,6,192]{2,0,1:T(2,128)}, u32[]{:S(2)}, u32[]{:S(2)}) collective-permute-start(f32[2,6,192]{2,0,1:T(2,128)} %param.45), channel_id=1, source_target_pairs={{0,2},{2,0},{1,3},{3,1},{4,6},{6,4},{5,7},{7,5},{8,10},{10,8},{9,1... | collective-permute-start | bytes 27656 | tf_op jit(solution)/shard_map/ppermute | solution.py:882
  35.2 187.2 %all-gather.5.cloned.1.call-start = ((), (), s32[]{:S(2)}) async-start(), calls=%async_computation.7 | async-start | bytes 5013504 | tf_op jit(solution)/shard_map/all_gather | solution.py:889
  42.0 24.8 %collective-permute-start.4 = (bf16[384,384]{1,0:T(8,128)(2,1)}, bf16[384,384]{1,0:T(8,128)(2,1)}, u32[]{:S(2)}, u32[]{:S(2)}) collective-permute-start(bf16[384,384]{1,0:T(8,128)(2,1)} %get-tuple-element.116.refs_0_.refs_4_.refs_2_.refs_5_), channel_id=1, source_target_pairs={{0,4},{4,0},{1,5},{5,1},{2,6},{6,2},{3,7},{7,3},{8,12},{12,8},{9,1... | collective-permute-start | bytes 884744 | tf_op jit(solution)/shard_map/ppermute | solution.py:882
  43.6 32.6 %collective-permute-start.5 = (bf16[384,384]{1,0:T(8,128)(2,1)}, bf16[384,384]{1,0:T(8,128)(2,1)}, u32[]{:S(2)}, u32[]{:S(2)}) collective-permute-start(bf16[384,384]{1,0:T(8,128)(2,1)} %get-tuple-element.116.refs_0_.refs_4_.refs_2_.refs_5_), channel_id=1, source_target_pairs={{0,2},{2,0},{1,3},{3,1},{4,6},{6,4},{5,7},{7,5},{8,10},{10,8},{9,1... | collective-permute-start | bytes 884744 | tf_op jit(solution)/shard_map/ppermute | solution.py:882
  59.1 17.6 %collective-permute-start.10 = (bf16[256,768]{1,0:T(8,128)(2,1)S(1)}, bf16[256,768]{1,0:T(8,128)(2,1)}, u32[]{:S(2)}, u32[]{:S(2)}) collective-permute-start(bf16[256,768]{1,0:T(8,128)(2,1)S(1)} %shard_map.393), channel_id=1, source_target_pairs={{0,1},{1,0},{2,3},{3,2},{4,5},{5,4},{6,7},{7,6},{8,9},{9,8},{10,11... | collective-permute-start | bytes 1179656 | tf_op jit(solution)/shard_map/ppermute | solution.py:882
  66.3 33.4 %collective-permute-start.12 = (bf16[384,768]{1,0:T(8,128)(2,1)}, bf16[384,768]{1,0:T(8,128)(2,1)}, u32[]{:S(2)}, u32[]{:S(2)}) collective-permute-start(bf16[384,768]{1,0:T(8,128)(2,1)} %get-tuple-element.118.refs_5_.refs_2_.refs_6_), channel_id=1, source_target_pairs={{0,4},{4,0},{1,5},{5,1},{2,6},{6,2},{3,7},{7,3},{8,12},{12,8},{9,1... | collective-permute-start | bytes 1769480 | tf_op jit(solution)/shard_map/ppermute | solution.py:882
  66.8 33.6 %collective-permute-start.13 = (bf16[384,768]{1,0:T(8,128)(2,1)}, bf16[384,768]{1,0:T(8,128)(2,1)}, u32[]{:S(2)}, u32[]{:S(2)}) collective-permute-start(bf16[384,768]{1,0:T(8,128)(2,1)} %get-tuple-element.119.refs_9_.refs_10_), channel_id=1, source_target_pairs={{0,2},{2,0},{1,3},{3,1},{4,6},{6,4},{5,7},{7,5},{8,10},{10,8},{9,1... | collective-permute-start | bytes 1769480 | tf_op jit(solution)/shard_map/ppermute | solution.py:882
  75.7 17.5 %collective-permute-start.7 = (bf16[384,384]{1,0:T(8,128)(2,1)}, bf16[384,384]{1,0:T(8,128)(2,1)S(1)}, u32[]{:S(2)}, u32[]{:S(2)}) collective-permute-start(bf16[384,384]{1,0:T(8,128)(2,1)} %get-tuple-element.117.refs_8_.refs_0_.refs_9_.refs_4_), channel_id=1, source_target_pairs={{0,4},{4,0},{1,5},{5,1},{2,6},{6,2},{3,7},{7,3},{8,12},{12,8},{9,1... | collective-permute-start | bytes 884744 | tf_op jit(solution)/shard_map/ppermute | solution.py:882
  76.2 23.5 %collective-permute-start.6 = (bf16[384,384]{1,0:T(8,128)(2,1)}, bf16[384,384]{1,0:T(8,128)(2,1)S(1)}, u32[]{:S(2)}, u32[]{:S(2)}) collective-permute-start(bf16[384,384]{1,0:T(8,128)(2,1)} %collective-permute-done.4.refs_5_.refs_6_.refs_1_), channel_id=1, source_target_pairs={{0,2},{2,0},{1,3},{3,1},{4,6},{6,4},{5,7},{7,5},{8,10},{10,8},{9,1... | collective-permute-start | bytes 884744 | tf_op jit(solution)/shard_map/ppermute | solution.py:882
  76.7 29.1 %collective-permute-start.9 = (bf16[384,384]{1,0:T(8,128)(2,1)}, bf16[384,384]{1,0:T(8,128)(2,1)S(1)}, u32[]{:S(2)}, u32[]{:S(2)}) collective-permute-start(bf16[384,384]{1,0:T(8,128)(2,1)} %collective-permute-done.8.refs_10_.refs_2_.refs_11_.refs_6_), channel_id=1, source_target_pairs={{0,4},{4,0},{1,5},{5,1},{2,6},{6,2},{3,7},{7,3},{8,12},{12,8},{9,1... | collective-permute-start | bytes 884744 | tf_op jit(solution)/shard_map/ppermute | solution.py:882
  93.2 28.2 %collective-permute-start.15 = (bf16[384,768]{1,0:T(8,128)(2,1)}, bf16[384,768]{1,0:T(8,128)(2,1)}, u32[]{:S(2)}, u32[]{:S(2)}) collective-permute-start(bf16[384,768]{1,0:T(8,128)(2,1)} %get-tuple-element.118.refs_5_.refs_2_.refs_6_), channel_id=1, source_target_pairs={{0,2},{2,0},{1,3},{3,1},{4,6},{6,4},{5,7},{7,5},{8,10},{10,8},{9,1... | collective-permute-start | bytes 1769480 | tf_op jit(solution)/shard_map/ppermute | solution.py:882
  99.7 21.6 %collective-permute-start.17 = (bf16[384,768]{1,0:T(8,128)(2,1)}, bf16[384,768]{1,0:T(8,128)(2,1)}, u32[]{:S(2)}, u32[]{:S(2)}) collective-permute-start(bf16[384,768]{1,0:T(8,128)(2,1)} %get-tuple-element.119.refs_9_.refs_10_), channel_id=1, source_target_pairs={{0,4},{4,0},{1,5},{5,1},{2,6},{6,2},{3,7},{7,3},{8,12},{12,8},{9,1... | collective-permute-start | bytes 1769480 | tf_op jit(solution)/shard_map/ppermute | solution.py:882
  99.7 38.8 %collective-permute-start.16 = (bf16[384,768]{1,0:T(8,128)(2,1)}, bf16[384,768]{1,0:T(8,128)(2,1)}, u32[]{:S(2)}, u32[]{:S(2)}) collective-permute-start(bf16[384,768]{1,0:T(8,128)(2,1)} %collective-permute-done.12.refs_15_.refs_4_.refs_6_.refs_7_), channel_id=1, source_target_pairs={{0,2},{2,0},{1,3},{3,1},{4,6},{6,4},{5,7},{7,5},{8,10},{10,8},{9,1... | collective-permute-start | bytes 1769480 | tf_op jit(solution)/shard_map/ppermute | solution.py:882
  100.4 38.0 %collective-permute-start.18 = (bf16[384,768]{1,0:T(8,128)(2,1)}, bf16[384,768]{1,0:T(8,128)(2,1)}, u32[]{:S(2)}, u32[]{:S(2)}) collective-permute-start(bf16[384,768]{1,0:T(8,128)(2,1)} %collective-permute-done.13.refs_16_.refs_8_.refs_11_.refs_12_), channel_id=1, source_target_pairs={{0,4},{4,0},{1,5},{5,1},{2,6},{6,2},{3,7},{7,3},{8,12},{12,8},{9,1... | collective-permute-start | bytes 1769480 | tf_op jit(solution)/shard_map/ppermute | solution.py:882
  119.0 19.5 %collective-permute-start.14 = (bf16[2,256,384]{2,1,0:T(8,128)(2,1)}, bf16[2,256,384]{2,1,0:T(8,128)(2,1)}, u32[]{:S(2)}, u32[]{:S(2)}) collective-permute-start(bf16[2,256,384]{2,1,0:T(8,128)(2,1)} %get-tuple-element.122), channel_id=1, source_target_pairs={{0,2},{2,0},{1,3},{3,1},{4,6},{6,4},{5,7},{7,5},{8,10},{10,8},{9,1... | collective-permute-start | bytes 1179656 | tf_op jit(solution)/shard_map/ppermute | solution.py:882
  260.6 34.0 %collective-permute-start.27 = (bf16[2,384,768]{2,1,0:T(8,128)(2,1)}, bf16[2,384,768]{2,1,0:T(8,128)(2,1)}, u32[]{:S(2)}, u32[]{:S(2)}) collective-permute-start(bf16[2,384,768]{2,1,0:T(8,128)(2,1)} %get-tuple-element.142.refs_9_), channel_id=1, source_target_pairs={{0,4},{4,0},{1,5},{5,1},{2,6},{6,2},{3,7},{7,3},{8,12},{12,8},{9,1... | collective-permute-start | bytes 3538952 | tf_op jit(solution)/shard_map/ppermute | solution.py:882
  261.1 33.5 %collective-permute-start.28 = (bf16[2,384,768]{2,1,0:T(8,128)(2,1)}, bf16[2,384,768]{2,1,0:T(8,128)(2,1)S(1)}, u32[]{:S(2)}, u32[]{:S(2)}) collective-permute-start(bf16[2,384,768]{2,1,0:T(8,128)(2,1)} %get-tuple-element.154), channel_id=1, source_target_pairs={{0,2},{2,0},{1,3},{3,1},{4,6},{6,4},{5,7},{7,5},{8,10},{10,8},{9,1... | collective-permute-start | bytes 3538952 | tf_op jit(solution)/shard_map/ppermute | solution.py:882
  263.5 35.0 %collective-permute-start.23 = (bf16[1024,768]{1,0:T(8,128)(2,1)S(1)}, bf16[1024,768]{1,0:T(8,128)(2,1)S(1)}, u32[]{:S(2)}, u32[]{:S(2)}) collective-permute-start(bf16[1024,768]{1,0:T(8,128)(2,1)S(1)} %get-tuple-element.133), channel_id=1, source_target_pairs={{0,1},{1,0},{2,3},{3,2},{4,5},{5,4},{6,7},{7,6},{8,9},{9,8},{10,11... | collective-permute-start | bytes 4718600 | tf_op jit(solution)/shard_map/ppermute | solution.py:882
  288.0 12.9 %collective-permute-start.26 = (bf16[2,256,384]{2,1,0:T(8,128)(2,1)S(1)}, bf16[2,256,384]{2,1,0:T(8,128)(2,1)S(1)}, u32[]{:S(2)}, u32[]{:S(2)}) collective-permute-start(bf16[2,256,384]{2,1,0:T(8,128)(2,1)S(1)} %get-tuple-element.151), channel_id=1, source_target_pairs={{0,2},{2,0},{1,3},{3,1},{4,6},{6,4},{5,7},{7,5},{8,10},{10,8},{9,1... | collective-permute-start | bytes 1179656 | tf_op jit(solution)/shard_map/ppermute | solution.py:882
  296.5 22.3 %collective-permute-start.30 = (bf16[384,768]{1,0:T(8,128)(2,1)S(1)}, bf16[384,768]{1,0:T(8,128)(2,1)S(1)}, u32[]{:S(2)}, u32[]{:S(2)}) collective-permute-start(bf16[384,768]{1,0:T(8,128)(2,1)S(1)} %get-tuple-element.155.refs_4_), channel_id=1, source_target_pairs={{0,2},{2,0},{1,3},{3,1},{4,6},{6,4},{5,7},{7,5},{8,10},{10,8},{9,1... | collective-permute-start | bytes 1769480 | tf_op jit(solution)/shard_map/ppermute | solution.py:882
  297.1 24.8 %collective-permute-start.31 = (bf16[384,768]{1,0:T(8,128)(2,1)S(1)}, bf16[384,768]{1,0:T(8,128)(2,1)S(1)}, u32[]{:S(2)}, u32[]{:S(2)}) collective-permute-start(bf16[384,768]{1,0:T(8,128)(2,1)S(1)} %get-tuple-element.162), channel_id=1, source_target_pairs={{0,4},{4,0},{1,5},{5,1},{2,6},{6,2},{3,7},{7,3},{8,12},{12,8},{9,1... | collective-permute-start | bytes 1769480 | tf_op jit(solution)/shard_map/ppermute | solution.py:882
  299.2 189.7 %collective-permute-start.24 = (bf16[1024,768]{1,0:T(8,128)(2,1)S(1)}, bf16[1024,768]{1,0:T(8,128)(2,1)}, u32[]{:S(2)}, u32[]{:S(2)}) collective-permute-start(bf16[1024,768]{1,0:T(8,128)(2,1)S(1)} %add_convert_fusion.own_ref), channel_id=1, source_target_pairs={{0,2},{2,0},{1,3},{3,1},{4,6},{6,4},{5,7},{7,5},{8,10},{10,8},{9,1... | collective-permute-start | bytes 4718600 | tf_op jit(solution)/shard_map/ppermute | solution.py:882
  309.3 18.6 %collective-permute-start.29 = (bf16[1024,768]{1,0:T(8,128)(2,1)}, bf16[1024,768]{1,0:T(8,128)(2,1)}, u32[]{:S(2)}, u32[]{:S(2)}) collective-permute-start(bf16[1024,768]{1,0:T(8,128)(2,1)} %get-tuple-element.156.refs_2_), channel_id=1, source_target_pairs={{0,1},{1,0},{2,3},{3,2},{4,5},{5,4},{6,7},{7,6},{8,9},{9,8},{10,11... | collective-permute-start | bytes 4718600 | tf_op jit(solution)/shard_map/ppermute | solution.py:882
  318.3 25.4 %collective-permute-start.33 = (bf16[2,384,384]{2,1,0:T(8,128)(2,1)}, bf16[2,384,384]{2,1,0:T(8,128)(2,1)}, u32[]{:S(2)}, u32[]{:S(2)}) collective-permute-start(bf16[2,384,384]{2,1,0:T(8,128)(2,1)} %get-tuple-element.161.refs_14_), channel_id=1, source_target_pairs={{0,4},{4,0},{1,5},{5,1},{2,6},{6,2},{3,7},{7,3},{8,12},{12,8},{9,1... | collective-permute-start | bytes 1769480 | tf_op jit(solution)/shard_map/ppermute | solution.py:882
  318.8 39.9 %collective-permute-start.34 = (bf16[2,384,384]{2,1,0:T(8,128)(2,1)}, bf16[2,384,384]{2,1,0:T(8,128)(2,1)}, u32[]{:S(2)}, u32[]{:S(2)}) collective-permute-start(bf16[2,384,384]{2,1,0:T(8,128)(2,1)} %get-tuple-element.172), channel_id=1, source_target_pairs={{0,2},{2,0},{1,3},{3,1},{4,6},{6,4},{5,7},{7,5},{8,10},{10,8},{9,1... | collective-permute-start | bytes 1769480 | tf_op jit(solution)/shard_map/ppermute | solution.py:882
  323.3 55.0 %all-to-all-start.1 = ((bf16[4,96,1536]{2,1,0:T(8,128)(2,1)}), bf16[4,96,1536]{2,1,0:T(8,128)(2,1)S(1)}, u32[]{:S(2)}, u32[]{:S(2)}) async-start(bf16[4,96,1536]{2,1,0:T(8,128)(2,1)} %bitcast.23.refs_15_), calls=%async_computation.1 | async-start | bytes 2359296 | tf_op jit(solution)/shard_map/all_to_all | solution.py:950
  360.7 13.8 %collective-permute-start.35 = (bf16[384,384]{1,0:T(8,128)(2,1)}, bf16[384,384]{1,0:T(8,128)(2,1)}, u32[]{:S(2)}, u32[]{:S(2)}) collective-permute-start(bf16[384,384]{1,0:T(8,128)(2,1)} %get-tuple-element.173.refs_14_), channel_id=1, source_target_pairs={{0,2},{2,0},{1,3},{3,1},{4,6},{6,4},{5,7},{7,5},{8,10},{10,8},{9,1... | collective-permute-start | bytes 884744 | tf_op jit(solution)/shard_map/ppermute | solution.py:882
  362.2 14.0 %collective-permute-start.36 = (bf16[384,384]{1,0:T(8,128)(2,1)}, bf16[384,384]{1,0:T(8,128)(2,1)}, u32[]{:S(2)}, u32[]{:S(2)}) collective-permute-start(bf16[384,384]{1,0:T(8,128)(2,1)} %get-tuple-element.179), channel_id=1, source_target_pairs={{0,4},{4,0},{1,5},{5,1},{2,6},{6,2},{3,7},{7,3},{8,12},{12,8},{9,1... | collective-permute-start | bytes 884744 | tf_op jit(solution)/shard_map/ppermute | solution.py:882
  363.7 20.6 %collective-permute-start.32 = (bf16[1024,768]{1,0:T(8,128)(2,1)}, bf16[1024,768]{1,0:T(8,128)(2,1)}, u32[]{:S(2)}, u32[]{:S(2)}) collective-permute-start(bf16[1024,768]{1,0:T(8,128)(2,1)} %get-tuple-element.164.refs_2_), channel_id=1, source_target_pairs={{0,1},{1,0},{2,3},{3,2},{4,5},{5,4},{6,7},{7,6},{8,9},{9,8},{10,11... | collective-permute-start | bytes 4718600 | tf_op jit(solution)/shard_map/ppermute | solution.py:882
  370.4 45.5 %collective-permute-start.38 = (bf16[2,384,768]{2,1,0:T(8,128)(2,1)}, bf16[2,384,768]{2,1,0:T(8,128)(2,1)}, u32[]{:S(2)}, u32[]{:S(2)}) collective-permute-start(bf16[2,384,768]{2,1,0:T(8,128)(2,1)} %get-tuple-element.169.refs_13_), channel_id=1, source_target_pairs={{0,4},{4,0},{1,5},{5,1},{2,6},{6,2},{3,7},{7,3},{8,12},{12,8},{9,1... | collective-permute-start | bytes 3538952 | tf_op jit(solution)/shard_map/ppermute | solution.py:882
  374.4 41.5 %collective-permute-start.39 = (bf16[2,384,768]{2,1,0:T(8,128)(2,1)}, bf16[2,384,768]{2,1,0:T(8,128)(2,1)}, u32[]{:S(2)}, u32[]{:S(2)}) collective-permute-start(bf16[2,384,768]{2,1,0:T(8,128)(2,1)} %copy-done.43), channel_id=1, source_target_pairs={{0,2},{2,0},{1,3},{3,1},{4,6},{6,4},{5,7},{7,5},{8,10},{10,8},{9,1... | collective-permute-start | bytes 3538952 | tf_op jit(solution)/shard_map/ppermute | solution.py:882
  378.2 72.3 %all-to-all-start.3 = ((bf16[4,96,768]{2,1,0:T(8,128)(2,1)}), bf16[4,96,768]{2,1,0:T(8,128)(2,1)}, u32[]{:S(2)}, u32[]{:S(2)}) async-start(bf16[4,96,768]{2,1,0:T(8,128)(2,1)} %bitcast.26.refs_0_), calls=%async_computation.3 | async-start | bytes 1179648 | tf_op jit(solution)/shard_map/all_to_all | solution.py:950
  419.2 17.4 %collective-permute-start.41 = (bf16[384,768]{1,0:T(8,128)(2,1)}, bf16[384,768]{1,0:T(8,128)(2,1)}, u32[]{:S(2)}, u32[]{:S(2)}) collective-permute-start(bf16[384,768]{1,0:T(8,128)(2,1)} %get-tuple-element.187.refs_8_), channel_id=1, source_target_pairs={{0,2},{2,0},{1,3},{3,1},{4,6},{6,4},{5,7},{7,5},{8,10},{10,8},{9,1... | collective-permute-start | bytes 1769480 | tf_op jit(solution)/shard_map/ppermute | solution.py:882
  419.7 20.0 %collective-permute-start.42 = (bf16[384,768]{1,0:T(8,128)(2,1)}, bf16[384,768]{1,0:T(8,128)(2,1)}, u32[]{:S(2)}, u32[]{:S(2)}) collective-permute-start(bf16[384,768]{1,0:T(8,128)(2,1)} %get-tuple-element.192), channel_id=1, source_target_pairs={{0,4},{4,0},{1,5},{5,1},{2,6},{6,2},{3,7},{7,3},{8,12},{12,8},{9,1... | collective-permute-start | bytes 1769480 | tf_op jit(solution)/shard_map/ppermute | solution.py:882
  435.9 26.5 %collective-permute-start.43 = (bf16[2,384,384]{2,1,0:T(8,128)(2,1)}, bf16[2,384,384]{2,1,0:T(8,128)(2,1)S(1)}, u32[]{:S(2)}, u32[]{:S(2)}) collective-permute-start(bf16[2,384,384]{2,1,0:T(8,128)(2,1)} %copy-done.45), channel_id=1, source_target_pairs={{0,4},{4,0},{1,5},{5,1},{2,6},{6,2},{3,7},{7,3},{8,12},{12,8},{9,1... | collective-permute-start | bytes 1769480 | tf_op jit(solution)/shard_map/ppermute | solution.py:882
  436.6 25.8 %collective-permute-start.44 = (bf16[2,384,384]{2,1,0:T(8,128)(2,1)}, bf16[2,384,384]{2,1,0:T(8,128)(2,1)}, u32[]{:S(2)}, u32[]{:S(2)}) collective-permute-start(bf16[2,384,384]{2,1,0:T(8,128)(2,1)} %copy-done.44), channel_id=1, source_target_pairs={{0,2},{2,0},{1,3},{3,1},{4,6},{6,4},{5,7},{7,5},{8,10},{10,8},{9,1... | collective-permute-start | bytes 1769480 | tf_op jit(solution)/shard_map/ppermute | solution.py:882
  449.9 15.1 %collective-permute-start.48 = (f32[11520]{0:T(1024)S(1)}, f32[11520]{0:T(1024)S(1)}, u32[]{:S(2)}, u32[]{:S(2)}) collective-permute-start(f32[11520]{0:T(1024)S(1)} %pad_maximum_fusion.8), channel_id=1, source_target_pairs={{0,2},{2,0},{1,3},{3,1},{4,6},{6,4},{5,7},{7,5},{8,10},{10,8},{9,1... | collective-permute-start | bytes 138248 | tf_op jit(solution)/shard_map/ppermute | solution.py:882
  450.5 34.3 %all-to-all-start.4 = ((bf16[4,96,1536]{2,1,0:T(8,128)(2,1)}), bf16[4,96,1536]{2,1,0:T(8,128)(2,1)}, u32[]{:S(2)}, u32[]{:S(2)}) async-start(bf16[4,96,1536]{2,1,0:T(8,128)(2,1)} %bitcast.29.refs_6_), calls=%async_computation.4 | async-start | bytes 2359296 | tf_op jit(solution)/shard_map/all_to_all | solution.py:950
  463.5 16.5 %collective-permute-start.46 = (bf16[384,384]{1,0:T(8,128)(2,1)S(1)}, bf16[384,384]{1,0:T(8,128)(2,1)S(1)}, u32[]{:S(2)}, u32[]{:S(2)}) collective-permute-start(bf16[384,384]{1,0:T(8,128)(2,1)S(1)} %get-tuple-element.197.refs_0_), channel_id=1, source_target_pairs={{0,2},{2,0},{1,3},{3,1},{4,6},{6,4},{5,7},{7,5},{8,10},{10,8},{9,1... | collective-permute-start | bytes 884744 | tf_op jit(solution)/shard_map/ppermute | solution.py:882
  472.6 37.3 %collective-permute-start.45 = (bf16[1024,768]{1,0:T(8,128)(2,1)}, bf16[1024,768]{1,0:T(8,128)(2,1)}, u32[]{:S(2)}, u32[]{:S(2)}) collective-permute-start(bf16[1024,768]{1,0:T(8,128)(2,1)} %get-tuple-element.193.refs_4_.refs_0_.own_ref), channel_id=1, source_target_pairs={{0,2},{2,0},{1,3},{3,1},{4,6},{6,4},{5,7},{7,5},{8,10},{10,8},{9,1... | collective-permute-start | bytes 4718600 | tf_op jit(solution)/shard_map/ppermute | solution.py:882
  474.8 21.2 %collective-permute-start.51 = (f32[11520]{0:T(1024)S(1)}, f32[11520]{0:T(1024)S(1)}, u32[]{:S(2)}, u32[]{:S(2)}) collective-permute-start(f32[11520]{0:T(1024)S(1)} %add.337), channel_id=1, source_target_pairs={{0,16},{8,24},{16,0},{24,8},{1,17},{9,25},{17,1},{25,9},{2,18},{10... | collective-permute-start | bytes 138248 | tf_op jit(solution)/shard_map/ppermute | solution.py:933
  484.8 19.1 %all-to-all-start.2 = ((bf16[4,96,768]{2,1,0:T(8,128)(2,1)}), bf16[4,96,768]{2,1,0:T(8,128)(2,1)}, u32[]{:S(2)}, u32[]{:S(2)}) async-start(bf16[4,96,768]{2,1,0:T(8,128)(2,1)} %bitcast.129), calls=%async_computation.2 | async-start | bytes 1179648 | tf_op jit(solution)/shard_map/all_to_all | solution.py:950
  (114 other events, 934.8 us)
Sparse Core Ops, SparseCore 0:
  35.3 78.8 all-gather.2
  121.4 78.6 all-gather.4
